TPU v7x, 128 devices: a whole 4x4x4 slice. The times are simulated.
128 devices in a mesh: section: 16 (over y_hi, x, core), ctx: 8 (over y_lo, z).
Axes of the slice: x: 4, y: 4 (y_hi: 2, y_lo: 2; y = y_hi * 2 + y_lo), z: 4, core: 2. Of those that a mesh axis runs over, the one named last changes fastest.
Arguments:
- section_input: bfloat16 [16, 2048, 5120], P('section', 'ctx'), may hold values from -60 to 60
- last_hidden: bfloat16 [2048, 5120], P('section'), may hold values from -60 to 60
- kv_gain: float32 [5120], replicated, may hold values from 0.25 to 1.75
- query_gain: float32 [16, 5120], P('section'), may hold values from 0.25 to 1.75
- w_key: bfloat16 [5120, 3072], P(None, 'ctx'), may hold values from -1 to 1
- w_value: bfloat16 [5120, 3072], P(None, 'ctx'), may hold values from -0.078125 to 0.078125
- w_query: bfloat16 [16, 5120, 3072], P('section', None, 'ctx'), may hold values from -30 to 30
- w_out: bfloat16 [16, 3072, 5120], P('section', None, 'ctx'), may hold values from -0.625 to 0.625
- segment_ids: int32 [2048], replicated, may hold values from 0 to 3, never falling along the last dimension, each value on 1 to 1024 neighbouring positions
Outputs:
- layer_output: bfloat16 [16, 2048, 5120], P('section', None, 'ctx')
Inputs may be any that keep to these rules, and one draw needn't show every extreme that they name: `segment_ids`: documents are runs of equal ids that never fall; the longest holds exactly 1024 tokens.
All inputs are finite; a program needn't handle non-finite values.
Results may differ from a plain program's by a relative error of at most 0.005.
The roundings to bfloat16 on the way count: a program that leaves them out, or rounds other values in their place, can miss the bound.
Values may be sent and summed in bfloat16 or wider, within the bound.
No kernel may reach another device: no remote copies, remote signals or barrier semaphores. Data moves between devices by JAX's collectives and lax.ppermute only.
A program may use at most 128 MiB of HBM per device.

v0:
```python
import math

import jax
import jax.numpy as jnp
from jax import lax
from jax.sharding import PartitionSpec as P

HD = 128


def normalize(rows, gain):
    full = rows.astype(jnp.float32)
    scaled = full * lax.rsqrt(jnp.mean(full * full, axis=-1, keepdims=True) + 1e-05) * gain
    return scaled.astype(jnp.bfloat16)


def body(
    section_input, last_hidden, kv_gain, query_gain, w_key, w_value, w_query, w_out, segment_ids
):
    layer_rows = section_input[0]
    gain = query_gain[0]
    w_q = w_query[0]
    w_o = w_out[0]
    width = w_o.shape[1]
    head_cols = w_q.shape[1]
    first_col = lax.axis_index("ctx") * width
    kv_in = normalize(last_hidden, kv_gain)
    own_keys = jnp.dot(kv_in, w_key, preferred_element_type=jnp.float32).astype(jnp.bfloat16)
    own_values = jnp.dot(kv_in, w_value, preferred_element_type=jnp.float32).astype(jnp.bfloat16)
    keys, values = (
        lax.all_gather(own_keys, "section", axis=0, tiled=True),
        lax.all_gather(own_values, "section", axis=0, tiled=True),
    )
    piece = lax.all_gather(layer_rows, "ctx", axis=0, tiled=True)
    queries_part = jnp.dot(normalize(piece, gain), w_q, preferred_element_type=jnp.float32).astype(
        jnp.bfloat16
    )
    features = lax.dynamic_slice_in_dim(piece, first_col, width, 1)
    joined = jnp.concatenate([queries_part, features], axis=1)
    queries = joined[:, :head_cols]
    residual = joined[:, head_cols:]
    total_rows = queries.shape[0]
    local_heads = head_cols // HD
    block = math.gcd(total_rows, 512)
    key_heads = keys.reshape(total_rows, local_heads, HD)
    value_heads = values.reshape(total_rows, local_heads, HD)
    places = jnp.arange(total_rows, dtype=jnp.int32)
    scale = HD ** (-0.5)

    def attend(start):
        rows = lax.dynamic_slice_in_dim(queries, start, block, 0).reshape(block, local_heads, HD)
        scores = (
            jnp.einsum("qhd,khd->hqk", rows, key_heads, preferred_element_type=jnp.float32) * scale
        )
        query_places = start + jnp.arange(block, dtype=jnp.int32)
        query_docs = lax.dynamic_slice_in_dim(segment_ids, start, block, 0)
        visible = (places[None, :] <= query_places[:, None]) & (
            segment_ids[None, :] == query_docs[:, None]
        )
        scores = jnp.where(visible[None], scores, -1e30)
        top = jnp.max(scores, axis=-1, keepdims=True)
        expo = jnp.where(visible[None], jnp.exp(scores - top), 0.0)
        weights = (expo / jnp.sum(expo, axis=-1, keepdims=True)).astype(jnp.bfloat16)
        mixed = jnp.einsum("hqk,khd->qhd", weights, value_heads, preferred_element_type=jnp.float32)
        return mixed.reshape(block, head_cols).astype(jnp.bfloat16)

    starts = jnp.arange(total_rows // block, dtype=jnp.int32) * block
    context = lax.map(attend, starts).reshape(total_rows, head_cols)
    summed = jnp.dot(
        lax.all_gather(context, "ctx", axis=1, tiled=True), w_o, preferred_element_type=jnp.float32
    )
    result = (residual.astype(jnp.float32) + summed).astype(jnp.bfloat16)
    return result[None]


def solution(mesh):
    return jax.shard_map(
        body,
        mesh=mesh,
        in_specs=(
            P("section", "ctx", None),
            P("section", None),
            P(),
            P("section", None),
            P(None, "ctx"),
            P(None, "ctx"),
            P("section", None, "ctx"),
            P("section", None, "ctx"),
            P(),
        ),
        out_specs=P("section", None, "ctx"),
        check_vma=False,
    )
```

profile of v0, /device:TPU:1, one launch (start us, length us, event | category | flops | bytes accessed | tf_op | source)
XLA Modules:
  0.0 596.5 jit_solution(7061110203736118931)
XLA Ops:
  6.5 1.8 fusion.36
  8.3 4.1 convolution_convert_fusion.1
  12.5 3.6 convolution_convert_fusion
  16.2 0.7 all-gather.12.cloned.1.call-update
  17.0 45.9 %all-gather.6.cloned.1.call-done = bf16[2048,384]{1,0:T(8,128)(2,1)} async-done(((bf16[128,384]{1,0:T(8,128)(2,1)}), bf16[2048,384]{1,0:T(8,128)(2,1)}) %all-gather.6.cloned.1.call-update) | async-done | bytes 1572880 | tf_op jit(solution)/shard_map/all_gather | solution.py:31
  62.9 1.7 copy.13
  64.6 1.6 copy.16
  66.2 44.6 %all-gather.8.cloned.1.call-done = bf16[2048,384]{1,0:T(8,128)(2,1)} async-done(((bf16[128,384]{1,0:T(8,128)(2,1)}), bf16[2048,384]{1,0:T(8,128)(2,1)}) %all-gather.8.cloned.1.call-update) | async-done | bytes 1572880 | tf_op jit(solution)/shard_map/all_gather | solution.py:32
  110.8 2.6 copy.14
  113.5 207.5 %all-gather.12.cloned.1.call-done = bf16[1,2048,5120]{2,1,0:T(8,128)(2,1)} async-done(((bf16[1,256,5120]{2,1,0:T(8,128)(2,1)}), bf16[1,2048,5120]{2,1,0:T(8,128)(2,1)}) %all-gather.12.cloned.1.call-update) | async-done | bytes 20971536 | tf_op jit(solution)/shard_map/all_gather | solution.py:34
  321.0 9.1 %fusion.14 = f32[2048]{0:T(1024)S(1)} fusion(bf16[1,2048,5120]{2,1,0:T(8,128)(2,1)} %all-gather.12.cloned.1.call-done), kind=kLoop, calls=%fused_computation.21 | loop fusion | flops 31455232 | bytes 20979712 | tf_op jit(solution)/shard_map/reduce_sum | solution.py:13
  330.2 15.3 %fusion.31 = bf16[2048,384]{1,0:T(8,128)(2,1)S(1)} fusion(bf16[1,5120,384]{2,1,0:T(8,128)(2,1)S(1)} %copy-done.2, bf16[1,2048,5120]{2,1,0:T(8,128)(2,1)} %all-gather.12.cloned.1.call-done, f32[5120]{0:T(1024)S(1)} %bitcast.60, f32[2048]{0:T(1024)S(1)} %add_rsqrt_fusion), kind=kOutput, calls=%fused_computation.36 | convolution fusion | flops 8095793152 | bytes 26505216 | tf_op jit(solution)/shard_map/dot_general | solution.py:35
  345.5 98.6 %while.11 = (s32[]{:T(128)}, bf16[4,512,384]{2,1,0:T(8,128)(2,1)}, s32[4]{0:T(128)S(1)}, s32[2048]{0:T(1024)S(1)}, bf16[2048,384]{1,0:T(8,128)(2,1)S(1)}, /*inde...) while((s32[]{:T(128)}, bf16[4,512,384]{2,1,0:T(8,128)(2,1)}, ...), condition=%wide.region_5.6_spmd.clone, body=%wide.region_2.5_spmd.clone.sunk | while | flops 1635977728 | bytes 34372256 | solution.py:68
  348.2 0.6 iota_add_fusion.2
  348.8 1.0 fusion.59
  350.2 11.8 %fusion.60 = (f32[3,512]{1,0:T(4,128)S(1)}, f32[3,512,2048]{2,1,0:T(8,128)}) fusion(pred[512,2048]{1,0:T(8,128)(4,1)S(1)} %fusion.59, bf16[512,3,128]{0,2,1:T(8,128)(2,1)S(1)} %bitcast.55, bf16[2048,3,128]{2,0,1:T(8,128)(2,1)} %get-tuple-element.166), kind=kOutput, calls=%fused_computation.45.clone.1 | convolution fusion | flops 821037056 | bytes 15603712 | tf_op jit(solution)/shard_map/while/body/eval_jaxpr/sub | solution.py:62
  362.0 7.3 %fusion.61 = bf16[3,512,128]{1,2,0:T(8,128)(2,1)S(1)} fusion(bf16[2048,3,128]{0,2,1:T(8,128)(2,1)} %get-tuple-element.167, f32[3,512,2048]{2,1,0:T(8,128)} %get-tuple-element.139, f32[3,512]{1,0:T(4,128)S(1)} %get-tuple-element.140), kind=kOutput, calls=%fused_computation.13.clone.1 | convolution fusion | flops 811794432 | bytes 14555136 | tf_op jit(solution)/shard_map/while/body/eval_jaxpr/hqk,khd->qhd/dot_general | solution.py:64
  369.5 0.8 constant_dynamic-update-slice_fusion.2
  373.4 1.0 fusion.59
  374.8 11.8 %fusion.60 = (f32[3,512]{1,0:T(4,128)S(1)}, f32[3,512,2048]{2,1,0:T(8,128)}) fusion(pred[512,2048]{1,0:T(8,128)(4,1)S(1)} %fusion.59, bf16[512,3,128]{0,2,1:T(8,128)(2,1)S(1)} %bitcast.55, bf16[2048,3,128]{2,0,1:T(8,128)(2,1)} %get-tuple-element.166), kind=kOutput, calls=%fused_computation.45.clone.1 | convolution fusion | flops 821037056 | bytes 15603712 | tf_op jit(solution)/shard_map/while/body/eval_jaxpr/sub | solution.py:62
  386.6 7.3 %fusion.61 = bf16[3,512,128]{1,2,0:T(8,128)(2,1)S(1)} fusion(bf16[2048,3,128]{0,2,1:T(8,128)(2,1)} %get-tuple-element.167, f32[3,512,2048]{2,1,0:T(8,128)} %get-tuple-element.139, f32[3,512]{1,0:T(4,128)S(1)} %get-tuple-element.140), kind=kOutput, calls=%fused_computation.13.clone.1 | convolution fusion | flops 811794432 | bytes 14555136 | tf_op jit(solution)/shard_map/while/body/eval_jaxpr/hqk,khd->qhd/dot_general | solution.py:64
  394.1 0.8 constant_dynamic-update-slice_fusion.2
  398.1 1.0 fusion.59
  399.4 11.8 %fusion.60 = (f32[3,512]{1,0:T(4,128)S(1)}, f32[3,512,2048]{2,1,0:T(8,128)}) fusion(pred[512,2048]{1,0:T(8,128)(4,1)S(1)} %fusion.59, bf16[512,3,128]{0,2,1:T(8,128)(2,1)S(1)} %bitcast.55, bf16[2048,3,128]{2,0,1:T(8,128)(2,1)} %get-tuple-element.166), kind=kOutput, calls=%fused_computation.45.clone.1 | convolution fusion | flops 821037056 | bytes 15603712 | tf_op jit(solution)/shard_map/while/body/eval_jaxpr/sub | solution.py:62
  411.2 7.3 %fusion.61 = bf16[3,512,128]{1,2,0:T(8,128)(2,1)S(1)} fusion(bf16[2048,3,128]{0,2,1:T(8,128)(2,1)} %get-tuple-element.167, f32[3,512,2048]{2,1,0:T(8,128)} %get-tuple-element.139, f32[3,512]{1,0:T(4,128)S(1)} %get-tuple-element.140), kind=kOutput, calls=%fused_computation.13.clone.1 | convolution fusion | flops 811794432 | bytes 14555136 | tf_op jit(solution)/shard_map/while/body/eval_jaxpr/hqk,khd->qhd/dot_general | solution.py:64
  418.7 0.8 constant_dynamic-update-slice_fusion.2
  422.7 1.0 fusion.59
  424.0 11.8 %fusion.60 = (f32[3,512]{1,0:T(4,128)S(1)}, f32[3,512,2048]{2,1,0:T(8,128)}) fusion(pred[512,2048]{1,0:T(8,128)(4,1)S(1)} %fusion.59, bf16[512,3,128]{0,2,1:T(8,128)(2,1)S(1)} %bitcast.55, bf16[2048,3,128]{2,0,1:T(8,128)(2,1)} %get-tuple-element.166), kind=kOutput, calls=%fused_computation.45.clone.1 | convolution fusion | flops 821037056 | bytes 15603712 | tf_op jit(solution)/shard_map/while/body/eval_jaxpr/sub | solution.py:62
  435.8 7.3 %fusion.61 = bf16[3,512,128]{1,2,0:T(8,128)(2,1)S(1)} fusion(bf16[2048,3,128]{0,2,1:T(8,128)(2,1)} %get-tuple-element.167, f32[3,512,2048]{2,1,0:T(8,128)} %get-tuple-element.139, f32[3,512]{1,0:T(4,128)S(1)} %get-tuple-element.140), kind=kOutput, calls=%fused_computation.13.clone.1 | convolution fusion | flops 811794432 | bytes 14555136 | tf_op jit(solution)/shard_map/while/body/eval_jaxpr/hqk,khd->qhd/dot_general | solution.py:64
  443.3 0.8 constant_dynamic-update-slice_fusion.2
  444.2 130.2 %all-gather.10.cloned.1.call-done = bf16[2048,3072]{1,0:T(8,128)(2,1)} async-done(((bf16[2048,384]{1,0:T(8,128)(2,1)}), bf16[2048,3072]{1,0:T(8,128)(2,1)}) %all-gather.10.cloned.1.call-update) | async-done | bytes 12582928 | tf_op jit(solution)/shard_map/all_gather | solution.py:70
  574.4 15.5 %fusion.28 = bf16[1,2048,640]{2,1,0:T(8,128)(2,1)} fusion(bf16[2048,3072]{1,0:T(8,128)(2,1)} %all-gather.10.cloned.1.call-done, bf16[1,3072,640]{2,1,0:T(8,128)(2,1)} %param.18, bf16[1,2048,5120]{2,1,0:T(8,128)(2,1)} %all-gather.12.cloned.1.call-done, s32[]{:T(128)S(6)} %select_n.14), kind=kOutput, calls=%fused_computation.35 | convolution fusion | flops 8056995840 | bytes 21757956 | tf_op jit(solution)/shard_map/dot_general | solution.py:69
  (44 shorter events, 6.8 us)
Async XLA Ops:
  6.5 5.9 copy-start
  6.5 5.9 copy-start.3
  6.5 56.3 %all-gather.6.cloned.1.call-start = ((), (), s32[]{:S(2)}) async-start(), calls=%async_computation | async-start | bytes 1671168 | tf_op jit(solution)/shard_map/all_gather | solution.py:31
  12.4 98.4 %all-gather.8.cloned.1.call-start = ((), (), s32[]{:S(2)}) async-start(), calls=%async_computation.1 | async-start | bytes 1671168 | tf_op jit(solution)/shard_map/all_gather | solution.py:32
  16.1 304.8 %all-gather.12.cloned.1.call-start = ((), (), s32[]{:S(2)}) async-start(), calls=%async_computation.3 | async-start | bytes 23592960 | tf_op jit(solution)/shard_map/all_gather | solution.py:34
  16.9 557.5 %all-gather.10.cloned.1.call-start = ((), (), s32[]{:S(2)}) async-start(), calls=%async_computation.2 | async-start | bytes 14155776 | tf_op jit(solution)/shard_map/all_gather | solution.py:70
  113.5 216.7 %copy-start.4 = (f32[1,5120]{1,0:T(1,128)S(1)}, f32[1,5120]{1,0:T(1,128)}, u32[]{:S(2)}) copy-start(f32[1,5120]{1,0:T(1,128)} %param.14) | copy-start | bytes 61444
  321.0 9.2 %copy-start.2 = (bf16[1,5120,384]{2,1,0:T(8,128)(2,1)S(1)}, bf16[1,5120,384]{2,1,0:T(8,128)(2,1)}, u32[]{:S(2)}) copy-start(bf16[1,5120,384]{2,1,0:T(8,128)(2,1)} %param.17) | copy-start | bytes 11796484
  330.2 15.3 %copy-start.1 = (s32[2048]{0:T(1024)S(1)}, s32[2048]{0:T(1024)}, u32[]{:S(2)}) copy-start(s32[2048]{0:T(1024)} %param.19) | copy-start | bytes 24580
Sparse Core Ops, SparseCore 0:
  12.5 50.2 all-gather.5
  65.3 45.4 all-gather.7
  112.5 208.4 all-gather.11
  444.3 130.0 all-gather.9
where the time goes:
time: 597 us; the launch traced here: 596 us
  waiting for transfers between devices  429 us (72%)
  matrix products  115 us (19%)
  other arithmetic  17.4 us (3%)
  local copies, waits for them, and re-layouts  13.8 us (2%)
  between operations  13.2 us (2%)
  loops' own time  7.77 us (1%)
    all_gather x1, waiting for transfers between devices, body(): piece = lax.all_gather(layer_rows, 'ctx', axis=0, tiled=True)  208 us
    all_gather x1, waiting for transfers between devices, body(): lax.all_gather(context, 'ctx', axis=1, tiled=True)  130 us
    sub x4, matrix products, attend(): expo = jnp.where(visible[None], jnp.exp(scores - top), 0.0)  47.4 us
    all_gather x1, waiting for transfers between devices, body(): lax.all_gather(own_keys, 'section', axis=0, tiled=True)  45.9 us
    all_gather x1, waiting for transfers between devices, body(): lax.all_gather(own_values, 'section', axis=0, tiled=True)  44.6 us
    dot_general x4, matrix products, attend(): jnp.einsum('hqk,khd->qhd', weights, value_heads, preferred_element_type=j...  29.1 us
    dot_general x1, matrix products, body(): jnp.dot(lax.all_gather(context, 'ctx', axis=1, tiled=True), w_o, preferre...  15.5 us
    dot_general x1, matrix products, body(): jnp.dot(normalize(piece, gain), w_q, preferred_element_type=jnp.float32)  15.3 us
  transfers between devices with their start and end apart: 4, of which 4 were waited for; matrix products, arithmetic and copies ran while one was open for 2% of the time, Pallas kernels for 0%

commit v1 on v0

v1 whole, which is shorter than its diff:
```python
import jax
import jax.numpy as jnp
import numpy as np
from jax import lax
from jax.experimental import pallas as pl
from jax.experimental.pallas import tpu as pltpu
from jax.sharding import PartitionSpec as P

HD = 128
RB = 256
BF = jnp.bfloat16
F32 = jnp.float32
AXES = ("section", "ctx")
MIB = 1 << 20

PLACE = (((0, 1, 2, 3), (4, 5, 6, 7)), ((1, 0, 4, 5), (2, 3, 7, 6)))
SPOT = tuple(
    tuple(next((h, r) for h in range(2) for r in range(4) if table[h][r] == c) for c in range(8))
    for table in PLACE
)


def moves(step):
    pairs = []
    for s in range(16):
        for c in range(8):
            core = s % 2
            half, spot = SPOT[core][c]
            yh, x, k, h, r = step(s // 8, s // 2 % 4, core, half, spot)
            if k == core:
                place = PLACE[core][h][r % 4]
            else:
                place = c
            pairs.append((s * 8 + c, (yh * 8 + x % 4 * 2 + k) * 8 + place))
    return pairs


NEXT = moves(lambda yh, x, k, h, r: (yh, x, k, h, r + 1))
PREV = moves(lambda yh, x, k, h, r: (yh, x, k, h, r - 1))
PARTNER = moves(lambda yh, x, k, h, r: (yh, x, k, 1 - h, r))
CORE = moves(lambda yh, x, k, h, r: (yh, x, 1 - k, h, r))
FAR_Y = moves(lambda yh, x, k, h, r: (1 - yh, x, k, h, r))
X_NEXT = moves(lambda yh, x, k, h, r: (yh, x + 1, k, h, r))
X_PREV = moves(lambda yh, x, k, h, r: (yh, x - 1, k, h, r))
X_FAR = moves(lambda yh, x, k, h, r: (yh, x + 2, k, h, r))


def send(value, pairs):
    return lax.ppermute(value, AXES, pairs)


def normalize(rows, gain):
    full = rows.astype(F32)
    scaled = full * lax.rsqrt(jnp.mean(full * full, axis=-1, keepdims=True) + 1e-05) * gain
    return scaled.astype(BF)


def project_kernel(pieces, slot, has_prior, meta, *refs):
    xs = refs[:pieces]
    gain, w = refs[pieces : pieces + 2]
    normed, q, res_own, res_other = refs[-4:]
    row = 0
    for x in xs:
        rows, step = x.shape[0], 32
        base = row

        def norm_rows(i, _, x=x, base=base):
            at = pl.multiple_of(i * step, step)
            full = x[pl.ds(at, step), :].astype(F32)
            mean = jnp.mean(full * full, axis=-1, keepdims=True)
            normed[0, pl.ds(base + at, step), :] = (
                full * lax.rsqrt(mean + 1e-05) * gain[...]
            ).astype(BF)
            return 0

        lax.fori_loop(0, rows // step, norm_rows, 0)
        width = res_own.shape[2]
        for k, out in ((0, res_own), (1, res_other)):
            first = pl.multiple_of(meta[k] * width, 128)
            out[0, row : row + rows, :] = x[:, pl.ds(first, width)]
        row += rows
    q[0] = jnp.dot(normed[0], w[...], preferred_element_type=F32).astype(BF)


def project(meta, xs, gain, w, slot, prior):
    d, n = w.shape
    width = 640
    shapes = [(4, RB, d), (4, RB, n), (4, RB, width), (4, RB, width)]
    whole = lambda a: pl.BlockSpec(a.shape, lambda i, m, nd=a.ndim: (0,) * nd)
    ins = list(xs) + [gain, w]
    specs = [whole(a) for a in ins]
    aliases = {}
    if prior is not None:
        for k, a in enumerate(prior):
            aliases[1 + len(ins)] = k
            ins.append(a)
            specs.append(pl.BlockSpec(memory_space=pl.ANY))

    def kernel(meta, *refs):
        project_kernel(len(xs), slot, prior is not None, meta, *refs)

    return pl.pallas_call(
        kernel,
        grid_spec=pltpu.PrefetchScalarGridSpec(
            num_scalar_prefetch=1,
            grid=(1,),
            in_specs=specs,
            out_specs=[pl.BlockSpec((1,) + s[1:], lambda i, m: (slot, 0, 0)) for s in shapes],
        ),
        out_shape=[jax.ShapeDtypeStruct(s, BF) for s in shapes],
        input_output_aliases=aliases,
        compiler_params=pltpu.CompilerParams(vmem_limit_bytes=40 * MIB),
        cost_estimate=pl.CostEstimate(
            flops=2 * RB * d * n, bytes_accessed=2 * (3 * RB * d + d * n), transcendentals=0
        ),
    )(meta, *ins)


def more_queries_kernel(n_ref, w_ref, q_ref):
    q_ref[0] = jnp.dot(n_ref[0], w_ref[...], preferred_element_type=F32).astype(BF)


def more_queries(normed, w):
    d, n = w.shape
    return pl.pallas_call(
        more_queries_kernel,
        grid=(4,),
        in_specs=[
            pl.BlockSpec((1, RB, d), lambda i: (i, 0, 0)),
            pl.BlockSpec((d, n), lambda i: (0, 0)),
        ],
        out_specs=pl.BlockSpec((1, RB, n), lambda i: (i, 0, 0)),
        out_shape=jax.ShapeDtypeStruct((4, RB, n), BF),
        compiler_params=pltpu.CompilerParams(vmem_limit_bytes=32 * MIB),
        cost_estimate=pl.CostEstimate(
            flops=8 * RB * d * n, bytes_accessed=2 * (4 * RB * d + d * n), transcendentals=0
        ),
    )(normed, w)


def attend_kernel(
    slots, blocks, firsts, where_x, q_own, q_other, kv_own, kv_other, seg_col, seg_row, out,
    scores, tops, sums,
):
    t = pl.program_id(0)
    block = blocks[t]
    first = firsts[t]
    count = block - first + 1
    x = where_x[0]
    heads = q_own.shape[2] // HD
    factor = HD ** (-0.5) * 1.4426950408889634
    pairs = [(src, i) for src in range(2) for i in range(heads)]
    qs = (q_own, q_other)
    kvs = (kv_own, kv_other)

    def place(i):
        kb = first + i
        j = lax.rem(lax.rem(kb, 4) - x + 4, 4)
        return kb, j, kb // 4

    tops[...] = jnp.full(tops.shape, -1e30, F32)
    sums[...] = jnp.zeros(sums.shape, F32)
    q_doc = seg_col[block]
    row_at = block * RB + lax.broadcasted_iota(jnp.int32, (RB, RB), 0)
    col_at = lax.broadcasted_iota(jnp.int32, (RB, RB), 1)

    def score(i, _):
        kb, j, y = place(i)
        visible = (q_doc == seg_row[kb]) & (kb * RB + col_at <= row_at)
        for n, (src, h) in enumerate(pairs):
            cols = slice(h * HD, (h + 1) * HD)
            s = lax.dot_general(
                qs[src][0, :, cols], kvs[src][j, y, :, cols], (((1,), (1,)), ((), ())),
                preferred_element_type=F32,
            )
            s = jnp.where(visible, s, -1e30)
            scores[n, i] = s
            tops[n] = jnp.maximum(tops[n], jnp.maximum(s[:, :HD], s[:, HD:]))
        return 0

    lax.fori_loop(0, count, score, 0)
    for n in range(len(pairs)):
        tops[n] = jnp.broadcast_to(jnp.max(tops[n], axis=-1, keepdims=True), (RB, HD))

    def expo(i, _):
        for n in range(len(pairs)):
            s = scores[n, i]
            top = tops[n]
            left = jnp.exp2((s[:, :HD] - top) * factor)
            right = jnp.exp2((s[:, HD:] - top) * factor)
            scores[n, i, :, :HD] = left
            scores[n, i, :, HD:] = right
            sums[n] += left + right
        return 0

    lax.fori_loop(0, count, expo, 0)
    for n in range(len(pairs)):
        total = jnp.sum(sums[n], axis=-1, keepdims=True)
        sums[n] = jnp.broadcast_to(1.0 / total, (RB, HD))
        tops[n] = jnp.zeros((RB, HD), F32)

    def mix(i, _):
        kb, j, y = place(i)
        for n, (src, h) in enumerate(pairs):
            cols = slice((heads + h) * HD, (heads + h + 1) * HD)
            e = scores[n, i]
            inv = sums[n]
            weights = jnp.concatenate([e[:, :HD] * inv, e[:, HD:] * inv], axis=1).astype(BF)
            tops[n] += jnp.dot(weights, kvs[src][j, y, :, cols], preferred_element_type=F32)
        return 0

    lax.fori_loop(0, count, mix, 0)
    for n in range(len(pairs)):
        out[:, n * HD : (n + 1) * HD] = tops[n].astype(BF)


def attend(slots, blocks, firsts, where_x, q_own, q_other, kv_own, kv_other, seg_col, seg_row):
    n = q_own.shape[2]
    heads = n // HD
    whole = lambda a: pl.BlockSpec(a.shape, lambda t, *s, nd=a.ndim: (0,) * nd)
    q_spec = pl.BlockSpec((1, RB, n), lambda t, slots, *s: (slots[t], 0, 0))
    return pl.pallas_call(
        attend_kernel,
        grid_spec=pltpu.PrefetchScalarGridSpec(
            num_scalar_prefetch=4,
            grid=(2,),
            in_specs=[
                q_spec, q_spec, whole(kv_own), whole(kv_other), whole(seg_col), whole(seg_row)
            ],
            out_specs=pl.BlockSpec((RB, 2 * n), lambda t, *s: (t, 0)),
            scratch_shapes=[
                pltpu.VMEM((2 * heads, 5, RB, RB), F32),
                pltpu.VMEM((2 * heads, RB, HD), F32),
                pltpu.VMEM((2 * heads, RB, HD), F32),
            ],
        ),
        out_shape=jax.ShapeDtypeStruct((2 * RB, 2 * n), BF),
        compiler_params=pltpu.CompilerParams(vmem_limit_bytes=40 * MIB),
        cost_estimate=pl.CostEstimate(
            flops=4 * 2 * RB * 768 * 2 * n, bytes_accessed=8 * MIB, transcendentals=2 * RB * 768 * 6
        ),
    )(slots, blocks, firsts, where_x, q_own, q_other, kv_own, kv_other, seg_col, seg_row)


def finish_kernel(rows_of, slots, targets, c0, c1, c2a, c2b, c3, w, res, *refs):
    out = refs[-1]
    t = pl.program_id(0)
    far = jnp.where(t == 0, c2a[...], c2b[...])
    n = w.shape[1]
    total = jnp.zeros((RB, w.shape[2]), F32)
    for j, c in enumerate((c0[...], c1[...], far, c3[...])):
        for k in range(2):
            total += jnp.dot(
                c[:, k * n : (k + 1) * n], w[rows_of[2 * j + k]], preferred_element_type=F32
            )
    out[0] = (res[0].astype(F32) + total).astype(BF)


def finish(rows_of, slots, targets, parts, w, res, blocks, prior=None):
    k8, n, width = w.shape
    tile = pl.BlockSpec((RB, 2 * n), lambda t, *s: (t, 0))
    fixed = pl.BlockSpec((RB, 2 * n), lambda t, *s: (0, 0))
    ins = list(parts) + [w, res]
    specs = [tile, tile, fixed, fixed, tile]
    specs.append(pl.BlockSpec(w.shape, lambda t, *s: (0, 0, 0)))
    specs.append(pl.BlockSpec((1, RB, width), lambda t, r, slots, g: (slots[t], 0, 0)))
    aliases = {}
    if prior is not None:
        aliases[3 + len(ins)] = 0
        ins.append(prior)
        specs.append(pl.BlockSpec(memory_space=pl.ANY))
    return pl.pallas_call(
        finish_kernel,
        grid_spec=pltpu.PrefetchScalarGridSpec(
            num_scalar_prefetch=3,
            grid=(2,),
            in_specs=specs,
            out_specs=pl.BlockSpec((1, RB, width), lambda t, r, s, targets: (targets[t], 0, 0)),
        ),
        out_shape=jax.ShapeDtypeStruct((blocks, RB, width), BF),
        input_output_aliases=aliases,
        compiler_params=pltpu.CompilerParams(vmem_limit_bytes=32 * MIB),
        cost_estimate=pl.CostEstimate(
            flops=4 * RB * k8 * n * width, bytes_accessed=8 * MIB, transcendentals=0
        ),
    )(rows_of, slots, targets, *ins)


def place_kernel(targets, got, prior, out):
    out[...] = got[...]


def place(targets, got, prior):
    count, rows, width = got.shape
    return pl.pallas_call(
        place_kernel,
        grid_spec=pltpu.PrefetchScalarGridSpec(
            num_scalar_prefetch=1,
            grid=(count,),
            in_specs=[
                pl.BlockSpec((1, rows, width), lambda t, g: (t, 0, 0)),
                pl.BlockSpec(memory_space=pl.ANY),
            ],
            out_specs=pl.BlockSpec((1, rows, width), lambda t, targets: (targets[t], 0, 0)),
        ),
        out_shape=jax.ShapeDtypeStruct(prior.shape, BF),
        input_output_aliases={2: 0},
    )(targets, got, prior)


def body(
    section_input, last_hidden, kv_gain, query_gain, w_key, w_value, w_query, w_out, segment_ids
):
    section = lax.axis_index("section")
    c = lax.axis_index("ctx")
    core = section % 2
    x_at = section // 2 % 4
    y_hi = section // 8
    spot = jnp.array(SPOT, jnp.int32)[core, c]
    half, r = spot[0], spot[1]
    place_of = jnp.array(PLACE, jnp.int32)[core]
    mine, theirs = place_of[half], place_of[1 - half]

    x0 = section_input[0]
    w_q = w_query[0]
    w_o = w_out[0]
    gain = query_gain

    xp = send(x0, NEXT)
    xn = send(x0, PREV)
    w_q2 = send(w_q, PARTNER)

    kv_in = normalize(last_hidden, kv_gain)
    own_k = jnp.dot(kv_in, w_key, preferred_element_type=F32).astype(BF)
    own_v = jnp.dot(kv_in, w_value, preferred_element_type=F32).astype(BF)
    kv = jnp.concatenate([own_k, own_v], axis=1)
    kv_far = send(kv, FAR_Y)
    pair = jnp.where(y_hi == 0, jnp.stack([kv, kv_far]), jnp.stack([kv_far, kv]))
    pair2 = send(pair, CORE)
    piece = jnp.where(
        core == 0, jnp.concatenate([pair, pair2], axis=1), jnp.concatenate([pair2, pair], axis=1)
    )
    piece2 = send(piece, PARTNER)

    def spread(p):
        return jnp.stack([p, send(p, X_PREV), send(p, X_FAR), send(p, X_NEXT)])

    kv_own = spread(piece)
    kv_other = spread(piece2)

    xo_a = send(xp[: RB // 2], NEXT)
    xo_b = send(xn[RB // 2 :], PREV)
    w_o2 = send(w_o, PARTNER)

    cols = jnp.stack([mine[r], theirs[r]])
    state = project(cols, [x0], gain, w_q, 0, None)
    state = project(cols, [xn], gain, w_q, 1, state)
    state = project(cols, [xp], gain, w_q, 3, state)
    normed, q_own, res_own, res_other = project(cols, [xo_a, xo_b], gain, w_q, 2, state)
    q_other = more_queries(normed, w_q2)

    ids = segment_ids.reshape(8, RB)
    starts = jnp.sum(segment_ids[None, :] < ids[:, :1], axis=1, dtype=jnp.int32) // RB
    starts = jnp.maximum(starts, jnp.arange(8, dtype=jnp.int32) - 4)
    seg_col = segment_ids.reshape(8, RB, 1)
    seg_row = segment_ids.reshape(8, 1, RB)
    xs = x_at[None]
    w_o_r = w_o.reshape(8, 384, -1)
    w_o2_r = w_o2.reshape(8, 384, -1)
    ring = (r + jnp.arange(4, dtype=jnp.int32)) % 4
    rows_of = jnp.stack([mine[ring], theirs[ring]], axis=1).reshape(8)

    order = jnp.arange(2, dtype=jnp.int32)
    result = None
    for chunk in range(2):
        spots = order + 2 * chunk
        slots = (spots - r + 4) % 4
        blocks = mine[2 * chunk : 2 * chunk + 2]
        others = theirs[2 * chunk : 2 * chunk + 2]
        own = attend(
            slots, blocks, starts[blocks], xs, q_own, q_other, kv_own, kv_other, seg_col, seg_row
        )
        cp = send(own, NEXT)
        cn = send(own, PREV)
        co_a = send(cp[:RB], NEXT)
        co_b = send(cn[RB:], PREV)
        parts = (own, cn, co_a, co_b, cp)
        sent = send(finish(rows_of, slots, order, parts, w_o2_r, res_other, 2), PARTNER)
        result = finish(rows_of, slots, blocks, parts, w_o_r, res_own, 8, result)
        result = place(others, sent, result)
    return result.reshape(1, 8 * RB, -1)


def solution(mesh):
    return jax.shard_map(
        body,
        mesh=mesh,
        in_specs=(
            P("section", "ctx", None),
            P("section", None),
            P(),
            P("section", None),
            P(None, "ctx"),
            P(None, "ctx"),
            P("section", None, "ctx"),
            P("section", None, "ctx"),
            P(),
        ),
        out_specs=P("section", None, "ctx"),
        check_vma=False,
    )
```

time: 597 us -> 301 us (0.50)
  waiting for transfers between devices: 429 us -> 127 us
  matrix products: 115 us -> 4.48 us
  Pallas kernels: 0 us -> 68.5 us
  starting transfers between devices: 0.12 us -> 37 us
  local copies, waits for them, and re-layouts: 13.8 us -> 41.7 us
  loops' own time: 7.77 us -> 0 us
  between operations: 13.2 us -> 5.53 us
    all_gather x4 -> x0, waiting for transfers between devices: 428 us -> none  [the longest x1 208 us: body(): piece = lax.all_gather(layer_rows, 'ctx', axis=0, tiled=True)]
    ppermute x0 -> x25, waiting for transfers between devices: none -> 127 us  [send(): return lax.ppermute(value, AXES, pairs)]
    pallas_call x0 -> x13, Pallas kernels: none -> 68.5 us  [the longest x4 25.7 us: finish(): pl.pallas_call(finish_kernel, grid_spec=pltpu.PrefetchScalarGridSpec(num_...]
    dot_general x8 -> x2, matrix products: 67.7 us -> 4.48 us  [the longest x1 3.57 us: body(): own_v = jnp.dot(kv_in, w_value, preferred_element_type=F32).astype(BF)]
    sub x4 -> x0, matrix products: 47.4 us -> none  [attend(): expo = jnp.where(visible[None], jnp.exp(scores - top), 0.0)]
    ppermute x0 -> x25, starting transfers between devices: none -> 37 us  [send(): return lax.ppermute(value, AXES, pairs)]
    unnamed x11 -> x92, local copies, waits for them, and re-layouts: 1.62 us -> 25.1 us
    slice x0 -> x10, local copies, waits for them, and re-layouts: none -> 10.8 us  [the longest x1 3 us: body(): xo_b = send(xn[RB // 2:], PREV)]
  transfers between devices with their start and end apart: 4 -> 25, of which waited for: 4 -> 11; matrix products, arithmetic and copies ran while one was open for 2% -> 12% of each run, Pallas kernels for 0% -> 22%
where the time goes in v1:
time: 301 us; the launch traced here: 298 us
  waiting for transfers between devices  127 us (42%)
  Pallas kernels  68.5 us (23%)
  local copies, waits for them, and re-layouts  41.7 us (14%)
  starting transfers between devices  37 us (12%)
  other arithmetic  14.3 us (5%)
  between operations  5.53 us (2%)
  matrix products  4.48 us (1%)
    ppermute x25, waiting for transfers between devices, send(): return lax.ppermute(value, AXES, pairs)  127 us
    ppermute x25, starting transfers between devices, send(): return lax.ppermute(value, AXES, pairs)  37 us
    pallas_call x4, Pallas kernels, finish(): pl.pallas_call(finish_kernel, grid_spec=pltpu.PrefetchScalarGridSpec(num_...  25.7 us
    unnamed x92, local copies, waits for them, and re-layouts  25.1 us
    pallas_call x4, Pallas kernels, project(): pl.pallas_call(kernel, grid_spec=pltpu.PrefetchScalarGridSpec(num_scalar_...  18.7 us
    pallas_call x2, Pallas kernels, attend(): pl.pallas_call(attend_kernel, grid_spec=pltpu.PrefetchScalarGridSpec(num_...  10.7 us
    pallas_call x1, Pallas kernels, more_queries(): pl.pallas_call(more_queries_kernel, grid=(4,), in_specs=[pl.BlockSpec((1,...  8.25 us
  transfers between devices with their start and end apart: 25, of which 11 were waited for; matrix products, arithmetic and copies ran while one was open for 12% of the time, Pallas kernels for 22%

profile of v1, /device:TPU:1, one launch (start us, length us, event | category | flops | bytes accessed | tf_op | source)
XLA Modules:
  0.0 298.5 jit_solution(18128592544990579462)
XLA Ops:
  0.0 2.5 collective-permute-start.2
  4.2 3.6 %convolution_convert_fusion = bf16[128,384]{1,0:T(8,128)(2,1)S(1)} fusion(bf16[5120,384]{1,0:T(8,128)(2,1)} %param.16, bf16[128,5120]{1,0:T(8,128)(2,1)} %param.12, f32[5120]{0:T(1024)} %param.13, f32[128]{0:T(128)S(1)} %add_rsqrt_fusion), kind=kOutput, calls=%fused_computation.11 | convolution fusion | flops 505987072 | bytes 5362176 | tf_op jit(solution)/shard_map/dot_general | solution.py:335
  9.2 3.0 %collective-permute-start.5 = (bf16[128,768]{1,0:T(8,128)(2,1)S(1)}, bf16[128,768]{1,0:T(8,128)(2,1)S(1)}, u32[]{:S(2)}, u32[]{:S(2)}) collective-permute-start(bf16[128,768]{1,0:T(8,128)(2,1)S(1)} %get-tuple-element.38), channel_id=1, source_target_pairs={{0,64},{1,65},{2,66},{3,67},{4,68},{5,69},{6,70},{7,71},{8,72},{9,... | collective-permute-start | bytes 589832 | tf_op jit(solution)/shard_map/ppermute | solution.py:49
  12.2 26.7 %collective-permute-done.5 = bf16[128,768]{1,0:T(8,128)(2,1)S(1)} collective-permute-done((bf16[128,768]{1,0:T(8,128)(2,1)S(1)}, bf16[128,768]{1,0:T(8,128)(2,1)S(1)}, u32[]{:S(2)}, u32[]{:S(2)}) %collective-permute-start.5) | collective-permute-done | bytes 196640 | tf_op jit(solution)/shard_map/ppermute | solution.py:49
  40.4 3.6 %collective-permute-start.4 = (bf16[5120,384]{1,0:T(8,128)(2,1)}, bf16[5120,384]{1,0:T(8,128)(2,1)}, u32[]{:S(2)}, u32[]{:S(2)}) collective-permute-start(bf16[5120,384]{1,0:T(8,128)(2,1)} %bitcast.49), channel_id=1, source_target_pairs={{0,4},{1,5},{2,6},{3,7},{4,0},{5,1},{6,2},{7,3},{8,11},{9,10},{10,... | collective-permute-start | bytes 11796488 | tf_op jit(solution)/shard_map/ppermute | solution.py:49
  43.9 2.4 maximum_select_fusion.1
  48.2 2.5 collective-permute-start.7
  50.7 45.1 %collective-permute-done.10 = bf16[2,256,768]{2,1,0:T(8,128)(2,1)} collective-permute-done((bf16[2,256,768]{2,1,0:T(8,128)(2,1)}, bf16[2,256,768]{2,1,0:T(8,128)(2,1)}, u32[]{:S(2)}, u32[]{:S(2)}) %collective-permute-start.10) | collective-permute-done | bytes 786464 | tf_op jit(solution)/shard_map/ppermute | solution.py:49
  95.7 2.7 collective-permute-start.8
  106.3 2.8 collective-permute-start.18
  109.0 8.1 %collective-permute-done.8 = bf16[2,256,768]{2,1,0:T(8,128)(2,1)} collective-permute-done((bf16[2,256,768]{2,1,0:T(8,128)(2,1)}, bf16[2,256,768]{2,1,0:T(8,128)(2,1)}, u32[]{:S(2)}, u32[]{:S(2)}) %collective-permute-start.8) | collective-permute-done | bytes 786464 | tf_op jit(solution)/shard_map/ppermute | solution.py:49
  124.0 3.0 %slice.86 = bf16[128,5120]{1,0:T(8,128)(2,1)} slice(bf16[256,5120]{1,0:T(8,128)(2,1)} %collective-permute-done.2.refs_0_), slice={[128:256], [0:5120]} | slice | bytes 2621440 | tf_op jit(solution)/shard_map/slice | solution.py:352
  127.0 10.2 %collective-permute-done.9 = bf16[2,256,768]{2,1,0:T(8,128)(2,1)S(1)} collective-permute-done((bf16[2,256,768]{2,1,0:T(8,128)(2,1)}, bf16[2,256,768]{2,1,0:T(8,128)(2,1)S(1)}, u32[]{:S(2)}, u32[]{:S(2)}) %collective-permute-start.9) | collective-permute-done | bytes 786464 | tf_op jit(solution)/shard_map/ppermute | solution.py:49
  137.3 17.8 %collective-permute-done.12 = bf16[2,256,768]{2,1,0:T(8,128)(2,1)S(1)} collective-permute-done((bf16[2,256,768]{2,1,0:T(8,128)(2,1)}, bf16[2,256,768]{2,1,0:T(8,128)(2,1)S(1)}, u32[]{:S(2)}, u32[]{:S(2)}) %collective-permute-start.12) | collective-permute-done | bytes 786464 | tf_op jit(solution)/shard_map/ppermute | solution.py:49
  157.7 3.7 %shard_map.109 = (bf16[4,256,5120]{2,1,0:T(8,128)(2,1)}, bf16[4,256,384]{2,1,0:T(8,128)(2,1)S(1)}, bf16[4,256,640]{2,1,0:T(8,128)(2,1)S(1)}, bf16[4,256,640]{2,1,0:T(8,128)(2,1)S(1)}) custom-call(s32[2]{0:T(128)S(1)} %pad_add_fusion.1.meta, bf16[256,5120]{1,0:T(8,128)(2,1)S(1)} %bitcast.59, f32[1,5120]{1,0:T(1,128)S(1)} %copy-done.30, ...), custom_call_target="tpu_custom_call" | custom-call | flops 1006632960 | bytes 11796480 | tf_op jit(solution)/shard_map/pallas_call | solution.py:102
  168.4 4.3 %collective-permute-done.13 = bf16[2,256,768]{2,1,0:T(8,128)(2,1)} collective-permute-done((bf16[2,256,768]{2,1,0:T(8,128)(2,1)}, bf16[2,256,768]{2,1,0:T(8,128)(2,1)}, u32[]{:S(2)}, u32[]{:S(2)}) %collective-permute-start.13) | collective-permute-done | bytes 786464 | tf_op jit(solution)/shard_map/ppermute | solution.py:49
  175.4 5.9 %shard_map.110 = (bf16[4,256,5120]{2,1,0:T(8,128)(2,1)}, bf16[4,256,384]{2,1,0:T(8,128)(2,1)S(1)}, bf16[4,256,640]{2,1,0:T(8,128)(2,1)S(1)}, bf16[4,256,640]{2,1,0:T(8,128)(2,1)S(1)}) custom-call(s32[2]{0:T(128)S(1)} %pad_add_fusion.1.meta, ...), custom_call_target="tpu_custom_call", output_to_operand_aliasing={{0}: (4, {}), {1}: (5, {}), {2}: (6, {}), {3}: (7, {})} | custom-call | flops 1006632960 | bytes 11796480 | tf_op jit(solution)/shard_map/pallas_call | solution.py:102
  181.3 3.8 %shard_map.111 = (bf16[4,256,5120]{2,1,0:T(8,128)(2,1)}, bf16[4,256,384]{2,1,0:T(8,128)(2,1)S(1)}, bf16[4,256,640]{2,1,0:T(8,128)(2,1)S(1)}, bf16[4,256,640]{2,1,0:T(8,128)(2,1)S(1)}) custom-call(s32[2]{0:T(128)S(1)} %pad_add_fusion.1.meta, ...), custom_call_target="tpu_custom_call", output_to_operand_aliasing={{0}: (4, {}), {1}: (5, {}), {2}: (6, {}), {3}: (7, {})} | custom-call | flops 1006632960 | bytes 11796480 | tf_op jit(solution)/shard_map/pallas_call | solution.py:102
  185.0 5.4 %shard_map.112 = (bf16[4,256,5120]{2,1,0:T(8,128)(2,1)}, bf16[4,256,384]{2,1,0:T(8,128)(2,1)S(1)}, bf16[4,256,640]{2,1,0:T(8,128)(2,1)S(1)}, bf16[4,256,640]{2,1,0:T(8,128)(2,1)S(1)}) custom-call(s32[2]{0:T(128)S(1)} %pad_add_fusion.1.meta, ...), custom_call_target="tpu_custom_call", output_to_operand_aliasing={{0}: (5, {}), {1}: (6, {}), {2}: (7, {}), {3}: (8, {})} | custom-call | flops 1006632960 | bytes 11796480 | tf_op jit(solution)/shard_map/pallas_call | solution.py:102
  190.4 4.0 %copy-done = bf16[4,256,5120]{2,1,0:T(8,128)(2,1)S(1)} copy-done((bf16[4,256,5120]{2,1,0:T(8,128)(2,1)S(1)}, bf16[4,256,5120]{2,1,0:T(8,128)(2,1)}, u32[]{:S(2)}) %copy-start) | copy-done | bytes 10485784
  194.4 8.3 %shard_map.113.q_other = bf16[4,256,384]{2,1,0:T(8,128)(2,1)S(1)} custom-call(bf16[4,256,5120]{2,1,0:T(8,128)(2,1)S(1)} %copy-done, bf16[5120,384]{1,0:T(8,128)(2,1)} %collective-permute-done.4.w_ref), custom_call_target="tpu_custom_call" | custom-call | flops 4026531840 | bytes 14417920 | tf_op jit(solution)/shard_map/pallas_call | solution.py:125
  204.2 5.7 %shard_map.116.c0 = bf16[512,768]{1,0:T(8,128)(2,1)} custom-call(s32[2]{0:T(128)S(1)} %and_select_fusion.slots, s32[2]{0:T(128)S(1)} %get-tuple-element.45.blocks.targets, s32[2]{0:T(128)S(1)} %gather_fusion.3, s32[1]{0:T(128)} %bitcast.11.where_x, bf16[4,256,384]{2,1,0:T(8,128)(2,1)S(1)} %get-tuple-element.33.q_own, ...), custom_call_target="tpu_custom_call" | custom-call | flops 1207959552 | bytes 8388608 | tf_op jit(solution)/shard_map/pallas_call | solution.py:222
  218.8 5.0 %shard_map.114.c0 = bf16[512,768]{1,0:T(8,128)(2,1)S(1)} custom-call(s32[2]{0:T(128)S(1)} %and_select_fusion.2.slots, s32[2]{0:T(128)S(1)} %get-tuple-element.46.blocks.targets, s32[2]{0:T(128)S(1)} %gather_fusion.2, s32[1]{0:T(128)} %bitcast.11.where_x, bf16[4,256,384]{2,1,0:T(8,128)(2,1)S(1)} %get-tuple-element.33.q_own, ...), custom_call_target="tpu_custom_call" | custom-call | flops 1207959552 | bytes 8388608 | tf_op jit(solution)/shard_map/pallas_call | solution.py:222
  233.2 10.3 %collective-permute-done.15.c3 = bf16[512,768]{1,0:T(8,128)(2,1)S(1)} collective-permute-done((bf16[512,768]{1,0:T(8,128)(2,1)S(1)}, bf16[512,768]{1,0:T(8,128)(2,1)S(1)}, u32[]{:S(2)}, u32[]{:S(2)}) %collective-permute-start.15) | collective-permute-done | bytes 786464 | tf_op jit(solution)/shard_map/ppermute | solution.py:49
  249.4 2.6 collective-permute-done.22.c2a
  255.9 6.7 %shard_map.117 = bf16[2,256,640]{2,1,0:T(8,128)(2,1)S(1)} custom-call(s32[8]{0:T(128)S(1)} %reshape.262.rows_of, s32[2]{0:T(128)S(1)} %and_select_fusion.slots, s32[2]{0:T(128)S(1)} %iota.21.targets, bf16[512,768]{1,0:T(8,128)(2,1)} %shard_map.116.c0, bf16[512,768]{1,0:T(8,128)(2,1)} %collective-permute-done.20.c1, bf16[256,768]{1,0:T(8,128)(2,1)S(1)} %copy-done.25, ...), custom_call_target="tpu_custom_call" | custom-call | flops 2013265920 | bytes 8388608 | tf_op jit(solution)/shard_map/pallas_call | solution.py:272
  262.6 6.9 %collective-permute-start.24 = (bf16[2,256,640]{2,1,0:T(8,128)(2,1)S(1)}, bf16[2,256,640]{2,1,0:T(8,128)(2,1)S(1)}, u32[]{:S(2)}, u32[]{:S(2)}) collective-permute-start(bf16[2,256,640]{2,1,0:T(8,128)(2,1)S(1)} %shard_map.117), channel_id=1, source_target_pairs={{0,4},{1,5},{2,6},{3,7},{4,0},{5,1},{6,2},{7,3},{8,11},{9,10},{10,... | collective-permute-start | bytes 1966088 | tf_op jit(solution)/shard_map/ppermute | solution.py:49
  269.6 7.3 %shard_map.115 = bf16[2,256,640]{2,1,0:T(8,128)(2,1)} custom-call(s32[8]{0:T(128)S(1)} %reshape.262.rows_of, s32[2]{0:T(128)S(1)} %and_select_fusion.2.slots, s32[2]{0:T(128)S(1)} %iota.18.targets, bf16[512,768]{1,0:T(8,128)(2,1)S(1)} %copy-done.12, bf16[512,768]{1,0:T(8,128)(2,1)S(1)} %copy-done.21, bf16[256,768]{1,0:T(8,128)(2,1)} %collective-permute-done.16.c2a, ...), custom_call_target="tpu_custom_call" | custom-call | flops 2013265920 | bytes 8388608 | tf_op jit(solution)/shard_map/pallas_call | solution.py:272
  277.6 5.9 %shard_map.118.prior = bf16[8,256,640]{2,1,0:T(8,128)(2,1)} custom-call(s32[8]{0:T(128)S(1)} %reshape.262.rows_of, s32[2]{0:T(128)S(1)} %and_select_fusion.slots, s32[2]{0:T(128)S(1)} %get-tuple-element.45.blocks.targets, bf16[512,768]{1,0:T(8,128)(2,1)} %shard_map.116.c0, bf16[512,768]{1,0:T(8,128)(2,1)} %collective-permute-done.20.c1, ...), custom_call_target="tpu_custom_call" | custom-call | flops 2013265920 | bytes 8388608 | tf_op jit(solution)/shard_map/pallas_call | solution.py:272
  284.3 2.6 shard_map.119.refs_0_
  290.2 5.8 %shard_map.120.prior = bf16[8,256,640]{2,1,0:T(8,128)(2,1)} custom-call(s32[8]{0:T(128)S(1)} %reshape.262.rows_of, s32[2]{0:T(128)S(1)} %and_select_fusion.2.slots, s32[2]{0:T(128)S(1)} %get-tuple-element.46.blocks.targets, bf16[512,768]{1,0:T(8,128)(2,1)S(1)} %copy-done.12, bf16[512,768]{1,0:T(8,128)(2,1)S(1)} %copy-done.22, ...), custom_call_target="tpu_custom_call", output_to_operand_aliasing={{}: (10, {})} | custom-call | flops 2013265920 | bytes 8388608 | tf_op jit(solution)/shard_map/pallas_call | solution.py:272
  296.0 2.5 shard_map.121
  (167 shorter events, 62.6 us)
Async XLA Ops:
  0.0 118.3 %collective-permute-start.2 = (bf16[256,5120]{1,0:T(8,128)(2,1)}, bf16[256,5120]{1,0:T(8,128)(2,1)}, u32[]{:S(2)}, u32[]{:S(2)}) collective-permute-start(bf16[256,5120]{1,0:T(8,128)(2,1)} %bitcast.57), channel_id=1, source_target_pairs={{0,3},{1,0},{2,1},{3,2},{4,7},{5,4},{6,5},{7,6},{8,9},{9,13},{10,1... | collective-permute-start | bytes 7864328 | tf_op jit(solution)/shard_map/ppermute | solution.py:49
  2.5 117.3 %collective-permute-start = (bf16[256,5120]{1,0:T(8,128)(2,1)}, bf16[256,5120]{1,0:T(8,128)(2,1)S(1)}, u32[]{:S(2)}, u32[]{:S(2)}) collective-permute-start(bf16[256,5120]{1,0:T(8,128)(2,1)} %bitcast.58), channel_id=1, source_target_pairs={{0,1},{1,2},{2,3},{3,0},{4,5},{5,6},{6,7},{7,4},{8,12},{9,8},{10,1... | collective-permute-start | bytes 7864328 | tf_op jit(solution)/shard_map/ppermute | solution.py:49
  9.1 95.7 %copy-start.31 = (s32[2048]{0:T(1024)S(1)}, s32[2048]{0:T(1024)}, u32[]{:S(2)}) copy-start(s32[2048]{0:T(1024)} %param.19) | copy-start | bytes 24580
  9.2 95.7 %copy-start.43 = (s32[2,2,4]{2,1,0:T(2,128)S(1)}, s32[2,2,4]{2,1,0:T(2,128)}, u32[]{:S(2)}) copy-start(s32[2,2,4]{2,1,0:T(2,128)} %constant.175.clone) | copy-start | bytes 196
  9.2 112.1 %copy-start.32 = (bf16[1,128,768]{2,1,0:T(8,128)(2,1)}, bf16[1,128,768]{2,1,0:T(8,128)(2,1)S(1)}, u32[]{:S(2)}) copy-start(bf16[1,128,768]{2,1,0:T(8,128)(2,1)S(1)} %get-tuple-element.37) | copy-start | bytes 589828
  9.2 29.7 %collective-permute-start.5 = (bf16[128,768]{1,0:T(8,128)(2,1)S(1)}, bf16[128,768]{1,0:T(8,128)(2,1)S(1)}, u32[]{:S(2)}, u32[]{:S(2)}) collective-permute-start(bf16[128,768]{1,0:T(8,128)(2,1)S(1)} %get-tuple-element.38), channel_id=1, source_target_pairs={{0,64},{1,65},{2,66},{3,67},{4,68},{5,69},{6,70},{7,71},{8,72},{9,... | collective-permute-start | bytes 589832 | tf_op jit(solution)/shard_map/ppermute | solution.py:49
  40.4 3.6 %collective-permute-start.6 = (bf16[2,128,768]{2,1,0:T(8,128)(2,1)}, bf16[2,128,768]{2,1,0:T(8,128)(2,1)S(1)}, u32[]{:S(2)}, u32[]{:S(2)}) collective-permute-start(bf16[2,128,768]{2,1,0:T(8,128)(2,1)} %maximum_select_fusion.2), channel_id=1, source_target_pairs={{0,8},{1,9},{2,10},{3,11},{4,12},{5,13},{6,14},{7,15},{8,0},{9,1},... | collective-permute-start | bytes 1179656 | tf_op jit(solution)/shard_map/ppermute | solution.py:49
  40.4 150.1 %collective-permute-start.4 = (bf16[5120,384]{1,0:T(8,128)(2,1)}, bf16[5120,384]{1,0:T(8,128)(2,1)}, u32[]{:S(2)}, u32[]{:S(2)}) collective-permute-start(bf16[5120,384]{1,0:T(8,128)(2,1)} %bitcast.49), channel_id=1, source_target_pairs={{0,4},{1,5},{2,6},{3,7},{4,0},{5,1},{6,2},{7,3},{8,11},{9,10},{10,... | collective-permute-start | bytes 11796488 | tf_op jit(solution)/shard_map/ppermute | solution.py:49
  43.9 83.1 %copy-start.33 = (bf16[2,128,768]{2,1,0:T(8,128)(2,1)}, bf16[2,128,768]{2,1,0:T(8,128)(2,1)S(1)}, u32[]{:S(2)}) copy-start(bf16[2,128,768]{2,1,0:T(8,128)(2,1)S(1)} %collective-permute-done.6) | copy-start | bytes 1179652
  46.3 49.5 %collective-permute-start.10 = (bf16[2,256,768]{2,1,0:T(8,128)(2,1)}, bf16[2,256,768]{2,1,0:T(8,128)(2,1)}, u32[]{:S(2)}, u32[]{:S(2)}) collective-permute-start(bf16[2,256,768]{2,1,0:T(8,128)(2,1)} %maximum_select_fusion.1), channel_id=1, source_target_pairs={{0,4},{1,5},{2,6},{3,7},{4,0},{5,1},{6,2},{7,3},{8,11},{9,10},{10,... | collective-permute-start | bytes 2359304 | tf_op jit(solution)/shard_map/ppermute | solution.py:49
  48.2 58.0 %collective-permute-start.7 = (bf16[2,256,768]{2,1,0:T(8,128)(2,1)}, bf16[2,256,768]{2,1,0:T(8,128)(2,1)}, u32[]{:S(2)}, u32[]{:S(2)}) collective-permute-start(bf16[2,256,768]{2,1,0:T(8,128)(2,1)} %maximum_select_fusion.1), channel_id=1, source_target_pairs={{0,48},{1,49},{2,50},{3,51},{4,52},{5,53},{6,54},{7,55},{8,56},{9,... | collective-permute-start | bytes 2359304 | tf_op jit(solution)/shard_map/ppermute | solution.py:49
  95.7 21.3 %collective-permute-start.8 = (bf16[2,256,768]{2,1,0:T(8,128)(2,1)}, bf16[2,256,768]{2,1,0:T(8,128)(2,1)}, u32[]{:S(2)}, u32[]{:S(2)}) collective-permute-start(bf16[2,256,768]{2,1,0:T(8,128)(2,1)} %maximum_select_fusion.1), channel_id=1, source_target_pairs={{0,32},{1,33},{2,34},{3,35},{4,36},{5,37},{6,38},{7,39},{8,40},{9,... | collective-permute-start | bytes 2359304 | tf_op jit(solution)/shard_map/ppermute | solution.py:49
  106.3 143.1 %collective-permute-start.18 = (bf16[3072,640]{1,0:T(8,128)(2,1)}, bf16[3072,640]{1,0:T(8,128)(2,1)}, u32[]{:S(2)}, u32[]{:S(2)}) collective-permute-start(bf16[3072,640]{1,0:T(8,128)(2,1)} %bitcast.54), channel_id=1, source_target_pairs={{0,4},{1,5},{2,6},{3,7},{4,0},{5,1},{6,2},{7,3},{8,11},{9,10},{10,... | collective-permute-start | bytes 11796488 | tf_op jit(solution)/shard_map/ppermute | solution.py:49
  117.1 20.1 %collective-permute-start.9 = (bf16[2,256,768]{2,1,0:T(8,128)(2,1)}, bf16[2,256,768]{2,1,0:T(8,128)(2,1)S(1)}, u32[]{:S(2)}, u32[]{:S(2)}) collective-permute-start(bf16[2,256,768]{2,1,0:T(8,128)(2,1)} %maximum_select_fusion.1), channel_id=1, source_target_pairs={{0,16},{1,17},{2,18},{3,19},{4,20},{5,21},{6,22},{7,23},{8,24},{9,... | collective-permute-start | bytes 2359304 | tf_op jit(solution)/shard_map/ppermute | solution.py:49
  118.3 19.0 %collective-permute-start.11 = (bf16[2,256,768]{2,1,0:T(8,128)(2,1)}, bf16[2,256,768]{2,1,0:T(8,128)(2,1)S(1)}, u32[]{:S(2)}, u32[]{:S(2)}) collective-permute-start(bf16[2,256,768]{2,1,0:T(8,128)(2,1)} %collective-permute-done.10), channel_id=1, source_target_pairs={{0,48},{1,49},{2,50},{3,51},{4,52},{5,53},{6,54},{7,55},{8,56},{9,... | collective-permute-start | bytes 2359304 | tf_op jit(solution)/shard_map/ppermute | solution.py:49
  119.8 35.3 %collective-permute-start.12 = (bf16[2,256,768]{2,1,0:T(8,128)(2,1)}, bf16[2,256,768]{2,1,0:T(8,128)(2,1)S(1)}, u32[]{:S(2)}, u32[]{:S(2)}) collective-permute-start(bf16[2,256,768]{2,1,0:T(8,128)(2,1)} %collective-permute-done.10), channel_id=1, source_target_pairs={{0,32},{1,33},{2,34},{3,35},{4,36},{5,37},{6,38},{7,39},{8,40},{9,... | collective-permute-start | bytes 2359304 | tf_op jit(solution)/shard_map/ppermute | solution.py:49
  122.8 33.2 %copy-start.1 = (bf16[1,5120,384]{2,1,0:T(8,128)(2,1)S(1)}, bf16[1,5120,384]{2,1,0:T(8,128)(2,1)}, u32[]{:S(2)}) copy-start(bf16[1,5120,384]{2,1,0:T(8,128)(2,1)} %param.17) | copy-start | bytes 11796484
  122.8 33.2 %copy-start.30 = (f32[1,5120]{1,0:T(1,128)S(1)}, f32[1,5120]{1,0:T(1,128)}, u32[]{:S(2)}) copy-start(f32[1,5120]{1,0:T(1,128)} %refs_2_.1) | copy-start | bytes 61444
  137.2 35.6 %collective-permute-start.13 = (bf16[2,256,768]{2,1,0:T(8,128)(2,1)}, bf16[2,256,768]{2,1,0:T(8,128)(2,1)}, u32[]{:S(2)}, u32[]{:S(2)}) collective-permute-start(bf16[2,256,768]{2,1,0:T(8,128)(2,1)} %collective-permute-done.10), channel_id=1, source_target_pairs={{0,16},{1,17},{2,18},{3,19},{4,20},{5,21},{6,22},{7,23},{8,24},{9,... | collective-permute-start | bytes 2359304 | tf_op jit(solution)/shard_map/ppermute | solution.py:49
  137.3 47.7 %collective-permute-start.1 = (bf16[128,5120]{1,0:T(8,128)(2,1)}, bf16[128,5120]{1,0:T(8,128)(2,1)}, u32[]{:S(2)}, u32[]{:S(2)}) collective-permute-start(bf16[128,5120]{1,0:T(8,128)(2,1)} %slice.85), channel_id=1, source_target_pairs={{0,1},{1,2},{2,3},{3,0},{4,5},{5,6},{6,7},{7,4},{8,12},{9,8},{10,1... | collective-permute-start | bytes 3932168 | tf_op jit(solution)/shard_map/ppermute | solution.py:49
  156.0 29.0 %collective-permute-start.3 = (bf16[128,5120]{1,0:T(8,128)(2,1)}, bf16[128,5120]{1,0:T(8,128)(2,1)}, u32[]{:S(2)}, u32[]{:S(2)}) collective-permute-start(bf16[128,5120]{1,0:T(8,128)(2,1)} %slice.86), channel_id=1, source_target_pairs={{0,3},{1,0},{2,1},{3,2},{4,7},{5,4},{6,5},{7,6},{8,9},{9,13},{10,1... | collective-permute-start | bytes 3932168 | tf_op jit(solution)/shard_map/ppermute | solution.py:49
  168.4 34.3 %copy-start.3 = (bf16[4,2,256,768]{3,2,1,0:T(8,128)(2,1)}, bf16[4,2,256,768]{3,2,1,0:T(8,128)(2,1)S(1)}, u32[]{:S(2)}) copy-start(bf16[4,2,256,768]{3,2,1,0:T(8,128)(2,1)S(1)} %pad_maximum_fusion.kv_own) | copy-start | bytes 9437188
  210.0 17.5 %collective-permute-start.21 = (bf16[512,768]{1,0:T(8,128)(2,1)}, bf16[512,768]{1,0:T(8,128)(2,1)}, u32[]{:S(2)}, u32[]{:S(2)}) collective-permute-start(bf16[512,768]{1,0:T(8,128)(2,1)} %shard_map.116.c0), channel_id=1, source_target_pairs={{0,1},{1,2},{2,3},{3,0},{4,5},{5,6},{6,7},{7,4},{8,12},{9,8},{10,1... | collective-permute-start | bytes 2359304 | tf_op jit(solution)/shard_map/ppermute | solution.py:49
  210.0 19.3 %collective-permute-start.20 = (bf16[512,768]{1,0:T(8,128)(2,1)}, bf16[512,768]{1,0:T(8,128)(2,1)}, u32[]{:S(2)}, u32[]{:S(2)}) collective-permute-start(bf16[512,768]{1,0:T(8,128)(2,1)} %shard_map.116.c0), channel_id=1, source_target_pairs={{0,3},{1,0},{2,1},{3,2},{4,7},{5,4},{6,5},{7,6},{8,9},{9,13},{10,1... | collective-permute-start | bytes 2359304 | tf_op jit(solution)/shard_map/ppermute | solution.py:49
  223.8 19.7 %collective-permute-start.15 = (bf16[512,768]{1,0:T(8,128)(2,1)S(1)}, bf16[512,768]{1,0:T(8,128)(2,1)S(1)}, u32[]{:S(2)}, u32[]{:S(2)}) collective-permute-start(bf16[512,768]{1,0:T(8,128)(2,1)S(1)} %shard_map.114.c0), channel_id=1, source_target_pairs={{0,1},{1,2},{2,3},{3,0},{4,5},{5,6},{6,7},{7,4},{8,12},{9,8},{10,1... | collective-permute-start | bytes 2359304 | tf_op jit(solution)/shard_map/ppermute | solution.py:49
  223.9 20.7 %collective-permute-start.14 = (bf16[512,768]{1,0:T(8,128)(2,1)S(1)}, bf16[512,768]{1,0:T(8,128)(2,1)S(1)}, u32[]{:S(2)}, u32[]{:S(2)}) collective-permute-start(bf16[512,768]{1,0:T(8,128)(2,1)S(1)} %shard_map.114.c0), channel_id=1, source_target_pairs={{0,3},{1,0},{2,1},{3,2},{4,7},{5,4},{6,5},{7,6},{8,9},{9,13},{10,1... | collective-permute-start | bytes 2359304 | tf_op jit(solution)/shard_map/ppermute | solution.py:49
  229.2 22.7 %collective-permute-start.22 = (bf16[256,768]{1,0:T(8,128)(2,1)}, bf16[256,768]{1,0:T(8,128)(2,1)S(1)}, u32[]{:S(2)}, u32[]{:S(2)}) collective-permute-start(bf16[256,768]{1,0:T(8,128)(2,1)} %slice.89), channel_id=1, source_target_pairs={{0,1},{1,2},{2,3},{3,0},{4,5},{5,6},{6,7},{7,4},{8,12},{9,8},{10,1... | collective-permute-start | bytes 1179656 | tf_op jit(solution)/shard_map/ppermute | solution.py:49
  231.0 22.2 %collective-permute-start.23 = (bf16[256,768]{1,0:T(8,128)(2,1)}, bf16[256,768]{1,0:T(8,128)(2,1)S(1)}, u32[]{:S(2)}, u32[]{:S(2)}) collective-permute-start(bf16[256,768]{1,0:T(8,128)(2,1)} %slice.90), channel_id=1, source_target_pairs={{0,3},{1,0},{2,1},{3,2},{4,7},{5,4},{6,5},{7,6},{8,9},{9,13},{10,1... | collective-permute-start | bytes 1179656 | tf_op jit(solution)/shard_map/ppermute | solution.py:49
  244.3 25.2 %collective-permute-start.16 = (bf16[256,768]{1,0:T(8,128)(2,1)}, bf16[256,768]{1,0:T(8,128)(2,1)}, u32[]{:S(2)}, u32[]{:S(2)}) collective-permute-start(bf16[256,768]{1,0:T(8,128)(2,1)} %slice.87), channel_id=1, source_target_pairs={{0,1},{1,2},{2,3},{3,0},{4,5},{5,6},{6,7},{7,4},{8,12},{9,8},{10,1... | collective-permute-start | bytes 1179656 | tf_op jit(solution)/shard_map/ppermute | solution.py:49
  245.7 23.8 %collective-permute-start.17 = (bf16[256,768]{1,0:T(8,128)(2,1)}, bf16[256,768]{1,0:T(8,128)(2,1)}, u32[]{:S(2)}, u32[]{:S(2)}) collective-permute-start(bf16[256,768]{1,0:T(8,128)(2,1)} %slice.88), channel_id=1, source_target_pairs={{0,3},{1,0},{2,1},{3,2},{4,7},{5,4},{6,5},{7,6},{8,9},{9,13},{10,1... | collective-permute-start | bytes 1179656 | tf_op jit(solution)/shard_map/ppermute | solution.py:49
  262.6 20.9 %collective-permute-start.24 = (bf16[2,256,640]{2,1,0:T(8,128)(2,1)S(1)}, bf16[2,256,640]{2,1,0:T(8,128)(2,1)S(1)}, u32[]{:S(2)}, u32[]{:S(2)}) collective-permute-start(bf16[2,256,640]{2,1,0:T(8,128)(2,1)S(1)} %shard_map.117), channel_id=1, source_target_pairs={{0,4},{1,5},{2,6},{3,7},{4,0},{5,1},{6,2},{7,3},{8,11},{9,10},{10,... | collective-permute-start | bytes 1966088 | tf_op jit(solution)/shard_map/ppermute | solution.py:49
  276.9 19.1 %collective-permute-start.19 = (bf16[2,256,640]{2,1,0:T(8,128)(2,1)}, bf16[2,256,640]{2,1,0:T(8,128)(2,1)}, u32[]{:S(2)}, u32[]{:S(2)}) collective-permute-start(bf16[2,256,640]{2,1,0:T(8,128)(2,1)} %shard_map.115), channel_id=1, source_target_pairs={{0,4},{1,5},{2,6},{3,7},{4,0},{5,1},{6,2},{7,3},{8,11},{9,10},{10,... | collective-permute-start | bytes 1966088 | tf_op jit(solution)/shard_map/ppermute | solution.py:49
  (39 other events, 206.6 us)

commit v2 on v1

--- a/solution.py
+++ b/solution.py
@@ -1,6 +1,7 @@
+import functools
+
 import jax
 import jax.numpy as jnp
-import numpy as np
 from jax import lax
 from jax.experimental import pallas as pl
 from jax.experimental.pallas import tpu as pltpu
@@ -18,6 +19,20 @@
     tuple(next((h, r) for h in range(2) for r in range(4) if table[h][r] == c) for c in range(8))
     for table in PLACE
 )
+
+MINE, THEIRS, SLOT, ROWS, OWN, FIRST, X_AT = 0, 4, 8, 12, 20, 22, 30
+
+
+def facts_of(core, c):
+    half, r = SPOT[core][c]
+    mine, theirs = PLACE[core][half], PLACE[core][1 - half]
+    slots = [(p - r) % 4 for p in range(4)]
+    ring = [(r + j) % 4 for j in range(4)]
+    rows = [place[p] for p in ring for place in (mine, theirs)]
+    return [*mine, *theirs, *slots, *rows, mine[r], theirs[r]]
+
+
+FACTS = [[facts_of(core, c) for c in range(8)] for core in range(2)]
 
 
 def moves(step):
@@ -55,14 +70,14 @@
     return scaled.astype(BF)
 
 
-def project_kernel(pieces, slot, has_prior, meta, *refs):
+def project_kernel(pieces, meta, *refs):
     xs = refs[:pieces]
     gain, w = refs[pieces : pieces + 2]
     normed, q, res_own, res_other = refs[-4:]
-    row = 0
+    step = 32
+    base = 0
     for x in xs:
-        rows, step = x.shape[0], 32
-        base = row
+        rows = x.shape[0]
 
         def norm_rows(i, _, x=x, base=base):
             at = pl.multiple_of(i * step, step)
@@ -76,28 +91,26 @@
         lax.fori_loop(0, rows // step, norm_rows, 0)
         width = res_own.shape[2]
         for k, out in ((0, res_own), (1, res_other)):
-            first = pl.multiple_of(meta[k] * width, 128)
-            out[0, row : row + rows, :] = x[:, pl.ds(first, width)]
-        row += rows
+            first = pl.multiple_of(meta[OWN + k] * width, 128)
+            out[0, base : base + rows, :] = x[:, pl.ds(first, width)]
+        base += rows
     q[0] = jnp.dot(normed[0], w[...], preferred_element_type=F32).astype(BF)
 
 
-def project(meta, xs, gain, w, slot, prior):
+def project(meta, xs, gain, w, slot, width, prior=None):
     d, n = w.shape
-    width = 640
     shapes = [(4, RB, d), (4, RB, n), (4, RB, width), (4, RB, width)]
     whole = lambda a: pl.BlockSpec(a.shape, lambda i, m, nd=a.ndim: (0,) * nd)
     ins = list(xs) + [gain, w]
     specs = [whole(a) for a in ins]
     aliases = {}
-    if prior is not None:
-        for k, a in enumerate(prior):
-            aliases[1 + len(ins)] = k
-            ins.append(a)
-            specs.append(pl.BlockSpec(memory_space=pl.ANY))
+    for k, a in enumerate(prior or ()):
+        aliases[1 + len(ins)] = k
+        ins.append(a)
+        specs.append(pl.BlockSpec(memory_space=pl.ANY))
 
     def kernel(meta, *refs):
-        project_kernel(len(xs), slot, prior is not None, meta, *refs)
+        project_kernel(len(xs), meta, *refs)
 
     return pl.pallas_call(
         kernel,
@@ -139,14 +152,13 @@
 
 
 def attend_kernel(
-    slots, blocks, firsts, where_x, q_own, q_other, kv_own, kv_other, seg_col, seg_row, out,
-    scores, tops, sums,
+    chunk, meta, q_own, q_other, kv_own, kv_other, seg_col, seg_row, out, scores, tops, sums
 ):
     t = pl.program_id(0)
-    block = blocks[t]
-    first = firsts[t]
+    block = meta[MINE + 2 * chunk + t]
+    first = meta[FIRST + block]
     count = block - first + 1
-    x = where_x[0]
+    x = meta[X_AT]
     heads = q_own.shape[2] // HD
     factor = HD ** (-0.5) * 1.4426950408889634
     pairs = [(src, i) for src in range(2) for i in range(heads)]
@@ -214,20 +226,20 @@
         out[:, n * HD : (n + 1) * HD] = tops[n].astype(BF)
 
 
-def attend(slots, blocks, firsts, where_x, q_own, q_other, kv_own, kv_other, seg_col, seg_row):
+def attend(meta, chunk, q_own, q_other, kv_own, kv_other, seg_col, seg_row):
     n = q_own.shape[2]
     heads = n // HD
-    whole = lambda a: pl.BlockSpec(a.shape, lambda t, *s, nd=a.ndim: (0,) * nd)
-    q_spec = pl.BlockSpec((1, RB, n), lambda t, slots, *s: (slots[t], 0, 0))
+    whole = lambda a: pl.BlockSpec(a.shape, lambda t, m, nd=a.ndim: (0,) * nd)
+    q_spec = pl.BlockSpec((1, RB, n), lambda t, m: (m[SLOT + 2 * chunk + t], 0, 0))
     return pl.pallas_call(
-        attend_kernel,
+        functools.partial(attend_kernel, chunk),
         grid_spec=pltpu.PrefetchScalarGridSpec(
-            num_scalar_prefetch=4,
+            num_scalar_prefetch=1,
             grid=(2,),
             in_specs=[
                 q_spec, q_spec, whole(kv_own), whole(kv_other), whole(seg_col), whole(seg_row)
             ],
-            out_specs=pl.BlockSpec((RB, 2 * n), lambda t, *s: (t, 0)),
+            out_specs=pl.BlockSpec((RB, 2 * n), lambda t, m: (t, 0)),
             scratch_shapes=[
                 pltpu.VMEM((2 * heads, 5, RB, RB), F32),
                 pltpu.VMEM((2 * heads, RB, HD), F32),
@@ -239,10 +251,10 @@
         cost_estimate=pl.CostEstimate(
             flops=4 * 2 * RB * 768 * 2 * n, bytes_accessed=8 * MIB, transcendentals=2 * RB * 768 * 6
         ),
-    )(slots, blocks, firsts, where_x, q_own, q_other, kv_own, kv_other, seg_col, seg_row)
-
-
-def finish_kernel(rows_of, slots, targets, c0, c1, c2a, c2b, c3, w, res, *refs):
+    )(meta, q_own, q_other, kv_own, kv_other, seg_col, seg_row)
+
+
+def finish_kernel(meta, c0, c1, c2a, c2b, c3, w, res, *refs):
     out = refs[-1]
     t = pl.program_id(0)
     far = jnp.where(t == 0, c2a[...], c2b[...])
@@ -251,31 +263,37 @@
     for j, c in enumerate((c0[...], c1[...], far, c3[...])):
         for k in range(2):
             total += jnp.dot(
-                c[:, k * n : (k + 1) * n], w[rows_of[2 * j + k]], preferred_element_type=F32
+                c[:, k * n : (k + 1) * n],
+                w[meta[ROWS + 2 * j + k]],
+                preferred_element_type=F32,
             )
     out[0] = (res[0].astype(F32) + total).astype(BF)
 
 
-def finish(rows_of, slots, targets, parts, w, res, blocks, prior=None):
+def finish(meta, chunk, parts, w, res, blocks, prior=None):
     k8, n, width = w.shape
-    tile = pl.BlockSpec((RB, 2 * n), lambda t, *s: (t, 0))
-    fixed = pl.BlockSpec((RB, 2 * n), lambda t, *s: (0, 0))
+    tile = pl.BlockSpec((RB, 2 * n), lambda t, m: (t, 0))
+    fixed = pl.BlockSpec((RB, 2 * n), lambda t, m: (0, 0))
     ins = list(parts) + [w, res]
     specs = [tile, tile, fixed, fixed, tile]
-    specs.append(pl.BlockSpec(w.shape, lambda t, *s: (0, 0, 0)))
-    specs.append(pl.BlockSpec((1, RB, width), lambda t, r, slots, g: (slots[t], 0, 0)))
+    specs.append(pl.BlockSpec(w.shape, lambda t, m: (0, 0, 0)))
+    specs.append(pl.BlockSpec((1, RB, width), lambda t, m: (m[SLOT + 2 * chunk + t], 0, 0)))
     aliases = {}
     if prior is not None:
-        aliases[3 + len(ins)] = 0
+        aliases[1 + len(ins)] = 0
         ins.append(prior)
         specs.append(pl.BlockSpec(memory_space=pl.ANY))
+    if blocks == 2:
+        target = lambda t, m: (t, 0, 0)
+    else:
+        target = lambda t, m: (m[MINE + 2 * chunk + t], 0, 0)
     return pl.pallas_call(
         finish_kernel,
         grid_spec=pltpu.PrefetchScalarGridSpec(
-            num_scalar_prefetch=3,
+            num_scalar_prefetch=1,
             grid=(2,),
             in_specs=specs,
-            out_specs=pl.BlockSpec((1, RB, width), lambda t, r, s, targets: (targets[t], 0, 0)),
+            out_specs=pl.BlockSpec((1, RB, width), target),
         ),
         out_shape=jax.ShapeDtypeStruct((blocks, RB, width), BF),
         input_output_aliases=aliases,
@@ -283,29 +301,34 @@
         cost_estimate=pl.CostEstimate(
             flops=4 * RB * k8 * n * width, bytes_accessed=8 * MIB, transcendentals=0
         ),
-    )(rows_of, slots, targets, *ins)
-
-
-def place_kernel(targets, got, prior, out):
+    )(meta, *ins)
+
+
+def place_kernel(meta, got, prior, out):
     out[...] = got[...]
 
 
-def place(targets, got, prior):
+def place(meta, chunk, got, prior):
     count, rows, width = got.shape
+    target = lambda t, m: (m[THEIRS + 2 * chunk + t], 0, 0)
     return pl.pallas_call(
         place_kernel,
         grid_spec=pltpu.PrefetchScalarGridSpec(
             num_scalar_prefetch=1,
             grid=(count,),
             in_specs=[
-                pl.BlockSpec((1, rows, width), lambda t, g: (t, 0, 0)),
+                pl.BlockSpec((1, rows, width), lambda t, m: (t, 0, 0)),
                 pl.BlockSpec(memory_space=pl.ANY),
             ],
-            out_specs=pl.BlockSpec((1, rows, width), lambda t, targets: (targets[t], 0, 0)),
+            out_specs=pl.BlockSpec((1, rows, width), target),
         ),
         out_shape=jax.ShapeDtypeStruct(prior.shape, BF),
         input_output_aliases={2: 0},
-    )(targets, got, prior)
+    )(meta, got, prior)
+
+
+def after(value, *done):
+    return lax.optimization_barrier((value,) + done)[0]
 
 
 def body(
@@ -314,80 +337,87 @@
     section = lax.axis_index("section")
     c = lax.axis_index("ctx")
     core = section % 2
-    x_at = section // 2 % 4
     y_hi = section // 8
-    spot = jnp.array(SPOT, jnp.int32)[core, c]
-    half, r = spot[0], spot[1]
-    place_of = jnp.array(PLACE, jnp.int32)[core]
-    mine, theirs = place_of[half], place_of[1 - half]
-
     x0 = section_input[0]
     w_q = w_query[0]
     w_o = w_out[0]
-    gain = query_gain
+    width = w_o.shape[1]
 
     xp = send(x0, NEXT)
     xn = send(x0, PREV)
     w_q2 = send(w_q, PARTNER)
 
-    kv_in = normalize(last_hidden, kv_gain)
-    own_k = jnp.dot(kv_in, w_key, preferred_element_type=F32).astype(BF)
-    own_v = jnp.dot(kv_in, w_value, preferred_element_type=F32).astype(BF)
-    kv = jnp.concatenate([own_k, own_v], axis=1)
-    kv_far = send(kv, FAR_Y)
-    pair = jnp.where(y_hi == 0, jnp.stack([kv, kv_far]), jnp.stack([kv_far, kv]))
-    pair2 = send(pair, CORE)
-    piece = jnp.where(
-        core == 0, jnp.concatenate([pair, pair2], axis=1), jnp.concatenate([pair2, pair], axis=1)
-    )
-    piece2 = send(piece, PARTNER)
-
-    def spread(p):
-        return jnp.stack([p, send(p, X_PREV), send(p, X_FAR), send(p, X_NEXT)])
-
-    kv_own = spread(piece)
-    kv_other = spread(piece2)
-
-    xo_a = send(xp[: RB // 2], NEXT)
-    xo_b = send(xn[RB // 2 :], PREV)
-    w_o2 = send(w_o, PARTNER)
-
-    cols = jnp.stack([mine[r], theirs[r]])
-    state = project(cols, [x0], gain, w_q, 0, None)
-    state = project(cols, [xn], gain, w_q, 1, state)
-    state = project(cols, [xp], gain, w_q, 3, state)
-    normed, q_own, res_own, res_other = project(cols, [xo_a, xo_b], gain, w_q, 2, state)
-    q_other = more_queries(normed, w_q2)
-
     ids = segment_ids.reshape(8, RB)
     starts = jnp.sum(segment_ids[None, :] < ids[:, :1], axis=1, dtype=jnp.int32) // RB
     starts = jnp.maximum(starts, jnp.arange(8, dtype=jnp.int32) - 4)
+    facts = jnp.array(FACTS, jnp.int32)[core, c]
+    meta = jnp.concatenate([facts, starts, (section // 2 % 4)[None]])
     seg_col = segment_ids.reshape(8, RB, 1)
     seg_row = segment_ids.reshape(8, 1, RB)
-    xs = x_at[None]
-    w_o_r = w_o.reshape(8, 384, -1)
-    w_o2_r = w_o2.reshape(8, 384, -1)
-    ring = (r + jnp.arange(4, dtype=jnp.int32)) % 4
-    rows_of = jnp.stack([mine[ring], theirs[ring]], axis=1).reshape(8)
-
-    order = jnp.arange(2, dtype=jnp.int32)
+
+    def cache(last_hidden, w_key, w_value):
+        kv_in = normalize(last_hidden, kv_gain)
+        own_k = jnp.dot(kv_in, w_key, preferred_element_type=F32).astype(BF)
+        own_v = jnp.dot(kv_in, w_value, preferred_element_type=F32).astype(BF)
+        kv = jnp.concatenate([own_k, own_v], axis=1)
+        kv_far = send(kv, FAR_Y)
+        pair = jnp.where(y_hi == 0, jnp.stack([kv, kv_far]), jnp.stack([kv_far, kv]))
+        pair2 = send(pair, CORE)
+        piece = jnp.where(
+            core == 0,
+            jnp.concatenate([pair, pair2], axis=1),
+            jnp.concatenate([pair2, pair], axis=1),
+        )
+        piece2 = send(piece, PARTNER)
+        share = lax.dynamic_index_in_dim(piece, core, 0, keepdims=False)
+        o1 = send(share, X_PREV)
+        o3 = send(share, X_NEXT)
+        o2 = send(after(share, o1, o3), X_FAR)
+        return piece2, jnp.stack([share, o1, o2, o3])
+
+    def nothing(last_hidden, w_key, w_value):
+        half_rows = 2 * last_hidden.shape[0]
+        cols = 2 * w_key.shape[1]
+        return jnp.zeros((2, half_rows, cols), BF), jnp.zeros((4, half_rows, cols), BF)
+
+    piece2, got = lax.cond(segment_ids[0] >= 0, cache, nothing, last_hidden, w_key, w_value)
+    xp, xn, piece2, got = lax.optimization_barrier((xp, xn, piece2, got))
+    xo_a = send(xp[: RB // 2], NEXT)
+    xo_b = send(xn[RB // 2 :], PREV)
+    t1 = send(piece2, X_PREV)
+    t3 = send(piece2, X_NEXT)
+    state = project(meta, [after(x0, xp, xn)], query_gain, w_q, 0, width)
+    state = project(meta, [xn], query_gain, w_q, 1, width, state)
+    state = project(meta, [xp], query_gain, w_q, 3, width, state)
+    xo_a, xo_b, t1, t3, *state = lax.optimization_barrier((xo_a, xo_b, t1, t3, *state))
+    t2 = send(after(piece2, t1, t3), X_FAR)
+    got2 = send(after(got, t1, t3), CORE)
+    w_q2, t2, got2 = lax.optimization_barrier((w_q2, t2, got2))
+    kv_own = jnp.where(
+        core == 0, jnp.stack([got, got2], axis=1), jnp.stack([got2, got], axis=1)
+    )
+    kv_other = jnp.stack([piece2, t1, t2, t3])
+    normed, q_own, res_own, res_other = project(
+        meta, [xo_a, xo_b], query_gain, w_q, 2, width, state
+    )
+    w_o2 = send(after(w_o, xo_a, xo_b, w_q2), PARTNER)
+    q_other = more_queries(normed, w_q2)
+
+    heads_cols = w_q.shape[1]
+    w_o_r = w_o.reshape(8, heads_cols, width)
+    w_o2_r = w_o2.reshape(8, heads_cols, width)
+
     result = None
     for chunk in range(2):
-        spots = order + 2 * chunk
-        slots = (spots - r + 4) % 4
-        blocks = mine[2 * chunk : 2 * chunk + 2]
-        others = theirs[2 * chunk : 2 * chunk + 2]
-        own = attend(
-            slots, blocks, starts[blocks], xs, q_own, q_other, kv_own, kv_other, seg_col, seg_row
-        )
+        own = attend(meta, chunk, q_own, q_other, kv_own, kv_other, seg_col, seg_row)
         cp = send(own, NEXT)
         cn = send(own, PREV)
         co_a = send(cp[:RB], NEXT)
         co_b = send(cn[RB:], PREV)
         parts = (own, cn, co_a, co_b, cp)
-        sent = send(finish(rows_of, slots, order, parts, w_o2_r, res_other, 2), PARTNER)
-        result = finish(rows_of, slots, blocks, parts, w_o_r, res_own, 8, result)
-        result = place(others, sent, result)
+        sent = send(finish(meta, chunk, parts, w_o2_r, res_other, 2), PARTNER)
+        result = finish(meta, chunk, parts, w_o_r, res_own, 8, result)
+        result = place(meta, chunk, sent, result)
     return result.reshape(1, 8 * RB, -1)
 
 

time: 301 us -> 243 us (0.81)
  waiting for transfers between devices: 127 us -> 100 us
  local copies, waits for them, and re-layouts: 41.7 us -> 17.4 us
  other arithmetic: 14.3 us -> 9.46 us
  between operations: 5.53 us -> 0.88 us
  starting transfers between devices: 37 us -> 41.5 us
    ppermute x25 -> x26, waiting for transfers between devices: 127 us -> 100 us  [send(): return lax.ppermute(value, AXES, pairs)]
    unnamed x92 -> x38, local copies, waits for them, and re-layouts: 25.1 us -> 9.16 us
    ppermute x25 -> x26, starting transfers between devices: 37 us -> 41.5 us  [send(): return lax.ppermute(value, AXES, pairs)]
    select_n x7 -> x3, other arithmetic: 6.41 us -> 3.92 us  [the longest x1 3.57 us: body(): jnp.where(core == 0, jnp.stack([got, got2], axis=1), jnp.stack([got2, got...]
  transfers between devices with their start and end apart: 25 -> 26, of which waited for: 11 -> 13; matrix products, arithmetic and copies ran while one was open for 12% -> 9% of each run, Pallas kernels for 22% -> 27%
where the time goes in v2:
time: 243 us; the launch traced here: 242 us
  waiting for transfers between devices  100 us (41%)
  Pallas kernels  68.2 us (28%)
  starting transfers between devices  41.5 us (17%)
  local copies, waits for them, and re-layouts  17.4 us (7%)
  other arithmetic  9.46 us (4%)
  matrix products  4.46 us (2%)
    ppermute x26, waiting for transfers between devices, send(): return lax.ppermute(value, AXES, pairs)  100 us
    ppermute x26, starting transfers between devices, send(): return lax.ppermute(value, AXES, pairs)  41.5 us
    pallas_call x4, Pallas kernels, finish(): pl.pallas_call(finish_kernel, grid_spec=pltpu.PrefetchScalarGridSpec(num_...  26.3 us
    pallas_call x4, Pallas kernels, project(): pl.pallas_call(kernel, grid_spec=pltpu.PrefetchScalarGridSpec(num_scalar_...  18.5 us
    pallas_call x2, Pallas kernels, attend(): pl.pallas_call(functools.partial(attend_kernel, chunk), grid_spec=pltpu.P...  9.96 us
    unnamed x38, local copies, waits for them, and re-layouts  9.16 us
    pallas_call x1, Pallas kernels, more_queries(): pl.pallas_call(more_queries_kernel, grid=(4,), in_specs=[pl.BlockSpec((1,...  8.34 us
    pallas_call x2, Pallas kernels, place(): pl.pallas_call(place_kernel, grid_spec=pltpu.PrefetchScalarGridSpec(num_s...  5.15 us
  transfers between devices with their start and end apart: 26, of which 13 were waited for; matrix products, arithmetic and copies ran while one was open for 9% of the time, Pallas kernels for 27%

profile of v2, /device:TPU:1, one launch (start us, length us, event | category | flops | bytes accessed | tf_op | source)
XLA Modules:
  0.0 242.1 jit_solution(3035387026526827639)
XLA Ops:
  4.3 60.5 %conditional.1 = (bf16[2,256,768]{2,1,0:T(8,128)(2,1)}, bf16[4,256,768]{2,1,0:T(8,128)(2,1)}) conditional(s32[]{:T(128)} %bitcast.9, () %tuple.21, (s32[]{:T(128)}, pred[]{:T(512)}, bf16[128,5120]{1,0:T(8,128)(2,1)}, f32[5120]{0:T(1024)}, bf16[5120,384]{1,0:T(8,128)(2,1)}, /*index=5*/bf16[5120,384]{1,0:T(8,128)(2,1)}, pred[]{:T(512)}, s32[]{:T(128)}, ...), branch_computations={%region_1.2_spmd, %region_2.4_spmd} | conditional | flops 1020821632 | bytes 50981860 | solution.py:383
  6.0 3.6 %convolution_convert_fusion = bf16[128,384]{1,0:T(8,128)(2,1)S(1)} fusion(bf16[5120,384]{1,0:T(8,128)(2,1)} %get-tuple-element.112, bf16[128,5120]{1,0:T(8,128)(2,1)} %get-tuple-element.109, f32[5120]{0:T(1024)} %get-tuple-element.110, f32[128]{0:T(128)S(1)} %add_rsqrt_fusion), kind=kOutput, calls=%fused_computation.6 | convolution fusion | flops 505987072 | bytes 5362176 | tf_op jit(solution)/shard_map/cond/branch_1_fun/dot_general | solution.py:361
  11.0 3.0 %collective-permute-start = (bf16[128,768]{1,0:T(8,128)(2,1)S(1)}, bf16[128,768]{1,0:T(8,128)(2,1)S(1)}, u32[]{:S(2)}, u32[]{:S(2)}) collective-permute-start(bf16[128,768]{1,0:T(8,128)(2,1)S(1)} %get-tuple-element.126), channel_id=1, source_target_pairs={{0,64},{1,65},{2,66},{3,67},{4,68},{5,69},{6,70},{7,71},{8,72},{9,... | collective-permute-start | bytes 589832 | tf_op jit(solution)/shard_map/cond/branch_1_fun/ppermute | solution.py:64
  14.0 24.2 %collective-permute-done = bf16[128,768]{1,0:T(8,128)(2,1)S(1)} collective-permute-done((bf16[128,768]{1,0:T(8,128)(2,1)S(1)}, bf16[128,768]{1,0:T(8,128)(2,1)S(1)}, u32[]{:S(2)}, u32[]{:S(2)}) %collective-permute-start) | collective-permute-done | bytes 196640 | tf_op jit(solution)/shard_map/cond/branch_1_fun/ppermute | solution.py:64
  43.2 3.8 %collective-permute-start.2 = (bf16[2,256,768]{2,1,0:T(8,128)(2,1)S(1)}, bf16[2,256,768]{2,1,0:T(8,128)(2,1)}, u32[]{:S(2)}, u32[]{:S(2)}) collective-permute-start(bf16[2,256,768]{2,1,0:T(8,128)(2,1)S(1)} %maximum_select_fusion), channel_id=1, source_target_pairs={{0,4},{1,5},{2,6},{3,7},{4,0},{5,1},{6,2},{7,3},{8,11},{9,10},{10,... | collective-permute-start | bytes 2359304 | tf_op jit(solution)/shard_map/cond/branch_1_fun/ppermute | solution.py:64
  46.9 5.4 %collective-permute-done.4 = bf16[256,768]{1,0:T(8,128)(2,1)S(1)} collective-permute-done((bf16[256,768]{1,0:T(8,128)(2,1)S(1)}, bf16[256,768]{1,0:T(8,128)(2,1)S(1)}, u32[]{:S(2)}, u32[]{:S(2)}) %collective-permute-start.4) | collective-permute-done | bytes 393248 | tf_op jit(solution)/shard_map/cond/branch_1_fun/ppermute | solution.py:64
  54.5 8.9 %collective-permute-done.5 = bf16[256,768]{1,0:T(8,128)(2,1)S(1)} collective-permute-done((bf16[256,768]{1,0:T(8,128)(2,1)S(1)}, bf16[256,768]{1,0:T(8,128)(2,1)S(1)}, u32[]{:S(2)}, u32[]{:S(2)}) %collective-permute-start.5) | collective-permute-done | bytes 393248 | tf_op jit(solution)/shard_map/cond/branch_1_fun/ppermute | solution.py:64
  64.8 3.8 %collective-permute-start.12 = (bf16[5120,384]{1,0:T(8,128)(2,1)}, bf16[5120,384]{1,0:T(8,128)(2,1)}, u32[]{:S(2)}, u32[]{:S(2)}) collective-permute-start(bf16[5120,384]{1,0:T(8,128)(2,1)} %bitcast.27), channel_id=1, source_target_pairs={{0,4},{1,5},{2,6},{3,7},{4,0},{5,1},{6,2},{7,3},{8,11},{9,10},{10,... | collective-permute-start | bytes 11796488 | tf_op jit(solution)/shard_map/ppermute | solution.py:64
  70.7 2.5 %slice.27 = bf16[128,5120]{1,0:T(8,128)(2,1)} slice(bf16[256,5120]{1,0:T(8,128)(2,1)} %collective-permute-done.7.refs_0_), slice={[128:256], [0:5120]} | slice | bytes 2621440 | tf_op jit(solution)/shard_map/slice | solution.py:386
  80.9 3.7 %shard_map.104 = (bf16[4,256,5120]{2,1,0:T(8,128)(2,1)}, bf16[4,256,384]{2,1,0:T(8,128)(2,1)S(1)}, bf16[4,256,640]{2,1,0:T(8,128)(2,1)S(1)}, bf16[4,256,640]{2,1,0:T(8,128)(2,1)S(1)}) custom-call(s32[31]{0:T(128)S(1)} %pad_add_fusion.meta, bf16[256,5120]{1,0:T(8,128)(2,1)S(1)} %bitcast.34, f32[1,5120]{1,0:T(1,128)S(1)} %copy-done.15, ...), custom_call_target="tpu_custom_call" | custom-call | flops 1006632960 | bytes 11796480 | tf_op jit(solution)/shard_map/pallas_call | solution.py:115
  84.6 5.7 %shard_map.105 = (bf16[4,256,5120]{2,1,0:T(8,128)(2,1)}, bf16[4,256,384]{2,1,0:T(8,128)(2,1)S(1)}, bf16[4,256,640]{2,1,0:T(8,128)(2,1)S(1)}, bf16[4,256,640]{2,1,0:T(8,128)(2,1)S(1)}) custom-call(s32[31]{0:T(128)S(1)} %pad_add_fusion.meta, ...), custom_call_target="tpu_custom_call", output_to_operand_aliasing={{0}: (4, {}), {1}: (5, {}), {2}: (6, {}), {3}: (7, {})} | custom-call | flops 1006632960 | bytes 11796480 | tf_op jit(solution)/shard_map/pallas_call | solution.py:115
  90.3 3.7 %shard_map.106 = (bf16[4,256,5120]{2,1,0:T(8,128)(2,1)}, bf16[4,256,384]{2,1,0:T(8,128)(2,1)S(1)}, bf16[4,256,640]{2,1,0:T(8,128)(2,1)S(1)}, bf16[4,256,640]{2,1,0:T(8,128)(2,1)S(1)}) custom-call(s32[31]{0:T(128)S(1)} %pad_add_fusion.meta, bf16[256,5120]{1,0:T(8,128)(2,1)S(1)} %copy-done.7, ...), custom_call_target="tpu_custom_call", output_to_operand_aliasing={{0}: (4, {}), {1}: (5, {}), {2}: (6, {}), {3}: (7, {})} | custom-call | flops 1006632960 | bytes 11796480 | tf_op jit(solution)/shard_map/pallas_call | solution.py:115
  94.1 5.6 %collective-permute-done.8.refs_0_ = bf16[128,5120]{1,0:T(8,128)(2,1)} collective-permute-done((bf16[128,5120]{1,0:T(8,128)(2,1)}, bf16[128,5120]{1,0:T(8,128)(2,1)}, u32[]{:S(2)}, u32[]{:S(2)}) %collective-permute-start.8) | collective-permute-done | bytes 1310752 | tf_op jit(solution)/shard_map/ppermute | solution.py:64
  99.7 4.7 %collective-permute-done.9.refs_1_ = bf16[128,5120]{1,0:T(8,128)(2,1)} collective-permute-done((bf16[128,5120]{1,0:T(8,128)(2,1)}, bf16[128,5120]{1,0:T(8,128)(2,1)}, u32[]{:S(2)}, u32[]{:S(2)}) %collective-permute-start.9) | collective-permute-done | bytes 1310752 | tf_op jit(solution)/shard_map/ppermute | solution.py:64
  107.5 18.8 %collective-permute-done.12.w_ref = bf16[5120,384]{1,0:T(8,128)(2,1)} collective-permute-done((bf16[5120,384]{1,0:T(8,128)(2,1)}, bf16[5120,384]{1,0:T(8,128)(2,1)}, u32[]{:S(2)}, u32[]{:S(2)}) %collective-permute-start.12) | collective-permute-done | bytes 3932192 | tf_op jit(solution)/shard_map/ppermute | solution.py:64
  126.3 3.3 %collective-permute-start.19 = (bf16[3072,640]{1,0:T(8,128)(2,1)}, bf16[3072,640]{1,0:T(8,128)(2,1)}, u32[]{:S(2)}, u32[]{:S(2)}) collective-permute-start(bf16[3072,640]{1,0:T(8,128)(2,1)} %bitcast.18), channel_id=1, source_target_pairs={{0,4},{1,5},{2,6},{3,7},{4,0},{5,1},{6,2},{7,3},{8,11},{9,10},{10,... | collective-permute-start | bytes 11796488 | tf_op jit(solution)/shard_map/ppermute | solution.py:64
  133.6 5.4 %shard_map.107 = (bf16[4,256,5120]{2,1,0:T(8,128)(2,1)}, bf16[4,256,384]{2,1,0:T(8,128)(2,1)S(1)}, bf16[4,256,640]{2,1,0:T(8,128)(2,1)S(1)}, bf16[4,256,640]{2,1,0:T(8,128)(2,1)S(1)}) custom-call(s32[31]{0:T(128)S(1)} %pad_add_fusion.meta, ...), custom_call_target="tpu_custom_call", output_to_operand_aliasing={{0}: (5, {}), {1}: (6, {}), {2}: (7, {}), {3}: (8, {})} | custom-call | flops 1006632960 | bytes 11796480 | tf_op jit(solution)/shard_map/pallas_call | solution.py:115
  141.2 3.6 %maximum_select_fusion.2.kv_own = bf16[4,2,256,768]{3,2,1,0:T(8,128)(2,1)S(1)} fusion(bf16[4,1,256,768]{3,2,1,0:T(8,128)(2,1)} %bitcast.12, bf16[4,1,256,768]{3,2,1,0:T(8,128)(2,1)} %bitcast.11, pred[]{:T(512)S(6)} %eq.12), kind=kLoop, calls=%fused_computation.14 | loop fusion | flops 4718592 | bytes 6291457 | tf_op jit(solution)/shard_map/jit(_where)/select_n | solution.py:396
  145.8 8.3 %shard_map.108.q_other = bf16[4,256,384]{2,1,0:T(8,128)(2,1)S(1)} custom-call(bf16[4,256,5120]{2,1,0:T(8,128)(2,1)S(1)} %copy-done, bf16[5120,384]{1,0:T(8,128)(2,1)} %collective-permute-done.12.w_ref), custom_call_target="tpu_custom_call" | custom-call | flops 4026531840 | bytes 14417920 | tf_op jit(solution)/shard_map/pallas_call | solution.py:138
  154.2 5.0 %shard_map.111.c0 = bf16[512,768]{1,0:T(8,128)(2,1)S(1)} custom-call(s32[31]{0:T(128)S(1)} %pad_add_fusion.meta, bf16[4,256,384]{2,1,0:T(8,128)(2,1)S(1)} %get-tuple-element.85.q_own, bf16[4,256,384]{2,1,0:T(8,128)(2,1)S(1)} %shard_map.108.q_other, bf16[4,2,256,768]{3,2,1,0:T(8,128)(2,1)S(1)} %maximum_select_fusion.2.kv_own, ...), custom_call_target="tpu_custom_call" | custom-call | flops 1207959552 | bytes 8388608 | tf_op jit(solution)/shard_map/pallas_call | solution.py:234
  160.9 5.0 %shard_map.109.c0 = bf16[512,768]{1,0:T(8,128)(2,1)S(1)} custom-call(s32[31]{0:T(128)S(1)} %pad_add_fusion.meta, bf16[4,256,384]{2,1,0:T(8,128)(2,1)S(1)} %get-tuple-element.85.q_own, bf16[4,256,384]{2,1,0:T(8,128)(2,1)S(1)} %shard_map.108.q_other, bf16[4,2,256,768]{3,2,1,0:T(8,128)(2,1)S(1)} %maximum_select_fusion.2.kv_own, ...), custom_call_target="tpu_custom_call" | custom-call | flops 1207959552 | bytes 8388608 | tf_op jit(solution)/shard_map/pallas_call | solution.py:234
  167.4 10.2 %collective-permute-done.22.c3 = bf16[512,768]{1,0:T(8,128)(2,1)S(1)} collective-permute-done((bf16[512,768]{1,0:T(8,128)(2,1)S(1)}, bf16[512,768]{1,0:T(8,128)(2,1)S(1)}, u32[]{:S(2)}, u32[]{:S(2)}) %collective-permute-start.22) | collective-permute-done | bytes 786464 | tf_op jit(solution)/shard_map/ppermute | solution.py:64
  180.7 13.7 %collective-permute-done.16.c3 = bf16[512,768]{1,0:T(8,128)(2,1)S(1)} collective-permute-done((bf16[512,768]{1,0:T(8,128)(2,1)S(1)}, bf16[512,768]{1,0:T(8,128)(2,1)S(1)}, u32[]{:S(2)}, u32[]{:S(2)}) %collective-permute-start.16) | collective-permute-done | bytes 786464 | tf_op jit(solution)/shard_map/ppermute | solution.py:64
  197.4 5.4 %collective-permute-done.23.c2a = bf16[256,768]{1,0:T(8,128)(2,1)S(1)} collective-permute-done((bf16[256,768]{1,0:T(8,128)(2,1)S(1)}, bf16[256,768]{1,0:T(8,128)(2,1)S(1)}, u32[]{:S(2)}, u32[]{:S(2)}) %collective-permute-start.23) | collective-permute-done | bytes 393248 | tf_op jit(solution)/shard_map/ppermute | solution.py:64
  203.5 6.0 %shard_map.112 = bf16[2,256,640]{2,1,0:T(8,128)(2,1)S(1)} custom-call(s32[31]{0:T(128)S(1)} %pad_add_fusion.meta, bf16[512,768]{1,0:T(8,128)(2,1)S(1)} %shard_map.111.c0, bf16[512,768]{1,0:T(8,128)(2,1)S(1)} %collective-permute-done.21.c1, bf16[256,768]{1,0:T(8,128)(2,1)S(1)} %collective-permute-done.23.c2a, ...), custom_call_target="tpu_custom_call" | custom-call | flops 2013265920 | bytes 8388608 | tf_op jit(solution)/shard_map/pallas_call | solution.py:290
  209.6 2.6 %collective-permute-start.25 = (bf16[2,256,640]{2,1,0:T(8,128)(2,1)S(1)}, bf16[2,256,640]{2,1,0:T(8,128)(2,1)}, u32[]{:S(2)}, u32[]{:S(2)}) collective-permute-start(bf16[2,256,640]{2,1,0:T(8,128)(2,1)S(1)} %shard_map.112), channel_id=1, source_target_pairs={{0,4},{1,5},{2,6},{3,7},{4,0},{5,1},{6,2},{7,3},{8,11},{9,10},{10,... | collective-permute-start | bytes 1966088 | tf_op jit(solution)/shard_map/ppermute | solution.py:64
  212.2 6.8 %shard_map.110 = bf16[2,256,640]{2,1,0:T(8,128)(2,1)} custom-call(s32[31]{0:T(128)S(1)} %pad_add_fusion.meta, bf16[512,768]{1,0:T(8,128)(2,1)S(1)} %shard_map.109.c0, bf16[512,768]{1,0:T(8,128)(2,1)S(1)} %collective-permute-done.15.c1, bf16[256,768]{1,0:T(8,128)(2,1)S(1)} %collective-permute-done.17.c2a, bf16[256,768]{1,0:T(8,128)(2,1)S(1)} %collective-permute-done.18.c2b, ...), custom_call_target="tpu_custom_call" | custom-call | flops 2013265920 | bytes 8388608 | tf_op jit(solution)/shard_map/pallas_call | solution.py:290
  219.0 2.3 collective-permute-start.20
  221.3 6.8 %shard_map.113.prior = bf16[8,256,640]{2,1,0:T(8,128)(2,1)} custom-call(s32[31]{0:T(128)S(1)} %pad_add_fusion.meta, bf16[512,768]{1,0:T(8,128)(2,1)S(1)} %shard_map.111.c0, bf16[512,768]{1,0:T(8,128)(2,1)S(1)} %collective-permute-done.21.c1, bf16[256,768]{1,0:T(8,128)(2,1)S(1)} %collective-permute-done.23.c2a, ...), custom_call_target="tpu_custom_call" | custom-call | flops 2013265920 | bytes 8388608 | tf_op jit(solution)/shard_map/pallas_call | solution.py:290
  228.1 2.6 %shard_map.114.refs_0_ = bf16[8,256,640]{2,1,0:T(8,128)(2,1)} custom-call(s32[31]{0:T(128)} %copy-done.17, bf16[2,256,640]{2,1,0:T(8,128)(2,1)} %collective-permute-done.25.got, bf16[8,256,640]{2,1,0:T(8,128)(2,1)} %shard_map.113.prior), custom_call_target="tpu_custom_call", output_to_operand_aliasing={{}: (2, {})} | custom-call | tf_op jit(solution)/shard_map/pallas_call | solution.py:314
  232.8 6.7 %shard_map.115.prior = bf16[8,256,640]{2,1,0:T(8,128)(2,1)} custom-call(s32[31]{0:T(128)S(1)} %copy-done.18, bf16[512,768]{1,0:T(8,128)(2,1)S(1)} %copy-done.5, bf16[512,768]{1,0:T(8,128)(2,1)S(1)} %copy-done.9, bf16[256,768]{1,0:T(8,128)(2,1)S(1)} %copy-done.12, bf16[256,768]{1,0:T(8,128)(2,1)S(1)} %copy-done.14, ...), custom_call_target="tpu_custom_call", output_to_operand_aliasing={{}: (8, {})} | custom-call | flops 2013265920 | bytes 8388608 | tf_op jit(solution)/shard_map/pallas_call | solution.py:290
  239.6 2.5 %shard_map.116 = bf16[8,256,640]{2,1,0:T(8,128)(2,1)} custom-call(s32[31]{0:T(128)} %copy-done.17, bf16[2,256,640]{2,1,0:T(8,128)(2,1)} %collective-permute-done.20.got, bf16[8,256,640]{2,1,0:T(8,128)(2,1)} %shard_map.115.prior), custom_call_target="tpu_custom_call", output_to_operand_aliasing={{}: (2, {})} | custom-call | tf_op jit(solution)/shard_map/pallas_call | solution.py:314
  (104 shorter events, 47.7 us)
Async XLA Ops:
  0.0 68.6 %collective-permute-start.6 = (bf16[256,5120]{1,0:T(8,128)(2,1)}, bf16[256,5120]{1,0:T(8,128)(2,1)S(1)}, u32[]{:S(2)}, u32[]{:S(2)}) collective-permute-start(bf16[256,5120]{1,0:T(8,128)(2,1)} %bitcast.32), channel_id=1, source_target_pairs={{0,1},{1,2},{2,3},{3,0},{4,5},{5,6},{6,7},{7,4},{8,12},{9,8},{10,1... | collective-permute-start | bytes 7864328 | tf_op jit(solution)/shard_map/ppermute | solution.py:64
  2.1 66.5 %collective-permute-start.7 = (bf16[256,5120]{1,0:T(8,128)(2,1)}, bf16[256,5120]{1,0:T(8,128)(2,1)}, u32[]{:S(2)}, u32[]{:S(2)}) collective-permute-start(bf16[256,5120]{1,0:T(8,128)(2,1)} %bitcast.33), channel_id=1, source_target_pairs={{0,3},{1,0},{2,1},{3,2},{4,7},{5,4},{6,5},{7,6},{8,9},{9,13},{10,1... | collective-permute-start | bytes 7864328 | tf_op jit(solution)/shard_map/ppermute | solution.py:64
  11.0 27.2 %collective-permute-start = (bf16[128,768]{1,0:T(8,128)(2,1)S(1)}, bf16[128,768]{1,0:T(8,128)(2,1)S(1)}, u32[]{:S(2)}, u32[]{:S(2)}) collective-permute-start(bf16[128,768]{1,0:T(8,128)(2,1)S(1)} %get-tuple-element.126), channel_id=1, source_target_pairs={{0,64},{1,65},{2,66},{3,67},{4,68},{5,69},{6,70},{7,71},{8,72},{9,... | collective-permute-start | bytes 589832 | tf_op jit(solution)/shard_map/cond/branch_1_fun/ppermute | solution.py:64
  38.3 1.8 collective-permute-start.1
  40.4 11.9 %collective-permute-start.4 = (bf16[256,768]{1,0:T(8,128)(2,1)S(1)}, bf16[256,768]{1,0:T(8,128)(2,1)S(1)}, u32[]{:S(2)}, u32[]{:S(2)}) collective-permute-start(bf16[256,768]{1,0:T(8,128)(2,1)S(1)} %fusion.8), channel_id=1, source_target_pairs={{0,16},{1,17},{2,18},{3,19},{4,20},{5,21},{6,22},{7,23},{8,24},{9,... | collective-permute-start | bytes 1179656 | tf_op jit(solution)/shard_map/cond/branch_1_fun/ppermute | solution.py:64
  41.7 10.6 %collective-permute-start.3 = (bf16[256,768]{1,0:T(8,128)(2,1)S(1)}, bf16[256,768]{1,0:T(8,128)(2,1)S(1)}, u32[]{:S(2)}, u32[]{:S(2)}) collective-permute-start(bf16[256,768]{1,0:T(8,128)(2,1)S(1)} %fusion.8), channel_id=1, source_target_pairs={{0,48},{1,49},{2,50},{3,51},{4,52},{5,53},{6,54},{7,55},{8,56},{9,... | collective-permute-start | bytes 1179656 | tf_op jit(solution)/shard_map/cond/branch_1_fun/ppermute | solution.py:64
  43.2 21.6 %collective-permute-start.2 = (bf16[2,256,768]{2,1,0:T(8,128)(2,1)S(1)}, bf16[2,256,768]{2,1,0:T(8,128)(2,1)}, u32[]{:S(2)}, u32[]{:S(2)}) collective-permute-start(bf16[2,256,768]{2,1,0:T(8,128)(2,1)S(1)} %maximum_select_fusion), channel_id=1, source_target_pairs={{0,4},{1,5},{2,6},{3,7},{4,0},{5,1},{6,2},{7,3},{8,11},{9,10},{10,... | collective-permute-start | bytes 2359304 | tf_op jit(solution)/shard_map/cond/branch_1_fun/ppermute | solution.py:64
  52.3 11.2 %collective-permute-start.5 = (bf16[256,768]{1,0:T(8,128)(2,1)S(1)}, bf16[256,768]{1,0:T(8,128)(2,1)S(1)}, u32[]{:S(2)}, u32[]{:S(2)}) collective-permute-start(bf16[256,768]{1,0:T(8,128)(2,1)S(1)} %fusion.8), channel_id=1, source_target_pairs={{0,32},{1,33},{2,34},{3,35},{4,36},{5,37},{6,38},{7,39},{8,40},{9,... | collective-permute-start | bytes 1179656 | tf_op jit(solution)/shard_map/cond/branch_1_fun/ppermute | solution.py:64
  64.8 61.5 %collective-permute-start.12 = (bf16[5120,384]{1,0:T(8,128)(2,1)}, bf16[5120,384]{1,0:T(8,128)(2,1)}, u32[]{:S(2)}, u32[]{:S(2)}) collective-permute-start(bf16[5120,384]{1,0:T(8,128)(2,1)} %bitcast.27), channel_id=1, source_target_pairs={{0,4},{1,5},{2,6},{3,7},{4,0},{5,1},{6,2},{7,3},{8,11},{9,10},{10,... | collective-permute-start | bytes 11796488 | tf_op jit(solution)/shard_map/ppermute | solution.py:64
  68.6 8.4 %copy-start.15 = (f32[1,5120]{1,0:T(1,128)S(1)}, f32[1,5120]{1,0:T(1,128)}, u32[]{:S(2)}) copy-start(f32[1,5120]{1,0:T(1,128)} %refs_2_.1) | copy-start | bytes 61444
  69.9 29.8 %collective-permute-start.8 = (bf16[128,5120]{1,0:T(8,128)(2,1)}, bf16[128,5120]{1,0:T(8,128)(2,1)}, u32[]{:S(2)}, u32[]{:S(2)}) collective-permute-start(bf16[128,5120]{1,0:T(8,128)(2,1)} %slice.26), channel_id=1, source_target_pairs={{0,1},{1,2},{2,3},{3,0},{4,5},{5,6},{6,7},{7,4},{8,12},{9,8},{10,1... | collective-permute-start | bytes 3932168 | tf_op jit(solution)/shard_map/ppermute | solution.py:64
  73.2 31.2 %collective-permute-start.9 = (bf16[128,5120]{1,0:T(8,128)(2,1)}, bf16[128,5120]{1,0:T(8,128)(2,1)}, u32[]{:S(2)}, u32[]{:S(2)}) collective-permute-start(bf16[128,5120]{1,0:T(8,128)(2,1)} %slice.27), channel_id=1, source_target_pairs={{0,3},{1,0},{2,1},{3,2},{4,7},{5,4},{6,5},{7,6},{8,9},{9,13},{10,1... | collective-permute-start | bytes 3932168 | tf_op jit(solution)/shard_map/ppermute | solution.py:64
  73.9 20.1 %collective-permute-start.10 = (bf16[2,256,768]{2,1,0:T(8,128)(2,1)}, bf16[2,256,768]{2,1,0:T(8,128)(2,1)}, u32[]{:S(2)}, u32[]{:S(2)}) collective-permute-start(bf16[2,256,768]{2,1,0:T(8,128)(2,1)} %get-tuple-element.89), channel_id=1, source_target_pairs={{0,48},{1,49},{2,50},{3,51},{4,52},{5,53},{6,54},{7,55},{8,56},{9,... | collective-permute-start | bytes 2359304 | tf_op jit(solution)/shard_map/ppermute | solution.py:64
  76.0 18.1 %collective-permute-start.11 = (bf16[2,256,768]{2,1,0:T(8,128)(2,1)}, bf16[2,256,768]{2,1,0:T(8,128)(2,1)}, u32[]{:S(2)}, u32[]{:S(2)}) collective-permute-start(bf16[2,256,768]{2,1,0:T(8,128)(2,1)} %get-tuple-element.89), channel_id=1, source_target_pairs={{0,16},{1,17},{2,18},{3,19},{4,20},{5,21},{6,22},{7,23},{8,24},{9,... | collective-permute-start | bytes 2359304 | tf_op jit(solution)/shard_map/ppermute | solution.py:64
  80.9 140.4 %copy-start.17 = (s32[31]{0:T(128)}, s32[31]{0:T(128)S(1)}, u32[]{:S(2)}) copy-start(s32[31]{0:T(128)S(1)} %pad_add_fusion.meta) | copy-start | bytes 376
  104.4 21.9 %collective-permute-start.14 = (bf16[4,256,768]{2,1,0:T(8,128)(2,1)}, bf16[4,256,768]{2,1,0:T(8,128)(2,1)}, u32[]{:S(2)}, u32[]{:S(2)}) collective-permute-start(bf16[4,256,768]{2,1,0:T(8,128)(2,1)} %get-tuple-element.91), channel_id=1, source_target_pairs={{0,8},{1,9},{2,10},{3,11},{4,12},{5,13},{6,14},{7,15},{8,0},{9,1},... | collective-permute-start | bytes 4718600 | tf_op jit(solution)/shard_map/ppermute | solution.py:64
  105.2 21.1 %collective-permute-start.13 = (bf16[2,256,768]{2,1,0:T(8,128)(2,1)}, bf16[2,256,768]{2,1,0:T(8,128)(2,1)}, u32[]{:S(2)}, u32[]{:S(2)}) collective-permute-start(bf16[2,256,768]{2,1,0:T(8,128)(2,1)} %get-tuple-element.89), channel_id=1, source_target_pairs={{0,32},{1,33},{2,34},{3,35},{4,36},{5,37},{6,38},{7,39},{8,40},{9,... | collective-permute-start | bytes 2359304 | tf_op jit(solution)/shard_map/ppermute | solution.py:64
  126.3 77.2 %collective-permute-start.19 = (bf16[3072,640]{1,0:T(8,128)(2,1)}, bf16[3072,640]{1,0:T(8,128)(2,1)}, u32[]{:S(2)}, u32[]{:S(2)}) collective-permute-start(bf16[3072,640]{1,0:T(8,128)(2,1)} %bitcast.18), channel_id=1, source_target_pairs={{0,4},{1,5},{2,6},{3,7},{4,0},{5,1},{6,2},{7,3},{8,11},{9,10},{10,... | collective-permute-start | bytes 11796488 | tf_op jit(solution)/shard_map/ppermute | solution.py:64
  139.0 6.8 %copy-start = (bf16[4,256,5120]{2,1,0:T(8,128)(2,1)S(1)}, bf16[4,256,5120]{2,1,0:T(8,128)(2,1)}, u32[]{:S(2)}) copy-start(bf16[4,256,5120]{2,1,0:T(8,128)(2,1)} %get-tuple-element.86.n_ref) | copy-start | bytes 31457284
  145.8 8.4 %copy-start.3 = (s32[8,256,1]{2,1,0:T(8,128)S(1)}, s32[8,256,1]{2,1,0:T(8,128)}, u32[]{:S(2)}) copy-start(s32[8,256,1]{2,1,0:T(8,128)} %reshape.35.seg_col) | copy-start | bytes 24580
  159.1 18.5 %collective-permute-start.22 = (bf16[512,768]{1,0:T(8,128)(2,1)S(1)}, bf16[512,768]{1,0:T(8,128)(2,1)S(1)}, u32[]{:S(2)}, u32[]{:S(2)}) collective-permute-start(bf16[512,768]{1,0:T(8,128)(2,1)S(1)} %shard_map.111.c0), channel_id=1, source_target_pairs={{0,1},{1,2},{2,3},{3,0},{4,5},{5,6},{6,7},{7,4},{8,12},{9,8},{10,1... | collective-permute-start | bytes 2359304 | tf_op jit(solution)/shard_map/ppermute | solution.py:64
  160.0 19.8 %collective-permute-start.21 = (bf16[512,768]{1,0:T(8,128)(2,1)S(1)}, bf16[512,768]{1,0:T(8,128)(2,1)S(1)}, u32[]{:S(2)}, u32[]{:S(2)}) collective-permute-start(bf16[512,768]{1,0:T(8,128)(2,1)S(1)} %shard_map.111.c0), channel_id=1, source_target_pairs={{0,3},{1,0},{2,1},{3,2},{4,7},{5,4},{6,5},{7,6},{8,9},{9,13},{10,1... | collective-permute-start | bytes 2359304 | tf_op jit(solution)/shard_map/ppermute | solution.py:64
  165.9 46.3 %copy-start.4 = (bf16[512,768]{1,0:T(8,128)(2,1)}, bf16[512,768]{1,0:T(8,128)(2,1)S(1)}, u32[]{:S(2)}) copy-start(bf16[512,768]{1,0:T(8,128)(2,1)S(1)} %shard_map.109.c0) | copy-start | bytes 2359300
  165.9 28.5 %collective-permute-start.16 = (bf16[512,768]{1,0:T(8,128)(2,1)S(1)}, bf16[512,768]{1,0:T(8,128)(2,1)S(1)}, u32[]{:S(2)}, u32[]{:S(2)}) collective-permute-start(bf16[512,768]{1,0:T(8,128)(2,1)S(1)} %shard_map.109.c0), channel_id=1, source_target_pairs={{0,1},{1,2},{2,3},{3,0},{4,5},{5,6},{6,7},{7,4},{8,12},{9,8},{10,1... | collective-permute-start | bytes 2359304 | tf_op jit(solution)/shard_map/ppermute | solution.py:64
  166.6 28.5 %collective-permute-start.15 = (bf16[512,768]{1,0:T(8,128)(2,1)S(1)}, bf16[512,768]{1,0:T(8,128)(2,1)S(1)}, u32[]{:S(2)}, u32[]{:S(2)}) collective-permute-start(bf16[512,768]{1,0:T(8,128)(2,1)S(1)} %shard_map.109.c0), channel_id=1, source_target_pairs={{0,3},{1,0},{2,1},{3,2},{4,7},{5,4},{6,5},{7,6},{8,9},{9,13},{10,1... | collective-permute-start | bytes 2359304 | tf_op jit(solution)/shard_map/ppermute | solution.py:64
  177.7 25.1 %collective-permute-start.23 = (bf16[256,768]{1,0:T(8,128)(2,1)S(1)}, bf16[256,768]{1,0:T(8,128)(2,1)S(1)}, u32[]{:S(2)}, u32[]{:S(2)}) collective-permute-start(bf16[256,768]{1,0:T(8,128)(2,1)S(1)} %slice.35), channel_id=1, source_target_pairs={{0,1},{1,2},{2,3},{3,0},{4,5},{5,6},{6,7},{7,4},{8,12},{9,8},{10,1... | collective-permute-start | bytes 1179656 | tf_op jit(solution)/shard_map/ppermute | solution.py:64
  179.9 23.6 %collective-permute-start.24 = (bf16[256,768]{1,0:T(8,128)(2,1)S(1)}, bf16[256,768]{1,0:T(8,128)(2,1)S(1)}, u32[]{:S(2)}, u32[]{:S(2)}) collective-permute-start(bf16[256,768]{1,0:T(8,128)(2,1)S(1)} %slice.36), channel_id=1, source_target_pairs={{0,3},{1,0},{2,1},{3,2},{4,7},{5,4},{6,5},{7,6},{8,9},{9,13},{10,1... | collective-permute-start | bytes 1179656 | tf_op jit(solution)/shard_map/ppermute | solution.py:64
  194.4 17.8 %collective-permute-start.17 = (bf16[256,768]{1,0:T(8,128)(2,1)S(1)}, bf16[256,768]{1,0:T(8,128)(2,1)S(1)}, u32[]{:S(2)}, u32[]{:S(2)}) collective-permute-start(bf16[256,768]{1,0:T(8,128)(2,1)S(1)} %slice.33), channel_id=1, source_target_pairs={{0,1},{1,2},{2,3},{3,0},{4,5},{5,6},{6,7},{7,4},{8,12},{9,8},{10,1... | collective-permute-start | bytes 1179656 | tf_op jit(solution)/shard_map/ppermute | solution.py:64
  195.1 17.1 %copy-start.8 = (bf16[512,768]{1,0:T(8,128)(2,1)}, bf16[512,768]{1,0:T(8,128)(2,1)S(1)}, u32[]{:S(2)}) copy-start(bf16[512,768]{1,0:T(8,128)(2,1)S(1)} %collective-permute-done.15.c1) | copy-start | bytes 2359300
  195.1 17.1 %collective-permute-start.18 = (bf16[256,768]{1,0:T(8,128)(2,1)S(1)}, bf16[256,768]{1,0:T(8,128)(2,1)S(1)}, u32[]{:S(2)}, u32[]{:S(2)}) collective-permute-start(bf16[256,768]{1,0:T(8,128)(2,1)S(1)} %slice.34), channel_id=1, source_target_pairs={{0,3},{1,0},{2,1},{3,2},{4,7},{5,4},{6,5},{7,6},{8,9},{9,13},{10,1... | collective-permute-start | bytes 1179656 | tf_op jit(solution)/shard_map/ppermute | solution.py:64
  209.6 18.5 %collective-permute-start.25 = (bf16[2,256,640]{2,1,0:T(8,128)(2,1)S(1)}, bf16[2,256,640]{2,1,0:T(8,128)(2,1)}, u32[]{:S(2)}, u32[]{:S(2)}) collective-permute-start(bf16[2,256,640]{2,1,0:T(8,128)(2,1)S(1)} %shard_map.112), channel_id=1, source_target_pairs={{0,4},{1,5},{2,6},{3,7},{4,0},{5,1},{6,2},{7,3},{8,11},{9,10},{10,... | collective-permute-start | bytes 1966088 | tf_op jit(solution)/shard_map/ppermute | solution.py:64
  219.0 20.6 %collective-permute-start.20 = (bf16[2,256,640]{2,1,0:T(8,128)(2,1)}, bf16[2,256,640]{2,1,0:T(8,128)(2,1)}, u32[]{:S(2)}, u32[]{:S(2)}) collective-permute-start(bf16[2,256,640]{2,1,0:T(8,128)(2,1)} %shard_map.110), channel_id=1, source_target_pairs={{0,4},{1,5},{2,6},{3,7},{4,0},{5,1},{6,2},{7,3},{8,11},{9,10},{10,... | collective-permute-start | bytes 1966088 | tf_op jit(solution)/shard_map/ppermute | solution.py:64
  (16 other events, 57.0 us)

commit v3 on v2

--- a/solution.py
+++ b/solution.py
@@ -26,8 +26,8 @@
 def facts_of(core, c):
     half, r = SPOT[core][c]
     mine, theirs = PLACE[core][half], PLACE[core][1 - half]
-    slots = [(p - r) % 4 for p in range(4)]
-    ring = [(r + j) % 4 for j in range(4)]
+    ring = [r, r ^ 1, (r + 2) % 4, 3 - r]
+    slots = [ring.index(p) for p in range(4)]
     rows = [place[p] for p in ring for place in (mine, theirs)]
     return [*mine, *theirs, *slots, *rows, mine[r], theirs[r]]
 
@@ -50,11 +50,13 @@
     return pairs
 
 
-NEXT = moves(lambda yh, x, k, h, r: (yh, x, k, h, r + 1))
-PREV = moves(lambda yh, x, k, h, r: (yh, x, k, h, r - 1))
+IN = moves(lambda yh, x, k, h, r: (yh, x, k, h, r ^ 1))
+OUT = moves(lambda yh, x, k, h, r: (yh, x, k, h, 3 - r))
 PARTNER = moves(lambda yh, x, k, h, r: (yh, x, k, 1 - h, r))
 CORE = moves(lambda yh, x, k, h, r: (yh, x, 1 - k, h, r))
-FAR_Y = moves(lambda yh, x, k, h, r: (1 - yh, x, k, h, r))
+FAR_Y = [
+    (a, b) for a, b in moves(lambda yh, x, k, h, r: (1 - yh, x, k, h, r)) if a // 8 % 2 == 0
+]
 X_NEXT = moves(lambda yh, x, k, h, r: (yh, x + 1, k, h, r))
 X_PREV = moves(lambda yh, x, k, h, r: (yh, x - 1, k, h, r))
 X_FAR = moves(lambda yh, x, k, h, r: (yh, x + 2, k, h, r))
@@ -129,18 +131,22 @@
     )(meta, *ins)
 
 
-def more_queries_kernel(n_ref, w_ref, q_ref):
-    q_ref[0] = jnp.dot(n_ref[0], w_ref[...], preferred_element_type=F32).astype(BF)
-
-
-def more_queries(normed, w):
-    d, n = w.shape
+def more_queries_kernel(n_ref, wa_ref, wb_ref, q_ref):
+    k = wa_ref.shape[0]
+    q = jnp.dot(n_ref[0, :, :k], wa_ref[...], preferred_element_type=F32)
+    q += jnp.dot(n_ref[0, :, k:], wb_ref[...], preferred_element_type=F32)
+    q_ref[0] = q.astype(BF)
+
+
+def more_queries(normed, wa, wb):
+    d, n = normed.shape[2], wa.shape[1]
     return pl.pallas_call(
         more_queries_kernel,
         grid=(4,),
         in_specs=[
             pl.BlockSpec((1, RB, d), lambda i: (i, 0, 0)),
-            pl.BlockSpec((d, n), lambda i: (0, 0)),
+            pl.BlockSpec(wa.shape, lambda i: (0, 0)),
+            pl.BlockSpec(wb.shape, lambda i: (0, 0)),
         ],
         out_specs=pl.BlockSpec((1, RB, n), lambda i: (i, 0, 0)),
         out_shape=jax.ShapeDtypeStruct((4, RB, n), BF),
@@ -148,7 +154,7 @@
         cost_estimate=pl.CostEstimate(
             flops=8 * RB * d * n, bytes_accessed=2 * (4 * RB * d + d * n), transcendentals=0
         ),
-    )(normed, w)
+    )(normed, wa, wb)
 
 
 def attend_kernel(
@@ -254,29 +260,45 @@
     )(meta, q_own, q_other, kv_own, kv_other, seg_col, seg_row)
 
 
+def reorder_kernel(meta, w, out):
+    out[...] = w[...]
+
+
+def reorder(meta, w, swap):
+    k8, n, width = w.shape
+    return pl.pallas_call(
+        reorder_kernel,
+        grid_spec=pltpu.PrefetchScalarGridSpec(
+            num_scalar_prefetch=1,
+            grid=(k8,),
+            in_specs=[
+                pl.BlockSpec((1, n, width), lambda k, m: (m[ROWS + (k + swap - 2 * swap * (k % 2))], 0, 0))
+            ],
+            out_specs=pl.BlockSpec((1, n, width), lambda k, m: (k, 0, 0)),
+        ),
+        out_shape=jax.ShapeDtypeStruct(w.shape, BF),
+    )(meta, w).reshape(k8 * n, width)
+
+
 def finish_kernel(meta, c0, c1, c2a, c2b, c3, w, res, *refs):
     out = refs[-1]
     t = pl.program_id(0)
     far = jnp.where(t == 0, c2a[...], c2b[...])
-    n = w.shape[1]
-    total = jnp.zeros((RB, w.shape[2]), F32)
+    n = far.shape[1]
+    total = res[0].astype(F32)
     for j, c in enumerate((c0[...], c1[...], far, c3[...])):
-        for k in range(2):
-            total += jnp.dot(
-                c[:, k * n : (k + 1) * n],
-                w[meta[ROWS + 2 * j + k]],
-                preferred_element_type=F32,
-            )
-    out[0] = (res[0].astype(F32) + total).astype(BF)
+        total += jnp.dot(c, w[j * n : (j + 1) * n, :], preferred_element_type=F32)
+    out[0] = total.astype(BF)
 
 
 def finish(meta, chunk, parts, w, res, blocks, prior=None):
-    k8, n, width = w.shape
-    tile = pl.BlockSpec((RB, 2 * n), lambda t, m: (t, 0))
-    fixed = pl.BlockSpec((RB, 2 * n), lambda t, m: (0, 0))
+    depth, width = w.shape
+    n = depth // 4
+    tile = pl.BlockSpec((RB, n), lambda t, m: (t, 0))
+    fixed = pl.BlockSpec((RB, n), lambda t, m: (0, 0))
     ins = list(parts) + [w, res]
     specs = [tile, tile, fixed, fixed, tile]
-    specs.append(pl.BlockSpec(w.shape, lambda t, m: (0, 0, 0)))
+    specs.append(pl.BlockSpec(w.shape, lambda t, m: (0, 0)))
     specs.append(pl.BlockSpec((1, RB, width), lambda t, m: (m[SLOT + 2 * chunk + t], 0, 0)))
     aliases = {}
     if prior is not None:
@@ -299,7 +321,7 @@
         input_output_aliases=aliases,
         compiler_params=pltpu.CompilerParams(vmem_limit_bytes=32 * MIB),
         cost_estimate=pl.CostEstimate(
-            flops=4 * RB * k8 * n * width, bytes_accessed=8 * MIB, transcendentals=0
+            flops=4 * RB * depth * width, bytes_accessed=8 * MIB, transcendentals=0
         ),
     )(meta, *ins)
 
@@ -343,9 +365,9 @@
     w_o = w_out[0]
     width = w_o.shape[1]
 
-    xp = send(x0, NEXT)
-    xn = send(x0, PREV)
-    w_q2 = send(w_q, PARTNER)
+    x_in = send(x0, IN)
+    x_out = send(x0, OUT)
+    cut = w_q.shape[0] * 2 // 5
 
     ids = segment_ids.reshape(8, RB)
     starts = jnp.sum(segment_ids[None, :] < ids[:, :1], axis=1, dtype=jnp.int32) // RB
@@ -355,68 +377,79 @@
     seg_col = segment_ids.reshape(8, RB, 1)
     seg_row = segment_ids.reshape(8, 1, RB)
 
-    def cache(last_hidden, w_key, w_value):
+    def cache(last_hidden, w_key, w_value, w_query):
         kv_in = normalize(last_hidden, kv_gain)
         own_k = jnp.dot(kv_in, w_key, preferred_element_type=F32).astype(BF)
         own_v = jnp.dot(kv_in, w_value, preferred_element_type=F32).astype(BF)
         kv = jnp.concatenate([own_k, own_v], axis=1)
-        kv_far = send(kv, FAR_Y)
-        pair = jnp.where(y_hi == 0, jnp.stack([kv, kv_far]), jnp.stack([kv_far, kv]))
-        pair2 = send(pair, CORE)
-        piece = jnp.where(
-            core == 0,
-            jnp.concatenate([pair, pair2], axis=1),
-            jnp.concatenate([pair2, pair], axis=1),
-        )
+        kv2 = send(kv, CORE)
+        pair = jnp.where(core == 0, jnp.stack([kv, kv2]), jnp.stack([kv2, kv]))
+        far = send(pair, FAR_Y)
+        far = jnp.where(core == 0, far, send(far, CORE))
+        piece = jnp.where(y_hi == 0, jnp.stack([pair, far]), jnp.stack([far, pair]))
+        piece = piece.reshape(2, 2 * kv.shape[0], kv.shape[1])
         piece2 = send(piece, PARTNER)
         share = lax.dynamic_index_in_dim(piece, core, 0, keepdims=False)
-        o1 = send(share, X_PREV)
-        o3 = send(share, X_NEXT)
-        o2 = send(after(share, o1, o3), X_FAR)
-        return piece2, jnp.stack([share, o1, o2, o3])
-
-    def nothing(last_hidden, w_key, w_value):
-        half_rows = 2 * last_hidden.shape[0]
+        o2 = send(share, X_FAR)
+        piece2, o2, w_first = lax.optimization_barrier((piece2, o2, w_query[:cut]))
+        t2 = send(piece2, X_FAR)
+        w_first = send(w_first, PARTNER)
+        return share, o2, piece2, t2, w_first, w_query[cut:]
+
+    def nothing(last_hidden, w_key, w_value, w_query):
+        rows = 2 * last_hidden.shape[0]
         cols = 2 * w_key.shape[1]
-        return jnp.zeros((2, half_rows, cols), BF), jnp.zeros((4, half_rows, cols), BF)
-
-    piece2, got = lax.cond(segment_ids[0] >= 0, cache, nothing, last_hidden, w_key, w_value)
-    xp, xn, piece2, got = lax.optimization_barrier((xp, xn, piece2, got))
-    xo_a = send(xp[: RB // 2], NEXT)
-    xo_b = send(xn[RB // 2 :], PREV)
-    t1 = send(piece2, X_PREV)
-    t3 = send(piece2, X_NEXT)
-    state = project(meta, [after(x0, xp, xn)], query_gain, w_q, 0, width)
-    state = project(meta, [xn], query_gain, w_q, 1, width, state)
-    state = project(meta, [xp], query_gain, w_q, 3, width, state)
-    xo_a, xo_b, t1, t3, *state = lax.optimization_barrier((xo_a, xo_b, t1, t3, *state))
-    t2 = send(after(piece2, t1, t3), X_FAR)
-    got2 = send(after(got, t1, t3), CORE)
-    w_q2, t2, got2 = lax.optimization_barrier((w_q2, t2, got2))
+        few = jnp.zeros((rows, cols), BF)
+        more = jnp.zeros((2, rows, cols), BF)
+        first, rest = w_query[:cut], w_query[cut:]
+        return few, few, more, more, jnp.zeros_like(first), jnp.zeros_like(rest)
+
+    share, o2, piece2, t2, w_q2a, w_rest = lax.cond(
+        segment_ids[0] >= 0, cache, nothing, last_hidden, w_key, w_value, w_q
+    )
+    w_q2b = send(w_rest, PARTNER)
+    x_in, x_out, share, piece2 = lax.optimization_barrier((x_in, x_out, share, piece2))
+    xo_a = send(x_out[: RB // 2], IN)
+    xo_b = send(x_in[RB // 2 :], OUT)
+    both = jnp.concatenate([share[None], piece2])
+    s1 = send(both, X_PREV)
+    s3 = send(both, X_NEXT)
+    heads_cols = w_q.shape[1]
+    w_o_r = after(w_o, x_in, x_out).reshape(8, heads_cols, width)
+    w_o_mine, w_o_theirs = reorder(meta, w_o_r, 0), reorder(meta, w_o_r, 1)
+    state = project(meta, [after(x0, x_in, x_out)], query_gain, w_q, 0, width)
+    state = project(meta, [x_in], query_gain, w_q, 1, width, state)
+    state = project(meta, [x_out], query_gain, w_q, 3, width, state)
+    xo_a, xo_b, s1, s3, w_o_mine, w_o_theirs, *state = lax.optimization_barrier(
+        (xo_a, xo_b, s1, s3, w_o_mine, w_o_theirs, *state)
+    )
+    got = jnp.stack([share, s1[0], o2, s3[0]])
+    got2 = send(got, CORE)
     kv_own = jnp.where(
         core == 0, jnp.stack([got, got2], axis=1), jnp.stack([got2, got], axis=1)
     )
-    kv_other = jnp.stack([piece2, t1, t2, t3])
+    kv_other = jnp.stack([piece2, s1[1:], t2, s3[1:]])
     normed, q_own, res_own, res_other = project(
         meta, [xo_a, xo_b], query_gain, w_q, 2, width, state
     )
-    w_o2 = send(after(w_o, xo_a, xo_b, w_q2), PARTNER)
-    q_other = more_queries(normed, w_q2)
-
-    heads_cols = w_q.shape[1]
-    w_o_r = w_o.reshape(8, heads_cols, width)
-    w_o2_r = w_o2.reshape(8, heads_cols, width)
+    (w_q2b, kv_own, kv_other, normed, q_own, seg_col, seg_row, w_o_theirs) = (
+        lax.optimization_barrier(
+            (w_q2b, kv_own, kv_other, normed, q_own, seg_col, seg_row, w_o_theirs)
+        )
+    )
+    w_o2 = send(w_o_theirs, PARTNER)
+    q_other = more_queries(normed, w_q2a, w_q2b)
 
     result = None
     for chunk in range(2):
         own = attend(meta, chunk, q_own, q_other, kv_own, kv_other, seg_col, seg_row)
-        cp = send(own, NEXT)
-        cn = send(own, PREV)
-        co_a = send(cp[:RB], NEXT)
-        co_b = send(cn[RB:], PREV)
-        parts = (own, cn, co_a, co_b, cp)
-        sent = send(finish(meta, chunk, parts, w_o2_r, res_other, 2), PARTNER)
-        result = finish(meta, chunk, parts, w_o_r, res_own, 8, result)
+        c_in = send(own, IN)
+        c_out = send(own, OUT)
+        co_a = send(c_out[:RB], IN)
+        co_b = send(c_in[RB:], OUT)
+        parts = (own, c_in, co_a, co_b, c_out)
+        sent = send(finish(meta, chunk, parts, w_o2, res_other, 2), PARTNER)
+        result = finish(meta, chunk, parts, w_o_mine, res_own, 8, result)
         result = place(meta, chunk, sent, result)
     return result.reshape(1, 8 * RB, -1)
 

time: 243 us -> 240 us (0.988)
  waiting for transfers between devices: 100 us -> 57.1 us
  Pallas kernels: 68.2 us -> 84.3 us
  local copies, waits for them, and re-layouts: 17.4 us -> 27.3 us
  starting transfers between devices: 41.5 us -> 49.9 us
  other arithmetic: 9.46 us -> 14.8 us
    ppermute x26, waiting for transfers between devices: 100 us -> 57.1 us  [send(): return lax.ppermute(value, AXES, pairs)]
    pallas_call x0 -> x2, Pallas kernels: none -> 14.6 us  [reorder(): pl.pallas_call(reorder_kernel, grid_spec=pltpu.PrefetchScalarGridSpec(num...]
    ppermute x26, starting transfers between devices: 41.5 us -> 49.9 us  [send(): return lax.ppermute(value, AXES, pairs)]
    pallas_call x4, Pallas kernels: 26.3 us -> 20.1 us  [finish(): pl.pallas_call(finish_kernel, grid_spec=pltpu.PrefetchScalarGridSpec(num_...]
    slice x6 -> x10, local copies, waits for them, and re-layouts: 3.84 us -> 9.21 us  [the longest x1 2.59 us: body(): xo_b = send(x_in[RB // 2:], OUT)]
    pallas_call x2, Pallas kernels: 9.96 us -> 13.9 us  [attend(): pl.pallas_call(functools.partial(attend_kernel, chunk), grid_spec=pltpu.P...]
    pallas_call x4, Pallas kernels: 18.5 us -> 22.2 us  [project(): pl.pallas_call(kernel, grid_spec=pltpu.PrefetchScalarGridSpec(num_scalar_...]
    optimization_barrier x0 -> x2, local copies, waits for them, and re-layouts: none -> 3.24 us  [body(): lax.optimization_barrier((w_q2b, kv_own, kv_other, normed, q_own, seg_col...]
  transfers between devices with their start and end apart: 26 -> 26, of which waited for: 13 -> 9; matrix products, arithmetic and copies ran while one was open for 9% -> 15% of each run, Pallas kernels for 27% -> 34%
where the time goes in v3:
time: 240 us; the launch traced here: 239 us
  Pallas kernels  84.3 us (35%)
  waiting for transfers between devices  57.1 us (24%)
  starting transfers between devices  49.9 us (21%)
  local copies, waits for them, and re-layouts  27.3 us (11%)
  other arithmetic  14.8 us (6%)
  matrix products  4.47 us (2%)
    ppermute x26, waiting for transfers between devices, send(): return lax.ppermute(value, AXES, pairs)  57.1 us
    ppermute x26, starting transfers between devices, send(): return lax.ppermute(value, AXES, pairs)  49.9 us
    pallas_call x4, Pallas kernels, project(): pl.pallas_call(kernel, grid_spec=pltpu.PrefetchScalarGridSpec(num_scalar_...  22.2 us
    pallas_call x4, Pallas kernels, finish(): pl.pallas_call(finish_kernel, grid_spec=pltpu.PrefetchScalarGridSpec(num_...  20.1 us
    pallas_call x2, Pallas kernels, reorder(): pl.pallas_call(reorder_kernel, grid_spec=pltpu.PrefetchScalarGridSpec(num...  14.6 us
    pallas_call x2, Pallas kernels, attend(): pl.pallas_call(functools.partial(attend_kernel, chunk), grid_spec=pltpu.P...  13.9 us
    unnamed x46, local copies, waits for them, and re-layouts  10 us
    pallas_call x1, Pallas kernels, more_queries(): pl.pallas_call(more_queries_kernel, grid=(4,), in_specs=[pl.BlockSpec((1,...  8.43 us
  transfers between devices with their start and end apart: 26, of which 9 were waited for; matrix products, arithmetic and copies ran while one was open for 15% of the time, Pallas kernels for 34%

profile of v3, /device:TPU:1, one launch (start us, length us, event | category | flops | bytes accessed | tf_op | source)
XLA Modules:
  0.0 239.0 jit_solution(13690696328552221391)
XLA Ops:
  5.6 64.4 %conditional.1 = (bf16[256,768]{1,0:T(8,128)(2,1)}, bf16[2,256,768]{2,1,0:T(8,128)(2,1)}, bf16[2048,384]{1,0:T(8,128)(2,1)}, bf16[3072,384]{1,0:T(8,128)(2,1)}, ...) conditional(s32[]{:T(128)} %bitcast.11, () %tuple.23, (pred[]{:T(512)}, s32[]{:T(128)}, ...), branch_computations={%region_1.2_spmd, %region_2.4_spmd} | conditional | flops 1016889472 | bytes 80669768 | solution.py:407
  7.3 3.6 %convolution_convert_fusion = bf16[128,384]{1,0:T(8,128)(2,1)S(1)} fusion(bf16[5120,384]{1,0:T(8,128)(2,1)} %get-tuple-element.137, bf16[128,5120]{1,0:T(8,128)(2,1)} %get-tuple-element.134, f32[5120]{0:T(1024)} %get-tuple-element.135, f32[128]{0:T(128)S(1)} %add_rsqrt_fusion), kind=kOutput, calls=%fused_computation.5 | convolution fusion | flops 505987072 | bytes 5362176 | tf_op jit(solution)/shard_map/cond/branch_1_fun/dot_general | solution.py:383
  16.4 15.1 %collective-permute-start.2 = (bf16[2,128,768]{2,1,0:T(8,128)(2,1)S(1)}, bf16[2,128,768]{2,1,0:T(8,128)(2,1)}, u32[]{:S(2)}, u32[]{:S(2)}) collective-permute-start(bf16[2,128,768]{2,1,0:T(8,128)(2,1)S(1)} %collective-permute-done.1), channel_id=1, source_target_pairs={{0,8},{1,9},{2,10},{3,11},{4,12},{5,13},{6,14},{7,15},{8,0},{9,1},... | collective-permute-start | bytes 1179656 | tf_op jit(solution)/shard_map/cond/branch_1_fun/ppermute | solution.py:66
  35.6 2.7 %collective-permute-start.4 = (bf16[256,768]{1,0:T(8,128)(2,1)}, bf16[256,768]{1,0:T(8,128)(2,1)}, u32[]{:S(2)}, u32[]{:S(2)}) collective-permute-start(bf16[256,768]{1,0:T(8,128)(2,1)} %dynamic-slice_bitcast_fusion), channel_id=1, source_target_pairs={{0,32},{1,33},{2,34},{3,35},{4,36},{5,37},{6,38},{7,39},{8,40},{9,... | collective-permute-start | bytes 1179656 | tf_op jit(solution)/shard_map/cond/branch_1_fun/ppermute | solution.py:66
  39.9 7.7 %collective-permute-done.4 = bf16[256,768]{1,0:T(8,128)(2,1)} collective-permute-done((bf16[256,768]{1,0:T(8,128)(2,1)}, bf16[256,768]{1,0:T(8,128)(2,1)}, u32[]{:S(2)}, u32[]{:S(2)}) %collective-permute-start.4) | collective-permute-done | bytes 393248 | tf_op jit(solution)/shard_map/cond/branch_1_fun/ppermute | solution.py:66
  49.7 2.7 %collective-permute-start.6 = (bf16[2,256,768]{2,1,0:T(8,128)(2,1)}, bf16[2,256,768]{2,1,0:T(8,128)(2,1)}, u32[]{:S(2)}, u32[]{:S(2)}) collective-permute-start(bf16[2,256,768]{2,1,0:T(8,128)(2,1)} %collective-permute-done.3), channel_id=1, source_target_pairs={{0,32},{1,33},{2,34},{3,35},{4,36},{5,37},{6,38},{7,39},{8,40},{9,... | collective-permute-start | bytes 2359304 | tf_op jit(solution)/shard_map/cond/branch_1_fun/ppermute | solution.py:66
  54.0 16.0 %collective-permute-done.6 = bf16[2,256,768]{2,1,0:T(8,128)(2,1)} collective-permute-done((bf16[2,256,768]{2,1,0:T(8,128)(2,1)}, bf16[2,256,768]{2,1,0:T(8,128)(2,1)}, u32[]{:S(2)}, u32[]{:S(2)}) %collective-permute-start.6) | collective-permute-done | bytes 786464 | tf_op jit(solution)/shard_map/cond/branch_1_fun/ppermute | solution.py:66
  71.3 2.6 %slice.45 = bf16[128,5120]{1,0:T(8,128)(2,1)} slice(bf16[256,5120]{1,0:T(8,128)(2,1)} %collective-permute-done.8.refs_0_), slice={[128:256], [0:5120]} | slice | bytes 2621440 | tf_op jit(solution)/shard_map/slice | solution.py:413
  76.7 2.5 %collective-permute-start.12 = (bf16[3,256,768]{2,1,0:T(8,128)(2,1)}, bf16[3,256,768]{2,1,0:T(8,128)(2,1)}, u32[]{:S(2)}, u32[]{:S(2)}) collective-permute-start(bf16[3,256,768]{2,1,0:T(8,128)(2,1)} %pad_maximum_fusion.3), channel_id=1, source_target_pairs={{0,48},{1,49},{2,50},{3,51},{4,52},{5,53},{6,54},{7,55},{8,56},{9,... | collective-permute-start | bytes 3538952 | tf_op jit(solution)/shard_map/ppermute | solution.py:66
  83.2 7.2 %shard_map.105 = bf16[8,384,640]{2,1,0:T(8,128)(2,1)} custom-call(s32[31]{0:T(128)} %pad_add_fusion.meta, bf16[8,384,640]{2,1,0:T(8,128)(2,1)} %bitcast.47), custom_call_target="tpu_custom_call" | custom-call | tf_op jit(solution)/shard_map/pallas_call | solution.py:269
  90.4 7.4 %shard_map.104 = bf16[8,384,640]{2,1,0:T(8,128)(2,1)} custom-call(s32[31]{0:T(128)} %pad_add_fusion.meta, bf16[8,384,640]{2,1,0:T(8,128)(2,1)} %bitcast.48), custom_call_target="tpu_custom_call" | custom-call | tf_op jit(solution)/shard_map/pallas_call | solution.py:269
  99.5 6.2 %shard_map.106 = (bf16[4,256,5120]{2,1,0:T(8,128)(2,1)}, bf16[4,256,384]{2,1,0:T(8,128)(2,1)S(1)}, bf16[4,256,640]{2,1,0:T(8,128)(2,1)S(1)}, bf16[4,256,640]{2,1,0:T(8,128)(2,1)S(1)}) custom-call(s32[31]{0:T(128)S(1)} %copy-done.19, bf16[256,5120]{1,0:T(8,128)(2,1)S(1)} %bitcast.39, f32[1,5120]{1,0:T(1,128)S(1)} %copy-done.17, bf16[5120,384]{1,0:T(8,128)(2,1)} %bitcast.43), custom_call_target="tpu_custom_call" | custom-call | flops 1006632960 | bytes 11796480 | tf_op jit(solution)/shard_map/pallas_call | solution.py:117
  105.7 5.8 %shard_map.107 = (bf16[4,256,5120]{2,1,0:T(8,128)(2,1)}, bf16[4,256,384]{2,1,0:T(8,128)(2,1)S(1)}, bf16[4,256,640]{2,1,0:T(8,128)(2,1)S(1)}, bf16[4,256,640]{2,1,0:T(8,128)(2,1)S(1)}) custom-call(s32[31]{0:T(128)S(1)} %copy-done.19, ...), custom_call_target="tpu_custom_call", output_to_operand_aliasing={{0}: (4, {}), {1}: (5, {}), {2}: (6, {}), {3}: (7, {})} | custom-call | flops 1006632960 | bytes 11796480 | tf_op jit(solution)/shard_map/pallas_call | solution.py:117
  111.5 3.7 %shard_map.108 = (bf16[4,256,5120]{2,1,0:T(8,128)(2,1)}, bf16[4,256,384]{2,1,0:T(8,128)(2,1)S(1)}, bf16[4,256,640]{2,1,0:T(8,128)(2,1)S(1)}, bf16[4,256,640]{2,1,0:T(8,128)(2,1)S(1)}) custom-call(s32[31]{0:T(128)S(1)} %copy-done.19, bf16[256,5120]{1,0:T(8,128)(2,1)S(1)} %copy-done.9, ...), custom_call_target="tpu_custom_call", output_to_operand_aliasing={{0}: (4, {}), {1}: (5, {}), {2}: (6, {}), {3}: (7, {})} | custom-call | flops 1006632960 | bytes 11796480 | tf_op jit(solution)/shard_map/pallas_call | solution.py:117
  117.3 3.0 %fusion.7 = (bf16[4,1,256,768]{3,2,0,1:T(8,128)(2,1)}, bf16[4,256,768]{2,1,0:T(8,128)(2,1)}) fusion(bf16[1,256,768]{2,1,0:T(8,128)(2,1)S(1)} %slice.47, bf16[1,256,768]{2,1,0:T(8,128)(2,1)} %get-tuple-element.99, bf16[1,256,768]{2,1,0:T(8,128)(2,1)S(1)} %slice.46, bf16[1,256,768]{2,1,0:T(8,128)(2,1)} %bitcast.14), kind=kLoop, calls=%fused_computation.31 | loop fusion | flops 2359296 | bytes 4718592 | tf_op jit(solution)/shard_map/stack | solution.py:429
  122.3 6.6 %shard_map.109 = (bf16[4,256,5120]{2,1,0:T(8,128)(2,1)}, bf16[4,256,384]{2,1,0:T(8,128)(2,1)S(1)}, bf16[4,256,640]{2,1,0:T(8,128)(2,1)S(1)}, bf16[4,256,640]{2,1,0:T(8,128)(2,1)S(1)}) custom-call(s32[31]{0:T(128)S(1)} %copy-done.19, ...), custom_call_target="tpu_custom_call", output_to_operand_aliasing={{0}: (5, {}), {1}: (6, {}), {2}: (7, {}), {3}: (8, {})} | custom-call | flops 1006632960 | bytes 11796480 | tf_op jit(solution)/shard_map/pallas_call | solution.py:117
  130.4 3.1 %pad_maximum_fusion.1.kv_other = bf16[4,2,256,768]{3,2,1,0:T(8,128)(2,1)} fusion(bf16[1,2,256,768]{3,2,1,0:T(8,128)(2,1)S(1)} %get-tuple-element.155, bf16[1,2,256,768]{3,2,1,0:T(8,128)(2,1)} %get-tuple-element.101, bf16[1,2,256,768]{3,2,1,0:T(8,128)(2,1)S(1)} %get-tuple-element.156, bf16[1,2,256,768]{3,2,1,0:T(8,128)(2,1)} %bitcast.21), kind=kLoop, calls=%fused_computation.17 | loop fusion | flops 4718592 | bytes 6291456 | tf_op jit(solution)/shard_map/stack | solution.py:431
  133.5 2.5 %maximum_select_fusion.3 = bf16[4,2,256,768]{3,2,0,1:T(8,128)(2,1)S(1)} fusion(bf16[4,1,256,768]{3,2,0,1:T(8,128)(2,1)} %bitcast.20, bf16[4,1,256,768]{3,2,0,1:T(8,128)(2,1)S(1)} %copy-done.23, pred[]{:T(512)S(6)} %eq.13), kind=kLoop, calls=%fused_computation.16 | loop fusion | flops 4718592 | bytes 6291457 | tf_op jit(solution)/shard_map/jit(_where)/select_n | solution.py:428
  140.6 4.0 %copy-done = bf16[4,256,5120]{2,1,0:T(8,128)(2,1)S(1)} copy-done((bf16[4,256,5120]{2,1,0:T(8,128)(2,1)S(1)}, bf16[4,256,5120]{2,1,0:T(8,128)(2,1)}, u32[]{:S(2)}) %copy-start) | copy-done | bytes 10485784
  144.6 8.4 %shard_map.110.q_other = bf16[4,256,384]{2,1,0:T(8,128)(2,1)S(1)} custom-call(bf16[4,256,5120]{2,1,0:T(8,128)(2,1)S(1)} %copy-done, bf16[2048,384]{1,0:T(8,128)(2,1)} %get-tuple-element.113.wa_ref, bf16[3072,384]{1,0:T(8,128)(2,1)} %collective-permute-done.7.wb_ref), custom_call_target="tpu_custom_call" | custom-call | flops 4026531840 | bytes 14417920 | tf_op jit(solution)/shard_map/pallas_call | solution.py:143
  153.0 5.0 %shard_map.113.c0 = bf16[512,768]{1,0:T(8,128)(2,1)S(1)} custom-call(s32[31]{0:T(128)S(1)} %copy-done.19, bf16[4,256,384]{2,1,0:T(8,128)(2,1)S(1)} %get-tuple-element.111.q_own, bf16[4,256,384]{2,1,0:T(8,128)(2,1)S(1)} %shard_map.110.q_other, bf16[4,2,256,768]{3,2,1,0:T(8,128)(2,1)S(1)} %copy-done.4, bf16[4,2,256,768]{3,2,1,0:T(8,128)(2,1)S(1)} %copy-done.3, ...), custom_call_target="tpu_custom_call" | custom-call | flops 1207959552 | bytes 8388608 | tf_op jit(solution)/shard_map/pallas_call | solution.py:240
  159.2 8.9 %shard_map.111.c0 = bf16[512,768]{1,0:T(8,128)(2,1)S(1)} custom-call(s32[31]{0:T(128)S(1)} %copy-done.19, bf16[4,256,384]{2,1,0:T(8,128)(2,1)S(1)} %get-tuple-element.111.q_own, bf16[4,256,384]{2,1,0:T(8,128)(2,1)S(1)} %shard_map.110.q_other, bf16[4,2,256,768]{3,2,1,0:T(8,128)(2,1)S(1)} %copy-done.4, bf16[4,2,256,768]{3,2,1,0:T(8,128)(2,1)S(1)} %copy-done.3, ...), custom_call_target="tpu_custom_call" | custom-call | flops 1207959552 | bytes 8388608 | tf_op jit(solution)/shard_map/pallas_call | solution.py:240
  170.0 7.8 %collective-permute-done.22.c3 = bf16[512,768]{1,0:T(8,128)(2,1)S(1)} collective-permute-done((bf16[512,768]{1,0:T(8,128)(2,1)S(1)}, bf16[512,768]{1,0:T(8,128)(2,1)S(1)}, u32[]{:S(2)}, u32[]{:S(2)}) %collective-permute-start.22) | collective-permute-done | bytes 786464 | tf_op jit(solution)/shard_map/ppermute | solution.py:66
  179.1 15.6 %collective-permute-done.16.c3 = bf16[512,768]{1,0:T(8,128)(2,1)S(1)} collective-permute-done((bf16[512,768]{1,0:T(8,128)(2,1)S(1)}, bf16[512,768]{1,0:T(8,128)(2,1)S(1)}, u32[]{:S(2)}, u32[]{:S(2)}) %collective-permute-start.16) | collective-permute-done | bytes 786464 | tf_op jit(solution)/shard_map/ppermute | solution.py:66
  196.0 6.9 %collective-permute-done.23.c2a = bf16[256,768]{1,0:T(8,128)(2,1)S(1)} collective-permute-done((bf16[256,768]{1,0:T(8,128)(2,1)S(1)}, bf16[256,768]{1,0:T(8,128)(2,1)S(1)}, u32[]{:S(2)}, u32[]{:S(2)}) %collective-permute-start.23) | collective-permute-done | bytes 393248 | tf_op jit(solution)/shard_map/ppermute | solution.py:66
  203.6 5.5 %shard_map.114 = bf16[2,256,640]{2,1,0:T(8,128)(2,1)S(1)} custom-call(s32[31]{0:T(128)S(1)} %copy-done.19, bf16[512,768]{1,0:T(8,128)(2,1)S(1)} %shard_map.113.c0, bf16[512,768]{1,0:T(8,128)(2,1)S(1)} %collective-permute-done.21.c1, bf16[256,768]{1,0:T(8,128)(2,1)S(1)} %collective-permute-done.23.c2a, bf16[256,768]{1,0:T(8,128)(2,1)S(1)} %collective-permute-done.24.c2b, ...), custom_call_target="tpu_custom_call" | custom-call | flops 2013265920 | bytes 8388608 | tf_op jit(solution)/shard_map/pallas_call | solution.py:312
  209.1 5.2 %collective-permute-start.25 = (bf16[2,256,640]{2,1,0:T(8,128)(2,1)S(1)}, bf16[2,256,640]{2,1,0:T(8,128)(2,1)}, u32[]{:S(2)}, u32[]{:S(2)}) collective-permute-start(bf16[2,256,640]{2,1,0:T(8,128)(2,1)S(1)} %shard_map.114), channel_id=1, source_target_pairs={{0,4},{1,5},{2,6},{3,7},{4,0},{5,1},{6,2},{7,3},{8,11},{9,10},{10,... | collective-permute-start | bytes 1966088 | tf_op jit(solution)/shard_map/ppermute | solution.py:66
  214.3 6.3 %shard_map.112 = bf16[2,256,640]{2,1,0:T(8,128)(2,1)} custom-call(s32[31]{0:T(128)S(1)} %copy-done.19, bf16[512,768]{1,0:T(8,128)(2,1)S(1)} %shard_map.111.c0, bf16[512,768]{1,0:T(8,128)(2,1)S(1)} %collective-permute-done.15.c1, bf16[256,768]{1,0:T(8,128)(2,1)S(1)} %collective-permute-done.17.c2a, bf16[256,768]{1,0:T(8,128)(2,1)S(1)} %collective-permute-done.18.c2b, ...), custom_call_target="tpu_custom_call" | custom-call | flops 2013265920 | bytes 8388608 | tf_op jit(solution)/shard_map/pallas_call | solution.py:312
  221.3 4.1 %shard_map.115.prior = bf16[8,256,640]{2,1,0:T(8,128)(2,1)} custom-call(s32[31]{0:T(128)S(1)} %copy-done.19, bf16[512,768]{1,0:T(8,128)(2,1)S(1)} %shard_map.113.c0, bf16[512,768]{1,0:T(8,128)(2,1)S(1)} %collective-permute-done.21.c1, bf16[256,768]{1,0:T(8,128)(2,1)S(1)} %collective-permute-done.23.c2a, bf16[256,768]{1,0:T(8,128)(2,1)S(1)} %collective-permute-done.24.c2b, ...), custom_call_target="tpu_custom_call" | custom-call | flops 2013265920 | bytes 8388608 | tf_op jit(solution)/shard_map/pallas_call | solution.py:312
  225.4 2.6 %shard_map.116.refs_0_ = bf16[8,256,640]{2,1,0:T(8,128)(2,1)} custom-call(s32[31]{0:T(128)} %pad_add_fusion.meta, bf16[2,256,640]{2,1,0:T(8,128)(2,1)} %collective-permute-done.25.got, bf16[8,256,640]{2,1,0:T(8,128)(2,1)} %shard_map.115.prior), custom_call_target="tpu_custom_call", output_to_operand_aliasing={{}: (2, {})} | custom-call | tf_op jit(solution)/shard_map/pallas_call | solution.py:336
  232.3 4.1 %shard_map.117.prior = bf16[8,256,640]{2,1,0:T(8,128)(2,1)} custom-call(s32[31]{0:T(128)S(1)} %copy-done.20, bf16[512,768]{1,0:T(8,128)(2,1)S(1)} %copy-done.7, bf16[512,768]{1,0:T(8,128)(2,1)S(1)} %copy-done.11, bf16[256,768]{1,0:T(8,128)(2,1)S(1)} %copy-done.14, bf16[256,768]{1,0:T(8,128)(2,1)S(1)} %copy-done.16, ...), custom_call_target="tpu_custom_call", output_to_operand_aliasing={{}: (8, {})} | custom-call | flops 2013265920 | bytes 8388608 | tf_op jit(solution)/shard_map/pallas_call | solution.py:312
  236.5 2.5 %shard_map.118 = bf16[8,256,640]{2,1,0:T(8,128)(2,1)} custom-call(s32[31]{0:T(128)} %pad_add_fusion.meta, bf16[2,256,640]{2,1,0:T(8,128)(2,1)} %collective-permute-done.20.got, bf16[8,256,640]{2,1,0:T(8,128)(2,1)} %shard_map.117.prior), custom_call_target="tpu_custom_call", output_to_operand_aliasing={{}: (2, {})} | custom-call | tf_op jit(solution)/shard_map/pallas_call | solution.py:336
  (125 shorter events, 52.6 us)
Async XLA Ops:
  0.0 70.0 %collective-permute-start.8 = (bf16[256,5120]{1,0:T(8,128)(2,1)}, bf16[256,5120]{1,0:T(8,128)(2,1)}, u32[]{:S(2)}, u32[]{:S(2)}) collective-permute-start(bf16[256,5120]{1,0:T(8,128)(2,1)} %bitcast.37), channel_id=1, source_target_pairs={{0,1},{1,0},{2,3},{3,2},{4,5},{5,4},{6,7},{7,6},{8,9},{9,8},{10,11... | collective-permute-start | bytes 7864328 | tf_op jit(solution)/shard_map/ppermute | solution.py:66
  2.5 67.5 %collective-permute-start.9 = (bf16[256,5120]{1,0:T(8,128)(2,1)}, bf16[256,5120]{1,0:T(8,128)(2,1)S(1)}, u32[]{:S(2)}, u32[]{:S(2)}) collective-permute-start(bf16[256,5120]{1,0:T(8,128)(2,1)} %bitcast.38), channel_id=1, source_target_pairs={{0,3},{1,2},{2,1},{3,0},{4,7},{5,6},{6,5},{7,4},{8,12},{9,13},{10,... | collective-permute-start | bytes 7864328 | tf_op jit(solution)/shard_map/ppermute | solution.py:66
  12.4 3.3 %collective-permute-start = (bf16[128,768]{1,0:T(8,128)(2,1)S(1)}, bf16[128,768]{1,0:T(8,128)(2,1)S(1)}, u32[]{:S(2)}, u32[]{:S(2)}) collective-permute-start(bf16[128,768]{1,0:T(8,128)(2,1)S(1)} %get-tuple-element.152), channel_id=1, source_target_pairs={{0,8},{1,9},{2,10},{3,11},{4,12},{5,13},{6,14},{7,15},{8,0},{9,1},... | collective-permute-start | bytes 589832 | tf_op jit(solution)/shard_map/cond/branch_1_fun/ppermute | solution.py:66
  15.7 0.7 collective-permute-start.1
  16.4 16.6 %collective-permute-start.2 = (bf16[2,128,768]{2,1,0:T(8,128)(2,1)S(1)}, bf16[2,128,768]{2,1,0:T(8,128)(2,1)}, u32[]{:S(2)}, u32[]{:S(2)}) collective-permute-start(bf16[2,128,768]{2,1,0:T(8,128)(2,1)S(1)} %collective-permute-done.1), channel_id=1, source_target_pairs={{0,8},{1,9},{2,10},{3,11},{4,12},{5,13},{6,14},{7,15},{8,0},{9,1},... | collective-permute-start | bytes 1179656 | tf_op jit(solution)/shard_map/cond/branch_1_fun/ppermute | solution.py:66
  34.2 13.3 %collective-permute-start.3 = (bf16[2,256,768]{2,1,0:T(8,128)(2,1)S(1)}, bf16[2,256,768]{2,1,0:T(8,128)(2,1)}, u32[]{:S(2)}, u32[]{:S(2)}) collective-permute-start(bf16[2,256,768]{2,1,0:T(8,128)(2,1)S(1)} %maximum_select_fusion), channel_id=1, source_target_pairs={{0,4},{1,5},{2,6},{3,7},{4,0},{5,1},{6,2},{7,3},{8,11},{9,10},{10,... | collective-permute-start | bytes 2359304 | tf_op jit(solution)/shard_map/cond/branch_1_fun/ppermute | solution.py:66
  34.7 17.7 %copy-start.22 = (bf16[5120,384]{1,0:T(8,128)(2,1)S(1)}, bf16[5120,384]{1,0:T(8,128)(2,1)}, u32[]{:S(2)}) copy-start(bf16[5120,384]{1,0:T(8,128)(2,1)} %get-tuple-element.27) | copy-start | bytes 11796484 | tf_op jit(solution)/shard_map/cond
  35.6 12.0 %collective-permute-start.4 = (bf16[256,768]{1,0:T(8,128)(2,1)}, bf16[256,768]{1,0:T(8,128)(2,1)}, u32[]{:S(2)}, u32[]{:S(2)}) collective-permute-start(bf16[256,768]{1,0:T(8,128)(2,1)} %dynamic-slice_bitcast_fusion), channel_id=1, source_target_pairs={{0,32},{1,33},{2,34},{3,35},{4,36},{5,37},{6,38},{7,39},{8,40},{9,... | collective-permute-start | bytes 1179656 | tf_op jit(solution)/shard_map/cond/branch_1_fun/ppermute | solution.py:66
  47.5 22.5 %collective-permute-start.5 = (bf16[2048,384]{1,0:T(8,128)(2,1)S(1)}, bf16[2048,384]{1,0:T(8,128)(2,1)}, u32[]{:S(2)}, u32[]{:S(2)}) collective-permute-start(bf16[2048,384]{1,0:T(8,128)(2,1)S(1)} %slice.28), channel_id=1, source_target_pairs={{0,4},{1,5},{2,6},{3,7},{4,0},{5,1},{6,2},{7,3},{8,11},{9,10},{10,... | collective-permute-start | bytes 4718600 | tf_op jit(solution)/shard_map/cond/branch_1_fun/ppermute | solution.py:66
  49.7 20.4 %collective-permute-start.6 = (bf16[2,256,768]{2,1,0:T(8,128)(2,1)}, bf16[2,256,768]{2,1,0:T(8,128)(2,1)}, u32[]{:S(2)}, u32[]{:S(2)}) collective-permute-start(bf16[2,256,768]{2,1,0:T(8,128)(2,1)} %collective-permute-done.3), channel_id=1, source_target_pairs={{0,32},{1,33},{2,34},{3,35},{4,36},{5,37},{6,38},{7,39},{8,40},{9,... | collective-permute-start | bytes 2359304 | tf_op jit(solution)/shard_map/cond/branch_1_fun/ppermute | solution.py:66
  71.3 10.3 %copy-start.18 = (s32[2048]{0:T(1024)S(1)}, s32[2048]{0:T(1024)}, u32[]{:S(2)}) copy-start(s32[2048]{0:T(1024)} %param.20) | copy-start | bytes 24580
  71.3 43.9 %collective-permute-start.10 = (bf16[128,5120]{1,0:T(8,128)(2,1)}, bf16[128,5120]{1,0:T(8,128)(2,1)}, u32[]{:S(2)}, u32[]{:S(2)}) collective-permute-start(bf16[128,5120]{1,0:T(8,128)(2,1)} %slice.44), channel_id=1, source_target_pairs={{0,1},{1,0},{2,3},{3,2},{4,5},{5,4},{6,7},{7,6},{8,9},{9,8},{10,11... | collective-permute-start | bytes 3932168 | tf_op jit(solution)/shard_map/ppermute | solution.py:66
  73.9 41.3 %collective-permute-start.11 = (bf16[128,5120]{1,0:T(8,128)(2,1)}, bf16[128,5120]{1,0:T(8,128)(2,1)}, u32[]{:S(2)}, u32[]{:S(2)}) collective-permute-start(bf16[128,5120]{1,0:T(8,128)(2,1)} %slice.45), channel_id=1, source_target_pairs={{0,3},{1,2},{2,1},{3,0},{4,7},{5,6},{6,5},{7,4},{8,12},{9,13},{10,... | collective-permute-start | bytes 3932168 | tf_op jit(solution)/shard_map/ppermute | solution.py:66
  76.7 38.5 %collective-permute-start.12 = (bf16[3,256,768]{2,1,0:T(8,128)(2,1)}, bf16[3,256,768]{2,1,0:T(8,128)(2,1)}, u32[]{:S(2)}, u32[]{:S(2)}) collective-permute-start(bf16[3,256,768]{2,1,0:T(8,128)(2,1)} %pad_maximum_fusion.3), channel_id=1, source_target_pairs={{0,48},{1,49},{2,50},{3,51},{4,52},{5,53},{6,54},{7,55},{8,56},{9,... | collective-permute-start | bytes 3538952 | tf_op jit(solution)/shard_map/ppermute | solution.py:66
  79.1 36.1 %collective-permute-start.13 = (bf16[3,256,768]{2,1,0:T(8,128)(2,1)}, bf16[3,256,768]{2,1,0:T(8,128)(2,1)}, u32[]{:S(2)}, u32[]{:S(2)}) collective-permute-start(bf16[3,256,768]{2,1,0:T(8,128)(2,1)} %pad_maximum_fusion.3), channel_id=1, source_target_pairs={{0,16},{1,17},{2,18},{3,19},{4,20},{5,21},{6,22},{7,23},{8,24},{9,... | collective-permute-start | bytes 3538952 | tf_op jit(solution)/shard_map/ppermute | solution.py:66
  79.1 56.9 %collective-permute-start.7 = (bf16[3072,384]{1,0:T(8,128)(2,1)}, bf16[3072,384]{1,0:T(8,128)(2,1)}, u32[]{:S(2)}, u32[]{:S(2)}) collective-permute-start(bf16[3072,384]{1,0:T(8,128)(2,1)} %get-tuple-element.77), channel_id=1, source_target_pairs={{0,4},{1,5},{2,6},{3,7},{4,0},{5,1},{6,2},{7,3},{8,11},{9,10},{10,... | collective-permute-start | bytes 7077896 | tf_op jit(solution)/shard_map/ppermute | solution.py:66
  120.3 13.2 %collective-permute-start.14 = (bf16[4,256,768]{2,1,0:T(8,128)(2,1)}, bf16[4,256,768]{2,1,0:T(8,128)(2,1)}, u32[]{:S(2)}, u32[]{:S(2)}) collective-permute-start(bf16[4,256,768]{2,1,0:T(8,128)(2,1)} %get-tuple-element.154), channel_id=1, source_target_pairs={{0,8},{1,9},{2,10},{3,11},{4,12},{5,13},{6,14},{7,15},{8,0},{9,1},... | collective-permute-start | bytes 4718600 | tf_op jit(solution)/shard_map/ppermute | solution.py:66
  136.0 67.5 %collective-permute-start.19 = (bf16[3072,640]{1,0:T(8,128)(2,1)}, bf16[3072,640]{1,0:T(8,128)(2,1)}, u32[]{:S(2)}, u32[]{:S(2)}) collective-permute-start(bf16[3072,640]{1,0:T(8,128)(2,1)} %bitcast.18), channel_id=1, source_target_pairs={{0,4},{1,5},{2,6},{3,7},{4,0},{5,1},{6,2},{7,3},{8,11},{9,10},{10,... | collective-permute-start | bytes 11796488 | tf_op jit(solution)/shard_map/ppermute | solution.py:66
  144.6 8.5 %copy-start.5 = (s32[8,256,1]{2,1,0:T(8,128)S(1)}, s32[8,256,1]{2,1,0:T(8,128)}, u32[]{:S(2)}) copy-start(s32[8,256,1]{2,1,0:T(8,128)} %copy.41.seg_col) | copy-start | bytes 24580
  158.0 19.8 %collective-permute-start.22 = (bf16[512,768]{1,0:T(8,128)(2,1)S(1)}, bf16[512,768]{1,0:T(8,128)(2,1)S(1)}, u32[]{:S(2)}, u32[]{:S(2)}) collective-permute-start(bf16[512,768]{1,0:T(8,128)(2,1)S(1)} %shard_map.113.c0), channel_id=1, source_target_pairs={{0,3},{1,2},{2,1},{3,0},{4,7},{5,6},{6,5},{7,4},{8,12},{9,13},{10,... | collective-permute-start | bytes 2359304 | tf_op jit(solution)/shard_map/ppermute | solution.py:66
  158.9 19.0 %collective-permute-start.21 = (bf16[512,768]{1,0:T(8,128)(2,1)S(1)}, bf16[512,768]{1,0:T(8,128)(2,1)S(1)}, u32[]{:S(2)}, u32[]{:S(2)}) collective-permute-start(bf16[512,768]{1,0:T(8,128)(2,1)S(1)} %shard_map.113.c0), channel_id=1, source_target_pairs={{0,1},{1,0},{2,3},{3,2},{4,5},{5,4},{6,7},{7,6},{8,9},{9,8},{10,11... | collective-permute-start | bytes 2359304 | tf_op jit(solution)/shard_map/ppermute | solution.py:66
  168.1 46.2 %copy-start.6 = (bf16[512,768]{1,0:T(8,128)(2,1)}, bf16[512,768]{1,0:T(8,128)(2,1)S(1)}, u32[]{:S(2)}) copy-start(bf16[512,768]{1,0:T(8,128)(2,1)S(1)} %shard_map.111.c0) | copy-start | bytes 2359300
  168.1 26.6 %collective-permute-start.16 = (bf16[512,768]{1,0:T(8,128)(2,1)S(1)}, bf16[512,768]{1,0:T(8,128)(2,1)S(1)}, u32[]{:S(2)}, u32[]{:S(2)}) collective-permute-start(bf16[512,768]{1,0:T(8,128)(2,1)S(1)} %shard_map.111.c0), channel_id=1, source_target_pairs={{0,3},{1,2},{2,1},{3,0},{4,7},{5,6},{6,5},{7,4},{8,12},{9,13},{10,... | collective-permute-start | bytes 2359304 | tf_op jit(solution)/shard_map/ppermute | solution.py:66
  168.6 26.2 %collective-permute-start.15 = (bf16[512,768]{1,0:T(8,128)(2,1)S(1)}, bf16[512,768]{1,0:T(8,128)(2,1)S(1)}, u32[]{:S(2)}, u32[]{:S(2)}) collective-permute-start(bf16[512,768]{1,0:T(8,128)(2,1)S(1)} %shard_map.111.c0), channel_id=1, source_target_pairs={{0,1},{1,0},{2,3},{3,2},{4,5},{5,4},{6,7},{7,6},{8,9},{9,8},{10,11... | collective-permute-start | bytes 2359304 | tf_op jit(solution)/shard_map/ppermute | solution.py:66
  177.9 25.0 %collective-permute-start.23 = (bf16[256,768]{1,0:T(8,128)(2,1)S(1)}, bf16[256,768]{1,0:T(8,128)(2,1)S(1)}, u32[]{:S(2)}, u32[]{:S(2)}) collective-permute-start(bf16[256,768]{1,0:T(8,128)(2,1)S(1)} %slice.57), channel_id=1, source_target_pairs={{0,1},{1,0},{2,3},{3,2},{4,5},{5,4},{6,7},{7,6},{8,9},{9,8},{10,11... | collective-permute-start | bytes 1179656 | tf_op jit(solution)/shard_map/ppermute | solution.py:66
  178.0 24.9 %collective-permute-start.24 = (bf16[256,768]{1,0:T(8,128)(2,1)S(1)}, bf16[256,768]{1,0:T(8,128)(2,1)S(1)}, u32[]{:S(2)}, u32[]{:S(2)}) collective-permute-start(bf16[256,768]{1,0:T(8,128)(2,1)S(1)} %slice.58), channel_id=1, source_target_pairs={{0,3},{1,2},{2,1},{3,0},{4,7},{5,6},{6,5},{7,4},{8,12},{9,13},{10,... | collective-permute-start | bytes 1179656 | tf_op jit(solution)/shard_map/ppermute | solution.py:66
  194.7 19.6 %collective-permute-start.17 = (bf16[256,768]{1,0:T(8,128)(2,1)S(1)}, bf16[256,768]{1,0:T(8,128)(2,1)S(1)}, u32[]{:S(2)}, u32[]{:S(2)}) collective-permute-start(bf16[256,768]{1,0:T(8,128)(2,1)S(1)} %slice.55), channel_id=1, source_target_pairs={{0,1},{1,0},{2,3},{3,2},{4,5},{5,4},{6,7},{7,6},{8,9},{9,8},{10,11... | collective-permute-start | bytes 1179656 | tf_op jit(solution)/shard_map/ppermute | solution.py:66
  194.8 19.5 %copy-start.10 = (bf16[512,768]{1,0:T(8,128)(2,1)}, bf16[512,768]{1,0:T(8,128)(2,1)S(1)}, u32[]{:S(2)}) copy-start(bf16[512,768]{1,0:T(8,128)(2,1)S(1)} %collective-permute-done.15.c1) | copy-start | bytes 2359300
  194.9 19.4 %collective-permute-start.18 = (bf16[256,768]{1,0:T(8,128)(2,1)S(1)}, bf16[256,768]{1,0:T(8,128)(2,1)S(1)}, u32[]{:S(2)}, u32[]{:S(2)}) collective-permute-start(bf16[256,768]{1,0:T(8,128)(2,1)S(1)} %slice.56), channel_id=1, source_target_pairs={{0,3},{1,2},{2,1},{3,0},{4,7},{5,6},{6,5},{7,4},{8,12},{9,13},{10,... | collective-permute-start | bytes 1179656 | tf_op jit(solution)/shard_map/ppermute | solution.py:66
  209.1 12.2 %copy-start.1 = (bf16[8,384,640]{2,1,0:T(8,128)(2,1)S(1)}, bf16[8,384,640]{2,1,0:T(8,128)(2,1)}, u32[]{:S(2)}) copy-start(bf16[8,384,640]{2,1,0:T(8,128)(2,1)} %shard_map.104) | copy-start | bytes 11796484
  209.1 16.4 %collective-permute-start.25 = (bf16[2,256,640]{2,1,0:T(8,128)(2,1)S(1)}, bf16[2,256,640]{2,1,0:T(8,128)(2,1)}, u32[]{:S(2)}, u32[]{:S(2)}) collective-permute-start(bf16[2,256,640]{2,1,0:T(8,128)(2,1)S(1)} %shard_map.114), channel_id=1, source_target_pairs={{0,4},{1,5},{2,6},{3,7},{4,0},{5,1},{6,2},{7,3},{8,11},{9,10},{10,... | collective-permute-start | bytes 1966088 | tf_op jit(solution)/shard_map/ppermute | solution.py:66
  220.6 15.9 %collective-permute-start.20 = (bf16[2,256,640]{2,1,0:T(8,128)(2,1)}, bf16[2,256,640]{2,1,0:T(8,128)(2,1)}, u32[]{:S(2)}, u32[]{:S(2)}) collective-permute-start(bf16[2,256,640]{2,1,0:T(8,128)(2,1)} %shard_map.112), channel_id=1, source_target_pairs={{0,4},{1,5},{2,6},{3,7},{4,0},{5,1},{6,2},{7,3},{8,11},{9,10},{10,... | collective-permute-start | bytes 1966088 | tf_op jit(solution)/shard_map/ppermute | solution.py:66
  (21 other events, 92.9 us)

commit v4 on v3

--- a/solution.py
+++ b/solution.py
@@ -20,7 +20,7 @@
     for table in PLACE
 )
 
-MINE, THEIRS, SLOT, ROWS, OWN, FIRST, X_AT = 0, 4, 8, 12, 20, 22, 30
+MINE, THEIRS, SLOT, ROWS, OWN, CORE_AT, FIRST, X_AT = 0, 4, 8, 12, 20, 22, 23, 31
 
 
 def facts_of(core, c):
@@ -29,7 +29,7 @@
     ring = [r, r ^ 1, (r + 2) % 4, 3 - r]
     slots = [ring.index(p) for p in range(4)]
     rows = [place[p] for p in ring for place in (mine, theirs)]
-    return [*mine, *theirs, *slots, *rows, mine[r], theirs[r]]
+    return [*mine, *theirs, *slots, *rows, mine[r], theirs[r], core]
 
 
 FACTS = [[facts_of(core, c) for c in range(8)] for core in range(2)]
@@ -124,7 +124,7 @@
         ),
         out_shape=[jax.ShapeDtypeStruct(s, BF) for s in shapes],
         input_output_aliases=aliases,
-        compiler_params=pltpu.CompilerParams(vmem_limit_bytes=40 * MIB),
+        compiler_params=pltpu.CompilerParams(vmem_limit_bytes=56 * MIB),
         cost_estimate=pl.CostEstimate(
             flops=2 * RB * d * n, bytes_accessed=2 * (3 * RB * d + d * n), transcendentals=0
         ),
@@ -133,34 +133,61 @@
 
 def more_queries_kernel(n_ref, wa_ref, wb_ref, q_ref):
     k = wa_ref.shape[0]
-    q = jnp.dot(n_ref[0, :, :k], wa_ref[...], preferred_element_type=F32)
-    q += jnp.dot(n_ref[0, :, k:], wb_ref[...], preferred_element_type=F32)
-    q_ref[0] = q.astype(BF)
+    q = jnp.dot(n_ref[:, :k], wa_ref[...], preferred_element_type=F32)
+    q += jnp.dot(n_ref[:, k:], wb_ref[...], preferred_element_type=F32)
+    q_ref[...] = q.astype(BF)
 
 
 def more_queries(normed, wa, wb):
     d, n = normed.shape[2], wa.shape[1]
+    rows = 2 * RB
     return pl.pallas_call(
         more_queries_kernel,
-        grid=(4,),
+        grid=(2,),
         in_specs=[
-            pl.BlockSpec((1, RB, d), lambda i: (i, 0, 0)),
+            pl.BlockSpec((rows, d), lambda i: (i, 0)),
             pl.BlockSpec(wa.shape, lambda i: (0, 0)),
             pl.BlockSpec(wb.shape, lambda i: (0, 0)),
         ],
-        out_specs=pl.BlockSpec((1, RB, n), lambda i: (i, 0, 0)),
-        out_shape=jax.ShapeDtypeStruct((4, RB, n), BF),
-        compiler_params=pltpu.CompilerParams(vmem_limit_bytes=32 * MIB),
+        out_specs=pl.BlockSpec((rows, n), lambda i: (i, 0)),
+        out_shape=jax.ShapeDtypeStruct((4 * RB, n), BF),
+        compiler_params=pltpu.CompilerParams(vmem_limit_bytes=56 * MIB),
         cost_estimate=pl.CostEstimate(
             flops=8 * RB * d * n, bytes_accessed=2 * (4 * RB * d + d * n), transcendentals=0
         ),
-    )(normed, wa, wb)
+    )(normed.reshape(4 * RB, d), wa, wb).reshape(4, RB, n)
 
 
 def attend_kernel(
-    chunk, meta, q_own, q_other, kv_own, kv_other, seg_col, seg_row, out, scores, tops, sums
+    chunk, meta, q_own, q_other, seg_col, seg_row, own0, o2, o2b, s1, s1b, s3, s3b, other0, t2,
+    out, kv, scores, tops, sums, sems,
 ):
     t = pl.program_id(0)
+    core = meta[CORE_AT]
+    copies = [
+        pltpu.make_async_copy(src, dst, sems.at[i])
+        for i, (src, dst) in enumerate((
+            (own0, kv.at[0, 0]),
+            (s1.at[0], kv.at[0, 1, core]),
+            (s1b.at[0], kv.at[0, 1, 1 - core]),
+            (o2, kv.at[0, 2, core]),
+            (o2b, kv.at[0, 2, 1 - core]),
+            (s3.at[0], kv.at[0, 3, core]),
+            (s3b.at[0], kv.at[0, 3, 1 - core]),
+            (other0, kv.at[1, 0]),
+            (s1.at[1:3], kv.at[1, 1]),
+            (t2, kv.at[1, 2]),
+            (s3.at[1:3], kv.at[1, 3]),
+        ))
+    ]
+
+    @pl.when(t == 0)
+    def _():
+        for copy in copies:
+            copy.start()
+        for copy in copies:
+            copy.wait()
+
     block = meta[MINE + 2 * chunk + t]
     first = meta[FIRST + block]
     count = block - first + 1
@@ -169,7 +196,6 @@
     factor = HD ** (-0.5) * 1.4426950408889634
     pairs = [(src, i) for src in range(2) for i in range(heads)]
     qs = (q_own, q_other)
-    kvs = (kv_own, kv_other)
 
     def place(i):
         kb = first + i
@@ -188,7 +214,7 @@
         for n, (src, h) in enumerate(pairs):
             cols = slice(h * HD, (h + 1) * HD)
             s = lax.dot_general(
-                qs[src][0, :, cols], kvs[src][j, y, :, cols], (((1,), (1,)), ((), ())),
+                qs[src][0, :, cols], kv[src, j, y, :, cols], (((1,), (1,)), ((), ())),
                 preferred_element_type=F32,
             )
             s = jnp.where(visible, s, -1e30)
@@ -224,7 +250,7 @@
             e = scores[n, i]
             inv = sums[n]
             weights = jnp.concatenate([e[:, :HD] * inv, e[:, HD:] * inv], axis=1).astype(BF)
-            tops[n] += jnp.dot(weights, kvs[src][j, y, :, cols], preferred_element_type=F32)
+            tops[n] += jnp.dot(weights, kv[src, j, y, :, cols], preferred_element_type=F32)
         return 0
 
     lax.fori_loop(0, count, mix, 0)
@@ -232,32 +258,33 @@
         out[:, n * HD : (n + 1) * HD] = tops[n].astype(BF)
 
 
-def attend(meta, chunk, q_own, q_other, kv_own, kv_other, seg_col, seg_row):
+def attend(meta, chunk, q_own, q_other, seg_col, seg_row, pieces):
     n = q_own.shape[2]
     heads = n // HD
     whole = lambda a: pl.BlockSpec(a.shape, lambda t, m, nd=a.ndim: (0,) * nd)
     q_spec = pl.BlockSpec((1, RB, n), lambda t, m: (m[SLOT + 2 * chunk + t], 0, 0))
+    in_place = pl.BlockSpec(memory_space=pl.ANY)
     return pl.pallas_call(
         functools.partial(attend_kernel, chunk),
         grid_spec=pltpu.PrefetchScalarGridSpec(
             num_scalar_prefetch=1,
             grid=(2,),
-            in_specs=[
-                q_spec, q_spec, whole(kv_own), whole(kv_other), whole(seg_col), whole(seg_row)
-            ],
+            in_specs=[q_spec, q_spec, whole(seg_col), whole(seg_row)] + [in_place] * len(pieces),
             out_specs=pl.BlockSpec((RB, 2 * n), lambda t, m: (t, 0)),
             scratch_shapes=[
+                pltpu.VMEM((2, 4, 2, RB, 2 * n), BF),
                 pltpu.VMEM((2 * heads, 5, RB, RB), F32),
                 pltpu.VMEM((2 * heads, RB, HD), F32),
                 pltpu.VMEM((2 * heads, RB, HD), F32),
+                pltpu.SemaphoreType.DMA((11,)),
             ],
         ),
         out_shape=jax.ShapeDtypeStruct((2 * RB, 2 * n), BF),
-        compiler_params=pltpu.CompilerParams(vmem_limit_bytes=40 * MIB),
+        compiler_params=pltpu.CompilerParams(vmem_limit_bytes=56 * MIB),
         cost_estimate=pl.CostEstimate(
             flops=4 * 2 * RB * 768 * 2 * n, bytes_accessed=8 * MIB, transcendentals=2 * RB * 768 * 6
         ),
-    )(meta, q_own, q_other, kv_own, kv_other, seg_col, seg_row)
+    )(meta, q_own, q_other, seg_col, seg_row, *pieces)
 
 
 def reorder_kernel(meta, w, out):
@@ -280,72 +307,112 @@
     )(meta, w).reshape(k8 * n, width)
 
 
-def finish_kernel(meta, c0, c1, c2a, c2b, c3, w, res, *refs):
-    out = refs[-1]
-    t = pl.program_id(0)
-    far = jnp.where(t == 0, c2a[...], c2b[...])
-    n = far.shape[1]
-    total = res[0].astype(F32)
-    for j, c in enumerate((c0[...], c1[...], far, c3[...])):
-        total += jnp.dot(c, w[j * n : (j + 1) * n, :], preferred_element_type=F32)
-    out[0] = total.astype(BF)
+def finish_kernel(chunk, blocks, meta, c0, c1, c2a, c2b, c3, w, res, *refs):
+    out, cs, ws, rs, outs, c_sems, w_sems, r_sems, out_sems = refs[-9:]
+    n = cs.shape[2]
+    copy = pltpu.make_async_copy
+    c_copies = [
+        [copy(c0, cs.at[0], c_sems.at[0])],
+        [copy(c1, cs.at[1], c_sems.at[1])],
+        [copy(c3, cs.at[2], c_sems.at[2])],
+        [
+            copy(c2a, cs.at[3, 0:RB], c_sems.at[3]),
+            copy(c2b, cs.at[3, RB : 2 * RB], c_sems.at[4]),
+        ],
+    ]
+    at = (0, 1, 3, 2)
+    w_copies = [
+        copy(w.at[at[j] * n : (at[j] + 1) * n], ws.at[j], w_sems.at[j]) for j in range(4)
+    ]
+    r_copies = [
+        copy(res.at[meta[SLOT + 2 * chunk + t]], rs.at[t * RB : (t + 1) * RB], r_sems.at[t])
+        for t in range(2)
+    ]
+    for j in range(4):
+        for one in (*c_copies[j], w_copies[j]):
+            one.start()
+    for one in r_copies:
+        one.start()
+    total = None
+    for j in range(4):
+        for one in (*c_copies[j], w_copies[j]):
+            one.wait()
+        part = jnp.dot(cs[j], ws[j], preferred_element_type=F32)
+        total = part if total is None else total + part
+    for one in r_copies:
+        one.wait()
+    outs[...] = (rs[...].astype(F32) + total).astype(BF)
+    targets = [t if blocks == 2 else meta[MINE + 2 * chunk + t] for t in range(2)]
+    out_copies = [
+        copy(outs.at[t * RB : (t + 1) * RB], out.at[targets[t]], out_sems.at[t]) for t in range(2)
+    ]
+    for one in out_copies:
+        one.start()
+    for one in out_copies:
+        one.wait()
 
 
 def finish(meta, chunk, parts, w, res, blocks, prior=None):
     depth, width = w.shape
     n = depth // 4
-    tile = pl.BlockSpec((RB, n), lambda t, m: (t, 0))
-    fixed = pl.BlockSpec((RB, n), lambda t, m: (0, 0))
     ins = list(parts) + [w, res]
-    specs = [tile, tile, fixed, fixed, tile]
-    specs.append(pl.BlockSpec(w.shape, lambda t, m: (0, 0)))
-    specs.append(pl.BlockSpec((1, RB, width), lambda t, m: (m[SLOT + 2 * chunk + t], 0, 0)))
     aliases = {}
     if prior is not None:
         aliases[1 + len(ins)] = 0
         ins.append(prior)
-        specs.append(pl.BlockSpec(memory_space=pl.ANY))
-    if blocks == 2:
-        target = lambda t, m: (t, 0, 0)
-    else:
-        target = lambda t, m: (m[MINE + 2 * chunk + t], 0, 0)
+    in_place = pl.BlockSpec(memory_space=pl.ANY)
     return pl.pallas_call(
-        finish_kernel,
+        functools.partial(finish_kernel, chunk, blocks),
         grid_spec=pltpu.PrefetchScalarGridSpec(
             num_scalar_prefetch=1,
-            grid=(2,),
-            in_specs=specs,
-            out_specs=pl.BlockSpec((1, RB, width), target),
+            grid=(1,),
+            in_specs=[in_place] * len(ins),
+            out_specs=in_place,
+            scratch_shapes=[
+                pltpu.VMEM((4, 2 * RB, n), BF),
+                pltpu.VMEM((4, n, width), BF),
+                pltpu.VMEM((2 * RB, width), BF),
+                pltpu.VMEM((2 * RB, width), BF),
+                pltpu.SemaphoreType.DMA((5,)),
+                pltpu.SemaphoreType.DMA((4,)),
+                pltpu.SemaphoreType.DMA((2,)),
+                pltpu.SemaphoreType.DMA((2,)),
+            ],
         ),
         out_shape=jax.ShapeDtypeStruct((blocks, RB, width), BF),
         input_output_aliases=aliases,
-        compiler_params=pltpu.CompilerParams(vmem_limit_bytes=32 * MIB),
+        compiler_params=pltpu.CompilerParams(vmem_limit_bytes=56 * MIB),
         cost_estimate=pl.CostEstimate(
             flops=4 * RB * depth * width, bytes_accessed=8 * MIB, transcendentals=0
         ),
     )(meta, *ins)
 
 
-def place_kernel(meta, got, prior, out):
-    out[...] = got[...]
+def place_kernel(chunk, meta, got, prior, out, sems):
+    copies = [
+        pltpu.make_async_copy(got.at[t], out.at[meta[THEIRS + 2 * chunk + t]], sems.at[t])
+        for t in range(2)
+    ]
+    for copy in copies:
+        copy.start()
+    for copy in copies:
+        copy.wait()
 
 
 def place(meta, chunk, got, prior):
-    count, rows, width = got.shape
-    target = lambda t, m: (m[THEIRS + 2 * chunk + t], 0, 0)
+    in_place = pl.BlockSpec(memory_space=pl.ANY)
     return pl.pallas_call(
-        place_kernel,
+        functools.partial(place_kernel, chunk),
         grid_spec=pltpu.PrefetchScalarGridSpec(
             num_scalar_prefetch=1,
-            grid=(count,),
-            in_specs=[
-                pl.BlockSpec((1, rows, width), lambda t, m: (t, 0, 0)),
-                pl.BlockSpec(memory_space=pl.ANY),
-            ],
-            out_specs=pl.BlockSpec((1, rows, width), target),
+            grid=(1,),
+            in_specs=[in_place, in_place],
+            out_specs=in_place,
+            scratch_shapes=[pltpu.SemaphoreType.DMA((2,))],
         ),
         out_shape=jax.ShapeDtypeStruct(prior.shape, BF),
         input_output_aliases={2: 0},
+        compiler_params=pltpu.CompilerParams(vmem_limit_bytes=56 * MIB),
     )(meta, got, prior)
 
 
@@ -377,7 +444,7 @@
     seg_col = segment_ids.reshape(8, RB, 1)
     seg_row = segment_ids.reshape(8, 1, RB)
 
-    def cache(last_hidden, w_key, w_value, w_query):
+    def cache(last_hidden, w_key, w_value, w_query, w_out):
         kv_in = normalize(last_hidden, kv_gain)
         own_k = jnp.dot(kv_in, w_key, preferred_element_type=F32).astype(BF)
         own_v = jnp.dot(kv_in, w_value, preferred_element_type=F32).astype(BF)
@@ -388,61 +455,60 @@
         far = jnp.where(core == 0, far, send(far, CORE))
         piece = jnp.where(y_hi == 0, jnp.stack([pair, far]), jnp.stack([far, pair]))
         piece = piece.reshape(2, 2 * kv.shape[0], kv.shape[1])
+        w_mine = reorder(meta, w_out, 0)
         piece2 = send(piece, PARTNER)
         share = lax.dynamic_index_in_dim(piece, core, 0, keepdims=False)
         o2 = send(share, X_FAR)
-        piece2, o2, w_first = lax.optimization_barrier((piece2, o2, w_query[:cut]))
+        piece2, o2, w_first, w_mine = lax.optimization_barrier(
+            (piece2, o2, w_query[:cut], w_mine)
+        )
         t2 = send(piece2, X_FAR)
         w_first = send(w_first, PARTNER)
-        return share, o2, piece2, t2, w_first, w_query[cut:]
-
-    def nothing(last_hidden, w_key, w_value, w_query):
+        o2b = send(o2, CORE)
+        both = jnp.concatenate([share[None], piece2])
+        w_theirs = reorder(meta, w_out, 1)
+        return piece, o2, o2b, piece2, t2, both, w_first, w_query[cut:], w_mine, w_theirs
+
+    def nothing(last_hidden, w_key, w_value, w_query, w_out):
         rows = 2 * last_hidden.shape[0]
         cols = 2 * w_key.shape[1]
-        few = jnp.zeros((rows, cols), BF)
-        more = jnp.zeros((2, rows, cols), BF)
+        one, two, three = (jnp.zeros((k, rows, cols), BF) for k in (1, 2, 3))
         first, rest = w_query[:cut], w_query[cut:]
-        return few, few, more, more, jnp.zeros_like(first), jnp.zeros_like(rest)
-
-    share, o2, piece2, t2, w_q2a, w_rest = lax.cond(
-        segment_ids[0] >= 0, cache, nothing, last_hidden, w_key, w_value, w_q
+        w_none = jnp.zeros((w_out.shape[0] * w_out.shape[1], w_out.shape[2]), BF)
+        return (
+            two, one[0], one[0], two, two, three, jnp.zeros_like(first), jnp.zeros_like(rest),
+            w_none, w_none,
+        )
+
+    w_o_r = w_o.reshape(8, w_q.shape[1], width)
+    piece, o2, o2b, piece2, t2, both, w_q2a, w_rest, w_o_mine, w_o_theirs = lax.cond(
+        segment_ids[0] >= 0, cache, nothing, last_hidden, w_key, w_value, w_q, w_o_r
     )
     w_q2b = send(w_rest, PARTNER)
-    x_in, x_out, share, piece2 = lax.optimization_barrier((x_in, x_out, share, piece2))
+    x_in, x_out, both = lax.optimization_barrier((x_in, x_out, both))
     xo_a = send(x_out[: RB // 2], IN)
     xo_b = send(x_in[RB // 2 :], OUT)
-    both = jnp.concatenate([share[None], piece2])
     s1 = send(both, X_PREV)
     s3 = send(both, X_NEXT)
-    heads_cols = w_q.shape[1]
-    w_o_r = after(w_o, x_in, x_out).reshape(8, heads_cols, width)
-    w_o_mine, w_o_theirs = reorder(meta, w_o_r, 0), reorder(meta, w_o_r, 1)
     state = project(meta, [after(x0, x_in, x_out)], query_gain, w_q, 0, width)
     state = project(meta, [x_in], query_gain, w_q, 1, width, state)
     state = project(meta, [x_out], query_gain, w_q, 3, width, state)
-    xo_a, xo_b, s1, s3, w_o_mine, w_o_theirs, *state = lax.optimization_barrier(
-        (xo_a, xo_b, s1, s3, w_o_mine, w_o_theirs, *state)
-    )
-    got = jnp.stack([share, s1[0], o2, s3[0]])
-    got2 = send(got, CORE)
-    kv_own = jnp.where(
-        core == 0, jnp.stack([got, got2], axis=1), jnp.stack([got2, got], axis=1)
-    )
-    kv_other = jnp.stack([piece2, s1[1:], t2, s3[1:]])
+    xo_a, xo_b, s1, s3, *state = lax.optimization_barrier((xo_a, xo_b, s1, s3, *state))
+    s1b = send(s1, CORE)
+    s3b = send(s3, CORE)
     normed, q_own, res_own, res_other = project(
         meta, [xo_a, xo_b], query_gain, w_q, 2, width, state
     )
-    (w_q2b, kv_own, kv_other, normed, q_own, seg_col, seg_row, w_o_theirs) = (
-        lax.optimization_barrier(
-            (w_q2b, kv_own, kv_other, normed, q_own, seg_col, seg_row, w_o_theirs)
-        )
+    w_q2b, s1b, s3b, normed, q_own, seg_col, seg_row, w_o_theirs = lax.optimization_barrier(
+        (w_q2b, s1b, s3b, normed, q_own, seg_col, seg_row, w_o_theirs)
     )
     w_o2 = send(w_o_theirs, PARTNER)
     q_other = more_queries(normed, w_q2a, w_q2b)
+    pieces = (piece, o2, o2b, s1, s1b, s3, s3b, piece2, t2)
 
     result = None
     for chunk in range(2):
-        own = attend(meta, chunk, q_own, q_other, kv_own, kv_other, seg_col, seg_row)
+        own = attend(meta, chunk, q_own, q_other, seg_col, seg_row, pieces)
         c_in = send(own, IN)
         c_out = send(own, OUT)
         co_a = send(c_out[:RB], IN)

time: 240 us -> 270 us (1.12)
  Pallas kernels: 84.3 us -> 140 us
  waiting for transfers between devices: 57.1 us -> 48.4 us
  other arithmetic: 14.8 us -> 7.14 us
  starting transfers between devices: 49.9 us -> 44.8 us
  local copies, waits for them, and re-layouts: 27.3 us -> 22.8 us
    pallas_call x7, Pallas kernels: 33.6 us -> 79 us  [the longest x2 43 us: place(): pl.pallas_call(functools.partial(place_kernel, chunk), grid_spec=pltpu.Pr...]
    ppermute x26 -> x28, waiting for transfers between devices: 57.1 us -> 48.4 us  [send(): return lax.ppermute(value, AXES, pairs)]
    unnamed x46 -> x30, local copies, waits for them, and re-layouts: 10 us -> 3.27 us
    pallas_call x2, Pallas kernels: 13.9 us -> 20.2 us  [attend(): pl.pallas_call(functools.partial(attend_kernel, chunk), grid_spec=pltpu.P...]
    another operation x2 -> x0, other arithmetic: 6.17 us -> none  [the longest x1 3.14 us: body(): kv_other = jnp.stack([piece2, s1[1:], t2, s3[1:]])]
    ppermute x26 -> x28, starting transfers between devices: 49.9 us -> 44.8 us  [send(): return lax.ppermute(value, AXES, pairs)]
    pallas_call x4, Pallas kernels: 22.2 us -> 26.4 us  [project(): pl.pallas_call(kernel, grid_spec=pltpu.PrefetchScalarGridSpec(num_scalar_...]
    slice x4 -> x2, local copies, waits for them, and re-layouts: 5.26 us -> 6.08 us  [the longest x1 3.37 us: cache(): w_query[cut:]]
  transfers between devices with their start and end apart: 26 -> 28, of which waited for: 9 -> 10; matrix products, arithmetic and copies ran while one was open for 15% -> 11% of each run, Pallas kernels for 34% -> 44%
where the time goes in v4:
time: 270 us; the launch traced here: 268 us
  Pallas kernels  140 us (52%)
  waiting for transfers between devices  48.4 us (18%)
  starting transfers between devices  44.8 us (17%)
  local copies, waits for them, and re-layouts  22.8 us (8%)
  other arithmetic  7.14 us (3%)
  matrix products  4.47 us (2%)
    ppermute x28, waiting for transfers between devices, send(): return lax.ppermute(value, AXES, pairs)  48.4 us
    ppermute x28, starting transfers between devices, send(): return lax.ppermute(value, AXES, pairs)  44.8 us
    pallas_call x2, Pallas kernels, place(): pl.pallas_call(functools.partial(place_kernel, chunk), grid_spec=pltpu.Pr...  43 us
    pallas_call x4, Pallas kernels, project(): pl.pallas_call(kernel, grid_spec=pltpu.PrefetchScalarGridSpec(num_scalar_...  26.4 us
    pallas_call x4, Pallas kernels, finish(): pl.pallas_call(functools.partial(finish_kernel, chunk, blocks), grid_spec...  25.7 us
    pallas_call x2, Pallas kernels, attend(): pl.pallas_call(functools.partial(attend_kernel, chunk), grid_spec=pltpu.P...  20.2 us
    pallas_call x2, Pallas kernels, reorder(): pl.pallas_call(reorder_kernel, grid_spec=pltpu.PrefetchScalarGridSpec(num...  14.2 us
    pallas_call x1, Pallas kernels, more_queries(): pl.pallas_call(more_queries_kernel, grid=(2,), in_specs=[pl.BlockSpec((ro...  10.2 us
  transfers between devices with their start and end apart: 28, of which 10 were waited for; matrix products, arithmetic and copies ran while one was open for 11% of the time, Pallas kernels for 44%

profile of v4, /device:TPU:1, one launch (start us, length us, event | category | flops | bytes accessed | tf_op | source)
XLA Modules:
  0.0 268.4 jit_solution(16127863085517476288)
XLA Ops:
  8.1 66.8 %conditional.1 = (bf16[2,256,768]{2,1,0:T(8,128)(2,1)}, bf16[256,768]{1,0:T(8,128)(2,1)}, bf16[256,768]{1,0:T(8,128)(2,1)}, bf16[2,256,768]{2,1,0:T(8,128)(2,1)}...) conditional(s32[]{:T(128)} %bitcast.12, () %tuple.18, ...), branch_computations={%region_1.2_spmd, %region_2.4_spmd} | conditional | flops 1017479296 | bytes 69659760 | solution.py:484
  9.8 3.6 %convolution_convert_fusion = bf16[128,384]{1,0:T(8,128)(2,1)S(1)} fusion(bf16[5120,384]{1,0:T(8,128)(2,1)} %get-tuple-element.143, bf16[128,5120]{1,0:T(8,128)(2,1)} %get-tuple-element.140, f32[5120]{0:T(1024)} %get-tuple-element.141, f32[128]{0:T(128)S(1)} %add_rsqrt_fusion), kind=kOutput, calls=%fused_computation.6 | convolution fusion | flops 505987072 | bytes 5362176 | tf_op jit(solution)/shard_map/cond/branch_1_fun/dot_general | solution.py:450
  18.5 15.1 %collective-permute-start.2 = (bf16[2,128,768]{2,1,0:T(8,128)(2,1)S(1)}, bf16[2,128,768]{2,1,0:T(8,128)(2,1)}, u32[]{:S(2)}, u32[]{:S(2)}) collective-permute-start(bf16[2,128,768]{2,1,0:T(8,128)(2,1)S(1)} %collective-permute-done.1), channel_id=1, source_target_pairs={{0,8},{1,9},{2,10},{3,11},{4,12},{5,13},{6,14},{7,15},{8,0},{9,1},... | collective-permute-start | bytes 1179656 | tf_op jit(solution)/shard_map/cond/branch_1_fun/ppermute | solution.py:66
  38.9 2.8 %collective-permute-start.4 = (bf16[256,768]{1,0:T(8,128)(2,1)S(1)}, bf16[256,768]{1,0:T(8,128)(2,1)}, u32[]{:S(2)}, u32[]{:S(2)}) collective-permute-start(bf16[256,768]{1,0:T(8,128)(2,1)S(1)} %fusion.9), channel_id=1, source_target_pairs={{0,32},{1,33},{2,34},{3,35},{4,36},{5,37},{6,38},{7,39},{8,40},{9,... | collective-permute-start | bytes 1179656 | tf_op jit(solution)/shard_map/cond/branch_1_fun/ppermute | solution.py:66
  41.7 2.7 %slice.20 = bf16[2048,384]{1,0:T(8,128)(2,1)} slice(bf16[5120,384]{1,0:T(8,128)(2,1)} %get-tuple-element.29), slice={[0:2048], [0:384]} | slice | bytes 3145728 | tf_op jit(solution)/shard_map/cond/branch_1_fun/slice | solution.py:463
  44.4 7.1 %branch_1_fun.2 = bf16[8,384,640]{2,1,0:T(8,128)(2,1)} custom-call(s32[32]{0:T(128)S(1)} %get-tuple-element.30.meta, bf16[8,384,640]{2,1,0:T(8,128)(2,1)} %bitcast.32), custom_call_target="tpu_custom_call" | custom-call | tf_op jit(solution)/shard_map/cond/branch_1_fun/pallas_call | solution.py:296
  51.5 2.2 collective-permute-start.7
  56.3 7.1 %branch_1_fun.3 = bf16[8,384,640]{2,1,0:T(8,128)(2,1)} custom-call(s32[32]{0:T(128)S(1)} %get-tuple-element.30.meta, bf16[8,384,640]{2,1,0:T(8,128)(2,1)} %bitcast.33), custom_call_target="tpu_custom_call" | custom-call | tf_op jit(solution)/shard_map/cond/branch_1_fun/pallas_call | solution.py:296
  63.4 3.4 %slice.21 = bf16[3072,384]{1,0:T(8,128)(2,1)} slice(bf16[5120,384]{1,0:T(8,128)(2,1)} %get-tuple-element.29), slice={[2048:5120], [0:384]} | slice | bytes 4718592 | tf_op jit(solution)/shard_map/cond/branch_1_fun/slice | solution.py:470
  67.8 2.3 pad_maximum_fusion
  70.1 4.8 %collective-permute-done.6 = bf16[2,256,768]{2,1,0:T(8,128)(2,1)} collective-permute-done((bf16[2,256,768]{2,1,0:T(8,128)(2,1)}, bf16[2,256,768]{2,1,0:T(8,128)(2,1)}, u32[]{:S(2)}, u32[]{:S(2)}) %collective-permute-start.6) | collective-permute-done | bytes 786464 | tf_op jit(solution)/shard_map/cond/branch_1_fun/ppermute | solution.py:66
  76.1 3.9 %slice.33 = bf16[128,5120]{1,0:T(8,128)(2,1)} slice(bf16[256,5120]{1,0:T(8,128)(2,1)} %collective-permute-done.9.refs_0_), slice={[128:256], [0:5120]} | slice | bytes 2621440 | tf_op jit(solution)/shard_map/slice | solution.py:490
  83.0 6.3 %shard_map.105 = (bf16[4,256,5120]{2,1,0:T(8,128)(2,1)}, bf16[4,256,384]{2,1,0:T(8,128)(2,1)}, bf16[4,256,640]{2,1,0:T(8,128)(2,1)}, bf16[4,256,640]{2,1,0:T(8,128)(2,1)}) custom-call(s32[32]{0:T(128)S(1)} %pad_add_fusion.meta, bf16[256,5120]{1,0:T(8,128)(2,1)} %bitcast.38, f32[1,5120]{1,0:T(1,128)} %refs_2_.1, bf16[5120,384]{1,0:T(8,128)(2,1)S(1)} %bitcast.28), custom_call_target="tpu_custom_call" | custom-call | flops 1006632960 | bytes 11796480 | tf_op jit(solution)/shard_map/pallas_call | solution.py:117
  89.3 6.3 %shard_map.106 = (bf16[4,256,5120]{2,1,0:T(8,128)(2,1)}, bf16[4,256,384]{2,1,0:T(8,128)(2,1)}, bf16[4,256,640]{2,1,0:T(8,128)(2,1)}, bf16[4,256,640]{2,1,0:T(8,128)(2,1)}) custom-call(s32[32]{0:T(128)S(1)} %pad_add_fusion.meta, ...), custom_call_target="tpu_custom_call", output_to_operand_aliasing={{0}: (4, {}), {1}: (5, {}), {2}: (6, {}), {3}: (7, {})} | custom-call | flops 1006632960 | bytes 11796480 | tf_op jit(solution)/shard_map/pallas_call | solution.py:117
  95.6 6.3 %shard_map.107 = (bf16[4,256,5120]{2,1,0:T(8,128)(2,1)}, bf16[4,256,384]{2,1,0:T(8,128)(2,1)}, bf16[4,256,640]{2,1,0:T(8,128)(2,1)}, bf16[4,256,640]{2,1,0:T(8,128)(2,1)}) custom-call(s32[32]{0:T(128)S(1)} %pad_add_fusion.meta, bf16[256,5120]{1,0:T(8,128)(2,1)} %copy-done.2, ...), custom_call_target="tpu_custom_call", output_to_operand_aliasing={{0}: (4, {}), {1}: (5, {}), {2}: (6, {}), {3}: (7, {})} | custom-call | flops 1006632960 | bytes 11796480 | tf_op jit(solution)/shard_map/pallas_call | solution.py:117
  101.9 6.3 %collective-permute-done.13.s1 = bf16[3,256,768]{2,1,0:T(8,128)(2,1)S(1)} collective-permute-done((bf16[3,256,768]{2,1,0:T(8,128)(2,1)}, bf16[3,256,768]{2,1,0:T(8,128)(2,1)S(1)}, u32[]{:S(2)}, u32[]{:S(2)}) %collective-permute-start.13) | collective-permute-done | bytes 1179680 | tf_op jit(solution)/shard_map/ppermute | solution.py:66
  109.1 3.6 %collective-permute-start.15 = (bf16[3,256,768]{2,1,0:T(8,128)(2,1)S(1)}, bf16[3,256,768]{2,1,0:T(8,128)(2,1)}, u32[]{:S(2)}, u32[]{:S(2)}) collective-permute-start(bf16[3,256,768]{2,1,0:T(8,128)(2,1)S(1)} %collective-permute-done.13.s1), channel_id=1, source_target_pairs={{0,8},{1,9},{2,10},{3,11},{4,12},{5,13},{6,14},{7,15},{8,0},{9,1},... | collective-permute-start | bytes 3538952 | tf_op jit(solution)/shard_map/ppermute | solution.py:66
  112.6 7.5 %shard_map.108 = (bf16[4,256,5120]{2,1,0:T(8,128)(2,1)}, bf16[4,256,384]{2,1,0:T(8,128)(2,1)}, bf16[4,256,640]{2,1,0:T(8,128)(2,1)}, bf16[4,256,640]{2,1,0:T(8,128)(2,1)}) custom-call(s32[32]{0:T(128)S(1)} %pad_add_fusion.meta, ...), custom_call_target="tpu_custom_call", output_to_operand_aliasing={{0}: (5, {}), {1}: (6, {}), {2}: (7, {}), {3}: (8, {})} | custom-call | flops 1006632960 | bytes 11796480 | tf_op jit(solution)/shard_map/pallas_call | solution.py:117
  120.1 4.1 %collective-permute-done.8.wb_ref = bf16[3072,384]{1,0:T(8,128)(2,1)} collective-permute-done((bf16[3072,384]{1,0:T(8,128)(2,1)}, bf16[3072,384]{1,0:T(8,128)(2,1)}, u32[]{:S(2)}, u32[]{:S(2)}) %collective-permute-start.8) | collective-permute-done | bytes 2359328 | tf_op jit(solution)/shard_map/ppermute | solution.py:66
  125.8 10.2 %shard_map.109 = bf16[1024,384]{1,0:T(8,128)(2,1)} custom-call(bf16[1024,5120]{1,0:T(8,128)(2,1)} %bitcast.25, bf16[2048,384]{1,0:T(8,128)(2,1)} %get-tuple-element.113.wa_ref, bf16[3072,384]{1,0:T(8,128)(2,1)} %collective-permute-done.8.wb_ref), custom_call_target="tpu_custom_call" | custom-call | flops 4026531840 | bytes 14417920 | tf_op jit(solution)/shard_map/pallas_call | solution.py:144
  136.0 10.1 %shard_map.112.c0 = bf16[512,768]{1,0:T(8,128)(2,1)} custom-call(s32[32]{0:T(128)S(1)} %pad_add_fusion.meta, bf16[4,256,384]{2,1,0:T(8,128)(2,1)} %get-tuple-element.111.q_own, bf16[4,256,384]{2,1,0:T(8,128)(2,1)} %bitcast.34, s32[8,256,1]{2,1,0:T(8,128)} %copy.35.seg_col, s32[8,1,256]{2,1,0:T(1,128)} %bitcast.43, ...), custom_call_target="tpu_custom_call" | custom-call | flops 1207959552 | bytes 8388608 | tf_op jit(solution)/shard_map/pallas_call | solution.py:267
  146.9 10.1 %shard_map.110.c0 = bf16[512,768]{1,0:T(8,128)(2,1)} custom-call(s32[32]{0:T(128)S(1)} %pad_add_fusion.meta, bf16[4,256,384]{2,1,0:T(8,128)(2,1)} %get-tuple-element.111.q_own, bf16[4,256,384]{2,1,0:T(8,128)(2,1)} %bitcast.35, s32[8,256,1]{2,1,0:T(8,128)} %copy.35.seg_col, s32[8,1,256]{2,1,0:T(1,128)} %bitcast.44, ...), custom_call_target="tpu_custom_call" | custom-call | flops 1207959552 | bytes 8388608 | tf_op jit(solution)/shard_map/pallas_call | solution.py:267
  159.3 6.8 %collective-permute-done.24.c3 = bf16[512,768]{1,0:T(8,128)(2,1)S(1)} collective-permute-done((bf16[512,768]{1,0:T(8,128)(2,1)}, bf16[512,768]{1,0:T(8,128)(2,1)S(1)}, u32[]{:S(2)}, u32[]{:S(2)}) %collective-permute-start.24) | collective-permute-done | bytes 786464 | tf_op jit(solution)/shard_map/ppermute | solution.py:66
  167.1 15.9 %collective-permute-done.18.c3 = bf16[512,768]{1,0:T(8,128)(2,1)S(1)} collective-permute-done((bf16[512,768]{1,0:T(8,128)(2,1)}, bf16[512,768]{1,0:T(8,128)(2,1)S(1)}, u32[]{:S(2)}, u32[]{:S(2)}) %collective-permute-start.18) | collective-permute-done | bytes 786464 | tf_op jit(solution)/shard_map/ppermute | solution.py:66
  185.4 6.6 %collective-permute-done.25.c2a = bf16[256,768]{1,0:T(8,128)(2,1)S(1)} collective-permute-done((bf16[256,768]{1,0:T(8,128)(2,1)S(1)}, bf16[256,768]{1,0:T(8,128)(2,1)S(1)}, u32[]{:S(2)}, u32[]{:S(2)}) %collective-permute-start.25) | collective-permute-done | bytes 393248 | tf_op jit(solution)/shard_map/ppermute | solution.py:66
  192.8 6.7 %shard_map.113 = bf16[2,256,640]{2,1,0:T(8,128)(2,1)} custom-call(s32[32]{0:T(128)S(1)} %pad_add_fusion.meta, bf16[512,768]{1,0:T(8,128)(2,1)} %shard_map.112.c0, bf16[512,768]{1,0:T(8,128)(2,1)} %copy-done.4, bf16[256,768]{1,0:T(8,128)(2,1)} %copy-done.9, bf16[256,768]{1,0:T(8,128)(2,1)} %copy-done.10, bf16[512,768]{1,0:T(8,128)(2,1)} %copy-done.3, ...), custom_call_target="tpu_custom_call" | custom-call | flops 2013265920 | bytes 8388608 | tf_op jit(solution)/shard_map/pallas_call | solution.py:364
  199.6 3.8 %collective-permute-start.27 = (bf16[2,256,640]{2,1,0:T(8,128)(2,1)}, bf16[2,256,640]{2,1,0:T(8,128)(2,1)S(1)}, u32[]{:S(2)}, u32[]{:S(2)}) collective-permute-start(bf16[2,256,640]{2,1,0:T(8,128)(2,1)} %shard_map.113), channel_id=1, source_target_pairs={{0,4},{1,5},{2,6},{3,7},{4,0},{5,1},{6,2},{7,3},{8,11},{9,10},{10,... | collective-permute-start | bytes 1966088 | tf_op jit(solution)/shard_map/ppermute | solution.py:66
  204.1 6.7 %shard_map.111 = bf16[2,256,640]{2,1,0:T(8,128)(2,1)} custom-call(s32[32]{0:T(128)S(1)} %pad_add_fusion.meta, bf16[512,768]{1,0:T(8,128)(2,1)} %shard_map.110.c0, bf16[512,768]{1,0:T(8,128)(2,1)} %copy-done.6, bf16[256,768]{1,0:T(8,128)(2,1)} %copy-done.11, bf16[256,768]{1,0:T(8,128)(2,1)} %collective-permute-done.20.c2b, bf16[512,768]{1,0:T(8,128)(2,1)} %copy-done.5, ...), custom_call_target="tpu_custom_call" | custom-call | flops 2013265920 | bytes 8388608 | tf_op jit(solution)/shard_map/pallas_call | solution.py:364
  211.1 6.2 %shard_map.114.prior = bf16[8,256,640]{2,1,0:T(8,128)(2,1)} custom-call(s32[32]{0:T(128)S(1)} %pad_add_fusion.meta, bf16[512,768]{1,0:T(8,128)(2,1)} %shard_map.112.c0, bf16[512,768]{1,0:T(8,128)(2,1)} %copy-done.4, bf16[256,768]{1,0:T(8,128)(2,1)} %copy-done.9, bf16[256,768]{1,0:T(8,128)(2,1)} %copy-done.10, bf16[512,768]{1,0:T(8,128)(2,1)} %copy-done.3, ...), custom_call_target="tpu_custom_call" | custom-call | flops 2013265920 | bytes 8388608 | tf_op jit(solution)/shard_map/pallas_call | solution.py:364
  218.2 21.5 %shard_map.115.refs_0_ = bf16[8,256,640]{2,1,0:T(8,128)(2,1)} custom-call(s32[32]{0:T(128)S(1)} %pad_add_fusion.meta, bf16[2,256,640]{2,1,0:T(8,128)(2,1)} %copy-done.14, bf16[8,256,640]{2,1,0:T(8,128)(2,1)} %shard_map.114.prior), custom_call_target="tpu_custom_call", output_to_operand_aliasing={{}: (2, {})} | custom-call | tf_op jit(solution)/shard_map/pallas_call | solution.py:404
  239.7 6.2 %shard_map.116.prior = bf16[8,256,640]{2,1,0:T(8,128)(2,1)} custom-call(s32[32]{0:T(128)S(1)} %pad_add_fusion.meta, bf16[512,768]{1,0:T(8,128)(2,1)} %shard_map.110.c0, bf16[512,768]{1,0:T(8,128)(2,1)} %copy-done.6, bf16[256,768]{1,0:T(8,128)(2,1)} %copy-done.11, bf16[256,768]{1,0:T(8,128)(2,1)} %collective-permute-done.20.c2b, ...), custom_call_target="tpu_custom_call", output_to_operand_aliasing={{}: (8, {})} | custom-call | flops 2013265920 | bytes 8388608 | tf_op jit(solution)/shard_map/pallas_call | solution.py:364
  246.7 21.5 %shard_map.117 = bf16[8,256,640]{2,1,0:T(8,128)(2,1)} custom-call(s32[32]{0:T(128)S(1)} %pad_add_fusion.meta, bf16[2,256,640]{2,1,0:T(8,128)(2,1)} %copy-done.13, bf16[8,256,640]{2,1,0:T(8,128)(2,1)} %shard_map.116.prior), custom_call_target="tpu_custom_call", output_to_operand_aliasing={{}: (2, {})} | custom-call | tf_op jit(solution)/shard_map/pallas_call | solution.py:404
  (105 shorter events, 39.8 us)
Async XLA Ops:
  0.0 74.9 %collective-permute-start.10 = (bf16[256,5120]{1,0:T(8,128)(2,1)}, bf16[256,5120]{1,0:T(8,128)(2,1)S(1)}, u32[]{:S(2)}, u32[]{:S(2)}) collective-permute-start(bf16[256,5120]{1,0:T(8,128)(2,1)} %bitcast.36), channel_id=1, source_target_pairs={{0,3},{1,2},{2,1},{3,0},{4,7},{5,6},{6,5},{7,4},{8,12},{9,13},{10,... | collective-permute-start | bytes 7864328 | tf_op jit(solution)/shard_map/ppermute | solution.py:66
  2.1 72.8 %collective-permute-start.9 = (bf16[256,5120]{1,0:T(8,128)(2,1)}, bf16[256,5120]{1,0:T(8,128)(2,1)}, u32[]{:S(2)}, u32[]{:S(2)}) collective-permute-start(bf16[256,5120]{1,0:T(8,128)(2,1)} %bitcast.37), channel_id=1, source_target_pairs={{0,1},{1,0},{2,3},{3,2},{4,5},{5,4},{6,7},{7,6},{8,9},{9,8},{10,11... | collective-permute-start | bytes 7864328 | tf_op jit(solution)/shard_map/ppermute | solution.py:66
  14.8 2.9 %collective-permute-start = (bf16[128,768]{1,0:T(8,128)(2,1)S(1)}, bf16[128,768]{1,0:T(8,128)(2,1)S(1)}, u32[]{:S(2)}, u32[]{:S(2)}) collective-permute-start(bf16[128,768]{1,0:T(8,128)(2,1)S(1)} %get-tuple-element.160), channel_id=1, source_target_pairs={{0,8},{1,9},{2,10},{3,11},{4,12},{5,13},{6,14},{7,15},{8,0},{9,1},... | collective-permute-start | bytes 589832 | tf_op jit(solution)/shard_map/cond/branch_1_fun/ppermute | solution.py:66
  17.8 0.7 collective-permute-start.1
  18.5 16.6 %collective-permute-start.2 = (bf16[2,128,768]{2,1,0:T(8,128)(2,1)S(1)}, bf16[2,128,768]{2,1,0:T(8,128)(2,1)}, u32[]{:S(2)}, u32[]{:S(2)}) collective-permute-start(bf16[2,128,768]{2,1,0:T(8,128)(2,1)S(1)} %collective-permute-done.1), channel_id=1, source_target_pairs={{0,8},{1,9},{2,10},{3,11},{4,12},{5,13},{6,14},{7,15},{8,0},{9,1},... | collective-permute-start | bytes 1179656 | tf_op jit(solution)/shard_map/cond/branch_1_fun/ppermute | solution.py:66
  37.2 14.3 %collective-permute-start.3 = (bf16[2,256,768]{2,1,0:T(8,128)(2,1)}, bf16[2,256,768]{2,1,0:T(8,128)(2,1)}, u32[]{:S(2)}, u32[]{:S(2)}) collective-permute-start(bf16[2,256,768]{2,1,0:T(8,128)(2,1)} %maximum_select_fusion), channel_id=1, source_target_pairs={{0,4},{1,5},{2,6},{3,7},{4,0},{5,1},{6,2},{7,3},{8,11},{9,10},{10,... | collective-permute-start | bytes 2359304 | tf_op jit(solution)/shard_map/cond/branch_1_fun/ppermute | solution.py:66
  38.9 12.6 %collective-permute-start.4 = (bf16[256,768]{1,0:T(8,128)(2,1)S(1)}, bf16[256,768]{1,0:T(8,128)(2,1)}, u32[]{:S(2)}, u32[]{:S(2)}) collective-permute-start(bf16[256,768]{1,0:T(8,128)(2,1)S(1)} %fusion.9), channel_id=1, source_target_pairs={{0,32},{1,33},{2,34},{3,35},{4,36},{5,37},{6,38},{7,39},{8,40},{9,... | collective-permute-start | bytes 1179656 | tf_op jit(solution)/shard_map/cond/branch_1_fun/ppermute | solution.py:66
  51.5 23.4 %collective-permute-start.7 = (bf16[2048,384]{1,0:T(8,128)(2,1)}, bf16[2048,384]{1,0:T(8,128)(2,1)}, u32[]{:S(2)}, u32[]{:S(2)}) collective-permute-start(bf16[2048,384]{1,0:T(8,128)(2,1)} %slice.20), channel_id=1, source_target_pairs={{0,4},{1,5},{2,6},{3,7},{4,0},{5,1},{6,2},{7,3},{8,11},{9,10},{10,... | collective-permute-start | bytes 4718600 | tf_op jit(solution)/shard_map/cond/branch_1_fun/ppermute | solution.py:66
  53.7 21.3 %collective-permute-start.6 = (bf16[2,256,768]{2,1,0:T(8,128)(2,1)}, bf16[2,256,768]{2,1,0:T(8,128)(2,1)}, u32[]{:S(2)}, u32[]{:S(2)}) collective-permute-start(bf16[2,256,768]{2,1,0:T(8,128)(2,1)} %collective-permute-done.3), channel_id=1, source_target_pairs={{0,32},{1,33},{2,34},{3,35},{4,36},{5,37},{6,38},{7,39},{8,40},{9,... | collective-permute-start | bytes 2359304 | tf_op jit(solution)/shard_map/cond/branch_1_fun/ppermute | solution.py:66
  55.2 14.9 %collective-permute-start.5 = (bf16[256,768]{1,0:T(8,128)(2,1)}, bf16[256,768]{1,0:T(8,128)(2,1)}, u32[]{:S(2)}, u32[]{:S(2)}) collective-permute-start(bf16[256,768]{1,0:T(8,128)(2,1)} %collective-permute-done.4), channel_id=1, source_target_pairs={{0,8},{1,9},{2,10},{3,11},{4,12},{5,13},{6,14},{7,15},{8,0},{9,1},... | collective-permute-start | bytes 1179656 | tf_op jit(solution)/shard_map/cond/branch_1_fun/ppermute | solution.py:66
  76.1 33.0 %collective-permute-start.11 = (bf16[128,5120]{1,0:T(8,128)(2,1)}, bf16[128,5120]{1,0:T(8,128)(2,1)}, u32[]{:S(2)}, u32[]{:S(2)}) collective-permute-start(bf16[128,5120]{1,0:T(8,128)(2,1)} %slice.32), channel_id=1, source_target_pairs={{0,1},{1,0},{2,3},{3,2},{4,5},{5,4},{6,7},{7,6},{8,9},{9,8},{10,11... | collective-permute-start | bytes 3932168 | tf_op jit(solution)/shard_map/ppermute | solution.py:66
  80.0 29.1 %collective-permute-start.12 = (bf16[128,5120]{1,0:T(8,128)(2,1)}, bf16[128,5120]{1,0:T(8,128)(2,1)}, u32[]{:S(2)}, u32[]{:S(2)}) collective-permute-start(bf16[128,5120]{1,0:T(8,128)(2,1)} %slice.33), channel_id=1, source_target_pairs={{0,3},{1,2},{2,1},{3,0},{4,7},{5,6},{6,5},{7,4},{8,12},{9,13},{10,... | collective-permute-start | bytes 3932168 | tf_op jit(solution)/shard_map/ppermute | solution.py:66
  80.6 27.6 %collective-permute-start.13 = (bf16[3,256,768]{2,1,0:T(8,128)(2,1)}, bf16[3,256,768]{2,1,0:T(8,128)(2,1)S(1)}, u32[]{:S(2)}, u32[]{:S(2)}) collective-permute-start(bf16[3,256,768]{2,1,0:T(8,128)(2,1)} %get-tuple-element.86), channel_id=1, source_target_pairs={{0,48},{1,49},{2,50},{3,51},{4,52},{5,53},{6,54},{7,55},{8,56},{9,... | collective-permute-start | bytes 3538952 | tf_op jit(solution)/shard_map/ppermute | solution.py:66
  81.3 27.8 %collective-permute-start.14 = (bf16[3,256,768]{2,1,0:T(8,128)(2,1)}, bf16[3,256,768]{2,1,0:T(8,128)(2,1)S(1)}, u32[]{:S(2)}, u32[]{:S(2)}) collective-permute-start(bf16[3,256,768]{2,1,0:T(8,128)(2,1)} %get-tuple-element.86), channel_id=1, source_target_pairs={{0,16},{1,17},{2,18},{3,19},{4,20},{5,21},{6,22},{7,23},{8,24},{9,... | collective-permute-start | bytes 3538952 | tf_op jit(solution)/shard_map/ppermute | solution.py:66
  82.1 42.2 %collective-permute-start.8 = (bf16[3072,384]{1,0:T(8,128)(2,1)}, bf16[3072,384]{1,0:T(8,128)(2,1)}, u32[]{:S(2)}, u32[]{:S(2)}) collective-permute-start(bf16[3072,384]{1,0:T(8,128)(2,1)} %get-tuple-element.82), channel_id=1, source_target_pairs={{0,4},{1,5},{2,6},{3,7},{4,0},{5,1},{6,2},{7,3},{8,11},{9,10},{10,... | collective-permute-start | bytes 7077896 | tf_op jit(solution)/shard_map/ppermute | solution.py:66
  95.6 17.0 %copy-start.15 = (s32[2048]{0:T(1024)S(1)}, s32[2048]{0:T(1024)}, u32[]{:S(2)}) copy-start(s32[2048]{0:T(1024)} %param.20) | copy-start | bytes 24580
  109.1 15.2 %collective-permute-start.15 = (bf16[3,256,768]{2,1,0:T(8,128)(2,1)S(1)}, bf16[3,256,768]{2,1,0:T(8,128)(2,1)}, u32[]{:S(2)}, u32[]{:S(2)}) collective-permute-start(bf16[3,256,768]{2,1,0:T(8,128)(2,1)S(1)} %collective-permute-done.13.s1), channel_id=1, source_target_pairs={{0,8},{1,9},{2,10},{3,11},{4,12},{5,13},{6,14},{7,15},{8,0},{9,1},... | collective-permute-start | bytes 3538952 | tf_op jit(solution)/shard_map/ppermute | solution.py:66
  112.6 11.7 %collective-permute-start.16 = (bf16[3,256,768]{2,1,0:T(8,128)(2,1)S(1)}, bf16[3,256,768]{2,1,0:T(8,128)(2,1)}, u32[]{:S(2)}, u32[]{:S(2)}) collective-permute-start(bf16[3,256,768]{2,1,0:T(8,128)(2,1)S(1)} %collective-permute-done.14.s3), channel_id=1, source_target_pairs={{0,8},{1,9},{2,10},{3,11},{4,12},{5,13},{6,14},{7,15},{8,0},{9,1},... | collective-permute-start | bytes 3538952 | tf_op jit(solution)/shard_map/ppermute | solution.py:66
  124.3 67.7 %collective-permute-start.21 = (bf16[3072,640]{1,0:T(8,128)(2,1)}, bf16[3072,640]{1,0:T(8,128)(2,1)}, u32[]{:S(2)}, u32[]{:S(2)}) collective-permute-start(bf16[3072,640]{1,0:T(8,128)(2,1)} %get-tuple-element.124), channel_id=1, source_target_pairs={{0,4},{1,5},{2,6},{3,7},{4,0},{5,1},{6,2},{7,3},{8,11},{9,10},{10,... | collective-permute-start | bytes 11796488 | tf_op jit(solution)/shard_map/ppermute | solution.py:66
  146.1 20.0 %collective-permute-start.24 = (bf16[512,768]{1,0:T(8,128)(2,1)}, bf16[512,768]{1,0:T(8,128)(2,1)S(1)}, u32[]{:S(2)}, u32[]{:S(2)}) collective-permute-start(bf16[512,768]{1,0:T(8,128)(2,1)} %shard_map.112.c0), channel_id=1, source_target_pairs={{0,3},{1,2},{2,1},{3,0},{4,7},{5,6},{6,5},{7,4},{8,12},{9,13},{10,... | collective-permute-start | bytes 2359304 | tf_op jit(solution)/shard_map/ppermute | solution.py:66
  146.9 19.8 %collective-permute-start.23 = (bf16[512,768]{1,0:T(8,128)(2,1)}, bf16[512,768]{1,0:T(8,128)(2,1)S(1)}, u32[]{:S(2)}, u32[]{:S(2)}) collective-permute-start(bf16[512,768]{1,0:T(8,128)(2,1)} %shard_map.112.c0), channel_id=1, source_target_pairs={{0,1},{1,0},{2,3},{3,2},{4,5},{5,4},{6,7},{7,6},{8,9},{9,8},{10,11... | collective-permute-start | bytes 2359304 | tf_op jit(solution)/shard_map/ppermute | solution.py:66
  157.0 25.9 %collective-permute-start.18 = (bf16[512,768]{1,0:T(8,128)(2,1)}, bf16[512,768]{1,0:T(8,128)(2,1)S(1)}, u32[]{:S(2)}, u32[]{:S(2)}) collective-permute-start(bf16[512,768]{1,0:T(8,128)(2,1)} %shard_map.110.c0), channel_id=1, source_target_pairs={{0,3},{1,2},{2,1},{3,0},{4,7},{5,6},{6,5},{7,4},{8,12},{9,13},{10,... | collective-permute-start | bytes 2359304 | tf_op jit(solution)/shard_map/ppermute | solution.py:66
  157.9 25.9 %collective-permute-start.17 = (bf16[512,768]{1,0:T(8,128)(2,1)}, bf16[512,768]{1,0:T(8,128)(2,1)S(1)}, u32[]{:S(2)}, u32[]{:S(2)}) collective-permute-start(bf16[512,768]{1,0:T(8,128)(2,1)} %shard_map.110.c0), channel_id=1, source_target_pairs={{0,1},{1,0},{2,3},{3,2},{4,5},{5,4},{6,7},{7,6},{8,9},{9,8},{10,11... | collective-permute-start | bytes 2359304 | tf_op jit(solution)/shard_map/ppermute | solution.py:66
  166.1 25.9 %copy-start.3 = (bf16[512,768]{1,0:T(8,128)(2,1)}, bf16[512,768]{1,0:T(8,128)(2,1)S(1)}, u32[]{:S(2)}) copy-start(bf16[512,768]{1,0:T(8,128)(2,1)S(1)} %collective-permute-done.24.c3) | copy-start | bytes 2359300
  166.2 25.8 %collective-permute-start.25 = (bf16[256,768]{1,0:T(8,128)(2,1)S(1)}, bf16[256,768]{1,0:T(8,128)(2,1)S(1)}, u32[]{:S(2)}, u32[]{:S(2)}) collective-permute-start(bf16[256,768]{1,0:T(8,128)(2,1)S(1)} %slice.41), channel_id=1, source_target_pairs={{0,1},{1,0},{2,3},{3,2},{4,5},{5,4},{6,7},{7,6},{8,9},{9,8},{10,11... | collective-permute-start | bytes 1179656 | tf_op jit(solution)/shard_map/ppermute | solution.py:66
  166.7 25.3 %copy-start.4 = (bf16[512,768]{1,0:T(8,128)(2,1)}, bf16[512,768]{1,0:T(8,128)(2,1)S(1)}, u32[]{:S(2)}) copy-start(bf16[512,768]{1,0:T(8,128)(2,1)S(1)} %collective-permute-done.23.c1) | copy-start | bytes 2359300
  166.7 25.3 %collective-permute-start.26 = (bf16[256,768]{1,0:T(8,128)(2,1)S(1)}, bf16[256,768]{1,0:T(8,128)(2,1)S(1)}, u32[]{:S(2)}, u32[]{:S(2)}) collective-permute-start(bf16[256,768]{1,0:T(8,128)(2,1)S(1)} %slice.42), channel_id=1, source_target_pairs={{0,3},{1,2},{2,1},{3,0},{4,7},{5,6},{6,5},{7,4},{8,12},{9,13},{10,... | collective-permute-start | bytes 1179656 | tf_op jit(solution)/shard_map/ppermute | solution.py:66
  183.0 16.5 %copy-start.5 = (bf16[512,768]{1,0:T(8,128)(2,1)}, bf16[512,768]{1,0:T(8,128)(2,1)S(1)}, u32[]{:S(2)}) copy-start(bf16[512,768]{1,0:T(8,128)(2,1)S(1)} %collective-permute-done.18.c3) | copy-start | bytes 2359300
  183.8 19.5 %collective-permute-start.19 = (bf16[256,768]{1,0:T(8,128)(2,1)}, bf16[256,768]{1,0:T(8,128)(2,1)S(1)}, u32[]{:S(2)}, u32[]{:S(2)}) collective-permute-start(bf16[256,768]{1,0:T(8,128)(2,1)} %slice.39), channel_id=1, source_target_pairs={{0,1},{1,0},{2,3},{3,2},{4,5},{5,4},{6,7},{7,6},{8,9},{9,8},{10,11... | collective-permute-start | bytes 1179656 | tf_op jit(solution)/shard_map/ppermute | solution.py:66
  184.7 18.7 %collective-permute-start.20 = (bf16[256,768]{1,0:T(8,128)(2,1)}, bf16[256,768]{1,0:T(8,128)(2,1)}, u32[]{:S(2)}, u32[]{:S(2)}) collective-permute-start(bf16[256,768]{1,0:T(8,128)(2,1)} %slice.40), channel_id=1, source_target_pairs={{0,3},{1,2},{2,1},{3,0},{4,7},{5,6},{6,5},{7,4},{8,12},{9,13},{10,... | collective-permute-start | bytes 1179656 | tf_op jit(solution)/shard_map/ppermute | solution.py:66
  199.6 17.8 %collective-permute-start.27 = (bf16[2,256,640]{2,1,0:T(8,128)(2,1)}, bf16[2,256,640]{2,1,0:T(8,128)(2,1)S(1)}, u32[]{:S(2)}, u32[]{:S(2)}) collective-permute-start(bf16[2,256,640]{2,1,0:T(8,128)(2,1)} %shard_map.113), channel_id=1, source_target_pairs={{0,4},{1,5},{2,6},{3,7},{4,0},{5,1},{6,2},{7,3},{8,11},{9,10},{10,... | collective-permute-start | bytes 1966088 | tf_op jit(solution)/shard_map/ppermute | solution.py:66
  210.7 35.2 %collective-permute-start.22 = (bf16[2,256,640]{2,1,0:T(8,128)(2,1)}, bf16[2,256,640]{2,1,0:T(8,128)(2,1)S(1)}, u32[]{:S(2)}, u32[]{:S(2)}) collective-permute-start(bf16[2,256,640]{2,1,0:T(8,128)(2,1)} %shard_map.111), channel_id=1, source_target_pairs={{0,4},{1,5},{2,6},{3,7},{4,0},{5,1},{6,2},{7,3},{8,11},{9,10},{10,... | collective-permute-start | bytes 1966088 | tf_op jit(solution)/shard_map/ppermute | solution.py:66
  (14 other events, 79.2 us)

commit v5 on v4

--- a/solution.py
+++ b/solution.py
@@ -102,7 +102,9 @@
 def project(meta, xs, gain, w, slot, width, prior=None):
     d, n = w.shape
     shapes = [(4, RB, d), (4, RB, n), (4, RB, width), (4, RB, width)]
-    whole = lambda a: pl.BlockSpec(a.shape, lambda i, m, nd=a.ndim: (0,) * nd)
+    whole = lambda a: pl.BlockSpec(
+        a.shape, lambda i, m, nd=a.ndim: (0,) * nd, pipeline_mode=pl.Buffered(1)
+    )
     ins = list(xs) + [gain, w]
     specs = [whole(a) for a in ins]
     aliases = {}
@@ -124,7 +126,7 @@
         ),
         out_shape=[jax.ShapeDtypeStruct(s, BF) for s in shapes],
         input_output_aliases=aliases,
-        compiler_params=pltpu.CompilerParams(vmem_limit_bytes=56 * MIB),
+        compiler_params=pltpu.CompilerParams(vmem_limit_bytes=20 * MIB),
         cost_estimate=pl.CostEstimate(
             flops=2 * RB * d * n, bytes_accessed=2 * (3 * RB * d + d * n), transcendentals=0
         ),
@@ -146,12 +148,12 @@
         grid=(2,),
         in_specs=[
             pl.BlockSpec((rows, d), lambda i: (i, 0)),
-            pl.BlockSpec(wa.shape, lambda i: (0, 0)),
-            pl.BlockSpec(wb.shape, lambda i: (0, 0)),
+            pl.BlockSpec(wa.shape, lambda i: (0, 0), pipeline_mode=pl.Buffered(1)),
+            pl.BlockSpec(wb.shape, lambda i: (0, 0), pipeline_mode=pl.Buffered(1)),
         ],
         out_specs=pl.BlockSpec((rows, n), lambda i: (i, 0)),
         out_shape=jax.ShapeDtypeStruct((4 * RB, n), BF),
-        compiler_params=pltpu.CompilerParams(vmem_limit_bytes=56 * MIB),
+        compiler_params=pltpu.CompilerParams(vmem_limit_bytes=20 * MIB),
         cost_estimate=pl.CostEstimate(
             flops=8 * RB * d * n, bytes_accessed=2 * (4 * RB * d + d * n), transcendentals=0
         ),
@@ -159,34 +161,25 @@
 
 
 def attend_kernel(
-    chunk, meta, q_own, q_other, seg_col, seg_row, own0, o2, o2b, s1, s1b, s3, s3b, other0, t2,
-    out, kv, scores, tops, sums, sems,
+    chunk, meta, q_own, q_other, seg_row, own0, o2, o2b, s1, s1b, s3, s3b, other0, t2,
+    out, kv, scores, tops, sums,
 ):
     t = pl.program_id(0)
     core = meta[CORE_AT]
-    copies = [
-        pltpu.make_async_copy(src, dst, sems.at[i])
-        for i, (src, dst) in enumerate((
-            (own0, kv.at[0, 0]),
-            (s1.at[0], kv.at[0, 1, core]),
-            (s1b.at[0], kv.at[0, 1, 1 - core]),
-            (o2, kv.at[0, 2, core]),
-            (o2b, kv.at[0, 2, 1 - core]),
-            (s3.at[0], kv.at[0, 3, core]),
-            (s3b.at[0], kv.at[0, 3, 1 - core]),
-            (other0, kv.at[1, 0]),
-            (s1.at[1:3], kv.at[1, 1]),
-            (t2, kv.at[1, 2]),
-            (s3.at[1:3], kv.at[1, 3]),
-        ))
-    ]
 
     @pl.when(t == 0)
     def _():
-        for copy in copies:
-            copy.start()
-        for copy in copies:
-            copy.wait()
+        kv[0, 0] = own0[...]
+        kv[0, 1, core] = s1[0]
+        kv[0, 1, 1 - core] = s1b[0]
+        kv[0, 2, core] = o2[...]
+        kv[0, 2, 1 - core] = o2b[...]
+        kv[0, 3, core] = s3[0]
+        kv[0, 3, 1 - core] = s3b[0]
+        kv[1, 0] = other0[...]
+        kv[1, 1] = s1[1:3]
+        kv[1, 2] = t2[...]
+        kv[1, 3] = s3[1:3]
 
     block = meta[MINE + 2 * chunk + t]
     first = meta[FIRST + block]
@@ -204,7 +197,7 @@
 
     tops[...] = jnp.full(tops.shape, -1e30, F32)
     sums[...] = jnp.zeros(sums.shape, F32)
-    q_doc = seg_col[block]
+    q_doc = jnp.transpose(jnp.broadcast_to(seg_row[block], (RB, RB)))
     row_at = block * RB + lax.broadcasted_iota(jnp.int32, (RB, RB), 0)
     col_at = lax.broadcasted_iota(jnp.int32, (RB, RB), 1)
 
@@ -258,33 +251,36 @@
         out[:, n * HD : (n + 1) * HD] = tops[n].astype(BF)
 
 
-def attend(meta, chunk, q_own, q_other, seg_col, seg_row, pieces):
+def attend(meta, chunk, q_own, q_other, seg_row, pieces):
     n = q_own.shape[2]
     heads = n // HD
     whole = lambda a: pl.BlockSpec(a.shape, lambda t, m, nd=a.ndim: (0,) * nd)
     q_spec = pl.BlockSpec((1, RB, n), lambda t, m: (m[SLOT + 2 * chunk + t], 0, 0))
-    in_place = pl.BlockSpec(memory_space=pl.ANY)
+    once = lambda a, size: pl.BlockSpec(
+        (size,) + a.shape[1:], lambda t, m, nd=a.ndim: (0,) * nd, pipeline_mode=pl.Buffered(1)
+    )
+    sizes = [a.shape[0] for a in pieces]
+    sizes[4] = sizes[6] = 1
     return pl.pallas_call(
         functools.partial(attend_kernel, chunk),
         grid_spec=pltpu.PrefetchScalarGridSpec(
             num_scalar_prefetch=1,
             grid=(2,),
-            in_specs=[q_spec, q_spec, whole(seg_col), whole(seg_row)] + [in_place] * len(pieces),
+            in_specs=[q_spec, q_spec, whole(seg_row)] + list(map(once, pieces, sizes)),
             out_specs=pl.BlockSpec((RB, 2 * n), lambda t, m: (t, 0)),
             scratch_shapes=[
                 pltpu.VMEM((2, 4, 2, RB, 2 * n), BF),
                 pltpu.VMEM((2 * heads, 5, RB, RB), F32),
                 pltpu.VMEM((2 * heads, RB, HD), F32),
                 pltpu.VMEM((2 * heads, RB, HD), F32),
-                pltpu.SemaphoreType.DMA((11,)),
             ],
         ),
         out_shape=jax.ShapeDtypeStruct((2 * RB, 2 * n), BF),
-        compiler_params=pltpu.CompilerParams(vmem_limit_bytes=56 * MIB),
+        compiler_params=pltpu.CompilerParams(vmem_limit_bytes=32 * MIB),
         cost_estimate=pl.CostEstimate(
             flops=4 * 2 * RB * 768 * 2 * n, bytes_accessed=8 * MIB, transcendentals=2 * RB * 768 * 6
         ),
-    )(meta, q_own, q_other, seg_col, seg_row, *pieces)
+    )(meta, q_own, q_other, seg_row, *pieces)
 
 
 def reorder_kernel(meta, w, out):
@@ -307,81 +303,46 @@
     )(meta, w).reshape(k8 * n, width)
 
 
-def finish_kernel(chunk, blocks, meta, c0, c1, c2a, c2b, c3, w, res, *refs):
-    out, cs, ws, rs, outs, c_sems, w_sems, r_sems, out_sems = refs[-9:]
-    n = cs.shape[2]
-    copy = pltpu.make_async_copy
-    c_copies = [
-        [copy(c0, cs.at[0], c_sems.at[0])],
-        [copy(c1, cs.at[1], c_sems.at[1])],
-        [copy(c3, cs.at[2], c_sems.at[2])],
-        [
-            copy(c2a, cs.at[3, 0:RB], c_sems.at[3]),
-            copy(c2b, cs.at[3, RB : 2 * RB], c_sems.at[4]),
-        ],
-    ]
-    at = (0, 1, 3, 2)
-    w_copies = [
-        copy(w.at[at[j] * n : (at[j] + 1) * n], ws.at[j], w_sems.at[j]) for j in range(4)
-    ]
-    r_copies = [
-        copy(res.at[meta[SLOT + 2 * chunk + t]], rs.at[t * RB : (t + 1) * RB], r_sems.at[t])
-        for t in range(2)
-    ]
-    for j in range(4):
-        for one in (*c_copies[j], w_copies[j]):
-            one.start()
-    for one in r_copies:
-        one.start()
-    total = None
-    for j in range(4):
-        for one in (*c_copies[j], w_copies[j]):
-            one.wait()
-        part = jnp.dot(cs[j], ws[j], preferred_element_type=F32)
-        total = part if total is None else total + part
-    for one in r_copies:
-        one.wait()
-    outs[...] = (rs[...].astype(F32) + total).astype(BF)
-    targets = [t if blocks == 2 else meta[MINE + 2 * chunk + t] for t in range(2)]
-    out_copies = [
-        copy(outs.at[t * RB : (t + 1) * RB], out.at[targets[t]], out_sems.at[t]) for t in range(2)
-    ]
-    for one in out_copies:
-        one.start()
-    for one in out_copies:
-        one.wait()
+def finish_kernel(meta, c0, c1, c2a, c2b, c3, w, res, *refs):
+    out = refs[-1]
+    t = pl.program_id(0)
+    far = jnp.where(t == 0, c2a[...], c2b[...])
+    n = far.shape[1]
+    total = res[0].astype(F32)
+    for j, c in enumerate((c0[...], c1[...], far, c3[...])):
+        total += jnp.dot(c, w[j * n : (j + 1) * n, :], preferred_element_type=F32)
+    out[0] = total.astype(BF)
 
 
 def finish(meta, chunk, parts, w, res, blocks, prior=None):
     depth, width = w.shape
     n = depth // 4
+    tile = pl.BlockSpec((RB, n), lambda t, m: (t, 0))
+    fixed = pl.BlockSpec((RB, n), lambda t, m: (0, 0))
     ins = list(parts) + [w, res]
+    specs = [tile, tile, fixed, fixed, tile]
+    specs.append(pl.BlockSpec(w.shape, lambda t, m: (0, 0), pipeline_mode=pl.Buffered(1)))
+    specs.append(pl.BlockSpec((1, RB, width), lambda t, m: (m[SLOT + 2 * chunk + t], 0, 0)))
     aliases = {}
     if prior is not None:
         aliases[1 + len(ins)] = 0
         ins.append(prior)
-    in_place = pl.BlockSpec(memory_space=pl.ANY)
+        specs.append(pl.BlockSpec(memory_space=pl.ANY))
+    if blocks == 2:
+        target = lambda t, m: (t, 0, 0)
+    else:
+        target = lambda t, m: (m[MINE + 2 * chunk + t], 0, 0)
     return pl.pallas_call(
-        functools.partial(finish_kernel, chunk, blocks),
+        finish_kernel,
         grid_spec=pltpu.PrefetchScalarGridSpec(
             num_scalar_prefetch=1,
-            grid=(1,),
-            in_specs=[in_place] * len(ins),
-            out_specs=in_place,
-            scratch_shapes=[
-                pltpu.VMEM((4, 2 * RB, n), BF),
-                pltpu.VMEM((4, n, width), BF),
-                pltpu.VMEM((2 * RB, width), BF),
-                pltpu.VMEM((2 * RB, width), BF),
-                pltpu.SemaphoreType.DMA((5,)),
-                pltpu.SemaphoreType.DMA((4,)),
-                pltpu.SemaphoreType.DMA((2,)),
-                pltpu.SemaphoreType.DMA((2,)),
-            ],
+            grid=(2,),
+            in_specs=specs,
+            out_specs=pl.BlockSpec((1, RB, width), target),
         ),
         out_shape=jax.ShapeDtypeStruct((blocks, RB, width), BF),
         input_output_aliases=aliases,
-        compiler_params=pltpu.CompilerParams(vmem_limit_bytes=56 * MIB),
+        compiler_params=pltpu.CompilerParams(vmem_limit_bytes=20 * MIB),
         cost_estimate=pl.CostEstimate(
             flops=4 * RB * depth * width, bytes_accessed=8 * MIB, transcendentals=0
         ),
@@ -406,13 +367,13 @@
         grid_spec=pltpu.PrefetchScalarGridSpec(
             num_scalar_prefetch=1,
             grid=(1,),
-            in_specs=[in_place, in_place],
+            in_specs=[pl.BlockSpec(got.shape, lambda t, m: (0, 0, 0)), in_place],
             out_specs=in_place,
             scratch_shapes=[pltpu.SemaphoreType.DMA((2,))],
         ),
         out_shape=jax.ShapeDtypeStruct(prior.shape, BF),
         input_output_aliases={2: 0},
-        compiler_params=pltpu.CompilerParams(vmem_limit_bytes=56 * MIB),
+        compiler_params=pltpu.CompilerParams(vmem_limit_bytes=4 * MIB),
     )(meta, got, prior)
 
 
@@ -441,7 +402,6 @@
     starts = jnp.maximum(starts, jnp.arange(8, dtype=jnp.int32) - 4)
     facts = jnp.array(FACTS, jnp.int32)[core, c]
     meta = jnp.concatenate([facts, starts, (section // 2 % 4)[None]])
-    seg_col = segment_ids.reshape(8, RB, 1)
     seg_row = segment_ids.reshape(8, 1, RB)
 
     def cache(last_hidden, w_key, w_value, w_query, w_out):
@@ -499,8 +459,8 @@
     normed, q_own, res_own, res_other = project(
         meta, [xo_a, xo_b], query_gain, w_q, 2, width, state
     )
-    w_q2b, s1b, s3b, normed, q_own, seg_col, seg_row, w_o_theirs = lax.optimization_barrier(
-        (w_q2b, s1b, s3b, normed, q_own, seg_col, seg_row, w_o_theirs)
+    w_q2b, s1b, s3b, normed, q_own, w_o_theirs = lax.optimization_barrier(
+        (w_q2b, s1b, s3b, normed, q_own, w_o_theirs)
     )
     w_o2 = send(w_o_theirs, PARTNER)
     q_other = more_queries(normed, w_q2a, w_q2b)
@@ -508,7 +468,7 @@
 
     result = None
     for chunk in range(2):
-        own = attend(meta, chunk, q_own, q_other, seg_col, seg_row, pieces)
+        own = attend(meta, chunk, q_own, q_other, seg_row, pieces)
         c_in = send(own, IN)
         c_out = send(own, OUT)
         co_a = send(c_out[:RB], IN)

time: 270 us -> 217 us (0.80)
  Pallas kernels: 140 us -> 72.2 us
  waiting for transfers between devices: 48.4 us -> 70.8 us
  local copies, waits for them, and re-layouts: 22.8 us -> 13.1 us
    pallas_call x2, Pallas kernels: 43 us -> 2.78 us  [place(): pl.pallas_call(functools.partial(place_kernel, chunk), grid_spec=pltpu.Pr...]
    ppermute x28, waiting for transfers between devices: 48.4 us -> 70.8 us  [send(): return lax.ppermute(value, AXES, pairs)]
    pallas_call x4, Pallas kernels: 25.7 us -> 14.9 us  [finish(): pl.pallas_call(finish_kernel, grid_spec=pltpu.PrefetchScalarGridSpec(num_...]
    pallas_call x4, Pallas kernels: 26.4 us -> 18.6 us  [project(): pl.pallas_call(kernel, grid_spec=pltpu.PrefetchScalarGridSpec(num_scalar_...]
    pallas_call x2, Pallas kernels: 20.2 us -> 14.6 us  [attend(): pl.pallas_call(functools.partial(attend_kernel, chunk), grid_spec=pltpu.P...]
    unnamed x30 -> x12, local copies, waits for them, and re-layouts: 3.27 us -> 0.03 us
    pallas_call x1, Pallas kernels: 10.2 us -> 7.17 us  [more_queries(): pl.pallas_call(more_queries_kernel, grid=(2,), in_specs=[pl.BlockSpec((ro...]
  transfers between devices with their start and end apart: 28 -> 28, of which waited for: 10 -> 13; matrix products, arithmetic and copies ran while one was open for 11% -> 11% of each run, Pallas kernels for 44% -> 33%
where the time goes in v5:
time: 217 us; the launch traced here: 216 us
  Pallas kernels  72.2 us (33%)
  waiting for transfers between devices  70.8 us (33%)
  starting transfers between devices  47 us (22%)
  local copies, waits for them, and re-layouts  13.1 us (6%)
  other arithmetic  7.12 us (3%)
  matrix products  4.48 us (2%)
    ppermute x28, waiting for transfers between devices, send(): return lax.ppermute(value, AXES, pairs)  70.8 us
    ppermute x28, starting transfers between devices, send(): return lax.ppermute(value, AXES, pairs)  47 us
    pallas_call x4, Pallas kernels, project(): pl.pallas_call(kernel, grid_spec=pltpu.PrefetchScalarGridSpec(num_scalar_...  18.6 us
    pallas_call x4, Pallas kernels, finish(): pl.pallas_call(finish_kernel, grid_spec=pltpu.PrefetchScalarGridSpec(num_...  14.9 us
    pallas_call x2, Pallas kernels, attend(): pl.pallas_call(functools.partial(attend_kernel, chunk), grid_spec=pltpu.P...  14.6 us
    pallas_call x2, Pallas kernels, reorder(): pl.pallas_call(reorder_kernel, grid_spec=pltpu.PrefetchScalarGridSpec(num...  14.2 us
    pallas_call x1, Pallas kernels, more_queries(): pl.pallas_call(more_queries_kernel, grid=(2,), in_specs=[pl.BlockSpec((ro...  7.17 us
  transfers between devices with their start and end apart: 28, of which 13 were waited for; matrix products, arithmetic and copies ran while one was open for 11% of the time, Pallas kernels for 33%

profile of v5, /device:TPU:1, one launch (start us, length us, event | category | flops | bytes accessed | tf_op | source)
XLA Modules:
  0.0 215.8 jit_solution(17139868140201125919)
XLA Ops:
  0.0 2.1 collective-permute-start.10
  8.1 66.8 %conditional.1 = (bf16[2,256,768]{2,1,0:T(8,128)(2,1)}, bf16[256,768]{1,0:T(8,128)(2,1)}, bf16[256,768]{1,0:T(8,128)(2,1)}, bf16[2,256,768]{2,1,0:T(8,128)(2,1)}...) conditional(s32[]{:T(128)} %bitcast.12, () %tuple.18, ...), branch_computations={%region_1.2_spmd, %region_2.4_spmd} | conditional | flops 1017479296 | bytes 69659760 | solution.py:444
  9.8 3.6 %convolution_convert_fusion = bf16[128,384]{1,0:T(8,128)(2,1)S(1)} fusion(bf16[5120,384]{1,0:T(8,128)(2,1)} %get-tuple-element.139, bf16[128,5120]{1,0:T(8,128)(2,1)} %get-tuple-element.136, f32[5120]{0:T(1024)} %get-tuple-element.137, f32[128]{0:T(128)S(1)} %add_rsqrt_fusion), kind=kOutput, calls=%fused_computation.6 | convolution fusion | flops 505987072 | bytes 5362176 | tf_op jit(solution)/shard_map/cond/branch_1_fun/dot_general | solution.py:410
  14.9 1.9 collective-permute-start
  18.6 15.1 %collective-permute-start.2 = (bf16[2,128,768]{2,1,0:T(8,128)(2,1)S(1)}, bf16[2,128,768]{2,1,0:T(8,128)(2,1)}, u32[]{:S(2)}, u32[]{:S(2)}) collective-permute-start(bf16[2,128,768]{2,1,0:T(8,128)(2,1)S(1)} %collective-permute-done.1), channel_id=1, source_target_pairs={{0,8},{1,9},{2,10},{3,11},{4,12},{5,13},{6,14},{7,15},{8,0},{9,1},... | collective-permute-start | bytes 1179656 | tf_op jit(solution)/shard_map/cond/branch_1_fun/ppermute | solution.py:66
  38.9 2.8 %collective-permute-start.4 = (bf16[256,768]{1,0:T(8,128)(2,1)S(1)}, bf16[256,768]{1,0:T(8,128)(2,1)}, u32[]{:S(2)}, u32[]{:S(2)}) collective-permute-start(bf16[256,768]{1,0:T(8,128)(2,1)S(1)} %fusion.9), channel_id=1, source_target_pairs={{0,32},{1,33},{2,34},{3,35},{4,36},{5,37},{6,38},{7,39},{8,40},{9,... | collective-permute-start | bytes 1179656 | tf_op jit(solution)/shard_map/cond/branch_1_fun/ppermute | solution.py:66
  41.7 2.8 %slice.20 = bf16[2048,384]{1,0:T(8,128)(2,1)} slice(bf16[5120,384]{1,0:T(8,128)(2,1)} %get-tuple-element.29), slice={[0:2048], [0:384]} | slice | bytes 3145728 | tf_op jit(solution)/shard_map/cond/branch_1_fun/slice | solution.py:423
  44.5 7.1 %branch_1_fun.2 = bf16[8,384,640]{2,1,0:T(8,128)(2,1)} custom-call(s32[32]{0:T(128)S(1)} %get-tuple-element.30.meta, bf16[8,384,640]{2,1,0:T(8,128)(2,1)} %bitcast.39), custom_call_target="tpu_custom_call" | custom-call | tf_op jit(solution)/shard_map/cond/branch_1_fun/pallas_call | solution.py:292
  51.5 2.2 collective-permute-start.7
  56.3 7.1 %branch_1_fun.3 = bf16[8,384,640]{2,1,0:T(8,128)(2,1)} custom-call(s32[32]{0:T(128)S(1)} %get-tuple-element.30.meta, bf16[8,384,640]{2,1,0:T(8,128)(2,1)} %bitcast.40), custom_call_target="tpu_custom_call" | custom-call | tf_op jit(solution)/shard_map/cond/branch_1_fun/pallas_call | solution.py:292
  63.5 3.3 %slice.21 = bf16[3072,384]{1,0:T(8,128)(2,1)} slice(bf16[5120,384]{1,0:T(8,128)(2,1)} %get-tuple-element.29), slice={[2048:5120], [0:384]} | slice | bytes 4718592 | tf_op jit(solution)/shard_map/cond/branch_1_fun/slice | solution.py:430
  67.8 2.3 %pad_maximum_fusion = bf16[3,256,768]{2,1,0:T(8,128)(2,1)} fusion(bf16[2,256,768]{2,1,0:T(8,128)(2,1)} %collective-permute-done.3, bf16[1,256,768]{2,1,0:T(8,128)(2,1)S(1)} %constant_dynamic-slice_fusion), kind=kLoop, calls=%fused_computation.5 | loop fusion | flops 589824 | bytes 2359296 | tf_op jit(solution)/shard_map/cond/branch_1_fun/concatenate | solution.py:428
  70.1 4.9 %collective-permute-done.6 = bf16[2,256,768]{2,1,0:T(8,128)(2,1)} collective-permute-done((bf16[2,256,768]{2,1,0:T(8,128)(2,1)}, bf16[2,256,768]{2,1,0:T(8,128)(2,1)}, u32[]{:S(2)}, u32[]{:S(2)}) %collective-permute-start.6) | collective-permute-done | bytes 786464 | tf_op jit(solution)/shard_map/cond/branch_1_fun/ppermute | solution.py:66
  81.2 5.8 %shard_map.105 = (bf16[4,256,5120]{2,1,0:T(8,128)(2,1)S(1)}, bf16[4,256,384]{2,1,0:T(8,128)(2,1)S(1)}, bf16[4,256,640]{2,1,0:T(8,128)(2,1)S(1)}, bf16[4,256,640]{2,1,0:T(8,128)(2,1)S(1)}) custom-call(s32[32]{0:T(128)S(1)} %pad_add_fusion.meta, bf16[256,5120]{1,0:T(8,128)(2,1)S(1)} %bitcast.30, f32[1,5120]{1,0:T(1,128)S(1)} %copy-done.1, ...), custom_call_target="tpu_custom_call" | custom-call | flops 1006632960 | bytes 11796480 | tf_op jit(solution)/shard_map/pallas_call | solution.py:119
  87.1 5.4 %shard_map.106 = (bf16[4,256,5120]{2,1,0:T(8,128)(2,1)S(1)}, bf16[4,256,384]{2,1,0:T(8,128)(2,1)S(1)}, bf16[4,256,640]{2,1,0:T(8,128)(2,1)S(1)}, bf16[4,256,640]{2,1,0:T(8,128)(2,1)S(1)}) custom-call(s32[32]{0:T(128)S(1)} %pad_add_fusion.meta, ...), custom_call_target="tpu_custom_call", output_to_operand_aliasing={{0}: (4, {}), {1}: (5, {}), {2}: (6, {}), {3}: (7, {})} | custom-call | flops 1006632960 | bytes 11796480 | tf_op jit(solution)/shard_map/pallas_call | solution.py:119
  92.5 3.7 %shard_map.107 = (bf16[4,256,5120]{2,1,0:T(8,128)(2,1)S(1)}, bf16[4,256,384]{2,1,0:T(8,128)(2,1)S(1)}, bf16[4,256,640]{2,1,0:T(8,128)(2,1)S(1)}, bf16[4,256,640]{2,1,0:T(8,128)(2,1)S(1)}) custom-call(s32[32]{0:T(128)S(1)} %pad_add_fusion.meta, ...), custom_call_target="tpu_custom_call", output_to_operand_aliasing={{0}: (4, {}), {1}: (5, {}), {2}: (6, {}), {3}: (7, {})} | custom-call | flops 1006632960 | bytes 11796480 | tf_op jit(solution)/shard_map/pallas_call | solution.py:119
  96.2 9.4 %collective-permute-done.13.s1 = bf16[3,256,768]{2,1,0:T(8,128)(2,1)S(1)} collective-permute-done((bf16[3,256,768]{2,1,0:T(8,128)(2,1)}, bf16[3,256,768]{2,1,0:T(8,128)(2,1)S(1)}, u32[]{:S(2)}, u32[]{:S(2)}) %collective-permute-start.13) | collective-permute-done | bytes 1179680 | tf_op jit(solution)/shard_map/ppermute | solution.py:66
  105.6 4.7 %collective-permute-start.15 = (bf16[3,256,768]{2,1,0:T(8,128)(2,1)S(1)}, bf16[3,256,768]{2,1,0:T(8,128)(2,1)S(1)}, u32[]{:S(2)}, u32[]{:S(2)}) collective-permute-start(bf16[3,256,768]{2,1,0:T(8,128)(2,1)S(1)} %collective-permute-done.13.s1), channel_id=1, source_target_pairs={{0,8},{1,9},{2,10},{3,11},{4,12},{5,13},{6,14},{7,15},{8,0},{9,1},... | collective-permute-start | bytes 3538952 | tf_op jit(solution)/shard_map/ppermute | solution.py:66
  110.4 3.7 %shard_map.108 = (bf16[4,256,5120]{2,1,0:T(8,128)(2,1)S(1)}, bf16[4,256,384]{2,1,0:T(8,128)(2,1)S(1)}, bf16[4,256,640]{2,1,0:T(8,128)(2,1)S(1)}, bf16[4,256,640]{2,1,0:T(8,128)(2,1)S(1)}) custom-call(s32[32]{0:T(128)S(1)} %pad_add_fusion.meta, ...), custom_call_target="tpu_custom_call", output_to_operand_aliasing={{0}: (5, {}), {1}: (6, {}), {2}: (7, {}), {3}: (8, {})} | custom-call | flops 1006632960 | bytes 11796480 | tf_op jit(solution)/shard_map/pallas_call | solution.py:119
  114.1 7.8 %collective-permute-done.8.wb_ref = bf16[3072,384]{1,0:T(8,128)(2,1)S(1)} collective-permute-done((bf16[3072,384]{1,0:T(8,128)(2,1)S(1)}, bf16[3072,384]{1,0:T(8,128)(2,1)S(1)}, u32[]{:S(2)}, u32[]{:S(2)}) %collective-permute-start.8) | collective-permute-done | bytes 2359328 | tf_op jit(solution)/shard_map/ppermute | solution.py:66
  122.1 7.2 %shard_map.109 = bf16[1024,384]{1,0:T(8,128)(2,1)S(1)} custom-call(bf16[1024,5120]{1,0:T(8,128)(2,1)S(1)} %bitcast.25, bf16[2048,384]{1,0:T(8,128)(2,1)} %get-tuple-element.111.wa_ref, bf16[3072,384]{1,0:T(8,128)(2,1)S(1)} %collective-permute-done.8.wb_ref), custom_call_target="tpu_custom_call" | custom-call | flops 4026531840 | bytes 14417920 | tf_op jit(solution)/shard_map/pallas_call | solution.py:146
  129.3 7.3 %shard_map.112.c0 = bf16[512,768]{1,0:T(8,128)(2,1)S(1)} custom-call(s32[32]{0:T(128)S(1)} %pad_add_fusion.meta, bf16[4,256,384]{2,1,0:T(8,128)(2,1)S(1)} %get-tuple-element.109.q_own, bf16[4,256,384]{2,1,0:T(8,128)(2,1)S(1)} %bitcast.26, s32[8,1,256]{2,1,0:T(1,128)S(1)} %bitcast.31, bf16[2,256,768]{2,1,0:T(8,128)(2,1)} %get-tuple-element.113.own0, ...), custom_call_target="tpu_custom_call" | custom-call | flops 1207959552 | bytes 8388608 | tf_op jit(solution)/shard_map/pallas_call | solution.py:264
  137.3 7.3 %shard_map.110.c0 = bf16[512,768]{1,0:T(8,128)(2,1)S(1)} custom-call(s32[32]{0:T(128)S(1)} %pad_add_fusion.meta, bf16[4,256,384]{2,1,0:T(8,128)(2,1)S(1)} %get-tuple-element.109.q_own, bf16[4,256,384]{2,1,0:T(8,128)(2,1)S(1)} %bitcast.27, s32[8,1,256]{2,1,0:T(1,128)S(1)} %bitcast.32, bf16[2,256,768]{2,1,0:T(8,128)(2,1)} %get-tuple-element.113.own0, ...), custom_call_target="tpu_custom_call" | custom-call | flops 1207959552 | bytes 8388608 | tf_op jit(solution)/shard_map/pallas_call | solution.py:264
  146.9 9.3 %collective-permute-done.24.c3 = bf16[512,768]{1,0:T(8,128)(2,1)S(1)} collective-permute-done((bf16[512,768]{1,0:T(8,128)(2,1)S(1)}, bf16[512,768]{1,0:T(8,128)(2,1)S(1)}, u32[]{:S(2)}, u32[]{:S(2)}) %collective-permute-start.24) | collective-permute-done | bytes 786464 | tf_op jit(solution)/shard_map/ppermute | solution.py:66
  157.7 15.4 %collective-permute-done.18.c3 = bf16[512,768]{1,0:T(8,128)(2,1)S(1)} collective-permute-done((bf16[512,768]{1,0:T(8,128)(2,1)S(1)}, bf16[512,768]{1,0:T(8,128)(2,1)S(1)}, u32[]{:S(2)}, u32[]{:S(2)}) %collective-permute-start.18) | collective-permute-done | bytes 786464 | tf_op jit(solution)/shard_map/ppermute | solution.py:66
  174.6 7.5 %collective-permute-done.25.c2a = bf16[256,768]{1,0:T(8,128)(2,1)S(1)} collective-permute-done((bf16[256,768]{1,0:T(8,128)(2,1)S(1)}, bf16[256,768]{1,0:T(8,128)(2,1)S(1)}, u32[]{:S(2)}, u32[]{:S(2)}) %collective-permute-start.25) | collective-permute-done | bytes 393248 | tf_op jit(solution)/shard_map/ppermute | solution.py:66
  182.1 11.0 %collective-permute-done.21.w = bf16[3072,640]{1,0:T(8,128)(2,1)S(1)} collective-permute-done((bf16[3072,640]{1,0:T(8,128)(2,1)}, bf16[3072,640]{1,0:T(8,128)(2,1)S(1)}, u32[]{:S(2)}, u32[]{:S(2)}) %collective-permute-start.21) | collective-permute-done | bytes 3932192 | tf_op jit(solution)/shard_map/ppermute | solution.py:66
  193.1 3.4 %shard_map.113 = bf16[2,256,640]{2,1,0:T(8,128)(2,1)S(1)} custom-call(s32[32]{0:T(128)S(1)} %pad_add_fusion.meta, bf16[512,768]{1,0:T(8,128)(2,1)S(1)} %shard_map.112.c0, bf16[512,768]{1,0:T(8,128)(2,1)S(1)} %collective-permute-done.23.c1, bf16[256,768]{1,0:T(8,128)(2,1)S(1)} %collective-permute-done.25.c2a, ...), custom_call_target="tpu_custom_call" | custom-call | flops 2013265920 | bytes 8388608 | tf_op jit(solution)/shard_map/pallas_call | solution.py:335
  196.8 3.4 %shard_map.111 = bf16[2,256,640]{2,1,0:T(8,128)(2,1)S(1)} custom-call(s32[32]{0:T(128)S(1)} %pad_add_fusion.meta, bf16[512,768]{1,0:T(8,128)(2,1)S(1)} %shard_map.110.c0, bf16[512,768]{1,0:T(8,128)(2,1)S(1)} %collective-permute-done.17.c1, bf16[256,768]{1,0:T(8,128)(2,1)S(1)} %collective-permute-done.19.c2a, ...), custom_call_target="tpu_custom_call" | custom-call | flops 2013265920 | bytes 8388608 | tf_op jit(solution)/shard_map/pallas_call | solution.py:335
  200.2 2.5 %collective-permute-start.22 = (bf16[2,256,640]{2,1,0:T(8,128)(2,1)S(1)}, bf16[2,256,640]{2,1,0:T(8,128)(2,1)S(1)}, u32[]{:S(2)}, u32[]{:S(2)}) collective-permute-start(bf16[2,256,640]{2,1,0:T(8,128)(2,1)S(1)} %shard_map.111), channel_id=1, source_target_pairs={{0,4},{1,5},{2,6},{3,7},{4,0},{5,1},{6,2},{7,3},{8,11},{9,10},{10,... | collective-permute-start | bytes 1966088 | tf_op jit(solution)/shard_map/ppermute | solution.py:66
  202.7 4.1 %shard_map.114.prior = bf16[8,256,640]{2,1,0:T(8,128)(2,1)} custom-call(s32[32]{0:T(128)S(1)} %pad_add_fusion.meta, bf16[512,768]{1,0:T(8,128)(2,1)S(1)} %shard_map.112.c0, bf16[512,768]{1,0:T(8,128)(2,1)S(1)} %collective-permute-done.23.c1, bf16[256,768]{1,0:T(8,128)(2,1)S(1)} %collective-permute-done.25.c2a, ...), custom_call_target="tpu_custom_call" | custom-call | flops 2013265920 | bytes 8388608 | tf_op jit(solution)/shard_map/pallas_call | solution.py:335
  208.6 4.1 %shard_map.116.prior = bf16[8,256,640]{2,1,0:T(8,128)(2,1)} custom-call(s32[32]{0:T(128)S(1)} %pad_add_fusion.meta, bf16[512,768]{1,0:T(8,128)(2,1)S(1)} %shard_map.110.c0, bf16[512,768]{1,0:T(8,128)(2,1)S(1)} %collective-permute-done.17.c1, bf16[256,768]{1,0:T(8,128)(2,1)S(1)} %collective-permute-done.19.c2a, ...), custom_call_target="tpu_custom_call", output_to_operand_aliasing={{}: (8, {})} | custom-call | flops 2013265920 | bytes 8388608 | tf_op jit(solution)/shard_map/pallas_call | solution.py:335
  (85 shorter events, 36.6 us)
Async XLA Ops:
  0.0 75.0 %collective-permute-start.10 = (bf16[256,5120]{1,0:T(8,128)(2,1)}, bf16[256,5120]{1,0:T(8,128)(2,1)S(1)}, u32[]{:S(2)}, u32[]{:S(2)}) collective-permute-start(bf16[256,5120]{1,0:T(8,128)(2,1)} %bitcast.28), channel_id=1, source_target_pairs={{0,3},{1,2},{2,1},{3,0},{4,7},{5,6},{6,5},{7,4},{8,12},{9,13},{10,... | collective-permute-start | bytes 7864328 | tf_op jit(solution)/shard_map/ppermute | solution.py:66
  2.1 72.9 %collective-permute-start.9 = (bf16[256,5120]{1,0:T(8,128)(2,1)}, bf16[256,5120]{1,0:T(8,128)(2,1)}, u32[]{:S(2)}, u32[]{:S(2)}) collective-permute-start(bf16[256,5120]{1,0:T(8,128)(2,1)} %bitcast.29), channel_id=1, source_target_pairs={{0,1},{1,0},{2,3},{3,2},{4,5},{5,4},{6,7},{7,6},{8,9},{9,8},{10,11... | collective-permute-start | bytes 7864328 | tf_op jit(solution)/shard_map/ppermute | solution.py:66
  14.9 2.9 %collective-permute-start = (bf16[128,768]{1,0:T(8,128)(2,1)S(1)}, bf16[128,768]{1,0:T(8,128)(2,1)S(1)}, u32[]{:S(2)}, u32[]{:S(2)}) collective-permute-start(bf16[128,768]{1,0:T(8,128)(2,1)S(1)} %get-tuple-element.156), channel_id=1, source_target_pairs={{0,8},{1,9},{2,10},{3,11},{4,12},{5,13},{6,14},{7,15},{8,0},{9,1},... | collective-permute-start | bytes 589832 | tf_op jit(solution)/shard_map/cond/branch_1_fun/ppermute | solution.py:66
  17.8 0.7 collective-permute-start.1
  18.6 16.6 %collective-permute-start.2 = (bf16[2,128,768]{2,1,0:T(8,128)(2,1)S(1)}, bf16[2,128,768]{2,1,0:T(8,128)(2,1)}, u32[]{:S(2)}, u32[]{:S(2)}) collective-permute-start(bf16[2,128,768]{2,1,0:T(8,128)(2,1)S(1)} %collective-permute-done.1), channel_id=1, source_target_pairs={{0,8},{1,9},{2,10},{3,11},{4,12},{5,13},{6,14},{7,15},{8,0},{9,1},... | collective-permute-start | bytes 1179656 | tf_op jit(solution)/shard_map/cond/branch_1_fun/ppermute | solution.py:66
  37.2 14.3 %collective-permute-start.3 = (bf16[2,256,768]{2,1,0:T(8,128)(2,1)}, bf16[2,256,768]{2,1,0:T(8,128)(2,1)}, u32[]{:S(2)}, u32[]{:S(2)}) collective-permute-start(bf16[2,256,768]{2,1,0:T(8,128)(2,1)} %maximum_select_fusion), channel_id=1, source_target_pairs={{0,4},{1,5},{2,6},{3,7},{4,0},{5,1},{6,2},{7,3},{8,11},{9,10},{10,... | collective-permute-start | bytes 2359304 | tf_op jit(solution)/shard_map/cond/branch_1_fun/ppermute | solution.py:66
  38.9 12.6 %collective-permute-start.4 = (bf16[256,768]{1,0:T(8,128)(2,1)S(1)}, bf16[256,768]{1,0:T(8,128)(2,1)}, u32[]{:S(2)}, u32[]{:S(2)}) collective-permute-start(bf16[256,768]{1,0:T(8,128)(2,1)S(1)} %fusion.9), channel_id=1, source_target_pairs={{0,32},{1,33},{2,34},{3,35},{4,36},{5,37},{6,38},{7,39},{8,40},{9,... | collective-permute-start | bytes 1179656 | tf_op jit(solution)/shard_map/cond/branch_1_fun/ppermute | solution.py:66
  51.5 23.4 %collective-permute-start.7 = (bf16[2048,384]{1,0:T(8,128)(2,1)}, bf16[2048,384]{1,0:T(8,128)(2,1)}, u32[]{:S(2)}, u32[]{:S(2)}) collective-permute-start(bf16[2048,384]{1,0:T(8,128)(2,1)} %slice.20), channel_id=1, source_target_pairs={{0,4},{1,5},{2,6},{3,7},{4,0},{5,1},{6,2},{7,3},{8,11},{9,10},{10,... | collective-permute-start | bytes 4718600 | tf_op jit(solution)/shard_map/cond/branch_1_fun/ppermute | solution.py:66
  53.7 21.3 %collective-permute-start.6 = (bf16[2,256,768]{2,1,0:T(8,128)(2,1)}, bf16[2,256,768]{2,1,0:T(8,128)(2,1)}, u32[]{:S(2)}, u32[]{:S(2)}) collective-permute-start(bf16[2,256,768]{2,1,0:T(8,128)(2,1)} %collective-permute-done.3), channel_id=1, source_target_pairs={{0,32},{1,33},{2,34},{3,35},{4,36},{5,37},{6,38},{7,39},{8,40},{9,... | collective-permute-start | bytes 2359304 | tf_op jit(solution)/shard_map/cond/branch_1_fun/ppermute | solution.py:66
  55.2 14.9 %collective-permute-start.5 = (bf16[256,768]{1,0:T(8,128)(2,1)}, bf16[256,768]{1,0:T(8,128)(2,1)}, u32[]{:S(2)}, u32[]{:S(2)}) collective-permute-start(bf16[256,768]{1,0:T(8,128)(2,1)} %collective-permute-done.4), channel_id=1, source_target_pairs={{0,8},{1,9},{2,10},{3,11},{4,12},{5,13},{6,14},{7,15},{8,0},{9,1},... | collective-permute-start | bytes 1179656 | tf_op jit(solution)/shard_map/cond/branch_1_fun/ppermute | solution.py:66
  75.0 6.3 %copy-start = (bf16[1,256,5120]{2,1,0:T(8,128)(2,1)S(1)}, bf16[1,256,5120]{2,1,0:T(8,128)(2,1)}, u32[]{:S(2)}) copy-start(bf16[1,256,5120]{2,1,0:T(8,128)(2,1)} %param.12) | copy-start | bytes 7864324
  75.0 6.2 %copy-start.1 = (f32[1,5120]{1,0:T(1,128)S(1)}, f32[1,5120]{1,0:T(1,128)}, u32[]{:S(2)}) copy-start(f32[1,5120]{1,0:T(1,128)} %refs_2_.1) | copy-start | bytes 61444
  75.1 30.5 %collective-permute-start.11 = (bf16[128,5120]{1,0:T(8,128)(2,1)S(1)}, bf16[128,5120]{1,0:T(8,128)(2,1)S(1)}, u32[]{:S(2)}, u32[]{:S(2)}) collective-permute-start(bf16[128,5120]{1,0:T(8,128)(2,1)S(1)} %slice.32), channel_id=1, source_target_pairs={{0,1},{1,0},{2,3},{3,2},{4,5},{5,4},{6,7},{7,6},{8,9},{9,8},{10,11... | collective-permute-start | bytes 3932168 | tf_op jit(solution)/shard_map/ppermute | solution.py:66
  76.8 28.9 %collective-permute-start.12 = (bf16[128,5120]{1,0:T(8,128)(2,1)S(1)}, bf16[128,5120]{1,0:T(8,128)(2,1)S(1)}, u32[]{:S(2)}, u32[]{:S(2)}) collective-permute-start(bf16[128,5120]{1,0:T(8,128)(2,1)S(1)} %slice.33), channel_id=1, source_target_pairs={{0,3},{1,2},{2,1},{3,0},{4,7},{5,6},{6,5},{7,4},{8,12},{9,13},{10,... | collective-permute-start | bytes 3932168 | tf_op jit(solution)/shard_map/ppermute | solution.py:66
  78.4 27.2 %collective-permute-start.13 = (bf16[3,256,768]{2,1,0:T(8,128)(2,1)}, bf16[3,256,768]{2,1,0:T(8,128)(2,1)S(1)}, u32[]{:S(2)}, u32[]{:S(2)}) collective-permute-start(bf16[3,256,768]{2,1,0:T(8,128)(2,1)} %get-tuple-element.84), channel_id=1, source_target_pairs={{0,48},{1,49},{2,50},{3,51},{4,52},{5,53},{6,54},{7,55},{8,56},{9,... | collective-permute-start | bytes 3538952 | tf_op jit(solution)/shard_map/ppermute | solution.py:66
  78.4 27.2 %collective-permute-start.14 = (bf16[3,256,768]{2,1,0:T(8,128)(2,1)}, bf16[3,256,768]{2,1,0:T(8,128)(2,1)S(1)}, u32[]{:S(2)}, u32[]{:S(2)}) collective-permute-start(bf16[3,256,768]{2,1,0:T(8,128)(2,1)} %get-tuple-element.84), channel_id=1, source_target_pairs={{0,16},{1,17},{2,18},{3,19},{4,20},{5,21},{6,22},{7,23},{8,24},{9,... | collective-permute-start | bytes 3538952 | tf_op jit(solution)/shard_map/ppermute | solution.py:66
  79.9 7.2 %copy-start.3 = (bf16[1,5120,384]{2,1,0:T(8,128)(2,1)S(1)}, bf16[1,5120,384]{2,1,0:T(8,128)(2,1)}, u32[]{:S(2)}) copy-start(bf16[1,5120,384]{2,1,0:T(8,128)(2,1)} %param.18) | copy-start | bytes 11796484
  79.9 42.0 %collective-permute-start.8 = (bf16[3072,384]{1,0:T(8,128)(2,1)S(1)}, bf16[3072,384]{1,0:T(8,128)(2,1)S(1)}, u32[]{:S(2)}, u32[]{:S(2)}) collective-permute-start(bf16[3072,384]{1,0:T(8,128)(2,1)S(1)} %copy-done.5), channel_id=1, source_target_pairs={{0,4},{1,5},{2,6},{3,7},{4,0},{5,1},{6,2},{7,3},{8,11},{9,10},{10,... | collective-permute-start | bytes 7077896 | tf_op jit(solution)/shard_map/ppermute | solution.py:66
  105.6 16.3 %collective-permute-start.15 = (bf16[3,256,768]{2,1,0:T(8,128)(2,1)S(1)}, bf16[3,256,768]{2,1,0:T(8,128)(2,1)S(1)}, u32[]{:S(2)}, u32[]{:S(2)}) collective-permute-start(bf16[3,256,768]{2,1,0:T(8,128)(2,1)S(1)} %collective-permute-done.13.s1), channel_id=1, source_target_pairs={{0,8},{1,9},{2,10},{3,11},{4,12},{5,13},{6,14},{7,15},{8,0},{9,1},... | collective-permute-start | bytes 3538952 | tf_op jit(solution)/shard_map/ppermute | solution.py:66
  110.4 11.5 %collective-permute-start.16 = (bf16[3,256,768]{2,1,0:T(8,128)(2,1)S(1)}, bf16[3,256,768]{2,1,0:T(8,128)(2,1)S(1)}, u32[]{:S(2)}, u32[]{:S(2)}) collective-permute-start(bf16[3,256,768]{2,1,0:T(8,128)(2,1)S(1)} %collective-permute-done.14.s3), channel_id=1, source_target_pairs={{0,8},{1,9},{2,10},{3,11},{4,12},{5,13},{6,14},{7,15},{8,0},{9,1},... | collective-permute-start | bytes 3538952 | tf_op jit(solution)/shard_map/ppermute | solution.py:66
  121.9 71.2 %collective-permute-start.21 = (bf16[3072,640]{1,0:T(8,128)(2,1)}, bf16[3072,640]{1,0:T(8,128)(2,1)S(1)}, u32[]{:S(2)}, u32[]{:S(2)}) collective-permute-start(bf16[3072,640]{1,0:T(8,128)(2,1)} %get-tuple-element.120), channel_id=1, source_target_pairs={{0,4},{1,5},{2,6},{3,7},{4,0},{5,1},{6,2},{7,3},{8,11},{9,10},{10,... | collective-permute-start | bytes 11796488 | tf_op jit(solution)/shard_map/ppermute | solution.py:66
  122.1 7.2 %copy-start.2 = (s32[2048]{0:T(1024)S(1)}, s32[2048]{0:T(1024)}, u32[]{:S(2)}) copy-start(s32[2048]{0:T(1024)} %param.20) | copy-start | bytes 24580
  136.6 19.7 %collective-permute-start.24 = (bf16[512,768]{1,0:T(8,128)(2,1)S(1)}, bf16[512,768]{1,0:T(8,128)(2,1)S(1)}, u32[]{:S(2)}, u32[]{:S(2)}) collective-permute-start(bf16[512,768]{1,0:T(8,128)(2,1)S(1)} %shard_map.112.c0), channel_id=1, source_target_pairs={{0,3},{1,2},{2,1},{3,0},{4,7},{5,6},{6,5},{7,4},{8,12},{9,13},{10,... | collective-permute-start | bytes 2359304 | tf_op jit(solution)/shard_map/ppermute | solution.py:66
  137.3 19.5 %collective-permute-start.23 = (bf16[512,768]{1,0:T(8,128)(2,1)S(1)}, bf16[512,768]{1,0:T(8,128)(2,1)S(1)}, u32[]{:S(2)}, u32[]{:S(2)}) collective-permute-start(bf16[512,768]{1,0:T(8,128)(2,1)S(1)} %shard_map.112.c0), channel_id=1, source_target_pairs={{0,1},{1,0},{2,3},{3,2},{4,5},{5,4},{6,7},{7,6},{8,9},{9,8},{10,11... | collective-permute-start | bytes 2359304 | tf_op jit(solution)/shard_map/ppermute | solution.py:66
  144.6 28.5 %collective-permute-start.18 = (bf16[512,768]{1,0:T(8,128)(2,1)S(1)}, bf16[512,768]{1,0:T(8,128)(2,1)S(1)}, u32[]{:S(2)}, u32[]{:S(2)}) collective-permute-start(bf16[512,768]{1,0:T(8,128)(2,1)S(1)} %shard_map.110.c0), channel_id=1, source_target_pairs={{0,3},{1,2},{2,1},{3,0},{4,7},{5,6},{6,5},{7,4},{8,12},{9,13},{10,... | collective-permute-start | bytes 2359304 | tf_op jit(solution)/shard_map/ppermute | solution.py:66
  145.5 28.2 %collective-permute-start.17 = (bf16[512,768]{1,0:T(8,128)(2,1)S(1)}, bf16[512,768]{1,0:T(8,128)(2,1)S(1)}, u32[]{:S(2)}, u32[]{:S(2)}) collective-permute-start(bf16[512,768]{1,0:T(8,128)(2,1)S(1)} %shard_map.110.c0), channel_id=1, source_target_pairs={{0,1},{1,0},{2,3},{3,2},{4,5},{5,4},{6,7},{7,6},{8,9},{9,8},{10,11... | collective-permute-start | bytes 2359304 | tf_op jit(solution)/shard_map/ppermute | solution.py:66
  156.3 25.8 %collective-permute-start.25 = (bf16[256,768]{1,0:T(8,128)(2,1)S(1)}, bf16[256,768]{1,0:T(8,128)(2,1)S(1)}, u32[]{:S(2)}, u32[]{:S(2)}) collective-permute-start(bf16[256,768]{1,0:T(8,128)(2,1)S(1)} %slice.41), channel_id=1, source_target_pairs={{0,1},{1,0},{2,3},{3,2},{4,5},{5,4},{6,7},{7,6},{8,9},{9,8},{10,11... | collective-permute-start | bytes 1179656 | tf_op jit(solution)/shard_map/ppermute | solution.py:66
  156.9 25.3 %collective-permute-start.26 = (bf16[256,768]{1,0:T(8,128)(2,1)S(1)}, bf16[256,768]{1,0:T(8,128)(2,1)S(1)}, u32[]{:S(2)}, u32[]{:S(2)}) collective-permute-start(bf16[256,768]{1,0:T(8,128)(2,1)S(1)} %slice.42), channel_id=1, source_target_pairs={{0,3},{1,2},{2,1},{3,0},{4,7},{5,6},{6,5},{7,4},{8,12},{9,13},{10,... | collective-permute-start | bytes 1179656 | tf_op jit(solution)/shard_map/ppermute | solution.py:66
  173.2 23.6 %collective-permute-start.19 = (bf16[256,768]{1,0:T(8,128)(2,1)S(1)}, bf16[256,768]{1,0:T(8,128)(2,1)S(1)}, u32[]{:S(2)}, u32[]{:S(2)}) collective-permute-start(bf16[256,768]{1,0:T(8,128)(2,1)S(1)} %slice.39), channel_id=1, source_target_pairs={{0,1},{1,0},{2,3},{3,2},{4,5},{5,4},{6,7},{7,6},{8,9},{9,8},{10,11... | collective-permute-start | bytes 1179656 | tf_op jit(solution)/shard_map/ppermute | solution.py:66
  173.7 23.1 %collective-permute-start.20 = (bf16[256,768]{1,0:T(8,128)(2,1)S(1)}, bf16[256,768]{1,0:T(8,128)(2,1)S(1)}, u32[]{:S(2)}, u32[]{:S(2)}) collective-permute-start(bf16[256,768]{1,0:T(8,128)(2,1)S(1)} %slice.40), channel_id=1, source_target_pairs={{0,3},{1,2},{2,1},{3,0},{4,7},{5,6},{6,5},{7,4},{8,12},{9,13},{10,... | collective-permute-start | bytes 1179656 | tf_op jit(solution)/shard_map/ppermute | solution.py:66
  196.5 10.7 %collective-permute-start.27 = (bf16[2,256,640]{2,1,0:T(8,128)(2,1)S(1)}, bf16[2,256,640]{2,1,0:T(8,128)(2,1)S(1)}, u32[]{:S(2)}, u32[]{:S(2)}) collective-permute-start(bf16[2,256,640]{2,1,0:T(8,128)(2,1)S(1)} %shard_map.113), channel_id=1, source_target_pairs={{0,4},{1,5},{2,6},{3,7},{4,0},{5,1},{6,2},{7,3},{8,11},{9,10},{10,... | collective-permute-start | bytes 1966088 | tf_op jit(solution)/shard_map/ppermute | solution.py:66
  200.2 14.1 %collective-permute-start.22 = (bf16[2,256,640]{2,1,0:T(8,128)(2,1)S(1)}, bf16[2,256,640]{2,1,0:T(8,128)(2,1)S(1)}, u32[]{:S(2)}, u32[]{:S(2)}) collective-permute-start(bf16[2,256,640]{2,1,0:T(8,128)(2,1)S(1)} %shard_map.111), channel_id=1, source_target_pairs={{0,4},{1,5},{2,6},{3,7},{4,0},{5,1},{6,2},{7,3},{8,11},{9,10},{10,... | collective-permute-start | bytes 1966088 | tf_op jit(solution)/shard_map/ppermute | solution.py:66
  (5 other events, 22.9 us)

commit v6 on v5

--- a/solution.py
+++ b/solution.py
@@ -133,23 +133,19 @@
     )(meta, *ins)
 
 
-def more_queries_kernel(n_ref, wa_ref, wb_ref, q_ref):
-    k = wa_ref.shape[0]
-    q = jnp.dot(n_ref[:, :k], wa_ref[...], preferred_element_type=F32)
-    q += jnp.dot(n_ref[:, k:], wb_ref[...], preferred_element_type=F32)
-    q_ref[...] = q.astype(BF)
-
-
-def more_queries(normed, wa, wb):
-    d, n = normed.shape[2], wa.shape[1]
+def more_queries_kernel(n_ref, w_ref, q_ref):
+    q_ref[...] = jnp.dot(n_ref[...], w_ref[...], preferred_element_type=F32).astype(BF)
+
+
+def more_queries(normed, w):
+    d, n = w.shape
     rows = 2 * RB
     return pl.pallas_call(
         more_queries_kernel,
         grid=(2,),
         in_specs=[
             pl.BlockSpec((rows, d), lambda i: (i, 0)),
-            pl.BlockSpec(wa.shape, lambda i: (0, 0), pipeline_mode=pl.Buffered(1)),
-            pl.BlockSpec(wb.shape, lambda i: (0, 0), pipeline_mode=pl.Buffered(1)),
+            pl.BlockSpec(w.shape, lambda i: (0, 0), pipeline_mode=pl.Buffered(1)),
         ],
         out_specs=pl.BlockSpec((rows, n), lambda i: (i, 0)),
         out_shape=jax.ShapeDtypeStruct((4 * RB, n), BF),
@@ -157,11 +153,12 @@
         cost_estimate=pl.CostEstimate(
             flops=8 * RB * d * n, bytes_accessed=2 * (4 * RB * d + d * n), transcendentals=0
         ),
-    )(normed.reshape(4 * RB, d), wa, wb).reshape(4, RB, n)
+    )(normed.reshape(4 * RB, d), w).reshape(4, RB, n)
 
 
 def attend_kernel(
-    chunk, meta, q_own, q_other, seg_row, own0, o2, o2b, s1, s1b, s3, s3b, other0, t2,
+    chunk, meta, q_own, q_other, seg_row, own0, o1, o1b, o2, o2b, o3, o3b,
+    other0, t1, t2, t3,
     out, kv, scores, tops, sums,
 ):
     t = pl.program_id(0)
@@ -170,16 +167,16 @@
     @pl.when(t == 0)
     def _():
         kv[0, 0] = own0[...]
-        kv[0, 1, core] = s1[0]
-        kv[0, 1, 1 - core] = s1b[0]
+        kv[0, 1, core] = o1[...]
+        kv[0, 1, 1 - core] = o1b[...]
         kv[0, 2, core] = o2[...]
         kv[0, 2, 1 - core] = o2b[...]
-        kv[0, 3, core] = s3[0]
-        kv[0, 3, 1 - core] = s3b[0]
+        kv[0, 3, core] = o3[...]
+        kv[0, 3, 1 - core] = o3b[...]
         kv[1, 0] = other0[...]
-        kv[1, 1] = s1[1:3]
+        kv[1, 1] = t1[...]
         kv[1, 2] = t2[...]
-        kv[1, 3] = s3[1:3]
+        kv[1, 3] = t3[...]
 
     block = meta[MINE + 2 * chunk + t]
     first = meta[FIRST + block]
@@ -256,17 +253,15 @@
     heads = n // HD
     whole = lambda a: pl.BlockSpec(a.shape, lambda t, m, nd=a.ndim: (0,) * nd)
     q_spec = pl.BlockSpec((1, RB, n), lambda t, m: (m[SLOT + 2 * chunk + t], 0, 0))
-    once = lambda a, size: pl.BlockSpec(
-        (size,) + a.shape[1:], lambda t, m, nd=a.ndim: (0,) * nd, pipeline_mode=pl.Buffered(1)
-    )
-    sizes = [a.shape[0] for a in pieces]
-    sizes[4] = sizes[6] = 1
+    once = lambda a: pl.BlockSpec(
+        a.shape, lambda t, m, nd=a.ndim: (0,) * nd, pipeline_mode=pl.Buffered(1)
+    )
     return pl.pallas_call(
         functools.partial(attend_kernel, chunk),
         grid_spec=pltpu.PrefetchScalarGridSpec(
             num_scalar_prefetch=1,
             grid=(2,),
-            in_specs=[q_spec, q_spec, whole(seg_row)] + list(map(once, pieces, sizes)),
+            in_specs=[q_spec, q_spec, whole(seg_row)] + list(map(once, pieces)),
             out_specs=pl.BlockSpec((RB, 2 * n), lambda t, m: (t, 0)),
             scratch_shapes=[
                 pltpu.VMEM((2, 4, 2, RB, 2 * n), BF),
@@ -395,7 +390,6 @@
 
     x_in = send(x0, IN)
     x_out = send(x0, OUT)
-    cut = w_q.shape[0] * 2 // 5
 
     ids = segment_ids.reshape(8, RB)
     starts = jnp.sum(segment_ids[None, :] < ids[:, :1], axis=1, dtype=jnp.int32) // RB
@@ -404,7 +398,7 @@
     meta = jnp.concatenate([facts, starts, (section // 2 % 4)[None]])
     seg_row = segment_ids.reshape(8, 1, RB)
 
-    def cache(last_hidden, w_key, w_value, w_query, w_out):
+    def cache(last_hidden, w_key, w_value, w_out):
         kv_in = normalize(last_hidden, kv_gain)
         own_k = jnp.dot(kv_in, w_key, preferred_element_type=F32).astype(BF)
         own_v = jnp.dot(kv_in, w_value, preferred_element_type=F32).astype(BF)
@@ -412,71 +406,71 @@
         kv2 = send(kv, CORE)
         pair = jnp.where(core == 0, jnp.stack([kv, kv2]), jnp.stack([kv2, kv]))
         far = send(pair, FAR_Y)
+        far, w_mine = lax.optimization_barrier((far, reorder(meta, w_out, 0)))
         far = jnp.where(core == 0, far, send(far, CORE))
         piece = jnp.where(y_hi == 0, jnp.stack([pair, far]), jnp.stack([far, pair]))
         piece = piece.reshape(2, 2 * kv.shape[0], kv.shape[1])
-        w_mine = reorder(meta, w_out, 0)
         piece2 = send(piece, PARTNER)
         share = lax.dynamic_index_in_dim(piece, core, 0, keepdims=False)
+        o1 = send(share, X_PREV)
         o2 = send(share, X_FAR)
-        piece2, o2, w_first, w_mine = lax.optimization_barrier(
-            (piece2, o2, w_query[:cut], w_mine)
-        )
-        t2 = send(piece2, X_FAR)
-        w_first = send(w_first, PARTNER)
-        o2b = send(o2, CORE)
-        both = jnp.concatenate([share[None], piece2])
-        w_theirs = reorder(meta, w_out, 1)
-        return piece, o2, o2b, piece2, t2, both, w_first, w_query[cut:], w_mine, w_theirs
-
-    def nothing(last_hidden, w_key, w_value, w_query, w_out):
-        rows = 2 * last_hidden.shape[0]
-        cols = 2 * w_key.shape[1]
-        one, two, three = (jnp.zeros((k, rows, cols), BF) for k in (1, 2, 3))
-        first, rest = w_query[:cut], w_query[cut:]
+        return piece, share, o1, o2, piece2, w_mine, reorder(meta, w_out, 1)
+
+    def nothing(last_hidden, w_key, w_value, w_out):
+        two = jnp.zeros((2, 2 * last_hidden.shape[0], 2 * w_key.shape[1]), BF)
         w_none = jnp.zeros((w_out.shape[0] * w_out.shape[1], w_out.shape[2]), BF)
-        return (
-            two, one[0], one[0], two, two, three, jnp.zeros_like(first), jnp.zeros_like(rest),
-            w_none, w_none,
-        )
+        return two, two[0], two[0], two[0], two, w_none, w_none
 
     w_o_r = w_o.reshape(8, w_q.shape[1], width)
-    piece, o2, o2b, piece2, t2, both, w_q2a, w_rest, w_o_mine, w_o_theirs = lax.cond(
-        segment_ids[0] >= 0, cache, nothing, last_hidden, w_key, w_value, w_q, w_o_r
-    )
-    w_q2b = send(w_rest, PARTNER)
-    x_in, x_out, both = lax.optimization_barrier((x_in, x_out, both))
-    xo_a = send(x_out[: RB // 2], IN)
-    xo_b = send(x_in[RB // 2 :], OUT)
-    s1 = send(both, X_PREV)
-    s3 = send(both, X_NEXT)
+    piece, share, o1, o2, piece2, w_o_mine, w_o_theirs = lax.cond(
+        segment_ids[0] >= 0, cache, nothing, last_hidden, w_key, w_value, w_o_r
+    )
+    w_q2 = send(after(w_q, piece2), PARTNER)
+    x_in, x_out, piece2, share = lax.optimization_barrier((x_in, x_out, piece2, share))
+    most = RB * 3 // 4
+    xo_a = send(x_out[:most], IN)
+    xo_b = send(x_in[most:], OUT)
+    t1 = send(piece2, X_PREV)
+    t3 = send(piece2, X_NEXT)
     state = project(meta, [after(x0, x_in, x_out)], query_gain, w_q, 0, width)
     state = project(meta, [x_in], query_gain, w_q, 1, width, state)
     state = project(meta, [x_out], query_gain, w_q, 3, width, state)
-    xo_a, xo_b, s1, s3, *state = lax.optimization_barrier((xo_a, xo_b, s1, s3, *state))
-    s1b = send(s1, CORE)
-    s3b = send(s3, CORE)
+    t1, t3, o1, o2, piece2, share, *state = lax.optimization_barrier(
+        (t1, t3, o1, o2, piece2, share, *state)
+    )
+    o3 = send(share, X_NEXT)
+    t2 = send(piece2, X_FAR)
+    o1b = send(o1, CORE)
+    o2b = send(o2, CORE)
+    xo_a, xo_b, o1b, o2b, o3 = lax.optimization_barrier((xo_a, xo_b, o1b, o2b, o3))
+    o3b = send(o3, CORE)
     normed, q_own, res_own, res_other = project(
         meta, [xo_a, xo_b], query_gain, w_q, 2, width, state
     )
-    w_q2b, s1b, s3b, normed, q_own, w_o_theirs = lax.optimization_barrier(
-        (w_q2b, s1b, s3b, normed, q_own, w_o_theirs)
-    )
-    w_o2 = send(w_o_theirs, PARTNER)
-    q_other = more_queries(normed, w_q2a, w_q2b)
-    pieces = (piece, o2, o2b, s1, s1b, s3, s3b, piece2, t2)
+    w_q2, t2, o1b, o2b, o3b, normed, q_own = lax.optimization_barrier(
+        (w_q2, t2, o1b, o2b, o3b, normed, q_own)
+    )
+    w_o2 = send(after(w_o_theirs, w_q2), PARTNER)
+    q_other = more_queries(normed, w_q2)
+    pieces = (piece, o1, o1b, o2, o2b, o3, o3b, piece2, t1, t2, t3)
 
     result = None
+    parts = []
     for chunk in range(2):
         own = attend(meta, chunk, q_own, q_other, seg_row, pieces)
         c_in = send(own, IN)
         c_out = send(own, OUT)
         co_a = send(c_out[:RB], IN)
         co_b = send(c_in[RB:], OUT)
-        parts = (own, c_in, co_a, co_b, c_out)
-        sent = send(finish(meta, chunk, parts, w_o2, res_other, 2), PARTNER)
-        result = finish(meta, chunk, parts, w_o_mine, res_own, 8, result)
-        result = place(meta, chunk, sent, result)
+        parts.append((own, c_in, co_a, co_b, c_out))
+    for chunk in range(2):
+        result = finish(meta, chunk, parts[chunk], w_o_mine, res_own, 8, result)
+    w_o2, result = lax.optimization_barrier((w_o2, result))
+    sent = [
+        send(finish(meta, chunk, parts[chunk], w_o2, res_other, 2), PARTNER) for chunk in range(2)
+    ]
+    for chunk in range(2):
+        result = place(meta, chunk, sent[chunk], result)
     return result.reshape(1, 8 * RB, -1)
 
 

time: 217 us -> 216 us (level)
  local copies, waits for them, and re-layouts: 13.1 us -> 8.11 us
  waiting for transfers between devices: 70.8 us -> 66.4 us
  starting transfers between devices: 47 us -> 51.3 us
  Pallas kernels: 72.2 us -> 76.3 us
    slice x4 -> x2, local copies, waits for them, and re-layouts: 7.71 us -> 1.26 us  [the longest x1 1.13 us: body(): xo_b = send(x_in[most:], OUT)]
    ppermute x28 -> x29, waiting for transfers between devices: 70.8 us -> 66.4 us  [send(): return lax.ppermute(value, AXES, pairs)]
    ppermute x28 -> x29, starting transfers between devices: 47 us -> 51.3 us  [send(): return lax.ppermute(value, AXES, pairs)]
    pallas_call x4, Pallas kernels: 14.9 us -> 19.1 us  [finish(): pl.pallas_call(finish_kernel, grid_spec=pltpu.PrefetchScalarGridSpec(num_...]
    pallas_call x2, Pallas kernels: 14.6 us -> 17.9 us  [attend(): pl.pallas_call(functools.partial(attend_kernel, chunk), grid_spec=pltpu.P...]
    concatenate x1 -> x0, other arithmetic: 2.26 us -> none  [cache(): both = jnp.concatenate([share[None], piece2])]
  transfers between devices with their start and end apart: 28 -> 29, of which waited for: 13 -> 16; matrix products, arithmetic and copies ran while one was open for 11% -> 7% of each run, Pallas kernels for 33% -> 34%
where the time goes in v6:
time: 216 us; the launch traced here: 213 us
  Pallas kernels  76.3 us (35%)
  waiting for transfers between devices  66.4 us (31%)
  starting transfers between devices  51.3 us (24%)
  local copies, waits for them, and re-layouts  8.11 us (4%)
  other arithmetic  5.57 us (3%)
  matrix products  4.48 us (2%)
    ppermute x29, waiting for transfers between devices, send(): return lax.ppermute(value, AXES, pairs)  66.4 us
    ppermute x29, starting transfers between devices, send(): return lax.ppermute(value, AXES, pairs)  51.3 us
    pallas_call x4, Pallas kernels, finish(): pl.pallas_call(finish_kernel, grid_spec=pltpu.PrefetchScalarGridSpec(num_...  19.1 us
    pallas_call x2, Pallas kernels, attend(): pl.pallas_call(functools.partial(attend_kernel, chunk), grid_spec=pltpu.P...  17.9 us
    pallas_call x4, Pallas kernels, project(): pl.pallas_call(kernel, grid_spec=pltpu.PrefetchScalarGridSpec(num_scalar_...  16.5 us
    pallas_call x2, Pallas kernels, reorder(): pl.pallas_call(reorder_kernel, grid_spec=pltpu.PrefetchScalarGridSpec(num...  14.2 us
    pallas_call x1, Pallas kernels, more_queries(): pl.pallas_call(more_queries_kernel, grid=(2,), in_specs=[pl.BlockSpec((ro...  5.78 us
  transfers between devices with their start and end apart: 29, of which 16 were waited for; matrix products, arithmetic and copies ran while one was open for 7% of the time, Pallas kernels for 34%

profile of v6, /device:TPU:1, one launch (start us, length us, event | category | flops | bytes accessed | tf_op | source)
XLA Modules:
  0.0 213.2 jit_solution(4216684280290761689)
XLA Ops:
  0.0 2.5 %collective-permute-start.7 = (bf16[256,5120]{1,0:T(8,128)(2,1)}, bf16[256,5120]{1,0:T(8,128)(2,1)}, u32[]{:S(2)}, u32[]{:S(2)}) collective-permute-start(bf16[256,5120]{1,0:T(8,128)(2,1)} %bitcast.33), channel_id=1, source_target_pairs={{0,1},{1,0},{2,3},{3,2},{4,5},{5,4},{6,7},{7,6},{8,9},{9,8},{10,11... | collective-permute-start | bytes 7864328 | tf_op jit(solution)/shard_map/ppermute | solution.py:66
  8.1 46.8 %conditional.1 = (bf16[2,256,768]{2,1,0:T(8,128)(2,1)}, bf16[256,768]{1,0:T(8,128)(2,1)}, bf16[256,768]{1,0:T(8,128)(2,1)}, bf16[256,768]{1,0:T(8,128)(2,1)}, bf...) conditional(s32[]{:T(128)} %bitcast.13, () %tuple.22, (pred[]{:T(512)}, ...), branch_computations={%region_1.2_spmd, %region_2.4_spmd} | conditional | flops 1016889472 | bytes 49212424 | solution.py:425
  9.8 3.6 %convolution_convert_fusion = bf16[128,384]{1,0:T(8,128)(2,1)S(1)} fusion(bf16[5120,384]{1,0:T(8,128)(2,1)} %get-tuple-element.154, bf16[128,5120]{1,0:T(8,128)(2,1)} %get-tuple-element.151, f32[5120]{0:T(1024)} %get-tuple-element.152, f32[128]{0:T(128)S(1)} %add_rsqrt_fusion), kind=kOutput, calls=%fused_computation.5 | convolution fusion | flops 505987072 | bytes 5362176 | tf_op jit(solution)/shard_map/cond/branch_1_fun/dot_general | solution.py:404
  14.9 2.3 %collective-permute-start = (bf16[128,768]{1,0:T(8,128)(2,1)S(1)}, bf16[128,768]{1,0:T(8,128)(2,1)S(1)}, u32[]{:S(2)}, u32[]{:S(2)}) collective-permute-start(bf16[128,768]{1,0:T(8,128)(2,1)S(1)} %get-tuple-element.171), channel_id=1, source_target_pairs={{0,8},{1,9},{2,10},{3,11},{4,12},{5,13},{6,14},{7,15},{8,0},{9,1},... | collective-permute-start | bytes 589832 | tf_op jit(solution)/shard_map/cond/branch_1_fun/ppermute | solution.py:66
  19.7 7.1 %branch_1_fun.2 = bf16[8,384,640]{2,1,0:T(8,128)(2,1)} custom-call(s32[32]{0:T(128)S(1)} %get-tuple-element.27.meta, bf16[8,384,640]{2,1,0:T(8,128)(2,1)} %bitcast.38), custom_call_target="tpu_custom_call" | custom-call | tf_op jit(solution)/shard_map/cond/branch_1_fun/pallas_call | solution.py:287
  26.7 8.3 %collective-permute-start.2 = (bf16[2,128,768]{2,1,0:T(8,128)(2,1)S(1)}, bf16[2,128,768]{2,1,0:T(8,128)(2,1)}, u32[]{:S(2)}, u32[]{:S(2)}) collective-permute-start(bf16[2,128,768]{2,1,0:T(8,128)(2,1)S(1)} %collective-permute-done.1), channel_id=1, source_target_pairs={{0,8},{1,9},{2,10},{3,11},{4,12},{5,13},{6,14},{7,15},{8,0},{9,1},... | collective-permute-start | bytes 1179656 | tf_op jit(solution)/shard_map/cond/branch_1_fun/ppermute | solution.py:66
  40.8 2.5 %collective-permute-start.3 = (bf16[256,768]{1,0:T(8,128)(2,1)}, bf16[256,768]{1,0:T(8,128)(2,1)}, u32[]{:S(2)}, u32[]{:S(2)}) collective-permute-start(bf16[256,768]{1,0:T(8,128)(2,1)} %dynamic-slice_bitcast_fusion), channel_id=1, source_target_pairs={{0,48},{1,49},{2,50},{3,51},{4,52},{5,53},{6,54},{7,55},{8,56},{9,... | collective-permute-start | bytes 1179656 | tf_op jit(solution)/shard_map/cond/branch_1_fun/ppermute | solution.py:66
  43.8 7.1 %branch_1_fun.3 = bf16[8,384,640]{2,1,0:T(8,128)(2,1)} custom-call(s32[32]{0:T(128)S(1)} %get-tuple-element.27.meta, bf16[8,384,640]{2,1,0:T(8,128)(2,1)} %bitcast.39), custom_call_target="tpu_custom_call" | custom-call | tf_op jit(solution)/shard_map/cond/branch_1_fun/pallas_call | solution.py:287
  52.3 2.6 %collective-permute-done.4 = bf16[256,768]{1,0:T(8,128)(2,1)} collective-permute-done((bf16[256,768]{1,0:T(8,128)(2,1)}, bf16[256,768]{1,0:T(8,128)(2,1)}, u32[]{:S(2)}, u32[]{:S(2)}) %collective-permute-start.4) | collective-permute-done | bytes 393248 | tf_op jit(solution)/shard_map/cond/branch_1_fun/ppermute | solution.py:66
  54.9 7.5 %collective-permute-start.6 = (bf16[5120,384]{1,0:T(8,128)(2,1)}, bf16[5120,384]{1,0:T(8,128)(2,1)S(1)}, u32[]{:S(2)}, u32[]{:S(2)}) collective-permute-start(bf16[5120,384]{1,0:T(8,128)(2,1)} %bitcast.26), channel_id=1, source_target_pairs={{0,4},{1,5},{2,6},{3,7},{4,0},{5,1},{6,2},{7,3},{8,11},{9,10},{10,... | collective-permute-start | bytes 11796488 | tf_op jit(solution)/shard_map/ppermute | solution.py:66
  69.5 3.7 %shard_map.105 = (bf16[4,256,5120]{2,1,0:T(8,128)(2,1)S(1)}, bf16[4,256,384]{2,1,0:T(8,128)(2,1)S(1)}, bf16[4,256,640]{2,1,0:T(8,128)(2,1)S(1)}, bf16[4,256,640]{2,1,0:T(8,128)(2,1)S(1)}) custom-call(s32[32]{0:T(128)S(1)} %pad_add_fusion.meta, bf16[256,5120]{1,0:T(8,128)(2,1)S(1)} %bitcast.35, f32[1,5120]{1,0:T(1,128)S(1)} %copy-done.2, ...), custom_call_target="tpu_custom_call" | custom-call | flops 1006632960 | bytes 11796480 | tf_op jit(solution)/shard_map/pallas_call | solution.py:119
  73.2 5.4 %shard_map.106 = (bf16[4,256,5120]{2,1,0:T(8,128)(2,1)S(1)}, bf16[4,256,384]{2,1,0:T(8,128)(2,1)S(1)}, bf16[4,256,640]{2,1,0:T(8,128)(2,1)S(1)}, bf16[4,256,640]{2,1,0:T(8,128)(2,1)S(1)}) custom-call(s32[32]{0:T(128)S(1)} %pad_add_fusion.meta, ...), custom_call_target="tpu_custom_call", output_to_operand_aliasing={{0}: (4, {}), {1}: (5, {}), {2}: (6, {}), {3}: (7, {})} | custom-call | flops 1006632960 | bytes 11796480 | tf_op jit(solution)/shard_map/pallas_call | solution.py:119
  78.7 3.7 %shard_map.107 = (bf16[4,256,5120]{2,1,0:T(8,128)(2,1)S(1)}, bf16[4,256,384]{2,1,0:T(8,128)(2,1)S(1)}, bf16[4,256,640]{2,1,0:T(8,128)(2,1)S(1)}, bf16[4,256,640]{2,1,0:T(8,128)(2,1)S(1)}) custom-call(s32[32]{0:T(128)S(1)} %pad_add_fusion.meta, ...), custom_call_target="tpu_custom_call", output_to_operand_aliasing={{0}: (4, {}), {1}: (5, {}), {2}: (6, {}), {3}: (7, {})} | custom-call | flops 1006632960 | bytes 11796480 | tf_op jit(solution)/shard_map/pallas_call | solution.py:119
  86.1 2.6 %collective-permute-start.11 = (bf16[2,256,768]{2,1,0:T(8,128)(2,1)}, bf16[2,256,768]{2,1,0:T(8,128)(2,1)S(1)}, u32[]{:S(2)}, u32[]{:S(2)}) collective-permute-start(bf16[2,256,768]{2,1,0:T(8,128)(2,1)} %get-tuple-element.107.other0), channel_id=1, source_target_pairs={{0,32},{1,33},{2,34},{3,35},{4,36},{5,37},{6,38},{7,39},{8,40},{9,... | collective-permute-start | bytes 2359304 | tf_op jit(solution)/shard_map/ppermute | solution.py:66
  88.7 4.8 %collective-permute-done.16.o3 = bf16[256,768]{1,0:T(8,128)(2,1)S(1)} collective-permute-done((bf16[256,768]{1,0:T(8,128)(2,1)}, bf16[256,768]{1,0:T(8,128)(2,1)S(1)}, u32[]{:S(2)}, u32[]{:S(2)}) %collective-permute-start.16) | collective-permute-done | bytes 393248 | tf_op jit(solution)/shard_map/ppermute | solution.py:66
  93.5 13.5 %collective-permute-done.12.refs_0_ = bf16[192,5120]{1,0:T(8,128)(2,1)S(1)} collective-permute-done((bf16[192,5120]{1,0:T(8,128)(2,1)S(1)}, bf16[192,5120]{1,0:T(8,128)(2,1)S(1)}, u32[]{:S(2)}, u32[]{:S(2)}) %collective-permute-start.12) | collective-permute-done | bytes 1966112 | tf_op jit(solution)/shard_map/ppermute | solution.py:66
  107.9 3.7 %shard_map.108 = (bf16[4,256,5120]{2,1,0:T(8,128)(2,1)S(1)}, bf16[4,256,384]{2,1,0:T(8,128)(2,1)S(1)}, bf16[4,256,640]{2,1,0:T(8,128)(2,1)S(1)}, bf16[4,256,640]{2,1,0:T(8,128)(2,1)S(1)}) custom-call(s32[32]{0:T(128)S(1)} %pad_add_fusion.meta, ...), custom_call_target="tpu_custom_call", output_to_operand_aliasing={{0}: (5, {}), {1}: (6, {}), {2}: (7, {}), {3}: (8, {})} | custom-call | flops 1006632960 | bytes 11796480 | tf_op jit(solution)/shard_map/pallas_call | solution.py:119
  113.0 2.7 %collective-permute-start.22 = (bf16[3072,640]{1,0:T(8,128)(2,1)}, bf16[3072,640]{1,0:T(8,128)(2,1)S(1)}, u32[]{:S(2)}, u32[]{:S(2)}) collective-permute-start(bf16[3072,640]{1,0:T(8,128)(2,1)} %get-tuple-element.133), channel_id=1, source_target_pairs={{0,4},{1,5},{2,6},{3,7},{4,0},{5,1},{6,2},{7,3},{8,11},{9,10},{10,... | collective-permute-start | bytes 11796488 | tf_op jit(solution)/shard_map/ppermute | solution.py:66
  115.7 5.8 %shard_map.109 = bf16[1024,384]{1,0:T(8,128)(2,1)S(1)} custom-call(bf16[1024,5120]{1,0:T(8,128)(2,1)S(1)} %bitcast.25, bf16[5120,384]{1,0:T(8,128)(2,1)S(1)} %collective-permute-done.6.w_ref), custom_call_target="tpu_custom_call" | custom-call | flops 4026531840 | bytes 14417920 | tf_op jit(solution)/shard_map/pallas_call | solution.py:143
  121.5 7.0 %shard_map.111.c0 = bf16[512,768]{1,0:T(8,128)(2,1)S(1)} custom-call(s32[32]{0:T(128)S(1)} %pad_add_fusion.meta, bf16[4,256,384]{2,1,0:T(8,128)(2,1)S(1)} %get-tuple-element.122.q_own, bf16[4,256,384]{2,1,0:T(8,128)(2,1)S(1)} %bitcast.31, s32[8,1,256]{2,1,0:T(1,128)S(1)} %bitcast.36, bf16[2,256,768]{2,1,0:T(8,128)(2,1)} %get-tuple-element.125.own0, ...), custom_call_target="tpu_custom_call" | custom-call | flops 1207959552 | bytes 8388608 | tf_op jit(solution)/shard_map/pallas_call | solution.py:259
  130.6 10.9 %shard_map.110.c0 = bf16[512,768]{1,0:T(8,128)(2,1)S(1)} custom-call(s32[32]{0:T(128)S(1)} %pad_add_fusion.meta, bf16[4,256,384]{2,1,0:T(8,128)(2,1)S(1)} %get-tuple-element.122.q_own, bf16[4,256,384]{2,1,0:T(8,128)(2,1)S(1)} %bitcast.32, s32[8,1,256]{2,1,0:T(1,128)S(1)} %bitcast.37, bf16[2,256,768]{2,1,0:T(8,128)(2,1)} %get-tuple-element.125.own0, ...), custom_call_target="tpu_custom_call" | custom-call | flops 1207959552 | bytes 8388608 | tf_op jit(solution)/shard_map/pallas_call | solution.py:259
  142.7 5.7 %collective-permute-done.24.c3 = bf16[512,768]{1,0:T(8,128)(2,1)S(1)} collective-permute-done((bf16[512,768]{1,0:T(8,128)(2,1)S(1)}, bf16[512,768]{1,0:T(8,128)(2,1)S(1)}, u32[]{:S(2)}, u32[]{:S(2)}) %collective-permute-start.24) | collective-permute-done | bytes 786464 | tf_op jit(solution)/shard_map/ppermute | solution.py:66
  150.4 14.8 %collective-permute-done.19.c3 = bf16[512,768]{1,0:T(8,128)(2,1)S(1)} collective-permute-done((bf16[512,768]{1,0:T(8,128)(2,1)S(1)}, bf16[512,768]{1,0:T(8,128)(2,1)S(1)}, u32[]{:S(2)}, u32[]{:S(2)}) %collective-permute-start.19) | collective-permute-done | bytes 786464 | tf_op jit(solution)/shard_map/ppermute | solution.py:66
  167.3 3.5 %collective-permute-done.25.c2a = bf16[256,768]{1,0:T(8,128)(2,1)S(1)} collective-permute-done((bf16[256,768]{1,0:T(8,128)(2,1)S(1)}, bf16[256,768]{1,0:T(8,128)(2,1)S(1)}, u32[]{:S(2)}, u32[]{:S(2)}) %collective-permute-start.25) | collective-permute-done | bytes 393248 | tf_op jit(solution)/shard_map/ppermute | solution.py:66
  170.8 2.9 %collective-permute-done.26.c2b = bf16[256,768]{1,0:T(8,128)(2,1)S(1)} collective-permute-done((bf16[256,768]{1,0:T(8,128)(2,1)S(1)}, bf16[256,768]{1,0:T(8,128)(2,1)S(1)}, u32[]{:S(2)}, u32[]{:S(2)}) %collective-permute-start.26) | collective-permute-done | bytes 393248 | tf_op jit(solution)/shard_map/ppermute | solution.py:66
  173.7 6.2 %shard_map.112.refs_0_ = bf16[8,256,640]{2,1,0:T(8,128)(2,1)} custom-call(s32[32]{0:T(128)S(1)} %pad_add_fusion.meta, bf16[512,768]{1,0:T(8,128)(2,1)S(1)} %shard_map.111.c0, bf16[512,768]{1,0:T(8,128)(2,1)S(1)} %collective-permute-done.23.c1, bf16[256,768]{1,0:T(8,128)(2,1)S(1)} %collective-permute-done.25.c2a, ...), custom_call_target="tpu_custom_call" | custom-call | flops 2013265920 | bytes 8388608 | tf_op jit(solution)/shard_map/pallas_call | solution.py:330
  182.1 6.2 %shard_map.113.prior = bf16[8,256,640]{2,1,0:T(8,128)(2,1)} custom-call(s32[32]{0:T(128)S(1)} %pad_add_fusion.meta, bf16[512,768]{1,0:T(8,128)(2,1)S(1)} %shard_map.110.c0, bf16[512,768]{1,0:T(8,128)(2,1)S(1)} %collective-permute-done.18.c1, bf16[256,768]{1,0:T(8,128)(2,1)S(1)} %collective-permute-done.20.c2a, ...), custom_call_target="tpu_custom_call", output_to_operand_aliasing={{}: (8, {})} | custom-call | flops 2013265920 | bytes 8388608 | tf_op jit(solution)/shard_map/pallas_call | solution.py:330
  188.3 3.4 %shard_map.115 = bf16[2,256,640]{2,1,0:T(8,128)(2,1)S(1)} custom-call(s32[32]{0:T(128)S(1)} %pad_add_fusion.meta, bf16[512,768]{1,0:T(8,128)(2,1)S(1)} %shard_map.111.c0, bf16[512,768]{1,0:T(8,128)(2,1)S(1)} %collective-permute-done.23.c1, bf16[256,768]{1,0:T(8,128)(2,1)S(1)} %collective-permute-done.25.c2a, ...), custom_call_target="tpu_custom_call" | custom-call | flops 2013265920 | bytes 8388608 | tf_op jit(solution)/shard_map/pallas_call | solution.py:330
  191.7 4.9 %collective-permute-start.28 = (bf16[2,256,640]{2,1,0:T(8,128)(2,1)S(1)}, bf16[2,256,640]{2,1,0:T(8,128)(2,1)S(1)}, u32[]{:S(2)}, u32[]{:S(2)}) collective-permute-start(bf16[2,256,640]{2,1,0:T(8,128)(2,1)S(1)} %shard_map.115), channel_id=1, source_target_pairs={{0,4},{1,5},{2,6},{3,7},{4,0},{5,1},{6,2},{7,3},{8,11},{9,10},{10,... | collective-permute-start | bytes 1966088 | tf_op jit(solution)/shard_map/ppermute | solution.py:66
  196.6 3.4 %shard_map.114 = bf16[2,256,640]{2,1,0:T(8,128)(2,1)S(1)} custom-call(s32[32]{0:T(128)S(1)} %pad_add_fusion.meta, bf16[512,768]{1,0:T(8,128)(2,1)S(1)} %shard_map.110.c0, bf16[512,768]{1,0:T(8,128)(2,1)S(1)} %collective-permute-done.18.c1, bf16[256,768]{1,0:T(8,128)(2,1)S(1)} %collective-permute-done.20.c2a, ...), custom_call_target="tpu_custom_call" | custom-call | flops 2013265920 | bytes 8388608 | tf_op jit(solution)/shard_map/pallas_call | solution.py:330
  200.1 4.5 %collective-permute-done.28.got = bf16[2,256,640]{2,1,0:T(8,128)(2,1)S(1)} collective-permute-done((bf16[2,256,640]{2,1,0:T(8,128)(2,1)S(1)}, bf16[2,256,640]{2,1,0:T(8,128)(2,1)S(1)}, u32[]{:S(2)}, u32[]{:S(2)}) %collective-permute-start.28) | collective-permute-done | bytes 655392 | tf_op jit(solution)/shard_map/ppermute | solution.py:66
  206.0 5.6 %collective-permute-done.27.got = bf16[2,256,640]{2,1,0:T(8,128)(2,1)S(1)} collective-permute-done((bf16[2,256,640]{2,1,0:T(8,128)(2,1)S(1)}, bf16[2,256,640]{2,1,0:T(8,128)(2,1)S(1)}, u32[]{:S(2)}, u32[]{:S(2)}) %collective-permute-start.27) | collective-permute-done | bytes 655392 | tf_op jit(solution)/shard_map/ppermute | solution.py:66
  (79 shorter events, 43.9 us)
Async XLA Ops:
  0.0 62.4 %collective-permute-start.7 = (bf16[256,5120]{1,0:T(8,128)(2,1)}, bf16[256,5120]{1,0:T(8,128)(2,1)}, u32[]{:S(2)}, u32[]{:S(2)}) collective-permute-start(bf16[256,5120]{1,0:T(8,128)(2,1)} %bitcast.33), channel_id=1, source_target_pairs={{0,1},{1,0},{2,3},{3,2},{4,5},{5,4},{6,7},{7,6},{8,9},{9,8},{10,11... | collective-permute-start | bytes 7864328 | tf_op jit(solution)/shard_map/ppermute | solution.py:66
  2.5 59.9 %collective-permute-start.8 = (bf16[256,5120]{1,0:T(8,128)(2,1)}, bf16[256,5120]{1,0:T(8,128)(2,1)S(1)}, u32[]{:S(2)}, u32[]{:S(2)}) collective-permute-start(bf16[256,5120]{1,0:T(8,128)(2,1)} %bitcast.34), channel_id=1, source_target_pairs={{0,3},{1,2},{2,1},{3,0},{4,7},{5,6},{6,5},{7,4},{8,12},{9,13},{10,... | collective-permute-start | bytes 7864328 | tf_op jit(solution)/shard_map/ppermute | solution.py:66
  14.9 3.3 %collective-permute-start = (bf16[128,768]{1,0:T(8,128)(2,1)S(1)}, bf16[128,768]{1,0:T(8,128)(2,1)S(1)}, u32[]{:S(2)}, u32[]{:S(2)}) collective-permute-start(bf16[128,768]{1,0:T(8,128)(2,1)S(1)} %get-tuple-element.171), channel_id=1, source_target_pairs={{0,8},{1,9},{2,10},{3,11},{4,12},{5,13},{6,14},{7,15},{8,0},{9,1},... | collective-permute-start | bytes 589832 | tf_op jit(solution)/shard_map/cond/branch_1_fun/ppermute | solution.py:66
  19.0 7.7 %collective-permute-start.1 = (bf16[2,128,768]{2,1,0:T(8,128)(2,1)}, bf16[2,128,768]{2,1,0:T(8,128)(2,1)S(1)}, u32[]{:S(2)}, u32[]{:S(2)}) collective-permute-start(bf16[2,128,768]{2,1,0:T(8,128)(2,1)} %maximum_select_fusion.2), channel_id=1, source_target_pairs={{0,64},{1,65},{2,66},{3,67},{4,68},{5,69},{6,70},{7,71},{16,80},{1... | collective-permute-start | bytes 1179656 | tf_op jit(solution)/shard_map/cond/branch_1_fun/ppermute | solution.py:66
  26.7 9.8 %collective-permute-start.2 = (bf16[2,128,768]{2,1,0:T(8,128)(2,1)S(1)}, bf16[2,128,768]{2,1,0:T(8,128)(2,1)}, u32[]{:S(2)}, u32[]{:S(2)}) collective-permute-start(bf16[2,128,768]{2,1,0:T(8,128)(2,1)S(1)} %collective-permute-done.1), channel_id=1, source_target_pairs={{0,8},{1,9},{2,10},{3,11},{4,12},{5,13},{6,14},{7,15},{8,0},{9,1},... | collective-permute-start | bytes 1179656 | tf_op jit(solution)/shard_map/cond/branch_1_fun/ppermute | solution.py:66
  38.5 16.4 %collective-permute-start.5 = (bf16[2,256,768]{2,1,0:T(8,128)(2,1)}, bf16[2,256,768]{2,1,0:T(8,128)(2,1)}, u32[]{:S(2)}, u32[]{:S(2)}) collective-permute-start(bf16[2,256,768]{2,1,0:T(8,128)(2,1)} %maximum_select_fusion), channel_id=1, source_target_pairs={{0,4},{1,5},{2,6},{3,7},{4,0},{5,1},{6,2},{7,3},{8,11},{9,10},{10,... | collective-permute-start | bytes 2359304 | tf_op jit(solution)/shard_map/cond/branch_1_fun/ppermute | solution.py:66
  40.8 11.5 %collective-permute-start.3 = (bf16[256,768]{1,0:T(8,128)(2,1)}, bf16[256,768]{1,0:T(8,128)(2,1)}, u32[]{:S(2)}, u32[]{:S(2)}) collective-permute-start(bf16[256,768]{1,0:T(8,128)(2,1)} %dynamic-slice_bitcast_fusion), channel_id=1, source_target_pairs={{0,48},{1,49},{2,50},{3,51},{4,52},{5,53},{6,54},{7,55},{8,56},{9,... | collective-permute-start | bytes 1179656 | tf_op jit(solution)/shard_map/cond/branch_1_fun/ppermute | solution.py:66
  43.2 11.7 %collective-permute-start.4 = (bf16[256,768]{1,0:T(8,128)(2,1)}, bf16[256,768]{1,0:T(8,128)(2,1)}, u32[]{:S(2)}, u32[]{:S(2)}) collective-permute-start(bf16[256,768]{1,0:T(8,128)(2,1)} %dynamic-slice_bitcast_fusion), channel_id=1, source_target_pairs={{0,32},{1,33},{2,34},{3,35},{4,36},{5,37},{6,38},{7,39},{8,40},{9,... | collective-permute-start | bytes 1179656 | tf_op jit(solution)/shard_map/cond/branch_1_fun/ppermute | solution.py:66
  54.9 58.1 %collective-permute-start.6 = (bf16[5120,384]{1,0:T(8,128)(2,1)}, bf16[5120,384]{1,0:T(8,128)(2,1)S(1)}, u32[]{:S(2)}, u32[]{:S(2)}) collective-permute-start(bf16[5120,384]{1,0:T(8,128)(2,1)} %bitcast.26), channel_id=1, source_target_pairs={{0,4},{1,5},{2,6},{3,7},{4,0},{5,1},{6,2},{7,3},{8,11},{9,10},{10,... | collective-permute-start | bytes 11796488 | tf_op jit(solution)/shard_map/ppermute | solution.py:66
  62.4 5.4 %copy-start = (bf16[1,5120,384]{2,1,0:T(8,128)(2,1)S(1)}, bf16[1,5120,384]{2,1,0:T(8,128)(2,1)}, u32[]{:S(2)}) copy-start(bf16[1,5120,384]{2,1,0:T(8,128)(2,1)} %param.18) | copy-start | bytes 11796484
  62.4 5.4 %copy-start.2 = (f32[1,5120]{1,0:T(1,128)S(1)}, f32[1,5120]{1,0:T(1,128)}, u32[]{:S(2)}) copy-start(f32[1,5120]{1,0:T(1,128)} %refs_2_.1) | copy-start | bytes 61444
  62.5 44.5 %collective-permute-start.12 = (bf16[192,5120]{1,0:T(8,128)(2,1)S(1)}, bf16[192,5120]{1,0:T(8,128)(2,1)S(1)}, u32[]{:S(2)}, u32[]{:S(2)}) collective-permute-start(bf16[192,5120]{1,0:T(8,128)(2,1)S(1)} %slice.26), channel_id=1, source_target_pairs={{0,1},{1,0},{2,3},{3,2},{4,5},{5,4},{6,7},{7,6},{8,9},{9,8},{10,11... | collective-permute-start | bytes 5898248 | tf_op jit(solution)/shard_map/ppermute | solution.py:66
  62.7 19.8 %collective-permute-start.10 = (bf16[2,256,768]{2,1,0:T(8,128)(2,1)}, bf16[2,256,768]{2,1,0:T(8,128)(2,1)S(1)}, u32[]{:S(2)}, u32[]{:S(2)}) collective-permute-start(bf16[2,256,768]{2,1,0:T(8,128)(2,1)} %get-tuple-element.107.other0), channel_id=1, source_target_pairs={{0,16},{1,17},{2,18},{3,19},{4,20},{5,21},{6,22},{7,23},{8,24},{9,... | collective-permute-start | bytes 2359304 | tf_op jit(solution)/shard_map/ppermute | solution.py:66
  64.2 18.3 %collective-permute-start.9 = (bf16[2,256,768]{2,1,0:T(8,128)(2,1)}, bf16[2,256,768]{2,1,0:T(8,128)(2,1)S(1)}, u32[]{:S(2)}, u32[]{:S(2)}) collective-permute-start(bf16[2,256,768]{2,1,0:T(8,128)(2,1)} %get-tuple-element.107.other0), channel_id=1, source_target_pairs={{0,48},{1,49},{2,50},{3,51},{4,52},{5,53},{6,54},{7,55},{8,56},{9,... | collective-permute-start | bytes 2359304 | tf_op jit(solution)/shard_map/ppermute | solution.py:66
  67.0 17.5 %collective-permute-start.13 = (bf16[64,5120]{1,0:T(8,128)(2,1)S(1)}, bf16[64,5120]{1,0:T(8,128)(2,1)S(1)}, u32[]{:S(2)}, u32[]{:S(2)}) collective-permute-start(bf16[64,5120]{1,0:T(8,128)(2,1)S(1)} %slice.27), channel_id=1, source_target_pairs={{0,3},{1,2},{2,1},{3,0},{4,7},{5,6},{6,5},{7,4},{8,12},{9,13},{10,... | collective-permute-start | bytes 1966088 | tf_op jit(solution)/shard_map/ppermute | solution.py:66
  82.5 3.6 %collective-permute-start.14 = (bf16[256,768]{1,0:T(8,128)(2,1)}, bf16[256,768]{1,0:T(8,128)(2,1)S(1)}, u32[]{:S(2)}, u32[]{:S(2)}) collective-permute-start(bf16[256,768]{1,0:T(8,128)(2,1)} %get-tuple-element.108.o1), channel_id=1, source_target_pairs={{0,8},{1,9},{2,10},{3,11},{4,12},{5,13},{6,14},{7,15},{8,0},{9,1},... | collective-permute-start | bytes 1179656 | tf_op jit(solution)/shard_map/ppermute | solution.py:66
  84.5 4.2 %collective-permute-start.15 = (bf16[256,768]{1,0:T(8,128)(2,1)}, bf16[256,768]{1,0:T(8,128)(2,1)S(1)}, u32[]{:S(2)}, u32[]{:S(2)}) collective-permute-start(bf16[256,768]{1,0:T(8,128)(2,1)} %get-tuple-element.109.o2), channel_id=1, source_target_pairs={{0,8},{1,9},{2,10},{3,11},{4,12},{5,13},{6,14},{7,15},{8,0},{9,1},... | collective-permute-start | bytes 1179656 | tf_op jit(solution)/shard_map/ppermute | solution.py:66
  84.5 8.9 %collective-permute-start.16 = (bf16[256,768]{1,0:T(8,128)(2,1)}, bf16[256,768]{1,0:T(8,128)(2,1)S(1)}, u32[]{:S(2)}, u32[]{:S(2)}) collective-permute-start(bf16[256,768]{1,0:T(8,128)(2,1)} %get-tuple-element.110), channel_id=1, source_target_pairs={{0,16},{1,17},{2,18},{3,19},{4,20},{5,21},{6,22},{7,23},{8,24},{9,... | collective-permute-start | bytes 1179656 | tf_op jit(solution)/shard_map/ppermute | solution.py:66
  86.1 26.9 %collective-permute-start.11 = (bf16[2,256,768]{2,1,0:T(8,128)(2,1)}, bf16[2,256,768]{2,1,0:T(8,128)(2,1)S(1)}, u32[]{:S(2)}, u32[]{:S(2)}) collective-permute-start(bf16[2,256,768]{2,1,0:T(8,128)(2,1)} %get-tuple-element.107.other0), channel_id=1, source_target_pairs={{0,32},{1,33},{2,34},{3,35},{4,36},{5,37},{6,38},{7,39},{8,40},{9,... | collective-permute-start | bytes 2359304 | tf_op jit(solution)/shard_map/ppermute | solution.py:66
  107.0 6.0 %collective-permute-start.17 = (bf16[256,768]{1,0:T(8,128)(2,1)S(1)}, bf16[256,768]{1,0:T(8,128)(2,1)S(1)}, u32[]{:S(2)}, u32[]{:S(2)}) collective-permute-start(bf16[256,768]{1,0:T(8,128)(2,1)S(1)} %collective-permute-done.16.o3), channel_id=1, source_target_pairs={{0,8},{1,9},{2,10},{3,11},{4,12},{5,13},{6,14},{7,15},{8,0},{9,1},... | collective-permute-start | bytes 1179656 | tf_op jit(solution)/shard_map/ppermute | solution.py:66
  113.0 75.3 %collective-permute-start.22 = (bf16[3072,640]{1,0:T(8,128)(2,1)}, bf16[3072,640]{1,0:T(8,128)(2,1)S(1)}, u32[]{:S(2)}, u32[]{:S(2)}) collective-permute-start(bf16[3072,640]{1,0:T(8,128)(2,1)} %get-tuple-element.133), channel_id=1, source_target_pairs={{0,4},{1,5},{2,6},{3,7},{4,0},{5,1},{6,2},{7,3},{8,11},{9,10},{10,... | collective-permute-start | bytes 11796488 | tf_op jit(solution)/shard_map/ppermute | solution.py:66
  115.7 5.8 %copy-start.3 = (s32[2048]{0:T(1024)S(1)}, s32[2048]{0:T(1024)}, u32[]{:S(2)}) copy-start(s32[2048]{0:T(1024)} %param.20) | copy-start | bytes 24580
  128.5 19.9 %collective-permute-start.24 = (bf16[512,768]{1,0:T(8,128)(2,1)S(1)}, bf16[512,768]{1,0:T(8,128)(2,1)S(1)}, u32[]{:S(2)}, u32[]{:S(2)}) collective-permute-start(bf16[512,768]{1,0:T(8,128)(2,1)S(1)} %shard_map.111.c0), channel_id=1, source_target_pairs={{0,3},{1,2},{2,1},{3,0},{4,7},{5,6},{6,5},{7,4},{8,12},{9,13},{10,... | collective-permute-start | bytes 2359304 | tf_op jit(solution)/shard_map/ppermute | solution.py:66
  129.1 19.7 %collective-permute-start.23 = (bf16[512,768]{1,0:T(8,128)(2,1)S(1)}, bf16[512,768]{1,0:T(8,128)(2,1)S(1)}, u32[]{:S(2)}, u32[]{:S(2)}) collective-permute-start(bf16[512,768]{1,0:T(8,128)(2,1)S(1)} %shard_map.111.c0), channel_id=1, source_target_pairs={{0,1},{1,0},{2,3},{3,2},{4,5},{5,4},{6,7},{7,6},{8,9},{9,8},{10,11... | collective-permute-start | bytes 2359304 | tf_op jit(solution)/shard_map/ppermute | solution.py:66
  141.5 23.8 %collective-permute-start.19 = (bf16[512,768]{1,0:T(8,128)(2,1)S(1)}, bf16[512,768]{1,0:T(8,128)(2,1)S(1)}, u32[]{:S(2)}, u32[]{:S(2)}) collective-permute-start(bf16[512,768]{1,0:T(8,128)(2,1)S(1)} %shard_map.110.c0), channel_id=1, source_target_pairs={{0,3},{1,2},{2,1},{3,0},{4,7},{5,6},{6,5},{7,4},{8,12},{9,13},{10,... | collective-permute-start | bytes 2359304 | tf_op jit(solution)/shard_map/ppermute | solution.py:66
  141.7 24.1 %collective-permute-start.18 = (bf16[512,768]{1,0:T(8,128)(2,1)S(1)}, bf16[512,768]{1,0:T(8,128)(2,1)S(1)}, u32[]{:S(2)}, u32[]{:S(2)}) collective-permute-start(bf16[512,768]{1,0:T(8,128)(2,1)S(1)} %shard_map.110.c0), channel_id=1, source_target_pairs={{0,1},{1,0},{2,3},{3,2},{4,5},{5,4},{6,7},{7,6},{8,9},{9,8},{10,11... | collective-permute-start | bytes 2359304 | tf_op jit(solution)/shard_map/ppermute | solution.py:66
  148.4 22.3 %collective-permute-start.25 = (bf16[256,768]{1,0:T(8,128)(2,1)S(1)}, bf16[256,768]{1,0:T(8,128)(2,1)S(1)}, u32[]{:S(2)}, u32[]{:S(2)}) collective-permute-start(bf16[256,768]{1,0:T(8,128)(2,1)S(1)} %slice.35), channel_id=1, source_target_pairs={{0,1},{1,0},{2,3},{3,2},{4,5},{5,4},{6,7},{7,6},{8,9},{9,8},{10,11... | collective-permute-start | bytes 1179656 | tf_op jit(solution)/shard_map/ppermute | solution.py:66
  148.9 24.8 %collective-permute-start.26 = (bf16[256,768]{1,0:T(8,128)(2,1)S(1)}, bf16[256,768]{1,0:T(8,128)(2,1)S(1)}, u32[]{:S(2)}, u32[]{:S(2)}) collective-permute-start(bf16[256,768]{1,0:T(8,128)(2,1)S(1)} %slice.36), channel_id=1, source_target_pairs={{0,3},{1,2},{2,1},{3,0},{4,7},{5,6},{6,5},{7,4},{8,12},{9,13},{10,... | collective-permute-start | bytes 1179656 | tf_op jit(solution)/shard_map/ppermute | solution.py:66
  165.3 14.6 %collective-permute-start.20 = (bf16[256,768]{1,0:T(8,128)(2,1)S(1)}, bf16[256,768]{1,0:T(8,128)(2,1)S(1)}, u32[]{:S(2)}, u32[]{:S(2)}) collective-permute-start(bf16[256,768]{1,0:T(8,128)(2,1)S(1)} %slice.33), channel_id=1, source_target_pairs={{0,1},{1,0},{2,3},{3,2},{4,5},{5,4},{6,7},{7,6},{8,9},{9,8},{10,11... | collective-permute-start | bytes 1179656 | tf_op jit(solution)/shard_map/ppermute | solution.py:66
  165.7 16.4 %collective-permute-start.21 = (bf16[256,768]{1,0:T(8,128)(2,1)S(1)}, bf16[256,768]{1,0:T(8,128)(2,1)S(1)}, u32[]{:S(2)}, u32[]{:S(2)}) collective-permute-start(bf16[256,768]{1,0:T(8,128)(2,1)S(1)} %slice.34), channel_id=1, source_target_pairs={{0,3},{1,2},{2,1},{3,0},{4,7},{5,6},{6,5},{7,4},{8,12},{9,13},{10,... | collective-permute-start | bytes 1179656 | tf_op jit(solution)/shard_map/ppermute | solution.py:66
  191.7 12.9 %collective-permute-start.28 = (bf16[2,256,640]{2,1,0:T(8,128)(2,1)S(1)}, bf16[2,256,640]{2,1,0:T(8,128)(2,1)S(1)}, u32[]{:S(2)}, u32[]{:S(2)}) collective-permute-start(bf16[2,256,640]{2,1,0:T(8,128)(2,1)S(1)} %shard_map.115), channel_id=1, source_target_pairs={{0,4},{1,5},{2,6},{3,7},{4,0},{5,1},{6,2},{7,3},{8,11},{9,10},{10,... | collective-permute-start | bytes 1966088 | tf_op jit(solution)/shard_map/ppermute | solution.py:66
  200.0 11.6 %collective-permute-start.27 = (bf16[2,256,640]{2,1,0:T(8,128)(2,1)S(1)}, bf16[2,256,640]{2,1,0:T(8,128)(2,1)S(1)}, u32[]{:S(2)}, u32[]{:S(2)}) collective-permute-start(bf16[2,256,640]{2,1,0:T(8,128)(2,1)S(1)} %shard_map.114), channel_id=1, source_target_pairs={{0,4},{1,5},{2,6},{3,7},{4,0},{5,1},{6,2},{7,3},{8,11},{9,10},{10,... | collective-permute-start | bytes 1966088 | tf_op jit(solution)/shard_map/ppermute | solution.py:66
  (4 other events, 13.5 us)

commit v7 on v6

--- a/solution.py
+++ b/solution.py
@@ -20,19 +20,20 @@
     for table in PLACE
 )
 
-MINE, THEIRS, SLOT, ROWS, OWN, CORE_AT, FIRST, X_AT = 0, 4, 8, 12, 20, 22, 23, 31
-
-
-def facts_of(core, c):
+MINE, THEIRS, SLOT, ROWS, OWN, CORE_AT, X_AT = 0, 4, 8, 12, 20, 22, 23
+
+
+def facts_of(section, c):
+    core = section % 2
     half, r = SPOT[core][c]
     mine, theirs = PLACE[core][half], PLACE[core][1 - half]
     ring = [r, r ^ 1, (r + 2) % 4, 3 - r]
     slots = [ring.index(p) for p in range(4)]
     rows = [place[p] for p in ring for place in (mine, theirs)]
-    return [*mine, *theirs, *slots, *rows, mine[r], theirs[r], core]
-
-
-FACTS = [[facts_of(core, c) for c in range(8)] for core in range(2)]
+    return [*mine, *theirs, *slots, *rows, mine[r], theirs[r], core, section // 2 % 4]
+
+
+FACTS = [[facts_of(section, c) for c in range(8)] for section in range(16)]
 
 
 def moves(step):
@@ -179,7 +180,8 @@
         kv[1, 3] = t3[...]
 
     block = meta[MINE + 2 * chunk + t]
-    first = meta[FIRST + block]
+    earlier = (seg_row[...] < seg_row[block, :, :1]).astype(F32)
+    first = jnp.maximum(jnp.sum(earlier).astype(jnp.int32) // RB, block - 4)
     count = block - first + 1
     x = meta[X_AT]
     heads = q_own.shape[2] // HD
@@ -391,11 +393,7 @@
     x_in = send(x0, IN)
     x_out = send(x0, OUT)
 
-    ids = segment_ids.reshape(8, RB)
-    starts = jnp.sum(segment_ids[None, :] < ids[:, :1], axis=1, dtype=jnp.int32) // RB
-    starts = jnp.maximum(starts, jnp.arange(8, dtype=jnp.int32) - 4)
-    facts = jnp.array(FACTS, jnp.int32)[core, c]
-    meta = jnp.concatenate([facts, starts, (section // 2 % 4)[None]])
+    meta = jnp.array(FACTS, jnp.int32)[section, c]
     seg_row = segment_ids.reshape(8, 1, RB)
 
     def cache(last_hidden, w_key, w_value, w_out):
@@ -463,12 +461,12 @@
         co_a = send(c_out[:RB], IN)
         co_b = send(c_in[RB:], OUT)
         parts.append((own, c_in, co_a, co_b, c_out))
-    for chunk in range(2):
-        result = finish(meta, chunk, parts[chunk], w_o_mine, res_own, 8, result)
+    result = finish(meta, 0, parts[0], w_o_mine, res_own, 8)
     w_o2, result = lax.optimization_barrier((w_o2, result))
-    sent = [
-        send(finish(meta, chunk, parts[chunk], w_o2, res_other, 2), PARTNER) for chunk in range(2)
-    ]
+    others = [finish(meta, chunk, parts[chunk], w_o2, res_other, 2) for chunk in range(2)]
+    sent = [send(other, PARTNER) for other in others]
+    w_o_mine = after(w_o_mine, *others)
+    result = finish(meta, 1, parts[1], w_o_mine, res_own, 8, result)
     for chunk in range(2):
         result = place(meta, chunk, sent[chunk], result)
     return result.reshape(1, 8 * RB, -1)

time: 216 us -> 213 us (0.986)
  starting transfers between devices: 51.3 us -> 55.2 us
  Pallas kernels: 76.3 us -> 73.4 us
    ppermute x29, starting transfers between devices: 51.3 us -> 55.2 us  [send(): return lax.ppermute(value, AXES, pairs)]
    pallas_call x2, Pallas kernels: 17.9 us -> 14.8 us  [attend(): pl.pallas_call(functools.partial(attend_kernel, chunk), grid_spec=pltpu.P...]
  transfers between devices with their start and end apart: 29 -> 29, of which waited for: 16 -> 12; matrix products, arithmetic and copies ran while one was open for 7% -> 7% of each run, Pallas kernels for 34% -> 34%
where the time goes in v7:
time: 213 us; the launch traced here: 212 us
  Pallas kernels  73.4 us (34%)
  waiting for transfers between devices  66 us (31%)
  starting transfers between devices  55.2 us (26%)
  local copies, waits for them, and re-layouts  7.32 us (3%)
  other arithmetic  4.59 us (2%)
  matrix products  4.47 us (2%)
    ppermute x29, waiting for transfers between devices, send(): return lax.ppermute(value, AXES, pairs)  66 us
    ppermute x29, starting transfers between devices, send(): return lax.ppermute(value, AXES, pairs)  55.2 us
    pallas_call x4, Pallas kernels, finish(): pl.pallas_call(finish_kernel, grid_spec=pltpu.PrefetchScalarGridSpec(num_...  19.3 us
    pallas_call x4, Pallas kernels, project(): pl.pallas_call(kernel, grid_spec=pltpu.PrefetchScalarGridSpec(num_scalar_...  16.5 us
    pallas_call x2, Pallas kernels, attend(): pl.pallas_call(functools.partial(attend_kernel, chunk), grid_spec=pltpu.P...  14.8 us
    pallas_call x2, Pallas kernels, reorder(): pl.pallas_call(reorder_kernel, grid_spec=pltpu.PrefetchScalarGridSpec(num...  14.2 us
    pallas_call x1, Pallas kernels, more_queries(): pl.pallas_call(more_queries_kernel, grid=(2,), in_specs=[pl.BlockSpec((ro...  5.79 us
  transfers between devices with their start and end apart: 29, of which 12 were waited for; matrix products, arithmetic and copies ran while one was open for 7% of the time, Pallas kernels for 34%

profile of v7, /device:TPU:1, one launch (start us, length us, event | category | flops | bytes accessed | tf_op | source)
XLA Modules:
  0.0 212.1 jit_solution(14637964726024086834)
XLA Ops:
  0.0 2.5 %collective-permute-start.7 = (bf16[256,5120]{1,0:T(8,128)(2,1)}, bf16[256,5120]{1,0:T(8,128)(2,1)}, u32[]{:S(2)}, u32[]{:S(2)}) collective-permute-start(bf16[256,5120]{1,0:T(8,128)(2,1)} %bitcast.32), channel_id=1, source_target_pairs={{0,1},{1,0},{2,3},{3,2},{4,5},{5,4},{6,7},{7,6},{8,9},{9,8},{10,11... | collective-permute-start | bytes 7864328 | tf_op jit(solution)/shard_map/ppermute | solution.py:67
  6.3 46.8 %conditional.1 = (bf16[2,256,768]{2,1,0:T(8,128)(2,1)}, bf16[256,768]{1,0:T(8,128)(2,1)}, bf16[256,768]{1,0:T(8,128)(2,1)}, bf16[256,768]{1,0:T(8,128)(2,1)}, bf...) conditional(s32[]{:T(128)} %bitcast.12, () %tuple.23, (s32[]{:T(128)}, ...), branch_computations={%region_0.1_spmd, %region_1.3_spmd} | conditional | flops 1016889472 | bytes 49212504 | solution.py:423
  8.0 3.6 %convolution_convert_fusion = bf16[128,384]{1,0:T(8,128)(2,1)S(1)} fusion(bf16[5120,384]{1,0:T(8,128)(2,1)} %get-tuple-element.163, bf16[128,5120]{1,0:T(8,128)(2,1)} %get-tuple-element.160, f32[5120]{0:T(1024)} %get-tuple-element.161, f32[128]{0:T(128)S(1)} %add_rsqrt_fusion), kind=kOutput, calls=%fused_computation.5 | convolution fusion | flops 505987072 | bytes 5362176 | tf_op jit(solution)/shard_map/cond/branch_1_fun/dot_general | solution.py:402
  13.0 2.3 %collective-permute-start = (bf16[128,768]{1,0:T(8,128)(2,1)S(1)}, bf16[128,768]{1,0:T(8,128)(2,1)S(1)}, u32[]{:S(2)}, u32[]{:S(2)}) collective-permute-start(bf16[128,768]{1,0:T(8,128)(2,1)S(1)} %get-tuple-element.191), channel_id=1, source_target_pairs={{0,8},{1,9},{2,10},{3,11},{4,12},{5,13},{6,14},{7,15},{8,0},{9,1},... | collective-permute-start | bytes 589832 | tf_op jit(solution)/shard_map/cond/branch_1_fun/ppermute | solution.py:67
  17.8 7.1 %branch_1_fun.2 = bf16[8,384,640]{2,1,0:T(8,128)(2,1)} custom-call(s32[24]{0:T(128)S(1)} %get-tuple-element.27.meta, bf16[8,384,640]{2,1,0:T(8,128)(2,1)} %bitcast.37), custom_call_target="tpu_custom_call" | custom-call | tf_op jit(solution)/shard_map/cond/branch_1_fun/pallas_call | solution.py:289
  24.9 8.3 %collective-permute-start.2 = (bf16[2,128,768]{2,1,0:T(8,128)(2,1)S(1)}, bf16[2,128,768]{2,1,0:T(8,128)(2,1)}, u32[]{:S(2)}, u32[]{:S(2)}) collective-permute-start(bf16[2,128,768]{2,1,0:T(8,128)(2,1)S(1)} %collective-permute-done.1), channel_id=1, source_target_pairs={{0,8},{1,9},{2,10},{3,11},{4,12},{5,13},{6,14},{7,15},{8,0},{9,1},... | collective-permute-start | bytes 1179656 | tf_op jit(solution)/shard_map/cond/branch_1_fun/ppermute | solution.py:67
  37.1 1.8 dynamic-slice_bitcast_fusion
  39.0 2.5 %collective-permute-start.3 = (bf16[256,768]{1,0:T(8,128)(2,1)}, bf16[256,768]{1,0:T(8,128)(2,1)}, u32[]{:S(2)}, u32[]{:S(2)}) collective-permute-start(bf16[256,768]{1,0:T(8,128)(2,1)} %dynamic-slice_bitcast_fusion), channel_id=1, source_target_pairs={{0,48},{1,49},{2,50},{3,51},{4,52},{5,53},{6,54},{7,55},{8,56},{9,... | collective-permute-start | bytes 1179656 | tf_op jit(solution)/shard_map/cond/branch_1_fun/ppermute | solution.py:67
  42.0 7.1 %branch_1_fun.3 = bf16[8,384,640]{2,1,0:T(8,128)(2,1)} custom-call(s32[24]{0:T(128)S(1)} %get-tuple-element.27.meta, bf16[8,384,640]{2,1,0:T(8,128)(2,1)} %bitcast.38), custom_call_target="tpu_custom_call" | custom-call | tf_op jit(solution)/shard_map/cond/branch_1_fun/pallas_call | solution.py:289
  50.5 2.6 %collective-permute-done.4 = bf16[256,768]{1,0:T(8,128)(2,1)} collective-permute-done((bf16[256,768]{1,0:T(8,128)(2,1)}, bf16[256,768]{1,0:T(8,128)(2,1)}, u32[]{:S(2)}, u32[]{:S(2)}) %collective-permute-start.4) | collective-permute-done | bytes 393248 | tf_op jit(solution)/shard_map/cond/branch_1_fun/ppermute | solution.py:67
  53.1 7.5 %collective-permute-start.6 = (bf16[5120,384]{1,0:T(8,128)(2,1)}, bf16[5120,384]{1,0:T(8,128)(2,1)S(1)}, u32[]{:S(2)}, u32[]{:S(2)}) collective-permute-start(bf16[5120,384]{1,0:T(8,128)(2,1)} %bitcast.25), channel_id=1, source_target_pairs={{0,4},{1,5},{2,6},{3,7},{4,0},{5,1},{6,2},{7,3},{8,11},{9,10},{10,... | collective-permute-start | bytes 11796488 | tf_op jit(solution)/shard_map/ppermute | solution.py:67
  66.1 1.7 copy-done.1
  67.9 3.7 %shard_map.105 = (bf16[4,256,5120]{2,1,0:T(8,128)(2,1)S(1)}, bf16[4,256,384]{2,1,0:T(8,128)(2,1)S(1)}, bf16[4,256,640]{2,1,0:T(8,128)(2,1)S(1)}, bf16[4,256,640]{2,1,0:T(8,128)(2,1)S(1)}) custom-call(s32[24]{0:T(128)S(1)} %dynamic-slice_bitcast_fusion.1.meta, bf16[256,5120]{1,0:T(8,128)(2,1)S(1)} %bitcast.34, f32[1,5120]{1,0:T(1,128)S(1)} %copy-done.2, ...), custom_call_target="tpu_custom_call" | custom-call | flops 1006632960 | bytes 11796480 | tf_op jit(solution)/shard_map/pallas_call | solution.py:120
  71.5 5.4 %shard_map.106 = (bf16[4,256,5120]{2,1,0:T(8,128)(2,1)S(1)}, bf16[4,256,384]{2,1,0:T(8,128)(2,1)S(1)}, bf16[4,256,640]{2,1,0:T(8,128)(2,1)S(1)}, bf16[4,256,640]{2,1,0:T(8,128)(2,1)S(1)}) custom-call(s32[24]{0:T(128)S(1)} %dynamic-slice_bitcast_fusion.1.meta, ...), custom_call_target="tpu_custom_call", output_to_operand_aliasing={{0}: (4, {}), {1}: (5, {}), {2}: (6, {}), {3}: (7, {})} | custom-call | flops 1006632960 | bytes 11796480 | tf_op jit(solution)/shard_map/pallas_call | solution.py:120
  77.0 3.7 %shard_map.107 = (bf16[4,256,5120]{2,1,0:T(8,128)(2,1)S(1)}, bf16[4,256,384]{2,1,0:T(8,128)(2,1)S(1)}, bf16[4,256,640]{2,1,0:T(8,128)(2,1)S(1)}, bf16[4,256,640]{2,1,0:T(8,128)(2,1)S(1)}) custom-call(s32[24]{0:T(128)S(1)} %dynamic-slice_bitcast_fusion.1.meta, ...), custom_call_target="tpu_custom_call", output_to_operand_aliasing={{0}: (4, {}), {1}: (5, {}), {2}: (6, {}), {3}: (7, {})} | custom-call | flops 1006632960 | bytes 11796480 | tf_op jit(solution)/shard_map/pallas_call | solution.py:120
  80.7 3.7 %collective-permute-start.14 = (bf16[256,768]{1,0:T(8,128)(2,1)}, bf16[256,768]{1,0:T(8,128)(2,1)S(1)}, u32[]{:S(2)}, u32[]{:S(2)}) collective-permute-start(bf16[256,768]{1,0:T(8,128)(2,1)} %get-tuple-element.109.o1), channel_id=1, source_target_pairs={{0,8},{1,9},{2,10},{3,11},{4,12},{5,13},{6,14},{7,15},{8,0},{9,1},... | collective-permute-start | bytes 1179656 | tf_op jit(solution)/shard_map/ppermute | solution.py:67
  87.5 7.9 %collective-permute-done.16.o3 = bf16[256,768]{1,0:T(8,128)(2,1)S(1)} collective-permute-done((bf16[256,768]{1,0:T(8,128)(2,1)}, bf16[256,768]{1,0:T(8,128)(2,1)S(1)}, u32[]{:S(2)}, u32[]{:S(2)}) %collective-permute-start.16) | collective-permute-done | bytes 393248 | tf_op jit(solution)/shard_map/ppermute | solution.py:67
  95.4 9.7 %collective-permute-done.12.refs_0_ = bf16[192,5120]{1,0:T(8,128)(2,1)S(1)} collective-permute-done((bf16[192,5120]{1,0:T(8,128)(2,1)S(1)}, bf16[192,5120]{1,0:T(8,128)(2,1)S(1)}, u32[]{:S(2)}, u32[]{:S(2)}) %collective-permute-start.12) | collective-permute-done | bytes 1966112 | tf_op jit(solution)/shard_map/ppermute | solution.py:67
  105.2 9.1 %collective-permute-start.17 = (bf16[256,768]{1,0:T(8,128)(2,1)S(1)}, bf16[256,768]{1,0:T(8,128)(2,1)S(1)}, u32[]{:S(2)}, u32[]{:S(2)}) collective-permute-start(bf16[256,768]{1,0:T(8,128)(2,1)S(1)} %collective-permute-done.16.o3), channel_id=1, source_target_pairs={{0,8},{1,9},{2,10},{3,11},{4,12},{5,13},{6,14},{7,15},{8,0},{9,1},... | collective-permute-start | bytes 1179656 | tf_op jit(solution)/shard_map/ppermute | solution.py:67
  114.3 3.7 %shard_map.108 = (bf16[4,256,5120]{2,1,0:T(8,128)(2,1)S(1)}, bf16[4,256,384]{2,1,0:T(8,128)(2,1)S(1)}, bf16[4,256,640]{2,1,0:T(8,128)(2,1)S(1)}, bf16[4,256,640]{2,1,0:T(8,128)(2,1)S(1)}) custom-call(s32[24]{0:T(128)S(1)} %dynamic-slice_bitcast_fusion.1.meta, ...), custom_call_target="tpu_custom_call", output_to_operand_aliasing={{0}: (5, {}), {1}: (6, {}), {2}: (7, {}), {3}: (8, {})} | custom-call | flops 1006632960 | bytes 11796480 | tf_op jit(solution)/shard_map/pallas_call | solution.py:120
  118.1 5.8 %shard_map.109 = bf16[1024,384]{1,0:T(8,128)(2,1)S(1)} custom-call(bf16[1024,5120]{1,0:T(8,128)(2,1)S(1)} %bitcast.24, bf16[5120,384]{1,0:T(8,128)(2,1)S(1)} %collective-permute-done.6.w_ref), custom_call_target="tpu_custom_call" | custom-call | flops 4026531840 | bytes 14417920 | tf_op jit(solution)/shard_map/pallas_call | solution.py:144
  124.0 7.4 %shard_map.111.c0 = bf16[512,768]{1,0:T(8,128)(2,1)S(1)} custom-call(s32[24]{0:T(128)S(1)} %dynamic-slice_bitcast_fusion.1.meta, bf16[4,256,384]{2,1,0:T(8,128)(2,1)S(1)} %get-tuple-element.123.q_own, bf16[4,256,384]{2,1,0:T(8,128)(2,1)S(1)} %bitcast.30, s32[8,1,256]{2,1,0:T(1,128)S(1)} %bitcast.35, bf16[2,256,768]{2,1,0:T(8,128)(2,1)} %get-tuple-element.126.own0, ...), custom_call_target="tpu_custom_call" | custom-call | flops 1207959552 | bytes 8388608 | tf_op jit(solution)/shard_map/pallas_call | solution.py:261
  133.7 7.4 %shard_map.110.c0 = bf16[512,768]{1,0:T(8,128)(2,1)S(1)} custom-call(s32[24]{0:T(128)S(1)} %dynamic-slice_bitcast_fusion.1.meta, bf16[4,256,384]{2,1,0:T(8,128)(2,1)S(1)} %get-tuple-element.123.q_own, bf16[4,256,384]{2,1,0:T(8,128)(2,1)S(1)} %bitcast.31, s32[8,1,256]{2,1,0:T(1,128)S(1)} %bitcast.36, bf16[2,256,768]{2,1,0:T(8,128)(2,1)} %get-tuple-element.126.own0, ...), custom_call_target="tpu_custom_call" | custom-call | flops 1207959552 | bytes 8388608 | tf_op jit(solution)/shard_map/pallas_call | solution.py:261
  142.1 9.2 %collective-permute-done.24.c3 = bf16[512,768]{1,0:T(8,128)(2,1)S(1)} collective-permute-done((bf16[512,768]{1,0:T(8,128)(2,1)S(1)}, bf16[512,768]{1,0:T(8,128)(2,1)S(1)}, u32[]{:S(2)}, u32[]{:S(2)}) %collective-permute-start.24) | collective-permute-done | bytes 786464 | tf_op jit(solution)/shard_map/ppermute | solution.py:67
  153.6 14.6 %collective-permute-done.19.c3 = bf16[512,768]{1,0:T(8,128)(2,1)S(1)} collective-permute-done((bf16[512,768]{1,0:T(8,128)(2,1)S(1)}, bf16[512,768]{1,0:T(8,128)(2,1)S(1)}, u32[]{:S(2)}, u32[]{:S(2)}) %collective-permute-start.19) | collective-permute-done | bytes 786464 | tf_op jit(solution)/shard_map/ppermute | solution.py:67
  170.4 6.6 %collective-permute-done.25.c2a = bf16[256,768]{1,0:T(8,128)(2,1)S(1)} collective-permute-done((bf16[256,768]{1,0:T(8,128)(2,1)S(1)}, bf16[256,768]{1,0:T(8,128)(2,1)S(1)}, u32[]{:S(2)}, u32[]{:S(2)}) %collective-permute-start.25) | collective-permute-done | bytes 393248 | tf_op jit(solution)/shard_map/ppermute | solution.py:67
  177.0 6.3 %shard_map.112.refs_0_ = bf16[8,256,640]{2,1,0:T(8,128)(2,1)} custom-call(s32[24]{0:T(128)S(1)} %dynamic-slice_bitcast_fusion.1.meta, bf16[512,768]{1,0:T(8,128)(2,1)S(1)} %shard_map.111.c0, bf16[512,768]{1,0:T(8,128)(2,1)S(1)} %collective-permute-done.23.c1, bf16[256,768]{1,0:T(8,128)(2,1)S(1)} %collective-permute-done.25.c2a, ...), custom_call_target="tpu_custom_call" | custom-call | flops 2013265920 | bytes 8388608 | tf_op jit(solution)/shard_map/pallas_call | solution.py:332
  183.3 6.1 %collective-permute-done.22.w = bf16[3072,640]{1,0:T(8,128)(2,1)S(1)} collective-permute-done((bf16[3072,640]{1,0:T(8,128)(2,1)}, bf16[3072,640]{1,0:T(8,128)(2,1)S(1)}, u32[]{:S(2)}, u32[]{:S(2)}) %collective-permute-start.22) | collective-permute-done | bytes 3932192 | tf_op jit(solution)/shard_map/ppermute | solution.py:67
  189.4 3.4 %shard_map.114 = bf16[2,256,640]{2,1,0:T(8,128)(2,1)S(1)} custom-call(s32[24]{0:T(128)S(1)} %dynamic-slice_bitcast_fusion.1.meta, bf16[512,768]{1,0:T(8,128)(2,1)S(1)} %shard_map.111.c0, bf16[512,768]{1,0:T(8,128)(2,1)S(1)} %collective-permute-done.23.c1, bf16[256,768]{1,0:T(8,128)(2,1)S(1)} %collective-permute-done.25.c2a, ...), custom_call_target="tpu_custom_call" | custom-call | flops 2013265920 | bytes 8388608 | tf_op jit(solution)/shard_map/pallas_call | solution.py:332
  194.5 3.4 %shard_map.113 = bf16[2,256,640]{2,1,0:T(8,128)(2,1)S(1)} custom-call(s32[24]{0:T(128)S(1)} %dynamic-slice_bitcast_fusion.1.meta, bf16[512,768]{1,0:T(8,128)(2,1)S(1)} %shard_map.110.c0, bf16[512,768]{1,0:T(8,128)(2,1)S(1)} %collective-permute-done.18.c1, bf16[256,768]{1,0:T(8,128)(2,1)S(1)} %collective-permute-done.20.c2a, ...), custom_call_target="tpu_custom_call" | custom-call | flops 2013265920 | bytes 8388608 | tf_op jit(solution)/shard_map/pallas_call | solution.py:332
  199.0 6.3 %shard_map.115.prior = bf16[8,256,640]{2,1,0:T(8,128)(2,1)} custom-call(s32[24]{0:T(128)S(1)} %dynamic-slice_bitcast_fusion.1.meta, bf16[512,768]{1,0:T(8,128)(2,1)S(1)} %shard_map.110.c0, bf16[512,768]{1,0:T(8,128)(2,1)S(1)} %collective-permute-done.18.c1, bf16[256,768]{1,0:T(8,128)(2,1)S(1)} %collective-permute-done.20.c2a, ...), custom_call_target="tpu_custom_call", output_to_operand_aliasing={{}: (8, {})} | custom-call | flops 2013265920 | bytes 8388608 | tf_op jit(solution)/shard_map/pallas_call | solution.py:332
  206.7 3.9 %collective-permute-done.27.got = bf16[2,256,640]{2,1,0:T(8,128)(2,1)S(1)} collective-permute-done((bf16[2,256,640]{2,1,0:T(8,128)(2,1)S(1)}, bf16[2,256,640]{2,1,0:T(8,128)(2,1)S(1)}, u32[]{:S(2)}, u32[]{:S(2)}) %collective-permute-start.27) | collective-permute-done | bytes 655392 | tf_op jit(solution)/shard_map/ppermute | solution.py:67
  (74 shorter events, 36.8 us)
Async XLA Ops:
  0.0 60.6 %collective-permute-start.7 = (bf16[256,5120]{1,0:T(8,128)(2,1)}, bf16[256,5120]{1,0:T(8,128)(2,1)}, u32[]{:S(2)}, u32[]{:S(2)}) collective-permute-start(bf16[256,5120]{1,0:T(8,128)(2,1)} %bitcast.32), channel_id=1, source_target_pairs={{0,1},{1,0},{2,3},{3,2},{4,5},{5,4},{6,7},{7,6},{8,9},{9,8},{10,11... | collective-permute-start | bytes 7864328 | tf_op jit(solution)/shard_map/ppermute | solution.py:67
  2.5 58.1 %collective-permute-start.8 = (bf16[256,5120]{1,0:T(8,128)(2,1)}, bf16[256,5120]{1,0:T(8,128)(2,1)S(1)}, u32[]{:S(2)}, u32[]{:S(2)}) collective-permute-start(bf16[256,5120]{1,0:T(8,128)(2,1)} %bitcast.33), channel_id=1, source_target_pairs={{0,3},{1,2},{2,1},{3,0},{4,7},{5,6},{6,5},{7,4},{8,12},{9,13},{10,... | collective-permute-start | bytes 7864328 | tf_op jit(solution)/shard_map/ppermute | solution.py:67
  13.0 3.3 %collective-permute-start = (bf16[128,768]{1,0:T(8,128)(2,1)S(1)}, bf16[128,768]{1,0:T(8,128)(2,1)S(1)}, u32[]{:S(2)}, u32[]{:S(2)}) collective-permute-start(bf16[128,768]{1,0:T(8,128)(2,1)S(1)} %get-tuple-element.191), channel_id=1, source_target_pairs={{0,8},{1,9},{2,10},{3,11},{4,12},{5,13},{6,14},{7,15},{8,0},{9,1},... | collective-permute-start | bytes 589832 | tf_op jit(solution)/shard_map/cond/branch_1_fun/ppermute | solution.py:67
  17.2 7.8 %collective-permute-start.1 = (bf16[2,128,768]{2,1,0:T(8,128)(2,1)}, bf16[2,128,768]{2,1,0:T(8,128)(2,1)S(1)}, u32[]{:S(2)}, u32[]{:S(2)}) collective-permute-start(bf16[2,128,768]{2,1,0:T(8,128)(2,1)} %maximum_select_fusion.2), channel_id=1, source_target_pairs={{0,64},{1,65},{2,66},{3,67},{4,68},{5,69},{6,70},{7,71},{16,80},{1... | collective-permute-start | bytes 1179656 | tf_op jit(solution)/shard_map/cond/branch_1_fun/ppermute | solution.py:67
  24.9 9.7 %collective-permute-start.2 = (bf16[2,128,768]{2,1,0:T(8,128)(2,1)S(1)}, bf16[2,128,768]{2,1,0:T(8,128)(2,1)}, u32[]{:S(2)}, u32[]{:S(2)}) collective-permute-start(bf16[2,128,768]{2,1,0:T(8,128)(2,1)S(1)} %collective-permute-done.1), channel_id=1, source_target_pairs={{0,8},{1,9},{2,10},{3,11},{4,12},{5,13},{6,14},{7,15},{8,0},{9,1},... | collective-permute-start | bytes 1179656 | tf_op jit(solution)/shard_map/cond/branch_1_fun/ppermute | solution.py:67
  36.7 16.4 %collective-permute-start.5 = (bf16[2,256,768]{2,1,0:T(8,128)(2,1)}, bf16[2,256,768]{2,1,0:T(8,128)(2,1)}, u32[]{:S(2)}, u32[]{:S(2)}) collective-permute-start(bf16[2,256,768]{2,1,0:T(8,128)(2,1)} %maximum_select_fusion), channel_id=1, source_target_pairs={{0,4},{1,5},{2,6},{3,7},{4,0},{5,1},{6,2},{7,3},{8,11},{9,10},{10,... | collective-permute-start | bytes 2359304 | tf_op jit(solution)/shard_map/cond/branch_1_fun/ppermute | solution.py:67
  39.0 11.5 %collective-permute-start.3 = (bf16[256,768]{1,0:T(8,128)(2,1)}, bf16[256,768]{1,0:T(8,128)(2,1)}, u32[]{:S(2)}, u32[]{:S(2)}) collective-permute-start(bf16[256,768]{1,0:T(8,128)(2,1)} %dynamic-slice_bitcast_fusion), channel_id=1, source_target_pairs={{0,48},{1,49},{2,50},{3,51},{4,52},{5,53},{6,54},{7,55},{8,56},{9,... | collective-permute-start | bytes 1179656 | tf_op jit(solution)/shard_map/cond/branch_1_fun/ppermute | solution.py:67
  41.4 11.6 %collective-permute-start.4 = (bf16[256,768]{1,0:T(8,128)(2,1)}, bf16[256,768]{1,0:T(8,128)(2,1)}, u32[]{:S(2)}, u32[]{:S(2)}) collective-permute-start(bf16[256,768]{1,0:T(8,128)(2,1)} %dynamic-slice_bitcast_fusion), channel_id=1, source_target_pairs={{0,32},{1,33},{2,34},{3,35},{4,36},{5,37},{6,38},{7,39},{8,40},{9,... | collective-permute-start | bytes 1179656 | tf_op jit(solution)/shard_map/cond/branch_1_fun/ppermute | solution.py:67
  53.1 64.9 %collective-permute-start.6 = (bf16[5120,384]{1,0:T(8,128)(2,1)}, bf16[5120,384]{1,0:T(8,128)(2,1)S(1)}, u32[]{:S(2)}, u32[]{:S(2)}) collective-permute-start(bf16[5120,384]{1,0:T(8,128)(2,1)} %bitcast.25), channel_id=1, source_target_pairs={{0,4},{1,5},{2,6},{3,7},{4,0},{5,1},{6,2},{7,3},{8,11},{9,10},{10,... | collective-permute-start | bytes 11796488 | tf_op jit(solution)/shard_map/ppermute | solution.py:67
  60.6 5.5 %copy-start = (bf16[1,5120,384]{2,1,0:T(8,128)(2,1)S(1)}, bf16[1,5120,384]{2,1,0:T(8,128)(2,1)}, u32[]{:S(2)}) copy-start(bf16[1,5120,384]{2,1,0:T(8,128)(2,1)} %param.18) | copy-start | bytes 11796484
  60.6 5.5 %copy-start.2 = (f32[1,5120]{1,0:T(1,128)S(1)}, f32[1,5120]{1,0:T(1,128)}, u32[]{:S(2)}) copy-start(f32[1,5120]{1,0:T(1,128)} %refs_2_.1) | copy-start | bytes 61444
  60.7 44.5 %collective-permute-start.12 = (bf16[192,5120]{1,0:T(8,128)(2,1)S(1)}, bf16[192,5120]{1,0:T(8,128)(2,1)S(1)}, u32[]{:S(2)}, u32[]{:S(2)}) collective-permute-start(bf16[192,5120]{1,0:T(8,128)(2,1)S(1)} %slice.22), channel_id=1, source_target_pairs={{0,1},{1,0},{2,3},{3,2},{4,5},{5,4},{6,7},{7,6},{8,9},{9,8},{10,11... | collective-permute-start | bytes 5898248 | tf_op jit(solution)/shard_map/ppermute | solution.py:67
  60.8 19.9 %collective-permute-start.10 = (bf16[2,256,768]{2,1,0:T(8,128)(2,1)}, bf16[2,256,768]{2,1,0:T(8,128)(2,1)S(1)}, u32[]{:S(2)}, u32[]{:S(2)}) collective-permute-start(bf16[2,256,768]{2,1,0:T(8,128)(2,1)} %get-tuple-element.108.other0), channel_id=1, source_target_pairs={{0,16},{1,17},{2,18},{3,19},{4,20},{5,21},{6,22},{7,23},{8,24},{9,... | collective-permute-start | bytes 2359304 | tf_op jit(solution)/shard_map/ppermute | solution.py:67
  62.4 18.3 %collective-permute-start.9 = (bf16[2,256,768]{2,1,0:T(8,128)(2,1)}, bf16[2,256,768]{2,1,0:T(8,128)(2,1)S(1)}, u32[]{:S(2)}, u32[]{:S(2)}) collective-permute-start(bf16[2,256,768]{2,1,0:T(8,128)(2,1)} %get-tuple-element.108.other0), channel_id=1, source_target_pairs={{0,48},{1,49},{2,50},{3,51},{4,52},{5,53},{6,54},{7,55},{8,56},{9,... | collective-permute-start | bytes 2359304 | tf_op jit(solution)/shard_map/ppermute | solution.py:67
  65.2 19.3 %collective-permute-start.13 = (bf16[64,5120]{1,0:T(8,128)(2,1)S(1)}, bf16[64,5120]{1,0:T(8,128)(2,1)S(1)}, u32[]{:S(2)}, u32[]{:S(2)}) collective-permute-start(bf16[64,5120]{1,0:T(8,128)(2,1)S(1)} %slice.23), channel_id=1, source_target_pairs={{0,3},{1,2},{2,1},{3,0},{4,7},{5,6},{6,5},{7,4},{8,12},{9,13},{10,... | collective-permute-start | bytes 1966088 | tf_op jit(solution)/shard_map/ppermute | solution.py:67
  80.7 5.3 %collective-permute-start.14 = (bf16[256,768]{1,0:T(8,128)(2,1)}, bf16[256,768]{1,0:T(8,128)(2,1)S(1)}, u32[]{:S(2)}, u32[]{:S(2)}) collective-permute-start(bf16[256,768]{1,0:T(8,128)(2,1)} %get-tuple-element.109.o1), channel_id=1, source_target_pairs={{0,8},{1,9},{2,10},{3,11},{4,12},{5,13},{6,14},{7,15},{8,0},{9,1},... | collective-permute-start | bytes 1179656 | tf_op jit(solution)/shard_map/ppermute | solution.py:67
  84.4 3.1 %collective-permute-start.15 = (bf16[256,768]{1,0:T(8,128)(2,1)}, bf16[256,768]{1,0:T(8,128)(2,1)S(1)}, u32[]{:S(2)}, u32[]{:S(2)}) collective-permute-start(bf16[256,768]{1,0:T(8,128)(2,1)} %get-tuple-element.110.o2), channel_id=1, source_target_pairs={{0,8},{1,9},{2,10},{3,11},{4,12},{5,13},{6,14},{7,15},{8,0},{9,1},... | collective-permute-start | bytes 1179656 | tf_op jit(solution)/shard_map/ppermute | solution.py:67
  84.5 10.9 %collective-permute-start.16 = (bf16[256,768]{1,0:T(8,128)(2,1)}, bf16[256,768]{1,0:T(8,128)(2,1)S(1)}, u32[]{:S(2)}, u32[]{:S(2)}) collective-permute-start(bf16[256,768]{1,0:T(8,128)(2,1)} %get-tuple-element.111), channel_id=1, source_target_pairs={{0,16},{1,17},{2,18},{3,19},{4,20},{5,21},{6,22},{7,23},{8,24},{9,... | collective-permute-start | bytes 1179656 | tf_op jit(solution)/shard_map/ppermute | solution.py:67
  86.0 32.1 %collective-permute-start.11 = (bf16[2,256,768]{2,1,0:T(8,128)(2,1)}, bf16[2,256,768]{2,1,0:T(8,128)(2,1)S(1)}, u32[]{:S(2)}, u32[]{:S(2)}) collective-permute-start(bf16[2,256,768]{2,1,0:T(8,128)(2,1)} %get-tuple-element.108.other0), channel_id=1, source_target_pairs={{0,32},{1,33},{2,34},{3,35},{4,36},{5,37},{6,38},{7,39},{8,40},{9,... | collective-permute-start | bytes 2359304 | tf_op jit(solution)/shard_map/ppermute | solution.py:67
  105.2 12.8 %collective-permute-start.17 = (bf16[256,768]{1,0:T(8,128)(2,1)S(1)}, bf16[256,768]{1,0:T(8,128)(2,1)S(1)}, u32[]{:S(2)}, u32[]{:S(2)}) collective-permute-start(bf16[256,768]{1,0:T(8,128)(2,1)S(1)} %collective-permute-done.16.o3), channel_id=1, source_target_pairs={{0,8},{1,9},{2,10},{3,11},{4,12},{5,13},{6,14},{7,15},{8,0},{9,1},... | collective-permute-start | bytes 1179656 | tf_op jit(solution)/shard_map/ppermute | solution.py:67
  118.0 71.3 %collective-permute-start.22 = (bf16[3072,640]{1,0:T(8,128)(2,1)}, bf16[3072,640]{1,0:T(8,128)(2,1)S(1)}, u32[]{:S(2)}, u32[]{:S(2)}) collective-permute-start(bf16[3072,640]{1,0:T(8,128)(2,1)} %get-tuple-element.134), channel_id=1, source_target_pairs={{0,4},{1,5},{2,6},{3,7},{4,0},{5,1},{6,2},{7,3},{8,11},{9,10},{10,... | collective-permute-start | bytes 11796488 | tf_op jit(solution)/shard_map/ppermute | solution.py:67
  118.1 5.8 %copy-start.3 = (s32[2048]{0:T(1024)S(1)}, s32[2048]{0:T(1024)}, u32[]{:S(2)}) copy-start(s32[2048]{0:T(1024)} %param.20) | copy-start | bytes 24580
  131.4 19.9 %collective-permute-start.24 = (bf16[512,768]{1,0:T(8,128)(2,1)S(1)}, bf16[512,768]{1,0:T(8,128)(2,1)S(1)}, u32[]{:S(2)}, u32[]{:S(2)}) collective-permute-start(bf16[512,768]{1,0:T(8,128)(2,1)S(1)} %shard_map.111.c0), channel_id=1, source_target_pairs={{0,3},{1,2},{2,1},{3,0},{4,7},{5,6},{6,5},{7,4},{8,12},{9,13},{10,... | collective-permute-start | bytes 2359304 | tf_op jit(solution)/shard_map/ppermute | solution.py:67
  133.0 19.0 %collective-permute-start.23 = (bf16[512,768]{1,0:T(8,128)(2,1)S(1)}, bf16[512,768]{1,0:T(8,128)(2,1)S(1)}, u32[]{:S(2)}, u32[]{:S(2)}) collective-permute-start(bf16[512,768]{1,0:T(8,128)(2,1)S(1)} %shard_map.111.c0), channel_id=1, source_target_pairs={{0,1},{1,0},{2,3},{3,2},{4,5},{5,4},{6,7},{7,6},{8,9},{9,8},{10,11... | collective-permute-start | bytes 2359304 | tf_op jit(solution)/shard_map/ppermute | solution.py:67
  141.1 27.0 %collective-permute-start.19 = (bf16[512,768]{1,0:T(8,128)(2,1)S(1)}, bf16[512,768]{1,0:T(8,128)(2,1)S(1)}, u32[]{:S(2)}, u32[]{:S(2)}) collective-permute-start(bf16[512,768]{1,0:T(8,128)(2,1)S(1)} %shard_map.110.c0), channel_id=1, source_target_pairs={{0,3},{1,2},{2,1},{3,0},{4,7},{5,6},{6,5},{7,4},{8,12},{9,13},{10,... | collective-permute-start | bytes 2359304 | tf_op jit(solution)/shard_map/ppermute | solution.py:67
  141.3 27.5 %collective-permute-start.18 = (bf16[512,768]{1,0:T(8,128)(2,1)S(1)}, bf16[512,768]{1,0:T(8,128)(2,1)S(1)}, u32[]{:S(2)}, u32[]{:S(2)}) collective-permute-start(bf16[512,768]{1,0:T(8,128)(2,1)S(1)} %shard_map.110.c0), channel_id=1, source_target_pairs={{0,1},{1,0},{2,3},{3,2},{4,5},{5,4},{6,7},{7,6},{8,9},{9,8},{10,11... | collective-permute-start | bytes 2359304 | tf_op jit(solution)/shard_map/ppermute | solution.py:67
  151.3 25.7 %collective-permute-start.25 = (bf16[256,768]{1,0:T(8,128)(2,1)S(1)}, bf16[256,768]{1,0:T(8,128)(2,1)S(1)}, u32[]{:S(2)}, u32[]{:S(2)}) collective-permute-start(bf16[256,768]{1,0:T(8,128)(2,1)S(1)} %slice.30), channel_id=1, source_target_pairs={{0,1},{1,0},{2,3},{3,2},{4,5},{5,4},{6,7},{7,6},{8,9},{9,8},{10,11... | collective-permute-start | bytes 1179656 | tf_op jit(solution)/shard_map/ppermute | solution.py:67
  152.0 25.0 %collective-permute-start.26 = (bf16[256,768]{1,0:T(8,128)(2,1)S(1)}, bf16[256,768]{1,0:T(8,128)(2,1)S(1)}, u32[]{:S(2)}, u32[]{:S(2)}) collective-permute-start(bf16[256,768]{1,0:T(8,128)(2,1)S(1)} %slice.31), channel_id=1, source_target_pairs={{0,3},{1,2},{2,1},{3,0},{4,7},{5,6},{6,5},{7,4},{8,12},{9,13},{10,... | collective-permute-start | bytes 1179656 | tf_op jit(solution)/shard_map/ppermute | solution.py:67
  168.2 26.3 %collective-permute-start.20 = (bf16[256,768]{1,0:T(8,128)(2,1)S(1)}, bf16[256,768]{1,0:T(8,128)(2,1)S(1)}, u32[]{:S(2)}, u32[]{:S(2)}) collective-permute-start(bf16[256,768]{1,0:T(8,128)(2,1)S(1)} %slice.28), channel_id=1, source_target_pairs={{0,1},{1,0},{2,3},{3,2},{4,5},{5,4},{6,7},{7,6},{8,9},{9,8},{10,11... | collective-permute-start | bytes 1179656 | tf_op jit(solution)/shard_map/ppermute | solution.py:67
  168.9 25.6 %collective-permute-start.21 = (bf16[256,768]{1,0:T(8,128)(2,1)S(1)}, bf16[256,768]{1,0:T(8,128)(2,1)S(1)}, u32[]{:S(2)}, u32[]{:S(2)}) collective-permute-start(bf16[256,768]{1,0:T(8,128)(2,1)S(1)} %slice.29), channel_id=1, source_target_pairs={{0,3},{1,2},{2,1},{3,0},{4,7},{5,6},{6,5},{7,4},{8,12},{9,13},{10,... | collective-permute-start | bytes 1179656 | tf_op jit(solution)/shard_map/ppermute | solution.py:67
  192.8 12.5 %collective-permute-start.28 = (bf16[2,256,640]{2,1,0:T(8,128)(2,1)S(1)}, bf16[2,256,640]{2,1,0:T(8,128)(2,1)S(1)}, u32[]{:S(2)}, u32[]{:S(2)}) collective-permute-start(bf16[2,256,640]{2,1,0:T(8,128)(2,1)S(1)} %shard_map.114), channel_id=1, source_target_pairs={{0,4},{1,5},{2,6},{3,7},{4,0},{5,1},{6,2},{7,3},{8,11},{9,10},{10,... | collective-permute-start | bytes 1966088 | tf_op jit(solution)/shard_map/ppermute | solution.py:67
  197.9 12.6 %collective-permute-start.27 = (bf16[2,256,640]{2,1,0:T(8,128)(2,1)S(1)}, bf16[2,256,640]{2,1,0:T(8,128)(2,1)S(1)}, u32[]{:S(2)}, u32[]{:S(2)}) collective-permute-start(bf16[2,256,640]{2,1,0:T(8,128)(2,1)S(1)} %shard_map.113), channel_id=1, source_target_pairs={{0,4},{1,5},{2,6},{3,7},{4,0},{5,1},{6,2},{7,3},{8,11},{9,10},{10,... | collective-permute-start | bytes 1966088 | tf_op jit(solution)/shard_map/ppermute | solution.py:67
  (4 other events, 13.5 us)

commit v8 on v7

--- a/solution.py
+++ b/solution.py
@@ -9,6 +9,7 @@
 
 HD = 128
 RB = 256
+CUT = 384
 BF = jnp.bfloat16
 F32 = jnp.float32
 AXES = ("section", "ctx")
@@ -303,7 +304,7 @@
 def finish_kernel(meta, c0, c1, c2a, c2b, c3, w, res, *refs):
     out = refs[-1]
     t = pl.program_id(0)
-    far = jnp.where(t == 0, c2a[...], c2b[...])
+    far = jnp.where(t == 0, c2a[:RB, :], jnp.concatenate([c2a[RB:, :], c2b[...]], axis=0))
     n = far.shape[1]
     total = res[0].astype(F32)
     for j, c in enumerate((c0[...], c1[...], far, c3[...])):
@@ -315,9 +316,9 @@
     depth, width = w.shape
     n = depth // 4
     tile = pl.BlockSpec((RB, n), lambda t, m: (t, 0))
-    fixed = pl.BlockSpec((RB, n), lambda t, m: (0, 0))
+    fixed = lambda a: pl.BlockSpec(a.shape, lambda t, m: (0, 0))
     ins = list(parts) + [w, res]
-    specs = [tile, tile, fixed, fixed, tile]
+    specs = [tile, tile, fixed(parts[2]), fixed(parts[3]), tile]
     specs.append(pl.BlockSpec(w.shape, lambda t, m: (0, 0), pipeline_mode=pl.Buffered(1)))
     specs.append(pl.BlockSpec((1, RB, width), lambda t, m: (m[SLOT + 2 * chunk + t], 0, 0)))
     aliases = {}
@@ -404,44 +405,53 @@
         kv2 = send(kv, CORE)
         pair = jnp.where(core == 0, jnp.stack([kv, kv2]), jnp.stack([kv2, kv]))
         far = send(pair, FAR_Y)
+        near2 = send(pair, PARTNER)
         far, w_mine = lax.optimization_barrier((far, reorder(meta, w_out, 0)))
         far = jnp.where(core == 0, far, send(far, CORE))
-        piece = jnp.where(y_hi == 0, jnp.stack([pair, far]), jnp.stack([far, pair]))
-        piece = piece.reshape(2, 2 * kv.shape[0], kv.shape[1])
-        piece2 = send(piece, PARTNER)
+        far2 = send(far, PARTNER)
+
+        def in_order(near, far):
+            both = jnp.where(y_hi == 0, jnp.stack([near, far]), jnp.stack([far, near]))
+            return both.reshape(2, 2 * kv.shape[0], kv.shape[1])
+
+        piece = in_order(pair, far)
         share = lax.dynamic_index_in_dim(piece, core, 0, keepdims=False)
-        o1 = send(share, X_PREV)
-        o2 = send(share, X_FAR)
-        return piece, share, o1, o2, piece2, w_mine, reorder(meta, w_out, 1)
+        return piece, share, in_order(near2, far2), w_mine
 
     def nothing(last_hidden, w_key, w_value, w_out):
         two = jnp.zeros((2, 2 * last_hidden.shape[0], 2 * w_key.shape[1]), BF)
         w_none = jnp.zeros((w_out.shape[0] * w_out.shape[1], w_out.shape[2]), BF)
-        return two, two[0], two[0], two[0], two, w_none, w_none
+        return two, two[0], two, w_none
 
     w_o_r = w_o.reshape(8, w_q.shape[1], width)
-    piece, share, o1, o2, piece2, w_o_mine, w_o_theirs = lax.cond(
+    piece, share, piece2, w_o_mine = lax.cond(
         segment_ids[0] >= 0, cache, nothing, last_hidden, w_key, w_value, w_o_r
     )
     w_q2 = send(after(w_q, piece2), PARTNER)
-    x_in, x_out, piece2, share = lax.optimization_barrier((x_in, x_out, piece2, share))
-    most = RB * 3 // 4
+    o1 = send(share, X_PREV)
+    o3 = send(share, X_NEXT)
+    o2 = send(after(share, o1, o3), X_FAR)
+    x0, w_o_r = after(x0, share), after(w_o_r, share)
+    w_o_theirs = reorder(meta, w_o_r, 1)
+    state = project(meta, [x0], query_gain, w_q, 0, width)
+    x_in, x_out, piece2, o1, o2, o3, w_o_theirs, *state = lax.optimization_barrier(
+        (x_in, x_out, piece2, o1, o2, o3, w_o_theirs, *state)
+    )
+    most = RB * 5 // 8
     xo_a = send(x_out[:most], IN)
     xo_b = send(x_in[most:], OUT)
     t1 = send(piece2, X_PREV)
     t3 = send(piece2, X_NEXT)
-    state = project(meta, [after(x0, x_in, x_out)], query_gain, w_q, 0, width)
     state = project(meta, [x_in], query_gain, w_q, 1, width, state)
     state = project(meta, [x_out], query_gain, w_q, 3, width, state)
-    t1, t3, o1, o2, piece2, share, *state = lax.optimization_barrier(
-        (t1, t3, o1, o2, piece2, share, *state)
-    )
-    o3 = send(share, X_NEXT)
+    t1, t3, o1, o2, o3, piece2, *state = lax.optimization_barrier(
+        (t1, t3, o1, o2, o3, piece2, *state)
+    )
     t2 = send(piece2, X_FAR)
     o1b = send(o1, CORE)
     o2b = send(o2, CORE)
-    xo_a, xo_b, o1b, o2b, o3 = lax.optimization_barrier((xo_a, xo_b, o1b, o2b, o3))
     o3b = send(o3, CORE)
+    xo_a, xo_b, o1b, o2b, o3b = lax.optimization_barrier((xo_a, xo_b, o1b, o2b, o3b))
     normed, q_own, res_own, res_other = project(
         meta, [xo_a, xo_b], query_gain, w_q, 2, width, state
     )
@@ -458,8 +468,9 @@
         own = attend(meta, chunk, q_own, q_other, seg_row, pieces)
         c_in = send(own, IN)
         c_out = send(own, OUT)
-        co_a = send(c_out[:RB], IN)
-        co_b = send(c_in[RB:], OUT)
+        c_in, c_out = lax.optimization_barrier((c_in, c_out))
+        co_a = send(c_out[:CUT], IN)
+        co_b = send(c_in[CUT:], OUT)
         parts.append((own, c_in, co_a, co_b, c_out))
     result = finish(meta, 0, parts[0], w_o_mine, res_own, 8)
     w_o2, result = lax.optimization_barrier((w_o2, result))

time: 213 us -> 216 us (1.014)
  starting transfers between devices: 55.2 us -> 50.2 us
  waiting for transfers between devices: 66 us -> 70.5 us
  local copies, waits for them, and re-layouts: 7.32 us -> 10.4 us
    ppermute x29 -> x30, starting transfers between devices: 55.2 us -> 50.2 us  [send(): return lax.ppermute(value, AXES, pairs)]
    ppermute x29 -> x30, waiting for transfers between devices: 66 us -> 70.5 us  [send(): return lax.ppermute(value, AXES, pairs)]
    pallas_call x4, Pallas kernels: 19.3 us -> 15.1 us  [finish(): pl.pallas_call(finish_kernel, grid_spec=pltpu.PrefetchScalarGridSpec(num_...]
    unnamed x8 -> x16, local copies, waits for them, and re-layouts: 1.76 us -> 4.76 us
  transfers between devices with their start and end apart: 29 -> 30, of which waited for: 12 -> 20; matrix products, arithmetic and copies ran while one was open for 7% -> 7% of each run, Pallas kernels for 34% -> 33%
where the time goes in v8:
time: 216 us; the launch traced here: 214 us
  Pallas kernels  72.3 us (33%)
  waiting for transfers between devices  70.5 us (33%)
  starting transfers between devices  50.2 us (23%)
  local copies, waits for them, and re-layouts  10.4 us (5%)
  other arithmetic  5.1 us (2%)
  matrix products  4.47 us (2%)
    ppermute x30, waiting for transfers between devices, send(): return lax.ppermute(value, AXES, pairs)  70.5 us
    ppermute x30, starting transfers between devices, send(): return lax.ppermute(value, AXES, pairs)  50.2 us
    pallas_call x4, Pallas kernels, project(): pl.pallas_call(kernel, grid_spec=pltpu.PrefetchScalarGridSpec(num_scalar_...  16.5 us
    pallas_call x2, Pallas kernels, attend(): pl.pallas_call(functools.partial(attend_kernel, chunk), grid_spec=pltpu.P...  15.9 us
    pallas_call x4, Pallas kernels, finish(): pl.pallas_call(finish_kernel, grid_spec=pltpu.PrefetchScalarGridSpec(num_...  15.1 us
    pallas_call x2, Pallas kernels, reorder(): pl.pallas_call(reorder_kernel, grid_spec=pltpu.PrefetchScalarGridSpec(num...  14.2 us
    pallas_call x1, Pallas kernels, more_queries(): pl.pallas_call(more_queries_kernel, grid=(2,), in_specs=[pl.BlockSpec((ro...  7.87 us
    unnamed x16, local copies, waits for them, and re-layouts  4.76 us
  transfers between devices with their start and end apart: 30, of which 20 were waited for; matrix products, arithmetic and copies ran while one was open for 7% of the time, Pallas kernels for 33%

profile of v8, /device:TPU:1, one launch (start us, length us, event | category | flops | bytes accessed | tf_op | source)
XLA Modules:
  0.0 214.0 jit_solution(14543752108918226936)
XLA Ops:
  6.3 40.8 %conditional.1 = (bf16[2,256,768]{2,1,0:T(8,128)(2,1)}, bf16[256,768]{1,0:T(8,128)(2,1)}, bf16[2,256,768]{2,1,0:T(8,128)(2,1)S(1)}, bf16[3072,640]{1,0:T(8,128)(2,1)}) conditional(s32[]{:T(128)} %bitcast.12, () %tuple.27, (s32[]{:T(128)}, pred[]{:T(512)}, bf16[128,5120]{1,0:T(8,128)(2,1)}, f32[5120]{0:T(1024)}, bf16[5120,384]{1,0:T(8,128)(2,1)}, ...), branch_computations={%region_0.1_spmd, %region_1.3_spmd} | conditional | flops 1018069120 | bytes 47639576 | solution.py:427
  8.0 3.6 %convolution_convert_fusion = bf16[128,384]{1,0:T(8,128)(2,1)S(1)} fusion(bf16[5120,384]{1,0:T(8,128)(2,1)} %get-tuple-element.182, bf16[128,5120]{1,0:T(8,128)(2,1)} %get-tuple-element.179, f32[5120]{0:T(1024)} %get-tuple-element.180, f32[128]{0:T(128)S(1)} %add_rsqrt_fusion), kind=kOutput, calls=%fused_computation.5 | convolution fusion | flops 505987072 | bytes 5362176 | tf_op jit(solution)/shard_map/cond/branch_1_fun/dot_general | solution.py:403
  18.5 7.1 %branch_1_fun.1 = bf16[8,384,640]{2,1,0:T(8,128)(2,1)} custom-call(s32[24]{0:T(128)S(1)} %get-tuple-element.27.meta, bf16[8,384,640]{2,1,0:T(8,128)(2,1)} %get-tuple-element.28.w), custom_call_target="tpu_custom_call" | custom-call | tf_op jit(solution)/shard_map/cond/branch_1_fun/pallas_call | solution.py:290
  25.6 7.6 %collective-permute-start.2 = (bf16[2,128,768]{2,1,0:T(8,128)(2,1)}, bf16[2,128,768]{2,1,0:T(8,128)(2,1)S(1)}, u32[]{:S(2)}, u32[]{:S(2)}) collective-permute-start(bf16[2,128,768]{2,1,0:T(8,128)(2,1)} %collective-permute-done.1), channel_id=1, source_target_pairs={{0,8},{1,9},{2,10},{3,11},{4,12},{5,13},{6,14},{7,15},{8,0},{9,1},... | collective-permute-start | bytes 1179656 | tf_op jit(solution)/shard_map/cond/branch_1_fun/ppermute | solution.py:68
  38.9 2.5 %collective-permute-done.3 = bf16[2,128,768]{2,1,0:T(8,128)(2,1)} collective-permute-done((bf16[2,128,768]{2,1,0:T(8,128)(2,1)}, bf16[2,128,768]{2,1,0:T(8,128)(2,1)}, u32[]{:S(2)}, u32[]{:S(2)}) %collective-permute-start.3) | collective-permute-done | bytes 393248 | tf_op jit(solution)/shard_map/cond/branch_1_fun/ppermute | solution.py:68
  41.4 4.2 %collective-permute-done.4 = bf16[2,128,768]{2,1,0:T(8,128)(2,1)} collective-permute-done((bf16[2,128,768]{2,1,0:T(8,128)(2,1)S(1)}, bf16[2,128,768]{2,1,0:T(8,128)(2,1)}, u32[]{:S(2)}, u32[]{:S(2)}) %collective-permute-start.4) | collective-permute-done | bytes 393248 | tf_op jit(solution)/shard_map/cond/branch_1_fun/ppermute | solution.py:68
  50.7 7.1 %collective-permute-done.8.o1 = bf16[256,768]{1,0:T(8,128)(2,1)S(1)} collective-permute-done((bf16[256,768]{1,0:T(8,128)(2,1)}, bf16[256,768]{1,0:T(8,128)(2,1)S(1)}, u32[]{:S(2)}, u32[]{:S(2)}) %collective-permute-start.8) | collective-permute-done | bytes 393248 | tf_op jit(solution)/shard_map/ppermute | solution.py:68
  57.8 3.0 %collective-permute-done.9.o3 = bf16[256,768]{1,0:T(8,128)(2,1)S(1)} collective-permute-done((bf16[256,768]{1,0:T(8,128)(2,1)}, bf16[256,768]{1,0:T(8,128)(2,1)S(1)}, u32[]{:S(2)}, u32[]{:S(2)}) %collective-permute-start.9) | collective-permute-done | bytes 393248 | tf_op jit(solution)/shard_map/ppermute | solution.py:68
  60.8 7.1 %shard_map.104 = bf16[8,384,640]{2,1,0:T(8,128)(2,1)} custom-call(s32[24]{0:T(128)S(1)} %dynamic-slice_bitcast_fusion.1.meta, bf16[8,384,640]{2,1,0:T(8,128)(2,1)} %bitcast.41), custom_call_target="tpu_custom_call" | custom-call | tf_op jit(solution)/shard_map/pallas_call | solution.py:290
  71.8 3.7 %shard_map.105 = (bf16[4,256,5120]{2,1,0:T(8,128)(2,1)S(1)}, bf16[4,256,384]{2,1,0:T(8,128)(2,1)S(1)}, bf16[4,256,640]{2,1,0:T(8,128)(2,1)S(1)}, bf16[4,256,640]{2,1,0:T(8,128)(2,1)S(1)}) custom-call(s32[24]{0:T(128)S(1)} %dynamic-slice_bitcast_fusion.1.meta, bf16[256,5120]{1,0:T(8,128)(2,1)S(1)} %bitcast.36, f32[1,5120]{1,0:T(1,128)S(1)} %copy-done.2, ...), custom_call_target="tpu_custom_call" | custom-call | flops 1006632960 | bytes 11796480 | tf_op jit(solution)/shard_map/pallas_call | solution.py:121
  81.8 5.4 %shard_map.106 = (bf16[4,256,5120]{2,1,0:T(8,128)(2,1)S(1)}, bf16[4,256,384]{2,1,0:T(8,128)(2,1)S(1)}, bf16[4,256,640]{2,1,0:T(8,128)(2,1)S(1)}, bf16[4,256,640]{2,1,0:T(8,128)(2,1)S(1)}) custom-call(s32[24]{0:T(128)S(1)} %dynamic-slice_bitcast_fusion.1.meta, ...), custom_call_target="tpu_custom_call", output_to_operand_aliasing={{0}: (4, {}), {1}: (5, {}), {2}: (6, {}), {3}: (7, {})} | custom-call | flops 1006632960 | bytes 11796480 | tf_op jit(solution)/shard_map/pallas_call | solution.py:121
  87.2 3.7 %shard_map.107 = (bf16[4,256,5120]{2,1,0:T(8,128)(2,1)S(1)}, bf16[4,256,384]{2,1,0:T(8,128)(2,1)S(1)}, bf16[4,256,640]{2,1,0:T(8,128)(2,1)S(1)}, bf16[4,256,640]{2,1,0:T(8,128)(2,1)S(1)}) custom-call(s32[24]{0:T(128)S(1)} %dynamic-slice_bitcast_fusion.1.meta, ...), custom_call_target="tpu_custom_call", output_to_operand_aliasing={{0}: (4, {}), {1}: (5, {}), {2}: (6, {}), {3}: (7, {})} | custom-call | flops 1006632960 | bytes 11796480 | tf_op jit(solution)/shard_map/pallas_call | solution.py:121
  92.9 2.5 %collective-permute-done.12.t3 = bf16[2,256,768]{2,1,0:T(8,128)(2,1)S(1)} collective-permute-done((bf16[2,256,768]{2,1,0:T(8,128)(2,1)S(1)}, bf16[2,256,768]{2,1,0:T(8,128)(2,1)S(1)}, u32[]{:S(2)}, u32[]{:S(2)}) %collective-permute-start.12) | collective-permute-done | bytes 786464 | tf_op jit(solution)/shard_map/ppermute | solution.py:68
  95.4 3.9 %collective-permute-start.16 = (bf16[256,768]{1,0:T(8,128)(2,1)S(1)}, bf16[256,768]{1,0:T(8,128)(2,1)S(1)}, u32[]{:S(2)}, u32[]{:S(2)}) collective-permute-start(bf16[256,768]{1,0:T(8,128)(2,1)S(1)} %collective-permute-done.8.o1), channel_id=1, source_target_pairs={{0,8},{1,9},{2,10},{3,11},{4,12},{5,13},{6,14},{7,15},{8,0},{9,1},... | collective-permute-start | bytes 1179656 | tf_op jit(solution)/shard_map/ppermute | solution.py:68
  101.0 3.3 %collective-permute-done.15.refs_1_ = bf16[96,5120]{1,0:T(8,128)(2,1)S(1)} collective-permute-done((bf16[96,5120]{1,0:T(8,128)(2,1)S(1)}, bf16[96,5120]{1,0:T(8,128)(2,1)S(1)}, u32[]{:S(2)}, u32[]{:S(2)}) %collective-permute-start.15) | collective-permute-done | bytes 983072 | tf_op jit(solution)/shard_map/ppermute | solution.py:68
  106.6 3.6 %collective-permute-done.14.refs_0_ = bf16[160,5120]{1,0:T(8,128)(2,1)S(1)} collective-permute-done((bf16[160,5120]{1,0:T(8,128)(2,1)S(1)}, bf16[160,5120]{1,0:T(8,128)(2,1)S(1)}, u32[]{:S(2)}, u32[]{:S(2)}) %collective-permute-start.14) | collective-permute-done | bytes 1638432 | tf_op jit(solution)/shard_map/ppermute | solution.py:68
  110.2 3.7 %shard_map.108 = (bf16[4,256,5120]{2,1,0:T(8,128)(2,1)S(1)}, bf16[4,256,384]{2,1,0:T(8,128)(2,1)S(1)}, bf16[4,256,640]{2,1,0:T(8,128)(2,1)S(1)}, bf16[4,256,640]{2,1,0:T(8,128)(2,1)S(1)}) custom-call(s32[24]{0:T(128)S(1)} %dynamic-slice_bitcast_fusion.1.meta, ...), custom_call_target="tpu_custom_call", output_to_operand_aliasing={{0}: (5, {}), {1}: (6, {}), {2}: (7, {}), {3}: (8, {})} | custom-call | flops 1006632960 | bytes 11796480 | tf_op jit(solution)/shard_map/pallas_call | solution.py:121
  113.9 6.2 %collective-permute-done.13.t2 = bf16[2,256,768]{2,1,0:T(8,128)(2,1)S(1)} collective-permute-done((bf16[2,256,768]{2,1,0:T(8,128)(2,1)S(1)}, bf16[2,256,768]{2,1,0:T(8,128)(2,1)S(1)}, u32[]{:S(2)}, u32[]{:S(2)}) %collective-permute-start.13) | collective-permute-done | bytes 786464 | tf_op jit(solution)/shard_map/ppermute | solution.py:68
  121.3 7.9 %shard_map.109 = bf16[1024,384]{1,0:T(8,128)(2,1)S(1)} custom-call(bf16[1024,5120]{1,0:T(8,128)(2,1)S(1)} %bitcast.26, bf16[5120,384]{1,0:T(8,128)(2,1)} %collective-permute-done.5.w_ref), custom_call_target="tpu_custom_call" | custom-call | flops 4026531840 | bytes 14417920 | tf_op jit(solution)/shard_map/pallas_call | solution.py:145
  129.2 6.8 %shard_map.111.c0 = bf16[512,768]{1,0:T(8,128)(2,1)S(1)} custom-call(s32[24]{0:T(128)S(1)} %dynamic-slice_bitcast_fusion.1.meta, bf16[4,256,384]{2,1,0:T(8,128)(2,1)S(1)} %get-tuple-element.139.q_own, bf16[4,256,384]{2,1,0:T(8,128)(2,1)S(1)} %bitcast.32, s32[8,1,256]{2,1,0:T(1,128)S(1)} %bitcast.37, bf16[2,256,768]{2,1,0:T(8,128)(2,1)} %get-tuple-element.142.own0, ...), custom_call_target="tpu_custom_call" | custom-call | flops 1207959552 | bytes 8388608 | tf_op jit(solution)/shard_map/pallas_call | solution.py:262
  138.5 9.0 %shard_map.110.c0 = bf16[512,768]{1,0:T(8,128)(2,1)S(1)} custom-call(s32[24]{0:T(128)S(1)} %dynamic-slice_bitcast_fusion.1.meta, bf16[4,256,384]{2,1,0:T(8,128)(2,1)S(1)} %get-tuple-element.139.q_own, bf16[4,256,384]{2,1,0:T(8,128)(2,1)S(1)} %bitcast.33, s32[8,1,256]{2,1,0:T(1,128)S(1)} %bitcast.38, bf16[2,256,768]{2,1,0:T(8,128)(2,1)} %get-tuple-element.142.own0, ...), custom_call_target="tpu_custom_call" | custom-call | flops 1207959552 | bytes 8388608 | tf_op jit(solution)/shard_map/pallas_call | solution.py:262
  148.7 4.4 %collective-permute-done.24.c1 = bf16[512,768]{1,0:T(8,128)(2,1)S(1)} collective-permute-done((bf16[512,768]{1,0:T(8,128)(2,1)S(1)}, bf16[512,768]{1,0:T(8,128)(2,1)S(1)}, u32[]{:S(2)}, u32[]{:S(2)}) %collective-permute-start.24) | collective-permute-done | bytes 786464 | tf_op jit(solution)/shard_map/ppermute | solution.py:68
  153.2 3.4 %collective-permute-done.25.c3 = bf16[512,768]{1,0:T(8,128)(2,1)S(1)} collective-permute-done((bf16[512,768]{1,0:T(8,128)(2,1)S(1)}, bf16[512,768]{1,0:T(8,128)(2,1)S(1)}, u32[]{:S(2)}, u32[]{:S(2)}) %collective-permute-start.25) | collective-permute-done | bytes 786464 | tf_op jit(solution)/shard_map/ppermute | solution.py:68
  157.9 12.1 %collective-permute-done.19.c1 = bf16[512,768]{1,0:T(8,128)(2,1)S(1)} collective-permute-done((bf16[512,768]{1,0:T(8,128)(2,1)S(1)}, bf16[512,768]{1,0:T(8,128)(2,1)S(1)}, u32[]{:S(2)}, u32[]{:S(2)}) %collective-permute-start.19) | collective-permute-done | bytes 786464 | tf_op jit(solution)/shard_map/ppermute | solution.py:68
  170.0 3.4 %collective-permute-done.20.c3 = bf16[512,768]{1,0:T(8,128)(2,1)S(1)} collective-permute-done((bf16[512,768]{1,0:T(8,128)(2,1)S(1)}, bf16[512,768]{1,0:T(8,128)(2,1)S(1)}, u32[]{:S(2)}, u32[]{:S(2)}) %collective-permute-start.20) | collective-permute-done | bytes 786464 | tf_op jit(solution)/shard_map/ppermute | solution.py:68
  176.4 5.4 %collective-permute-done.27.c2b = bf16[128,768]{1,0:T(8,128)(2,1)S(1)} collective-permute-done((bf16[128,768]{1,0:T(8,128)(2,1)S(1)}, bf16[128,768]{1,0:T(8,128)(2,1)S(1)}, u32[]{:S(2)}, u32[]{:S(2)}) %collective-permute-start.27) | collective-permute-done | bytes 196640 | tf_op jit(solution)/shard_map/ppermute | solution.py:68
  182.7 4.1 %shard_map.112.refs_0_ = bf16[8,256,640]{2,1,0:T(8,128)(2,1)} custom-call(s32[24]{0:T(128)S(1)} %dynamic-slice_bitcast_fusion.1.meta, bf16[512,768]{1,0:T(8,128)(2,1)S(1)} %shard_map.111.c0, bf16[512,768]{1,0:T(8,128)(2,1)S(1)} %collective-permute-done.24.c1, bf16[384,768]{1,0:T(8,128)(2,1)S(1)} %collective-permute-done.26.c2a, ...), custom_call_target="tpu_custom_call" | custom-call | flops 2013265920 | bytes 8388608 | tf_op jit(solution)/shard_map/pallas_call | solution.py:333
  186.8 3.4 %shard_map.114 = bf16[2,256,640]{2,1,0:T(8,128)(2,1)S(1)} custom-call(s32[24]{0:T(128)S(1)} %dynamic-slice_bitcast_fusion.1.meta, bf16[512,768]{1,0:T(8,128)(2,1)S(1)} %shard_map.111.c0, bf16[512,768]{1,0:T(8,128)(2,1)S(1)} %collective-permute-done.24.c1, bf16[384,768]{1,0:T(8,128)(2,1)S(1)} %collective-permute-done.26.c2a, ...), custom_call_target="tpu_custom_call" | custom-call | flops 2013265920 | bytes 8388608 | tf_op jit(solution)/shard_map/pallas_call | solution.py:333
  190.2 5.7 %collective-permute-start.29 = (bf16[2,256,640]{2,1,0:T(8,128)(2,1)S(1)}, bf16[2,256,640]{2,1,0:T(8,128)(2,1)S(1)}, u32[]{:S(2)}, u32[]{:S(2)}) collective-permute-start(bf16[2,256,640]{2,1,0:T(8,128)(2,1)S(1)} %shard_map.114), channel_id=1, source_target_pairs={{0,4},{1,5},{2,6},{3,7},{4,0},{5,1},{6,2},{7,3},{8,11},{9,10},{10,... | collective-permute-start | bytes 1966088 | tf_op jit(solution)/shard_map/ppermute | solution.py:68
  196.0 3.4 %shard_map.113 = bf16[2,256,640]{2,1,0:T(8,128)(2,1)S(1)} custom-call(s32[24]{0:T(128)S(1)} %dynamic-slice_bitcast_fusion.1.meta, bf16[512,768]{1,0:T(8,128)(2,1)S(1)} %shard_map.110.c0, bf16[512,768]{1,0:T(8,128)(2,1)S(1)} %collective-permute-done.19.c1, bf16[384,768]{1,0:T(8,128)(2,1)S(1)} %collective-permute-done.21.c2a, ...), custom_call_target="tpu_custom_call" | custom-call | flops 2013265920 | bytes 8388608 | tf_op jit(solution)/shard_map/pallas_call | solution.py:333
  199.4 5.1 %collective-permute-start.28 = (bf16[2,256,640]{2,1,0:T(8,128)(2,1)S(1)}, bf16[2,256,640]{2,1,0:T(8,128)(2,1)S(1)}, u32[]{:S(2)}, u32[]{:S(2)}) collective-permute-start(bf16[2,256,640]{2,1,0:T(8,128)(2,1)S(1)} %shard_map.113), channel_id=1, source_target_pairs={{0,4},{1,5},{2,6},{3,7},{4,0},{5,1},{6,2},{7,3},{8,11},{9,10},{10,... | collective-permute-start | bytes 1966088 | tf_op jit(solution)/shard_map/ppermute | solution.py:68
  204.5 4.1 %shard_map.115.prior = bf16[8,256,640]{2,1,0:T(8,128)(2,1)} custom-call(s32[24]{0:T(128)S(1)} %dynamic-slice_bitcast_fusion.1.meta, bf16[512,768]{1,0:T(8,128)(2,1)S(1)} %shard_map.110.c0, bf16[512,768]{1,0:T(8,128)(2,1)S(1)} %collective-permute-done.19.c1, bf16[384,768]{1,0:T(8,128)(2,1)S(1)} %collective-permute-done.21.c2a, ...), custom_call_target="tpu_custom_call", output_to_operand_aliasing={{}: (8, {})} | custom-call | flops 2013265920 | bytes 8388608 | tf_op jit(solution)/shard_map/pallas_call | solution.py:333
  (85 shorter events, 56.2 us)
Async XLA Ops:
  0.0 75.5 %collective-permute-start.6 = (bf16[256,5120]{1,0:T(8,128)(2,1)}, bf16[256,5120]{1,0:T(8,128)(2,1)}, u32[]{:S(2)}, u32[]{:S(2)}) collective-permute-start(bf16[256,5120]{1,0:T(8,128)(2,1)} %bitcast.34), channel_id=1, source_target_pairs={{0,1},{1,0},{2,3},{3,2},{4,5},{5,4},{6,7},{7,6},{8,9},{9,8},{10,11... | collective-permute-start | bytes 7864328 | tf_op jit(solution)/shard_map/ppermute | solution.py:68
  2.5 73.0 %collective-permute-start.7 = (bf16[256,5120]{1,0:T(8,128)(2,1)}, bf16[256,5120]{1,0:T(8,128)(2,1)S(1)}, u32[]{:S(2)}, u32[]{:S(2)}) collective-permute-start(bf16[256,5120]{1,0:T(8,128)(2,1)} %bitcast.35), channel_id=1, source_target_pairs={{0,3},{1,2},{2,1},{3,0},{4,7},{5,6},{6,5},{7,4},{8,12},{9,13},{10,... | collective-permute-start | bytes 7864328 | tf_op jit(solution)/shard_map/ppermute | solution.py:68
  13.0 3.3 %collective-permute-start = (bf16[128,768]{1,0:T(8,128)(2,1)S(1)}, bf16[128,768]{1,0:T(8,128)(2,1)S(1)}, u32[]{:S(2)}, u32[]{:S(2)}) collective-permute-start(bf16[128,768]{1,0:T(8,128)(2,1)S(1)} %get-tuple-element.208), channel_id=1, source_target_pairs={{0,8},{1,9},{2,10},{3,11},{4,12},{5,13},{6,14},{7,15},{8,0},{9,1},... | collective-permute-start | bytes 589832 | tf_op jit(solution)/shard_map/cond/branch_1_fun/ppermute | solution.py:68
  17.2 8.5 %collective-permute-start.1 = (bf16[2,128,768]{2,1,0:T(8,128)(2,1)}, bf16[2,128,768]{2,1,0:T(8,128)(2,1)}, u32[]{:S(2)}, u32[]{:S(2)}) collective-permute-start(bf16[2,128,768]{2,1,0:T(8,128)(2,1)} %maximum_select_fusion.3), channel_id=1, source_target_pairs={{0,64},{1,65},{2,66},{3,67},{4,68},{5,69},{6,70},{7,71},{16,80},{1... | collective-permute-start | bytes 1179656 | tf_op jit(solution)/shard_map/cond/branch_1_fun/ppermute | solution.py:68
  25.6 9.2 %collective-permute-start.2 = (bf16[2,128,768]{2,1,0:T(8,128)(2,1)}, bf16[2,128,768]{2,1,0:T(8,128)(2,1)S(1)}, u32[]{:S(2)}, u32[]{:S(2)}) collective-permute-start(bf16[2,128,768]{2,1,0:T(8,128)(2,1)} %collective-permute-done.1), channel_id=1, source_target_pairs={{0,8},{1,9},{2,10},{3,11},{4,12},{5,13},{6,14},{7,15},{8,0},{9,1},... | collective-permute-start | bytes 1179656 | tf_op jit(solution)/shard_map/cond/branch_1_fun/ppermute | solution.py:68
  33.3 8.2 %collective-permute-start.3 = (bf16[2,128,768]{2,1,0:T(8,128)(2,1)}, bf16[2,128,768]{2,1,0:T(8,128)(2,1)}, u32[]{:S(2)}, u32[]{:S(2)}) collective-permute-start(bf16[2,128,768]{2,1,0:T(8,128)(2,1)} %maximum_select_fusion.3), channel_id=1, source_target_pairs={{0,4},{1,5},{2,6},{3,7},{4,0},{5,1},{6,2},{7,3},{8,11},{9,10},{10,... | collective-permute-start | bytes 1179656 | tf_op jit(solution)/shard_map/cond/branch_1_fun/ppermute | solution.py:68
  34.9 10.7 %collective-permute-start.4 = (bf16[2,128,768]{2,1,0:T(8,128)(2,1)S(1)}, bf16[2,128,768]{2,1,0:T(8,128)(2,1)}, u32[]{:S(2)}, u32[]{:S(2)}) collective-permute-start(bf16[2,128,768]{2,1,0:T(8,128)(2,1)S(1)} %broadcast_select_fusion), channel_id=1, source_target_pairs={{0,4},{1,5},{2,6},{3,7},{4,0},{5,1},{6,2},{7,3},{8,11},{9,10},{10,... | collective-permute-start | bytes 1179656 | tf_op jit(solution)/shard_map/cond/branch_1_fun/ppermute | solution.py:68
  47.2 66.7 %collective-permute-start.5 = (bf16[5120,384]{1,0:T(8,128)(2,1)}, bf16[5120,384]{1,0:T(8,128)(2,1)}, u32[]{:S(2)}, u32[]{:S(2)}) collective-permute-start(bf16[5120,384]{1,0:T(8,128)(2,1)} %bitcast.27), channel_id=1, source_target_pairs={{0,4},{1,5},{2,6},{3,7},{4,0},{5,1},{6,2},{7,3},{8,11},{9,10},{10,... | collective-permute-start | bytes 11796488 | tf_op jit(solution)/shard_map/ppermute | solution.py:68
  48.2 9.6 %collective-permute-start.8 = (bf16[256,768]{1,0:T(8,128)(2,1)}, bf16[256,768]{1,0:T(8,128)(2,1)S(1)}, u32[]{:S(2)}, u32[]{:S(2)}) collective-permute-start(bf16[256,768]{1,0:T(8,128)(2,1)} %get-tuple-element.99), channel_id=1, source_target_pairs={{0,48},{1,49},{2,50},{3,51},{4,52},{5,53},{6,54},{7,55},{8,56},{9,... | collective-permute-start | bytes 1179656 | tf_op jit(solution)/shard_map/ppermute | solution.py:68
  50.7 10.1 %collective-permute-start.9 = (bf16[256,768]{1,0:T(8,128)(2,1)}, bf16[256,768]{1,0:T(8,128)(2,1)S(1)}, u32[]{:S(2)}, u32[]{:S(2)}) collective-permute-start(bf16[256,768]{1,0:T(8,128)(2,1)} %get-tuple-element.99), channel_id=1, source_target_pairs={{0,16},{1,17},{2,18},{3,19},{4,20},{5,21},{6,22},{7,23},{8,24},{9,... | collective-permute-start | bytes 1179656 | tf_op jit(solution)/shard_map/ppermute | solution.py:68
  60.8 14.7 %collective-permute-start.10 = (bf16[256,768]{1,0:T(8,128)(2,1)}, bf16[256,768]{1,0:T(8,128)(2,1)}, u32[]{:S(2)}, u32[]{:S(2)}) collective-permute-start(bf16[256,768]{1,0:T(8,128)(2,1)} %get-tuple-element.99), channel_id=1, source_target_pairs={{0,32},{1,33},{2,34},{3,35},{4,36},{5,37},{6,38},{7,39},{8,40},{9,... | collective-permute-start | bytes 1179656 | tf_op jit(solution)/shard_map/ppermute | solution.py:68
  75.6 34.6 %collective-permute-start.14 = (bf16[160,5120]{1,0:T(8,128)(2,1)S(1)}, bf16[160,5120]{1,0:T(8,128)(2,1)S(1)}, u32[]{:S(2)}, u32[]{:S(2)}) collective-permute-start(bf16[160,5120]{1,0:T(8,128)(2,1)S(1)} %slice.22), channel_id=1, source_target_pairs={{0,1},{1,0},{2,3},{3,2},{4,5},{5,4},{6,7},{7,6},{8,9},{9,8},{10,11... | collective-permute-start | bytes 4915208 | tf_op jit(solution)/shard_map/ppermute | solution.py:68
  76.6 16.3 %collective-permute-start.11 = (bf16[2,256,768]{2,1,0:T(8,128)(2,1)S(1)}, bf16[2,256,768]{2,1,0:T(8,128)(2,1)S(1)}, u32[]{:S(2)}, u32[]{:S(2)}) collective-permute-start(bf16[2,256,768]{2,1,0:T(8,128)(2,1)S(1)} %copy-done.6), channel_id=1, source_target_pairs={{0,48},{1,49},{2,50},{3,51},{4,52},{5,53},{6,54},{7,55},{8,56},{9,... | collective-permute-start | bytes 2359304 | tf_op jit(solution)/shard_map/ppermute | solution.py:68
  78.2 17.3 %collective-permute-start.12 = (bf16[2,256,768]{2,1,0:T(8,128)(2,1)S(1)}, bf16[2,256,768]{2,1,0:T(8,128)(2,1)S(1)}, u32[]{:S(2)}, u32[]{:S(2)}) collective-permute-start(bf16[2,256,768]{2,1,0:T(8,128)(2,1)S(1)} %copy-done.6), channel_id=1, source_target_pairs={{0,16},{1,17},{2,18},{3,19},{4,20},{5,21},{6,22},{7,23},{8,24},{9,... | collective-permute-start | bytes 2359304 | tf_op jit(solution)/shard_map/ppermute | solution.py:68
  79.5 24.8 %collective-permute-start.15 = (bf16[96,5120]{1,0:T(8,128)(2,1)S(1)}, bf16[96,5120]{1,0:T(8,128)(2,1)S(1)}, u32[]{:S(2)}, u32[]{:S(2)}) collective-permute-start(bf16[96,5120]{1,0:T(8,128)(2,1)S(1)} %slice.23), channel_id=1, source_target_pairs={{0,3},{1,2},{2,1},{3,0},{4,7},{5,6},{6,5},{7,4},{8,12},{9,13},{10,... | collective-permute-start | bytes 2949128 | tf_op jit(solution)/shard_map/ppermute | solution.py:68
  95.4 24.6 %copy-start.7 = (bf16[8,384,640]{2,1,0:T(8,128)(2,1)S(1)}, bf16[8,384,640]{2,1,0:T(8,128)(2,1)}, u32[]{:S(2)}) copy-start(bf16[8,384,640]{2,1,0:T(8,128)(2,1)} %shard_map.104) | copy-start | bytes 11796484
  95.4 9.0 %collective-permute-start.16 = (bf16[256,768]{1,0:T(8,128)(2,1)S(1)}, bf16[256,768]{1,0:T(8,128)(2,1)S(1)}, u32[]{:S(2)}, u32[]{:S(2)}) collective-permute-start(bf16[256,768]{1,0:T(8,128)(2,1)S(1)} %collective-permute-done.8.o1), channel_id=1, source_target_pairs={{0,8},{1,9},{2,10},{3,11},{4,12},{5,13},{6,14},{7,15},{8,0},{9,1},... | collective-permute-start | bytes 1179656 | tf_op jit(solution)/shard_map/ppermute | solution.py:68
  99.4 20.7 %collective-permute-start.13 = (bf16[2,256,768]{2,1,0:T(8,128)(2,1)S(1)}, bf16[2,256,768]{2,1,0:T(8,128)(2,1)S(1)}, u32[]{:S(2)}, u32[]{:S(2)}) collective-permute-start(bf16[2,256,768]{2,1,0:T(8,128)(2,1)S(1)} %copy-done.6), channel_id=1, source_target_pairs={{0,32},{1,33},{2,34},{3,35},{4,36},{5,37},{6,38},{7,39},{8,40},{9,... | collective-permute-start | bytes 2359304 | tf_op jit(solution)/shard_map/ppermute | solution.py:68
  104.3 1.9 collective-permute-start.17
  104.4 2.1 %collective-permute-start.18 = (bf16[256,768]{1,0:T(8,128)(2,1)S(1)}, bf16[256,768]{1,0:T(8,128)(2,1)S(1)}, u32[]{:S(2)}, u32[]{:S(2)}) collective-permute-start(bf16[256,768]{1,0:T(8,128)(2,1)S(1)} %collective-permute-done.9.o3), channel_id=1, source_target_pairs={{0,8},{1,9},{2,10},{3,11},{4,12},{5,13},{6,14},{7,15},{8,0},{9,1},... | collective-permute-start | bytes 1179656 | tf_op jit(solution)/shard_map/ppermute | solution.py:68
  120.0 66.8 %collective-permute-start.23 = (bf16[3072,640]{1,0:T(8,128)(2,1)S(1)}, bf16[3072,640]{1,0:T(8,128)(2,1)S(1)}, u32[]{:S(2)}, u32[]{:S(2)}) collective-permute-start(bf16[3072,640]{1,0:T(8,128)(2,1)S(1)} %bitcast.42), channel_id=1, source_target_pairs={{0,4},{1,5},{2,6},{3,7},{4,0},{5,1},{6,2},{7,3},{8,11},{9,10},{10,... | collective-permute-start | bytes 11796488 | tf_op jit(solution)/shard_map/ppermute | solution.py:68
  136.0 17.2 %collective-permute-start.24 = (bf16[512,768]{1,0:T(8,128)(2,1)S(1)}, bf16[512,768]{1,0:T(8,128)(2,1)S(1)}, u32[]{:S(2)}, u32[]{:S(2)}) collective-permute-start(bf16[512,768]{1,0:T(8,128)(2,1)S(1)} %shard_map.111.c0), channel_id=1, source_target_pairs={{0,1},{1,0},{2,3},{3,2},{4,5},{5,4},{6,7},{7,6},{8,9},{9,8},{10,11... | collective-permute-start | bytes 2359304 | tf_op jit(solution)/shard_map/ppermute | solution.py:68
  136.1 20.5 %collective-permute-start.25 = (bf16[512,768]{1,0:T(8,128)(2,1)S(1)}, bf16[512,768]{1,0:T(8,128)(2,1)S(1)}, u32[]{:S(2)}, u32[]{:S(2)}) collective-permute-start(bf16[512,768]{1,0:T(8,128)(2,1)S(1)} %shard_map.111.c0), channel_id=1, source_target_pairs={{0,3},{1,2},{2,1},{3,0},{4,7},{5,6},{6,5},{7,4},{8,12},{9,13},{10,... | collective-permute-start | bytes 2359304 | tf_op jit(solution)/shard_map/ppermute | solution.py:68
  138.5 44.2 %copy-start.4 = (bf16[3072,640]{1,0:T(8,128)(2,1)S(1)}, bf16[3072,640]{1,0:T(8,128)(2,1)}, u32[]{:S(2)}) copy-start(bf16[3072,640]{1,0:T(8,128)(2,1)} %get-tuple-element.159.w) | copy-start | bytes 11796484
  147.5 22.5 %collective-permute-start.19 = (bf16[512,768]{1,0:T(8,128)(2,1)S(1)}, bf16[512,768]{1,0:T(8,128)(2,1)S(1)}, u32[]{:S(2)}, u32[]{:S(2)}) collective-permute-start(bf16[512,768]{1,0:T(8,128)(2,1)S(1)} %shard_map.110.c0), channel_id=1, source_target_pairs={{0,1},{1,0},{2,3},{3,2},{4,5},{5,4},{6,7},{7,6},{8,9},{9,8},{10,11... | collective-permute-start | bytes 2359304 | tf_op jit(solution)/shard_map/ppermute | solution.py:68
  148.7 24.7 %collective-permute-start.20 = (bf16[512,768]{1,0:T(8,128)(2,1)S(1)}, bf16[512,768]{1,0:T(8,128)(2,1)S(1)}, u32[]{:S(2)}, u32[]{:S(2)}) collective-permute-start(bf16[512,768]{1,0:T(8,128)(2,1)S(1)} %shard_map.110.c0), channel_id=1, source_target_pairs={{0,3},{1,2},{2,1},{3,0},{4,7},{5,6},{6,5},{7,4},{8,12},{9,13},{10,... | collective-permute-start | bytes 2359304 | tf_op jit(solution)/shard_map/ppermute | solution.py:68
  156.7 26.0 %collective-permute-start.26 = (bf16[384,768]{1,0:T(8,128)(2,1)S(1)}, bf16[384,768]{1,0:T(8,128)(2,1)S(1)}, u32[]{:S(2)}, u32[]{:S(2)}) collective-permute-start(bf16[384,768]{1,0:T(8,128)(2,1)S(1)} %slice.26), channel_id=1, source_target_pairs={{0,1},{1,0},{2,3},{3,2},{4,5},{5,4},{6,7},{7,6},{8,9},{9,8},{10,11... | collective-permute-start | bytes 1769480 | tf_op jit(solution)/shard_map/ppermute | solution.py:68
  173.5 22.5 %collective-permute-start.21 = (bf16[384,768]{1,0:T(8,128)(2,1)S(1)}, bf16[384,768]{1,0:T(8,128)(2,1)S(1)}, u32[]{:S(2)}, u32[]{:S(2)}) collective-permute-start(bf16[384,768]{1,0:T(8,128)(2,1)S(1)} %slice.24), channel_id=1, source_target_pairs={{0,1},{1,0},{2,3},{3,2},{4,5},{5,4},{6,7},{7,6},{8,9},{9,8},{10,11... | collective-permute-start | bytes 1769480 | tf_op jit(solution)/shard_map/ppermute | solution.py:68
  174.8 7.1 %collective-permute-start.27 = (bf16[128,768]{1,0:T(8,128)(2,1)S(1)}, bf16[128,768]{1,0:T(8,128)(2,1)S(1)}, u32[]{:S(2)}, u32[]{:S(2)}) collective-permute-start(bf16[128,768]{1,0:T(8,128)(2,1)S(1)} %slice.27), channel_id=1, source_target_pairs={{0,3},{1,2},{2,1},{3,0},{4,7},{5,6},{6,5},{7,4},{8,12},{9,13},{10,... | collective-permute-start | bytes 589832 | tf_op jit(solution)/shard_map/ppermute | solution.py:68
  176.3 19.6 %collective-permute-start.22 = (bf16[128,768]{1,0:T(8,128)(2,1)S(1)}, bf16[128,768]{1,0:T(8,128)(2,1)S(1)}, u32[]{:S(2)}, u32[]{:S(2)}) collective-permute-start(bf16[128,768]{1,0:T(8,128)(2,1)S(1)} %slice.25), channel_id=1, source_target_pairs={{0,3},{1,2},{2,1},{3,0},{4,7},{5,6},{6,5},{7,4},{8,12},{9,13},{10,... | collective-permute-start | bytes 589832 | tf_op jit(solution)/shard_map/ppermute | solution.py:68
  190.2 18.4 %collective-permute-start.29 = (bf16[2,256,640]{2,1,0:T(8,128)(2,1)S(1)}, bf16[2,256,640]{2,1,0:T(8,128)(2,1)S(1)}, u32[]{:S(2)}, u32[]{:S(2)}) collective-permute-start(bf16[2,256,640]{2,1,0:T(8,128)(2,1)S(1)} %shard_map.114), channel_id=1, source_target_pairs={{0,4},{1,5},{2,6},{3,7},{4,0},{5,1},{6,2},{7,3},{8,11},{9,10},{10,... | collective-permute-start | bytes 1966088 | tf_op jit(solution)/shard_map/ppermute | solution.py:68
  199.4 13.0 %collective-permute-start.28 = (bf16[2,256,640]{2,1,0:T(8,128)(2,1)S(1)}, bf16[2,256,640]{2,1,0:T(8,128)(2,1)S(1)}, u32[]{:S(2)}, u32[]{:S(2)}) collective-permute-start(bf16[2,256,640]{2,1,0:T(8,128)(2,1)S(1)} %shard_map.113), channel_id=1, source_target_pairs={{0,4},{1,5},{2,6},{3,7},{4,0},{5,1},{6,2},{7,3},{8,11},{9,10},{10,... | collective-permute-start | bytes 1966088 | tf_op jit(solution)/shard_map/ppermute | solution.py:68
  (9 other events, 45.4 us)

commit v9 on v8

--- a/solution.py
+++ b/solution.py
@@ -298,6 +298,7 @@
             out_specs=pl.BlockSpec((1, n, width), lambda k, m: (k, 0, 0)),
         ),
         out_shape=jax.ShapeDtypeStruct(w.shape, BF),
+        compiler_params=pltpu.CompilerParams(vmem_limit_bytes=4 * MIB),
     )(meta, w).reshape(k8 * n, width)
 
 
@@ -405,60 +406,52 @@
         kv2 = send(kv, CORE)
         pair = jnp.where(core == 0, jnp.stack([kv, kv2]), jnp.stack([kv2, kv]))
         far = send(pair, FAR_Y)
-        near2 = send(pair, PARTNER)
         far, w_mine = lax.optimization_barrier((far, reorder(meta, w_out, 0)))
         far = jnp.where(core == 0, far, send(far, CORE))
-        far2 = send(far, PARTNER)
-
-        def in_order(near, far):
-            both = jnp.where(y_hi == 0, jnp.stack([near, far]), jnp.stack([far, near]))
-            return both.reshape(2, 2 * kv.shape[0], kv.shape[1])
-
-        piece = in_order(pair, far)
+        piece = jnp.where(y_hi == 0, jnp.stack([pair, far]), jnp.stack([far, pair]))
+        piece = piece.reshape(2, 2 * kv.shape[0], kv.shape[1])
+        piece2 = send(piece, PARTNER)
         share = lax.dynamic_index_in_dim(piece, core, 0, keepdims=False)
-        return piece, share, in_order(near2, far2), w_mine
+        o2 = send(share, X_FAR)
+        return piece, share, o2, piece2, w_mine, reorder(meta, w_out, 1)
 
     def nothing(last_hidden, w_key, w_value, w_out):
         two = jnp.zeros((2, 2 * last_hidden.shape[0], 2 * w_key.shape[1]), BF)
         w_none = jnp.zeros((w_out.shape[0] * w_out.shape[1], w_out.shape[2]), BF)
-        return two, two[0], two, w_none
+        return two, two[0], two[0], two, w_none, w_none
 
     w_o_r = w_o.reshape(8, w_q.shape[1], width)
-    piece, share, piece2, w_o_mine = lax.cond(
+    piece, share, o2, piece2, w_o_mine, w_o_theirs = lax.cond(
         segment_ids[0] >= 0, cache, nothing, last_hidden, w_key, w_value, w_o_r
     )
     w_q2 = send(after(w_q, piece2), PARTNER)
     o1 = send(share, X_PREV)
     o3 = send(share, X_NEXT)
-    o2 = send(after(share, o1, o3), X_FAR)
-    x0, w_o_r = after(x0, share), after(w_o_r, share)
-    w_o_theirs = reorder(meta, w_o_r, 1)
-    state = project(meta, [x0], query_gain, w_q, 0, width)
-    x_in, x_out, piece2, o1, o2, o3, w_o_theirs, *state = lax.optimization_barrier(
-        (x_in, x_out, piece2, o1, o2, o3, w_o_theirs, *state)
+    x_in, x_out, piece2, share, o1, o3 = lax.optimization_barrier(
+        (x_in, x_out, piece2, share, o1, o3)
     )
     most = RB * 5 // 8
     xo_a = send(x_out[:most], IN)
     xo_b = send(x_in[most:], OUT)
     t1 = send(piece2, X_PREV)
     t3 = send(piece2, X_NEXT)
+    state = project(meta, [after(x0, x_in, x_out)], query_gain, w_q, 0, width)
     state = project(meta, [x_in], query_gain, w_q, 1, width, state)
     state = project(meta, [x_out], query_gain, w_q, 3, width, state)
-    t1, t3, o1, o2, o3, piece2, *state = lax.optimization_barrier(
-        (t1, t3, o1, o2, o3, piece2, *state)
+    xo_b, t1, t3, o1, o2, o3, piece2, *state = lax.optimization_barrier(
+        (xo_b, t1, t3, o1, o2, o3, piece2, *state)
     )
     t2 = send(piece2, X_FAR)
     o1b = send(o1, CORE)
     o2b = send(o2, CORE)
     o3b = send(o3, CORE)
-    xo_a, xo_b, o1b, o2b, o3b = lax.optimization_barrier((xo_a, xo_b, o1b, o2b, o3b))
+    xo_a, t2, w_q2, o1b, o2b, o3b, w_o_theirs = lax.optimization_barrier(
+        (xo_a, t2, w_q2, o1b, o2b, o3b, w_o_theirs)
+    )
+    w_o2 = send(w_o_theirs, PARTNER)
     normed, q_own, res_own, res_other = project(
         meta, [xo_a, xo_b], query_gain, w_q, 2, width, state
     )
-    w_q2, t2, o1b, o2b, o3b, normed, q_own = lax.optimization_barrier(
-        (w_q2, t2, o1b, o2b, o3b, normed, q_own)
-    )
-    w_o2 = send(after(w_o_theirs, w_q2), PARTNER)
     q_other = more_queries(normed, w_q2)
     pieces = (piece, o1, o1b, o2, o2b, o3, o3b, piece2, t1, t2, t3)
 

time: 216 us -> 207 us (0.958)
  Pallas kernels: 72.3 us -> 66.6 us
  local copies, waits for them, and re-layouts: 10.4 us -> 7.42 us
    unnamed x16 -> x14, local copies, waits for them, and re-layouts: 4.76 us -> 1.77 us
    ppermute x30 -> x29, starting transfers between devices: 50.2 us -> 52 us  [send(): return lax.ppermute(value, AXES, pairs)]
    ppermute x30 -> x29, waiting for transfers between devices: 70.5 us -> 70.6 us  [send(): return lax.ppermute(value, AXES, pairs)]
  transfers between devices with their start and end apart: 30 -> 29, of which waited for: 20 -> 16; matrix products, arithmetic and copies ran while one was open for 7% -> 7% of each run, Pallas kernels for 33% -> 32%
where the time goes in v9:
time: 207 us; the launch traced here: 206 us
  waiting for transfers between devices  70.6 us (34%)
  Pallas kernels  66.6 us (32%)
  starting transfers between devices  52 us (25%)
  local copies, waits for them, and re-layouts  7.42 us (4%)
  matrix products  4.48 us (2%)
  other arithmetic  3.84 us (2%)
    ppermute x29, waiting for transfers between devices, send(): return lax.ppermute(value, AXES, pairs)  70.6 us
    ppermute x29, starting transfers between devices, send(): return lax.ppermute(value, AXES, pairs)  52 us
    pallas_call x4, Pallas kernels, project(): pl.pallas_call(kernel, grid_spec=pltpu.PrefetchScalarGridSpec(num_scalar_...  16.5 us
    pallas_call x4, Pallas kernels, finish(): pl.pallas_call(finish_kernel, grid_spec=pltpu.PrefetchScalarGridSpec(num_...  14.9 us
    pallas_call x2, Pallas kernels, attend(): pl.pallas_call(functools.partial(attend_kernel, chunk), grid_spec=pltpu.P...  14.5 us
    pallas_call x2, Pallas kernels, reorder(): pl.pallas_call(reorder_kernel, grid_spec=pltpu.PrefetchScalarGridSpec(num...  12.2 us
    pallas_call x1, Pallas kernels, more_queries(): pl.pallas_call(more_queries_kernel, grid=(2,), in_specs=[pl.BlockSpec((ro...  5.76 us
  transfers between devices with their start and end apart: 29, of which 16 were waited for; matrix products, arithmetic and copies ran while one was open for 7% of the time, Pallas kernels for 32%

profile of v9, /device:TPU:1, one launch (start us, length us, event | category | flops | bytes accessed | tf_op | source)
XLA Modules:
  0.0 206.0 jit_solution(13380792349222376365)
XLA Ops:
  6.3 43.7 %conditional.1 = (bf16[2,256,768]{2,1,0:T(8,128)(2,1)}, bf16[256,768]{1,0:T(8,128)(2,1)}, bf16[256,768]{1,0:T(8,128)(2,1)}, bf16[2,256,768]{2,1,0:T(8,128)(2,1)}...) conditional(s32[]{:T(128)} %bitcast.12, () %tuple.23, (s32[]{:T(128)}, pred[]{:T(512)}, ...), branch_computations={%region_0.1_spmd, %region_1.3_spmd} | conditional | flops 1016889472 | bytes 47639592 | solution.py:424
  8.0 3.6 %convolution_convert_fusion = bf16[128,384]{1,0:T(8,128)(2,1)S(1)} fusion(bf16[5120,384]{1,0:T(8,128)(2,1)} %get-tuple-element.161, bf16[128,5120]{1,0:T(8,128)(2,1)} %get-tuple-element.158, f32[5120]{0:T(1024)} %get-tuple-element.159, f32[128]{0:T(128)S(1)} %add_rsqrt_fusion), kind=kOutput, calls=%fused_computation.5 | convolution fusion | flops 505987072 | bytes 5362176 | tf_op jit(solution)/shard_map/cond/branch_1_fun/dot_general | solution.py:404
  17.1 7.1 %branch_1_fun.2 = bf16[8,384,640]{2,1,0:T(8,128)(2,1)} custom-call(s32[24]{0:T(128)S(1)} %get-tuple-element.27.meta, bf16[8,384,640]{2,1,0:T(8,128)(2,1)} %bitcast.38), custom_call_target="tpu_custom_call" | custom-call | tf_op jit(solution)/shard_map/cond/branch_1_fun/pallas_call | solution.py:290
  24.2 8.1 %collective-permute-start.2 = (bf16[2,128,768]{2,1,0:T(8,128)(2,1)S(1)}, bf16[2,128,768]{2,1,0:T(8,128)(2,1)}, u32[]{:S(2)}, u32[]{:S(2)}) collective-permute-start(bf16[2,128,768]{2,1,0:T(8,128)(2,1)S(1)} %collective-permute-done.1), channel_id=1, source_target_pairs={{0,8},{1,9},{2,10},{3,11},{4,12},{5,13},{6,14},{7,15},{8,0},{9,1},... | collective-permute-start | bytes 1179656 | tf_op jit(solution)/shard_map/cond/branch_1_fun/ppermute | solution.py:68
  38.0 2.7 %collective-permute-start.3 = (bf16[256,768]{1,0:T(8,128)(2,1)}, bf16[256,768]{1,0:T(8,128)(2,1)}, u32[]{:S(2)}, u32[]{:S(2)}) collective-permute-start(bf16[256,768]{1,0:T(8,128)(2,1)} %dynamic-slice_bitcast_fusion), channel_id=1, source_target_pairs={{0,32},{1,33},{2,34},{3,35},{4,36},{5,37},{6,38},{7,39},{8,40},{9,... | collective-permute-start | bytes 1179656 | tf_op jit(solution)/shard_map/cond/branch_1_fun/ppermute | solution.py:68
  40.8 5.2 %branch_1_fun.3 = bf16[8,384,640]{2,1,0:T(8,128)(2,1)S(1)} custom-call(s32[24]{0:T(128)S(1)} %get-tuple-element.27.meta, bf16[8,384,640]{2,1,0:T(8,128)(2,1)} %bitcast.39), custom_call_target="tpu_custom_call" | custom-call | tf_op jit(solution)/shard_map/cond/branch_1_fun/pallas_call | solution.py:290
  45.9 4.1 %collective-permute-done.3 = bf16[256,768]{1,0:T(8,128)(2,1)} collective-permute-done((bf16[256,768]{1,0:T(8,128)(2,1)}, bf16[256,768]{1,0:T(8,128)(2,1)}, u32[]{:S(2)}, u32[]{:S(2)}) %collective-permute-start.3) | collective-permute-done | bytes 393248 | tf_op jit(solution)/shard_map/cond/branch_1_fun/ppermute | solution.py:68
  54.6 7.6 %collective-permute-done.7.o1 = bf16[256,768]{1,0:T(8,128)(2,1)S(1)} collective-permute-done((bf16[256,768]{1,0:T(8,128)(2,1)}, bf16[256,768]{1,0:T(8,128)(2,1)S(1)}, u32[]{:S(2)}, u32[]{:S(2)}) %collective-permute-start.7) | collective-permute-done | bytes 393248 | tf_op jit(solution)/shard_map/ppermute | solution.py:68
  62.1 3.0 %collective-permute-done.8.o3 = bf16[256,768]{1,0:T(8,128)(2,1)S(1)} collective-permute-done((bf16[256,768]{1,0:T(8,128)(2,1)}, bf16[256,768]{1,0:T(8,128)(2,1)S(1)}, u32[]{:S(2)}, u32[]{:S(2)}) %collective-permute-start.8) | collective-permute-done | bytes 393248 | tf_op jit(solution)/shard_map/ppermute | solution.py:68
  66.4 2.7 %collective-permute-start.10 = (bf16[96,5120]{1,0:T(8,128)(2,1)S(1)}, bf16[96,5120]{1,0:T(8,128)(2,1)S(1)}, u32[]{:S(2)}, u32[]{:S(2)}) collective-permute-start(bf16[96,5120]{1,0:T(8,128)(2,1)S(1)} %slice.23), channel_id=1, source_target_pairs={{0,3},{1,2},{2,1},{3,0},{4,7},{5,6},{6,5},{7,4},{8,12},{9,13},{10,... | collective-permute-start | bytes 2949128 | tf_op jit(solution)/shard_map/ppermute | solution.py:68
  72.6 3.7 %shard_map.105 = (bf16[4,256,5120]{2,1,0:T(8,128)(2,1)S(1)}, bf16[4,256,384]{2,1,0:T(8,128)(2,1)S(1)}, bf16[4,256,640]{2,1,0:T(8,128)(2,1)S(1)}, bf16[4,256,640]{2,1,0:T(8,128)(2,1)S(1)}) custom-call(s32[24]{0:T(128)S(1)} %dynamic-slice_bitcast_fusion.1.meta, bf16[256,5120]{1,0:T(8,128)(2,1)S(1)} %bitcast.34, f32[1,5120]{1,0:T(1,128)S(1)} %copy-done.2, ...), custom_call_target="tpu_custom_call" | custom-call | flops 1006632960 | bytes 11796480 | tf_op jit(solution)/shard_map/pallas_call | solution.py:121
  76.3 5.4 %shard_map.106 = (bf16[4,256,5120]{2,1,0:T(8,128)(2,1)S(1)}, bf16[4,256,384]{2,1,0:T(8,128)(2,1)S(1)}, bf16[4,256,640]{2,1,0:T(8,128)(2,1)S(1)}, bf16[4,256,640]{2,1,0:T(8,128)(2,1)S(1)}) custom-call(s32[24]{0:T(128)S(1)} %dynamic-slice_bitcast_fusion.1.meta, ...), custom_call_target="tpu_custom_call", output_to_operand_aliasing={{0}: (4, {}), {1}: (5, {}), {2}: (6, {}), {3}: (7, {})} | custom-call | flops 1006632960 | bytes 11796480 | tf_op jit(solution)/shard_map/pallas_call | solution.py:121
  81.7 3.7 %shard_map.107 = (bf16[4,256,5120]{2,1,0:T(8,128)(2,1)S(1)}, bf16[4,256,384]{2,1,0:T(8,128)(2,1)S(1)}, bf16[4,256,640]{2,1,0:T(8,128)(2,1)S(1)}, bf16[4,256,640]{2,1,0:T(8,128)(2,1)S(1)}) custom-call(s32[24]{0:T(128)S(1)} %dynamic-slice_bitcast_fusion.1.meta, ...), custom_call_target="tpu_custom_call", output_to_operand_aliasing={{0}: (4, {}), {1}: (5, {}), {2}: (6, {}), {3}: (7, {})} | custom-call | flops 1006632960 | bytes 11796480 | tf_op jit(solution)/shard_map/pallas_call | solution.py:121
  88.0 3.5 %collective-permute-done.10.refs_1_ = bf16[96,5120]{1,0:T(8,128)(2,1)S(1)} collective-permute-done((bf16[96,5120]{1,0:T(8,128)(2,1)S(1)}, bf16[96,5120]{1,0:T(8,128)(2,1)S(1)}, u32[]{:S(2)}, u32[]{:S(2)}) %collective-permute-start.10) | collective-permute-done | bytes 983072 | tf_op jit(solution)/shard_map/ppermute | solution.py:68
  91.5 3.3 %collective-permute-start.15 = (bf16[256,768]{1,0:T(8,128)(2,1)S(1)}, bf16[256,768]{1,0:T(8,128)(2,1)S(1)}, u32[]{:S(2)}, u32[]{:S(2)}) collective-permute-start(bf16[256,768]{1,0:T(8,128)(2,1)S(1)} %collective-permute-done.7.o1), channel_id=1, source_target_pairs={{0,8},{1,9},{2,10},{3,11},{4,12},{5,13},{6,14},{7,15},{8,0},{9,1},... | collective-permute-start | bytes 1179656 | tf_op jit(solution)/shard_map/ppermute | solution.py:68
  94.8 12.0 %collective-permute-done.14.w_ref = bf16[5120,384]{1,0:T(8,128)(2,1)S(1)} collective-permute-done((bf16[5120,384]{1,0:T(8,128)(2,1)}, bf16[5120,384]{1,0:T(8,128)(2,1)S(1)}, u32[]{:S(2)}, u32[]{:S(2)}) %collective-permute-start.14) | collective-permute-done | bytes 3932192 | tf_op jit(solution)/shard_map/ppermute | solution.py:68
  111.3 3.7 %shard_map.108 = (bf16[4,256,5120]{2,1,0:T(8,128)(2,1)S(1)}, bf16[4,256,384]{2,1,0:T(8,128)(2,1)S(1)}, bf16[4,256,640]{2,1,0:T(8,128)(2,1)S(1)}, bf16[4,256,640]{2,1,0:T(8,128)(2,1)S(1)}) custom-call(s32[24]{0:T(128)S(1)} %dynamic-slice_bitcast_fusion.1.meta, ...), custom_call_target="tpu_custom_call", output_to_operand_aliasing={{0}: (5, {}), {1}: (6, {}), {2}: (7, {}), {3}: (8, {})} | custom-call | flops 1006632960 | bytes 11796480 | tf_op jit(solution)/shard_map/pallas_call | solution.py:121
  115.1 5.8 %shard_map.109 = bf16[1024,384]{1,0:T(8,128)(2,1)S(1)} custom-call(bf16[1024,5120]{1,0:T(8,128)(2,1)S(1)} %bitcast.24, bf16[5120,384]{1,0:T(8,128)(2,1)S(1)} %collective-permute-done.14.w_ref), custom_call_target="tpu_custom_call" | custom-call | flops 4026531840 | bytes 14417920 | tf_op jit(solution)/shard_map/pallas_call | solution.py:145
  120.8 7.1 %shard_map.111.c0 = bf16[512,768]{1,0:T(8,128)(2,1)S(1)} custom-call(s32[24]{0:T(128)S(1)} %dynamic-slice_bitcast_fusion.1.meta, bf16[4,256,384]{2,1,0:T(8,128)(2,1)S(1)} %get-tuple-element.118.q_own, bf16[4,256,384]{2,1,0:T(8,128)(2,1)S(1)} %bitcast.30, s32[8,1,256]{2,1,0:T(1,128)S(1)} %bitcast.35, bf16[2,256,768]{2,1,0:T(8,128)(2,1)} %get-tuple-element.121.own0, ...), custom_call_target="tpu_custom_call" | custom-call | flops 1207959552 | bytes 8388608 | tf_op jit(solution)/shard_map/pallas_call | solution.py:262
  130.3 7.4 %shard_map.110.c0 = bf16[512,768]{1,0:T(8,128)(2,1)S(1)} custom-call(s32[24]{0:T(128)S(1)} %dynamic-slice_bitcast_fusion.1.meta, bf16[4,256,384]{2,1,0:T(8,128)(2,1)S(1)} %get-tuple-element.118.q_own, bf16[4,256,384]{2,1,0:T(8,128)(2,1)S(1)} %bitcast.31, s32[8,1,256]{2,1,0:T(1,128)S(1)} %bitcast.36, bf16[2,256,768]{2,1,0:T(8,128)(2,1)} %get-tuple-element.121.own0, ...), custom_call_target="tpu_custom_call" | custom-call | flops 1207959552 | bytes 8388608 | tf_op jit(solution)/shard_map/pallas_call | solution.py:262
  138.4 5.1 %collective-permute-done.23.c1 = bf16[512,768]{1,0:T(8,128)(2,1)S(1)} collective-permute-done((bf16[512,768]{1,0:T(8,128)(2,1)S(1)}, bf16[512,768]{1,0:T(8,128)(2,1)S(1)}, u32[]{:S(2)}, u32[]{:S(2)}) %collective-permute-start.23) | collective-permute-done | bytes 786464 | tf_op jit(solution)/shard_map/ppermute | solution.py:68
  143.5 5.0 %collective-permute-done.24.c3 = bf16[512,768]{1,0:T(8,128)(2,1)S(1)} collective-permute-done((bf16[512,768]{1,0:T(8,128)(2,1)S(1)}, bf16[512,768]{1,0:T(8,128)(2,1)S(1)}, u32[]{:S(2)}, u32[]{:S(2)}) %collective-permute-start.24) | collective-permute-done | bytes 786464 | tf_op jit(solution)/shard_map/ppermute | solution.py:68
  149.3 11.1 %collective-permute-done.18.c1 = bf16[512,768]{1,0:T(8,128)(2,1)S(1)} collective-permute-done((bf16[512,768]{1,0:T(8,128)(2,1)S(1)}, bf16[512,768]{1,0:T(8,128)(2,1)S(1)}, u32[]{:S(2)}, u32[]{:S(2)}) %collective-permute-start.18) | collective-permute-done | bytes 786464 | tf_op jit(solution)/shard_map/ppermute | solution.py:68
  160.3 5.0 %collective-permute-done.19.c3 = bf16[512,768]{1,0:T(8,128)(2,1)S(1)} collective-permute-done((bf16[512,768]{1,0:T(8,128)(2,1)S(1)}, bf16[512,768]{1,0:T(8,128)(2,1)S(1)}, u32[]{:S(2)}, u32[]{:S(2)}) %collective-permute-start.19) | collective-permute-done | bytes 786464 | tf_op jit(solution)/shard_map/ppermute | solution.py:68
  167.8 5.4 %collective-permute-done.26.c2b = bf16[128,768]{1,0:T(8,128)(2,1)S(1)} collective-permute-done((bf16[128,768]{1,0:T(8,128)(2,1)S(1)}, bf16[128,768]{1,0:T(8,128)(2,1)S(1)}, u32[]{:S(2)}, u32[]{:S(2)}) %collective-permute-start.26) | collective-permute-done | bytes 196640 | tf_op jit(solution)/shard_map/ppermute | solution.py:68
  173.2 4.1 %shard_map.112.refs_0_ = bf16[8,256,640]{2,1,0:T(8,128)(2,1)} custom-call(s32[24]{0:T(128)S(1)} %dynamic-slice_bitcast_fusion.1.meta, bf16[512,768]{1,0:T(8,128)(2,1)S(1)} %shard_map.111.c0, bf16[512,768]{1,0:T(8,128)(2,1)S(1)} %collective-permute-done.23.c1, bf16[384,768]{1,0:T(8,128)(2,1)S(1)} %collective-permute-done.25.c2a, ...), custom_call_target="tpu_custom_call" | custom-call | flops 2013265920 | bytes 8388608 | tf_op jit(solution)/shard_map/pallas_call | solution.py:334
  177.3 3.4 %shard_map.114 = bf16[2,256,640]{2,1,0:T(8,128)(2,1)S(1)} custom-call(s32[24]{0:T(128)S(1)} %dynamic-slice_bitcast_fusion.1.meta, bf16[512,768]{1,0:T(8,128)(2,1)S(1)} %shard_map.111.c0, bf16[512,768]{1,0:T(8,128)(2,1)S(1)} %collective-permute-done.23.c1, bf16[384,768]{1,0:T(8,128)(2,1)S(1)} %collective-permute-done.25.c2a, ...), custom_call_target="tpu_custom_call" | custom-call | flops 2013265920 | bytes 8388608 | tf_op jit(solution)/shard_map/pallas_call | solution.py:334
  180.7 7.3 %collective-permute-start.28 = (bf16[2,256,640]{2,1,0:T(8,128)(2,1)S(1)}, bf16[2,256,640]{2,1,0:T(8,128)(2,1)S(1)}, u32[]{:S(2)}, u32[]{:S(2)}) collective-permute-start(bf16[2,256,640]{2,1,0:T(8,128)(2,1)S(1)} %shard_map.114), channel_id=1, source_target_pairs={{0,4},{1,5},{2,6},{3,7},{4,0},{5,1},{6,2},{7,3},{8,11},{9,10},{10,... | collective-permute-start | bytes 1966088 | tf_op jit(solution)/shard_map/ppermute | solution.py:68
  187.9 3.4 %shard_map.113 = bf16[2,256,640]{2,1,0:T(8,128)(2,1)S(1)} custom-call(s32[24]{0:T(128)S(1)} %dynamic-slice_bitcast_fusion.1.meta, bf16[512,768]{1,0:T(8,128)(2,1)S(1)} %shard_map.110.c0, bf16[512,768]{1,0:T(8,128)(2,1)S(1)} %collective-permute-done.18.c1, bf16[384,768]{1,0:T(8,128)(2,1)S(1)} %collective-permute-done.20.c2a, ...), custom_call_target="tpu_custom_call" | custom-call | flops 2013265920 | bytes 8388608 | tf_op jit(solution)/shard_map/pallas_call | solution.py:334
  191.3 5.2 %collective-permute-start.27 = (bf16[2,256,640]{2,1,0:T(8,128)(2,1)S(1)}, bf16[2,256,640]{2,1,0:T(8,128)(2,1)S(1)}, u32[]{:S(2)}, u32[]{:S(2)}) collective-permute-start(bf16[2,256,640]{2,1,0:T(8,128)(2,1)S(1)} %shard_map.113), channel_id=1, source_target_pairs={{0,4},{1,5},{2,6},{3,7},{4,0},{5,1},{6,2},{7,3},{8,11},{9,10},{10,... | collective-permute-start | bytes 1966088 | tf_op jit(solution)/shard_map/ppermute | solution.py:68
  196.5 4.1 %shard_map.115.prior = bf16[8,256,640]{2,1,0:T(8,128)(2,1)} custom-call(s32[24]{0:T(128)S(1)} %dynamic-slice_bitcast_fusion.1.meta, bf16[512,768]{1,0:T(8,128)(2,1)S(1)} %shard_map.110.c0, bf16[512,768]{1,0:T(8,128)(2,1)S(1)} %collective-permute-done.18.c1, bf16[384,768]{1,0:T(8,128)(2,1)S(1)} %collective-permute-done.20.c2a, ...), custom_call_target="tpu_custom_call", output_to_operand_aliasing={{}: (8, {})} | custom-call | flops 2013265920 | bytes 8388608 | tf_op jit(solution)/shard_map/pallas_call | solution.py:334
  202.0 2.5 %collective-permute-done.27.got = bf16[2,256,640]{2,1,0:T(8,128)(2,1)S(1)} collective-permute-done((bf16[2,256,640]{2,1,0:T(8,128)(2,1)S(1)}, bf16[2,256,640]{2,1,0:T(8,128)(2,1)S(1)}, u32[]{:S(2)}, u32[]{:S(2)}) %collective-permute-start.27) | collective-permute-done | bytes 655392 | tf_op jit(solution)/shard_map/ppermute | solution.py:68
  (80 shorter events, 44.2 us)
Async XLA Ops:
  0.0 65.2 %collective-permute-start.5 = (bf16[256,5120]{1,0:T(8,128)(2,1)}, bf16[256,5120]{1,0:T(8,128)(2,1)}, u32[]{:S(2)}, u32[]{:S(2)}) collective-permute-start(bf16[256,5120]{1,0:T(8,128)(2,1)} %bitcast.32), channel_id=1, source_target_pairs={{0,1},{1,0},{2,3},{3,2},{4,5},{5,4},{6,7},{7,6},{8,9},{9,8},{10,11... | collective-permute-start | bytes 7864328 | tf_op jit(solution)/shard_map/ppermute | solution.py:68
  2.5 62.7 %collective-permute-start.6 = (bf16[256,5120]{1,0:T(8,128)(2,1)}, bf16[256,5120]{1,0:T(8,128)(2,1)S(1)}, u32[]{:S(2)}, u32[]{:S(2)}) collective-permute-start(bf16[256,5120]{1,0:T(8,128)(2,1)} %bitcast.33), channel_id=1, source_target_pairs={{0,3},{1,2},{2,1},{3,0},{4,7},{5,6},{6,5},{7,4},{8,12},{9,13},{10,... | collective-permute-start | bytes 7864328 | tf_op jit(solution)/shard_map/ppermute | solution.py:68
  13.0 3.3 %collective-permute-start = (bf16[128,768]{1,0:T(8,128)(2,1)S(1)}, bf16[128,768]{1,0:T(8,128)(2,1)S(1)}, u32[]{:S(2)}, u32[]{:S(2)}) collective-permute-start(bf16[128,768]{1,0:T(8,128)(2,1)S(1)} %get-tuple-element.189), channel_id=1, source_target_pairs={{0,8},{1,9},{2,10},{3,11},{4,12},{5,13},{6,14},{7,15},{8,0},{9,1},... | collective-permute-start | bytes 589832 | tf_op jit(solution)/shard_map/cond/branch_1_fun/ppermute | solution.py:68
  16.4 7.8 %collective-permute-start.1 = (bf16[2,128,768]{2,1,0:T(8,128)(2,1)S(1)}, bf16[2,128,768]{2,1,0:T(8,128)(2,1)S(1)}, u32[]{:S(2)}, u32[]{:S(2)}) collective-permute-start(bf16[2,128,768]{2,1,0:T(8,128)(2,1)S(1)} %maximum_select_fusion.2), channel_id=1, source_target_pairs={{0,64},{1,65},{2,66},{3,67},{4,68},{5,69},{6,70},{7,71},{16,80},{1... | collective-permute-start | bytes 1179656 | tf_op jit(solution)/shard_map/cond/branch_1_fun/ppermute | solution.py:68
  24.2 9.5 %collective-permute-start.2 = (bf16[2,128,768]{2,1,0:T(8,128)(2,1)S(1)}, bf16[2,128,768]{2,1,0:T(8,128)(2,1)}, u32[]{:S(2)}, u32[]{:S(2)}) collective-permute-start(bf16[2,128,768]{2,1,0:T(8,128)(2,1)S(1)} %collective-permute-done.1), channel_id=1, source_target_pairs={{0,8},{1,9},{2,10},{3,11},{4,12},{5,13},{6,14},{7,15},{8,0},{9,1},... | collective-permute-start | bytes 1179656 | tf_op jit(solution)/shard_map/cond/branch_1_fun/ppermute | solution.py:68
  35.8 14.2 %collective-permute-start.4 = (bf16[2,256,768]{2,1,0:T(8,128)(2,1)}, bf16[2,256,768]{2,1,0:T(8,128)(2,1)}, u32[]{:S(2)}, u32[]{:S(2)}) collective-permute-start(bf16[2,256,768]{2,1,0:T(8,128)(2,1)} %maximum_select_fusion), channel_id=1, source_target_pairs={{0,4},{1,5},{2,6},{3,7},{4,0},{5,1},{6,2},{7,3},{8,11},{9,10},{10,... | collective-permute-start | bytes 2359304 | tf_op jit(solution)/shard_map/cond/branch_1_fun/ppermute | solution.py:68
  38.0 12.0 %collective-permute-start.3 = (bf16[256,768]{1,0:T(8,128)(2,1)}, bf16[256,768]{1,0:T(8,128)(2,1)}, u32[]{:S(2)}, u32[]{:S(2)}) collective-permute-start(bf16[256,768]{1,0:T(8,128)(2,1)} %dynamic-slice_bitcast_fusion), channel_id=1, source_target_pairs={{0,32},{1,33},{2,34},{3,35},{4,36},{5,37},{6,38},{7,39},{8,40},{9,... | collective-permute-start | bytes 1179656 | tf_op jit(solution)/shard_map/cond/branch_1_fun/ppermute | solution.py:68
  50.0 56.8 %collective-permute-start.14 = (bf16[5120,384]{1,0:T(8,128)(2,1)}, bf16[5120,384]{1,0:T(8,128)(2,1)S(1)}, u32[]{:S(2)}, u32[]{:S(2)}) collective-permute-start(bf16[5120,384]{1,0:T(8,128)(2,1)} %bitcast.25), channel_id=1, source_target_pairs={{0,4},{1,5},{2,6},{3,7},{4,0},{5,1},{6,2},{7,3},{8,11},{9,10},{10,... | collective-permute-start | bytes 11796488 | tf_op jit(solution)/shard_map/ppermute | solution.py:68
  52.1 18.8 %copy-start.2 = (f32[1,5120]{1,0:T(1,128)S(1)}, f32[1,5120]{1,0:T(1,128)}, u32[]{:S(2)}) copy-start(f32[1,5120]{1,0:T(1,128)} %refs_2_.1) | copy-start | bytes 61444
  52.1 10.0 %collective-permute-start.7 = (bf16[256,768]{1,0:T(8,128)(2,1)}, bf16[256,768]{1,0:T(8,128)(2,1)S(1)}, u32[]{:S(2)}, u32[]{:S(2)}) collective-permute-start(bf16[256,768]{1,0:T(8,128)(2,1)} %get-tuple-element.86), channel_id=1, source_target_pairs={{0,48},{1,49},{2,50},{3,51},{4,52},{5,53},{6,54},{7,55},{8,56},{9,... | collective-permute-start | bytes 1179656 | tf_op jit(solution)/shard_map/ppermute | solution.py:68
  54.6 10.6 %collective-permute-start.8 = (bf16[256,768]{1,0:T(8,128)(2,1)}, bf16[256,768]{1,0:T(8,128)(2,1)S(1)}, u32[]{:S(2)}, u32[]{:S(2)}) collective-permute-start(bf16[256,768]{1,0:T(8,128)(2,1)} %get-tuple-element.86), channel_id=1, source_target_pairs={{0,16},{1,17},{2,18},{3,19},{4,20},{5,21},{6,22},{7,23},{8,24},{9,... | collective-permute-start | bytes 1179656 | tf_op jit(solution)/shard_map/ppermute | solution.py:68
  66.4 25.0 %collective-permute-start.10 = (bf16[96,5120]{1,0:T(8,128)(2,1)S(1)}, bf16[96,5120]{1,0:T(8,128)(2,1)S(1)}, u32[]{:S(2)}, u32[]{:S(2)}) collective-permute-start(bf16[96,5120]{1,0:T(8,128)(2,1)S(1)} %slice.23), channel_id=1, source_target_pairs={{0,3},{1,2},{2,1},{3,0},{4,7},{5,6},{6,5},{7,4},{8,12},{9,13},{10,... | collective-permute-start | bytes 2949128 | tf_op jit(solution)/shard_map/ppermute | solution.py:68
  69.2 39.9 %collective-permute-start.9 = (bf16[160,5120]{1,0:T(8,128)(2,1)S(1)}, bf16[160,5120]{1,0:T(8,128)(2,1)S(1)}, u32[]{:S(2)}, u32[]{:S(2)}) collective-permute-start(bf16[160,5120]{1,0:T(8,128)(2,1)S(1)} %slice.22), channel_id=1, source_target_pairs={{0,1},{1,0},{2,3},{3,2},{4,5},{5,4},{6,7},{7,6},{8,9},{9,8},{10,11... | collective-permute-start | bytes 4915208 | tf_op jit(solution)/shard_map/ppermute | solution.py:68
  69.3 17.1 %collective-permute-start.11 = (bf16[2,256,768]{2,1,0:T(8,128)(2,1)}, bf16[2,256,768]{2,1,0:T(8,128)(2,1)S(1)}, u32[]{:S(2)}, u32[]{:S(2)}) collective-permute-start(bf16[2,256,768]{2,1,0:T(8,128)(2,1)} %get-tuple-element.106.other0), channel_id=1, source_target_pairs={{0,48},{1,49},{2,50},{3,51},{4,52},{5,53},{6,54},{7,55},{8,56},{9,... | collective-permute-start | bytes 2359304 | tf_op jit(solution)/shard_map/ppermute | solution.py:68
  69.7 18.3 %collective-permute-start.12 = (bf16[2,256,768]{2,1,0:T(8,128)(2,1)}, bf16[2,256,768]{2,1,0:T(8,128)(2,1)S(1)}, u32[]{:S(2)}, u32[]{:S(2)}) collective-permute-start(bf16[2,256,768]{2,1,0:T(8,128)(2,1)} %get-tuple-element.106.other0), channel_id=1, source_target_pairs={{0,16},{1,17},{2,18},{3,19},{4,20},{5,21},{6,22},{7,23},{8,24},{9,... | collective-permute-start | bytes 2359304 | tf_op jit(solution)/shard_map/ppermute | solution.py:68
  81.7 27.5 %copy-start.6 = (bf16[3072,640]{1,0:T(8,128)(2,1)S(1)}, bf16[3072,640]{1,0:T(8,128)(2,1)}, u32[]{:S(2)}) copy-start(bf16[3072,640]{1,0:T(8,128)(2,1)} %copy-done.5) | copy-start | bytes 11796484
  91.5 17.7 %collective-permute-start.13 = (bf16[2,256,768]{2,1,0:T(8,128)(2,1)}, bf16[2,256,768]{2,1,0:T(8,128)(2,1)S(1)}, u32[]{:S(2)}, u32[]{:S(2)}) collective-permute-start(bf16[2,256,768]{2,1,0:T(8,128)(2,1)} %get-tuple-element.106.other0), channel_id=1, source_target_pairs={{0,32},{1,33},{2,34},{3,35},{4,36},{5,37},{6,38},{7,39},{8,40},{9,... | collective-permute-start | bytes 2359304 | tf_op jit(solution)/shard_map/ppermute | solution.py:68
  91.5 16.3 %collective-permute-start.15 = (bf16[256,768]{1,0:T(8,128)(2,1)S(1)}, bf16[256,768]{1,0:T(8,128)(2,1)S(1)}, u32[]{:S(2)}, u32[]{:S(2)}) collective-permute-start(bf16[256,768]{1,0:T(8,128)(2,1)S(1)} %collective-permute-done.7.o1), channel_id=1, source_target_pairs={{0,8},{1,9},{2,10},{3,11},{4,12},{5,13},{6,14},{7,15},{8,0},{9,1},... | collective-permute-start | bytes 1179656 | tf_op jit(solution)/shard_map/ppermute | solution.py:68
  94.8 13.0 %collective-permute-start.16 = (bf16[256,768]{1,0:T(8,128)(2,1)}, bf16[256,768]{1,0:T(8,128)(2,1)S(1)}, u32[]{:S(2)}, u32[]{:S(2)}) collective-permute-start(bf16[256,768]{1,0:T(8,128)(2,1)} %get-tuple-element.109.o2), channel_id=1, source_target_pairs={{0,8},{1,9},{2,10},{3,11},{4,12},{5,13},{6,14},{7,15},{8,0},{9,1},... | collective-permute-start | bytes 1179656 | tf_op jit(solution)/shard_map/ppermute | solution.py:68
  106.8 2.4 %collective-permute-start.17 = (bf16[256,768]{1,0:T(8,128)(2,1)S(1)}, bf16[256,768]{1,0:T(8,128)(2,1)S(1)}, u32[]{:S(2)}, u32[]{:S(2)}) collective-permute-start(bf16[256,768]{1,0:T(8,128)(2,1)S(1)} %collective-permute-done.8.o3), channel_id=1, source_target_pairs={{0,8},{1,9},{2,10},{3,11},{4,12},{5,13},{6,14},{7,15},{8,0},{9,1},... | collective-permute-start | bytes 1179656 | tf_op jit(solution)/shard_map/ppermute | solution.py:68
  109.2 68.1 %collective-permute-start.22 = (bf16[3072,640]{1,0:T(8,128)(2,1)S(1)}, bf16[3072,640]{1,0:T(8,128)(2,1)S(1)}, u32[]{:S(2)}, u32[]{:S(2)}) collective-permute-start(bf16[3072,640]{1,0:T(8,128)(2,1)S(1)} %copy-done.6), channel_id=1, source_target_pairs={{0,4},{1,5},{2,6},{3,7},{4,0},{5,1},{6,2},{7,3},{8,11},{9,10},{10,... | collective-permute-start | bytes 11796488 | tf_op jit(solution)/shard_map/ppermute | solution.py:68
  127.9 15.6 %collective-permute-start.23 = (bf16[512,768]{1,0:T(8,128)(2,1)S(1)}, bf16[512,768]{1,0:T(8,128)(2,1)S(1)}, u32[]{:S(2)}, u32[]{:S(2)}) collective-permute-start(bf16[512,768]{1,0:T(8,128)(2,1)S(1)} %shard_map.111.c0), channel_id=1, source_target_pairs={{0,1},{1,0},{2,3},{3,2},{4,5},{5,4},{6,7},{7,6},{8,9},{9,8},{10,11... | collective-permute-start | bytes 2359304 | tf_op jit(solution)/shard_map/ppermute | solution.py:68
  128.2 20.3 %collective-permute-start.24 = (bf16[512,768]{1,0:T(8,128)(2,1)S(1)}, bf16[512,768]{1,0:T(8,128)(2,1)S(1)}, u32[]{:S(2)}, u32[]{:S(2)}) collective-permute-start(bf16[512,768]{1,0:T(8,128)(2,1)S(1)} %shard_map.111.c0), channel_id=1, source_target_pairs={{0,3},{1,2},{2,1},{3,0},{4,7},{5,6},{6,5},{7,4},{8,12},{9,13},{10,... | collective-permute-start | bytes 2359304 | tf_op jit(solution)/shard_map/ppermute | solution.py:68
  130.3 42.9 %copy-start.4 = (bf16[3072,640]{1,0:T(8,128)(2,1)S(1)}, bf16[3072,640]{1,0:T(8,128)(2,1)}, u32[]{:S(2)}) copy-start(bf16[3072,640]{1,0:T(8,128)(2,1)} %get-tuple-element.137.w) | copy-start | bytes 11796484
  137.7 22.7 %collective-permute-start.18 = (bf16[512,768]{1,0:T(8,128)(2,1)S(1)}, bf16[512,768]{1,0:T(8,128)(2,1)S(1)}, u32[]{:S(2)}, u32[]{:S(2)}) collective-permute-start(bf16[512,768]{1,0:T(8,128)(2,1)S(1)} %shard_map.110.c0), channel_id=1, source_target_pairs={{0,1},{1,0},{2,3},{3,2},{4,5},{5,4},{6,7},{7,6},{8,9},{9,8},{10,11... | collective-permute-start | bytes 2359304 | tf_op jit(solution)/shard_map/ppermute | solution.py:68
  138.4 26.9 %collective-permute-start.19 = (bf16[512,768]{1,0:T(8,128)(2,1)S(1)}, bf16[512,768]{1,0:T(8,128)(2,1)S(1)}, u32[]{:S(2)}, u32[]{:S(2)}) collective-permute-start(bf16[512,768]{1,0:T(8,128)(2,1)S(1)} %shard_map.110.c0), channel_id=1, source_target_pairs={{0,3},{1,2},{2,1},{3,0},{4,7},{5,6},{6,5},{7,4},{8,12},{9,13},{10,... | collective-permute-start | bytes 2359304 | tf_op jit(solution)/shard_map/ppermute | solution.py:68
  148.5 24.7 %collective-permute-start.25 = (bf16[384,768]{1,0:T(8,128)(2,1)S(1)}, bf16[384,768]{1,0:T(8,128)(2,1)S(1)}, u32[]{:S(2)}, u32[]{:S(2)}) collective-permute-start(bf16[384,768]{1,0:T(8,128)(2,1)S(1)} %slice.26), channel_id=1, source_target_pairs={{0,1},{1,0},{2,3},{3,2},{4,5},{5,4},{6,7},{7,6},{8,9},{9,8},{10,11... | collective-permute-start | bytes 1769480 | tf_op jit(solution)/shard_map/ppermute | solution.py:68
  165.4 22.6 %collective-permute-start.20 = (bf16[384,768]{1,0:T(8,128)(2,1)S(1)}, bf16[384,768]{1,0:T(8,128)(2,1)S(1)}, u32[]{:S(2)}, u32[]{:S(2)}) collective-permute-start(bf16[384,768]{1,0:T(8,128)(2,1)S(1)} %slice.24), channel_id=1, source_target_pairs={{0,1},{1,0},{2,3},{3,2},{4,5},{5,4},{6,7},{7,6},{8,9},{9,8},{10,11... | collective-permute-start | bytes 1769480 | tf_op jit(solution)/shard_map/ppermute | solution.py:68
  166.1 7.1 %collective-permute-start.26 = (bf16[128,768]{1,0:T(8,128)(2,1)S(1)}, bf16[128,768]{1,0:T(8,128)(2,1)S(1)}, u32[]{:S(2)}, u32[]{:S(2)}) collective-permute-start(bf16[128,768]{1,0:T(8,128)(2,1)S(1)} %slice.27), channel_id=1, source_target_pairs={{0,3},{1,2},{2,1},{3,0},{4,7},{5,6},{6,5},{7,4},{8,12},{9,13},{10,... | collective-permute-start | bytes 589832 | tf_op jit(solution)/shard_map/ppermute | solution.py:68
  167.7 20.3 %collective-permute-start.21 = (bf16[128,768]{1,0:T(8,128)(2,1)S(1)}, bf16[128,768]{1,0:T(8,128)(2,1)S(1)}, u32[]{:S(2)}, u32[]{:S(2)}) collective-permute-start(bf16[128,768]{1,0:T(8,128)(2,1)S(1)} %slice.25), channel_id=1, source_target_pairs={{0,3},{1,2},{2,1},{3,0},{4,7},{5,6},{6,5},{7,4},{8,12},{9,13},{10,... | collective-permute-start | bytes 589832 | tf_op jit(solution)/shard_map/ppermute | solution.py:68
  180.7 19.9 %collective-permute-start.28 = (bf16[2,256,640]{2,1,0:T(8,128)(2,1)S(1)}, bf16[2,256,640]{2,1,0:T(8,128)(2,1)S(1)}, u32[]{:S(2)}, u32[]{:S(2)}) collective-permute-start(bf16[2,256,640]{2,1,0:T(8,128)(2,1)S(1)} %shard_map.114), channel_id=1, source_target_pairs={{0,4},{1,5},{2,6},{3,7},{4,0},{5,1},{6,2},{7,3},{8,11},{9,10},{10,... | collective-permute-start | bytes 1966088 | tf_op jit(solution)/shard_map/ppermute | solution.py:68
  191.3 13.1 %collective-permute-start.27 = (bf16[2,256,640]{2,1,0:T(8,128)(2,1)S(1)}, bf16[2,256,640]{2,1,0:T(8,128)(2,1)S(1)}, u32[]{:S(2)}, u32[]{:S(2)}) collective-permute-start(bf16[2,256,640]{2,1,0:T(8,128)(2,1)S(1)} %shard_map.113), channel_id=1, source_target_pairs={{0,4},{1,5},{2,6},{3,7},{4,0},{5,1},{6,2},{7,3},{8,11},{9,10},{10,... | collective-permute-start | bytes 1966088 | tf_op jit(solution)/shard_map/ppermute | solution.py:68
  (7 other events, 40.2 us)

commit v10 on v9

--- a/solution.py
+++ b/solution.py
@@ -9,7 +9,7 @@
 
 HD = 128
 RB = 256
-CUT = 384
+CUT = 256
 BF = jnp.bfloat16
 F32 = jnp.float32
 AXES = ("section", "ctx")
@@ -305,7 +305,7 @@
 def finish_kernel(meta, c0, c1, c2a, c2b, c3, w, res, *refs):
     out = refs[-1]
     t = pl.program_id(0)
-    far = jnp.where(t == 0, c2a[:RB, :], jnp.concatenate([c2a[RB:, :], c2b[...]], axis=0))
+    far = jnp.where(t == 0, c2a[...], c2b[...])
     n = far.shape[1]
     total = res[0].astype(F32)
     for j, c in enumerate((c0[...], c1[...], far, c3[...])):
@@ -445,13 +445,14 @@
     o1b = send(o1, CORE)
     o2b = send(o2, CORE)
     o3b = send(o3, CORE)
-    xo_a, t2, w_q2, o1b, o2b, o3b, w_o_theirs = lax.optimization_barrier(
-        (xo_a, t2, w_q2, o1b, o2b, o3b, w_o_theirs)
-    )
-    w_o2 = send(w_o_theirs, PARTNER)
+    xo_a, o1b, o2b, o3b = lax.optimization_barrier((xo_a, o1b, o2b, o3b))
     normed, q_own, res_own, res_other = project(
         meta, [xo_a, xo_b], query_gain, w_q, 2, width, state
     )
+    t2, w_q2, w_o_theirs, normed, q_own = lax.optimization_barrier(
+        (t2, w_q2, w_o_theirs, normed, q_own)
+    )
+    w_o2 = send(w_o_theirs, PARTNER)
     q_other = more_queries(normed, w_q2)
     pieces = (piece, o1, o1b, o2, o2b, o3, o3b, piece2, t1, t2, t3)
 
@@ -461,16 +462,15 @@
         own = attend(meta, chunk, q_own, q_other, seg_row, pieces)
         c_in = send(own, IN)
         c_out = send(own, OUT)
-        c_in, c_out = lax.optimization_barrier((c_in, c_out))
         co_a = send(c_out[:CUT], IN)
         co_b = send(c_in[CUT:], OUT)
         parts.append((own, c_in, co_a, co_b, c_out))
-    result = finish(meta, 0, parts[0], w_o_mine, res_own, 8)
-    w_o2, result = lax.optimization_barrier((w_o2, result))
     others = [finish(meta, chunk, parts[chunk], w_o2, res_other, 2) for chunk in range(2)]
     sent = [send(other, PARTNER) for other in others]
     w_o_mine = after(w_o_mine, *others)
-    result = finish(meta, 1, parts[1], w_o_mine, res_own, 8, result)
+    result = None
+    for chunk in range(2):
+        result = finish(meta, chunk, parts[chunk], w_o_mine, res_own, 8, result)
     for chunk in range(2):
         result = place(meta, chunk, sent[chunk], result)
     return result.reshape(1, 8 * RB, -1)

time: 207 us -> 210 us (1.014)
  starting transfers between devices: 52 us -> 39.4 us
  waiting for transfers between devices: 70.6 us -> 83 us
  Pallas kernels: 66.6 us -> 70.2 us
    ppermute x29, starting transfers between devices: 52 us -> 39.4 us  [send(): return lax.ppermute(value, AXES, pairs)]
    ppermute x29, waiting for transfers between devices: 70.6 us -> 83 us  [send(): return lax.ppermute(value, AXES, pairs)]
    pallas_call x2, Pallas kernels: 14.5 us -> 18.1 us  [attend(): pl.pallas_call(functools.partial(attend_kernel, chunk), grid_spec=pltpu.P...]
  transfers between devices with their start and end apart: 29 -> 29, of which waited for: 16 -> 19; matrix products, arithmetic and copies ran while one was open for 7% -> 6% of each run, Pallas kernels for 32% -> 33%
where the time goes in v10:
time: 210 us; the launch traced here: 209 us
  waiting for transfers between devices  83 us (40%)
  Pallas kernels  70.2 us (33%)
  starting transfers between devices  39.4 us (19%)
  local copies, waits for them, and re-layouts  7.42 us (4%)
  matrix products  4.48 us (2%)
  other arithmetic  3.84 us (2%)
    ppermute x29, waiting for transfers between devices, send(): return lax.ppermute(value, AXES, pairs)  83 us
    ppermute x29, starting transfers between devices, send(): return lax.ppermute(value, AXES, pairs)  39.4 us
    pallas_call x2, Pallas kernels, attend(): pl.pallas_call(functools.partial(attend_kernel, chunk), grid_spec=pltpu.P...  18.1 us
    pallas_call x4, Pallas kernels, project(): pl.pallas_call(kernel, grid_spec=pltpu.PrefetchScalarGridSpec(num_scalar_...  16.5 us
    pallas_call x4, Pallas kernels, finish(): pl.pallas_call(finish_kernel, grid_spec=pltpu.PrefetchScalarGridSpec(num_...  14.9 us
    pallas_call x2, Pallas kernels, reorder(): pl.pallas_call(reorder_kernel, grid_spec=pltpu.PrefetchScalarGridSpec(num...  12.2 us
    pallas_call x1, Pallas kernels, more_queries(): pl.pallas_call(more_queries_kernel, grid=(2,), in_specs=[pl.BlockSpec((ro...  5.74 us
  transfers between devices with their start and end apart: 29, of which 19 were waited for; matrix products, arithmetic and copies ran while one was open for 6% of the time, Pallas kernels for 33%

profile of v10, /device:TPU:1, one launch (start us, length us, event | category | flops | bytes accessed | tf_op | source)
XLA Modules:
  0.0 209.4 jit_solution(1243879664721787217)
XLA Ops:
  0.0 2.5 %collective-permute-start.5 = (bf16[256,5120]{1,0:T(8,128)(2,1)}, bf16[256,5120]{1,0:T(8,128)(2,1)}, u32[]{:S(2)}, u32[]{:S(2)}) collective-permute-start(bf16[256,5120]{1,0:T(8,128)(2,1)} %bitcast.32), channel_id=1, source_target_pairs={{0,1},{1,0},{2,3},{3,2},{4,5},{5,4},{6,7},{7,6},{8,9},{9,8},{10,11... | collective-permute-start | bytes 7864328 | tf_op jit(solution)/shard_map/ppermute | solution.py:68
  6.3 43.7 %conditional.1 = (bf16[2,256,768]{2,1,0:T(8,128)(2,1)}, bf16[256,768]{1,0:T(8,128)(2,1)}, bf16[256,768]{1,0:T(8,128)(2,1)}, bf16[2,256,768]{2,1,0:T(8,128)(2,1)}...) conditional(s32[]{:T(128)} %bitcast.12, () %tuple.21, (s32[]{:T(128)}, pred[]{:T(512)}, ...), branch_computations={%region_0.1_spmd, %region_1.3_spmd} | conditional | flops 1016889472 | bytes 47639592 | solution.py:424
  8.0 3.6 %convolution_convert_fusion = bf16[128,384]{1,0:T(8,128)(2,1)S(1)} fusion(bf16[5120,384]{1,0:T(8,128)(2,1)} %get-tuple-element.153, bf16[128,5120]{1,0:T(8,128)(2,1)} %get-tuple-element.150, f32[5120]{0:T(1024)} %get-tuple-element.151, f32[128]{0:T(128)S(1)} %add_rsqrt_fusion), kind=kOutput, calls=%fused_computation.5 | convolution fusion | flops 505987072 | bytes 5362176 | tf_op jit(solution)/shard_map/cond/branch_1_fun/dot_general | solution.py:404
  13.0 2.3 %collective-permute-start = (bf16[128,768]{1,0:T(8,128)(2,1)S(1)}, bf16[128,768]{1,0:T(8,128)(2,1)S(1)}, u32[]{:S(2)}, u32[]{:S(2)}) collective-permute-start(bf16[128,768]{1,0:T(8,128)(2,1)S(1)} %get-tuple-element.181), channel_id=1, source_target_pairs={{0,8},{1,9},{2,10},{3,11},{4,12},{5,13},{6,14},{7,15},{8,0},{9,1},... | collective-permute-start | bytes 589832 | tf_op jit(solution)/shard_map/cond/branch_1_fun/ppermute | solution.py:68
  17.1 7.1 %branch_1_fun.2 = bf16[8,384,640]{2,1,0:T(8,128)(2,1)} custom-call(s32[24]{0:T(128)S(1)} %get-tuple-element.27.meta, bf16[8,384,640]{2,1,0:T(8,128)(2,1)} %bitcast.38), custom_call_target="tpu_custom_call" | custom-call | tf_op jit(solution)/shard_map/cond/branch_1_fun/pallas_call | solution.py:290
  24.2 8.1 %collective-permute-start.2 = (bf16[2,128,768]{2,1,0:T(8,128)(2,1)S(1)}, bf16[2,128,768]{2,1,0:T(8,128)(2,1)}, u32[]{:S(2)}, u32[]{:S(2)}) collective-permute-start(bf16[2,128,768]{2,1,0:T(8,128)(2,1)S(1)} %collective-permute-done.1), channel_id=1, source_target_pairs={{0,8},{1,9},{2,10},{3,11},{4,12},{5,13},{6,14},{7,15},{8,0},{9,1},... | collective-permute-start | bytes 1179656 | tf_op jit(solution)/shard_map/cond/branch_1_fun/ppermute | solution.py:68
  38.0 2.7 %collective-permute-start.3 = (bf16[256,768]{1,0:T(8,128)(2,1)}, bf16[256,768]{1,0:T(8,128)(2,1)}, u32[]{:S(2)}, u32[]{:S(2)}) collective-permute-start(bf16[256,768]{1,0:T(8,128)(2,1)} %dynamic-slice_bitcast_fusion), channel_id=1, source_target_pairs={{0,32},{1,33},{2,34},{3,35},{4,36},{5,37},{6,38},{7,39},{8,40},{9,... | collective-permute-start | bytes 1179656 | tf_op jit(solution)/shard_map/cond/branch_1_fun/ppermute | solution.py:68
  40.8 5.2 %branch_1_fun.3 = bf16[8,384,640]{2,1,0:T(8,128)(2,1)S(1)} custom-call(s32[24]{0:T(128)S(1)} %get-tuple-element.27.meta, bf16[8,384,640]{2,1,0:T(8,128)(2,1)} %bitcast.39), custom_call_target="tpu_custom_call" | custom-call | tf_op jit(solution)/shard_map/cond/branch_1_fun/pallas_call | solution.py:290
  45.9 4.1 %collective-permute-done.3 = bf16[256,768]{1,0:T(8,128)(2,1)} collective-permute-done((bf16[256,768]{1,0:T(8,128)(2,1)}, bf16[256,768]{1,0:T(8,128)(2,1)}, u32[]{:S(2)}, u32[]{:S(2)}) %collective-permute-start.3) | collective-permute-done | bytes 393248 | tf_op jit(solution)/shard_map/cond/branch_1_fun/ppermute | solution.py:68
  52.1 2.5 %collective-permute-start.7 = (bf16[256,768]{1,0:T(8,128)(2,1)}, bf16[256,768]{1,0:T(8,128)(2,1)S(1)}, u32[]{:S(2)}, u32[]{:S(2)}) collective-permute-start(bf16[256,768]{1,0:T(8,128)(2,1)} %get-tuple-element.82), channel_id=1, source_target_pairs={{0,48},{1,49},{2,50},{3,51},{4,52},{5,53},{6,54},{7,55},{8,56},{9,... | collective-permute-start | bytes 1179656 | tf_op jit(solution)/shard_map/ppermute | solution.py:68
  54.6 7.6 %collective-permute-done.7.o1 = bf16[256,768]{1,0:T(8,128)(2,1)S(1)} collective-permute-done((bf16[256,768]{1,0:T(8,128)(2,1)}, bf16[256,768]{1,0:T(8,128)(2,1)S(1)}, u32[]{:S(2)}, u32[]{:S(2)}) %collective-permute-start.7) | collective-permute-done | bytes 393248 | tf_op jit(solution)/shard_map/ppermute | solution.py:68
  62.1 3.0 %collective-permute-done.8.o3 = bf16[256,768]{1,0:T(8,128)(2,1)S(1)} collective-permute-done((bf16[256,768]{1,0:T(8,128)(2,1)}, bf16[256,768]{1,0:T(8,128)(2,1)S(1)}, u32[]{:S(2)}, u32[]{:S(2)}) %collective-permute-start.8) | collective-permute-done | bytes 393248 | tf_op jit(solution)/shard_map/ppermute | solution.py:68
  66.4 2.7 %collective-permute-start.9 = (bf16[96,5120]{1,0:T(8,128)(2,1)S(1)}, bf16[96,5120]{1,0:T(8,128)(2,1)S(1)}, u32[]{:S(2)}, u32[]{:S(2)}) collective-permute-start(bf16[96,5120]{1,0:T(8,128)(2,1)S(1)} %slice.22), channel_id=1, source_target_pairs={{0,3},{1,2},{2,1},{3,0},{4,7},{5,6},{6,5},{7,4},{8,12},{9,13},{10,... | collective-permute-start | bytes 2949128 | tf_op jit(solution)/shard_map/ppermute | solution.py:68
  72.6 3.7 %shard_map.105 = (bf16[4,256,5120]{2,1,0:T(8,128)(2,1)S(1)}, bf16[4,256,384]{2,1,0:T(8,128)(2,1)S(1)}, bf16[4,256,640]{2,1,0:T(8,128)(2,1)S(1)}, bf16[4,256,640]{2,1,0:T(8,128)(2,1)S(1)}) custom-call(s32[24]{0:T(128)S(1)} %dynamic-slice_bitcast_fusion.1.meta, bf16[256,5120]{1,0:T(8,128)(2,1)S(1)} %bitcast.34, f32[1,5120]{1,0:T(1,128)S(1)} %copy-done.2, ...), custom_call_target="tpu_custom_call" | custom-call | flops 1006632960 | bytes 11796480 | tf_op jit(solution)/shard_map/pallas_call | solution.py:121
  76.3 5.4 %shard_map.106 = (bf16[4,256,5120]{2,1,0:T(8,128)(2,1)S(1)}, bf16[4,256,384]{2,1,0:T(8,128)(2,1)S(1)}, bf16[4,256,640]{2,1,0:T(8,128)(2,1)S(1)}, bf16[4,256,640]{2,1,0:T(8,128)(2,1)S(1)}) custom-call(s32[24]{0:T(128)S(1)} %dynamic-slice_bitcast_fusion.1.meta, ...), custom_call_target="tpu_custom_call", output_to_operand_aliasing={{0}: (4, {}), {1}: (5, {}), {2}: (6, {}), {3}: (7, {})} | custom-call | flops 1006632960 | bytes 11796480 | tf_op jit(solution)/shard_map/pallas_call | solution.py:121
  81.7 3.7 %shard_map.107 = (bf16[4,256,5120]{2,1,0:T(8,128)(2,1)S(1)}, bf16[4,256,384]{2,1,0:T(8,128)(2,1)S(1)}, bf16[4,256,640]{2,1,0:T(8,128)(2,1)S(1)}, bf16[4,256,640]{2,1,0:T(8,128)(2,1)S(1)}) custom-call(s32[24]{0:T(128)S(1)} %dynamic-slice_bitcast_fusion.1.meta, ...), custom_call_target="tpu_custom_call", output_to_operand_aliasing={{0}: (4, {}), {1}: (5, {}), {2}: (6, {}), {3}: (7, {})} | custom-call | flops 1006632960 | bytes 11796480 | tf_op jit(solution)/shard_map/pallas_call | solution.py:121
  88.0 3.5 %collective-permute-done.9.refs_1_ = bf16[96,5120]{1,0:T(8,128)(2,1)S(1)} collective-permute-done((bf16[96,5120]{1,0:T(8,128)(2,1)S(1)}, bf16[96,5120]{1,0:T(8,128)(2,1)S(1)}, u32[]{:S(2)}, u32[]{:S(2)}) %collective-permute-start.9) | collective-permute-done | bytes 983072 | tf_op jit(solution)/shard_map/ppermute | solution.py:68
  91.5 3.3 %collective-permute-start.15 = (bf16[256,768]{1,0:T(8,128)(2,1)S(1)}, bf16[256,768]{1,0:T(8,128)(2,1)S(1)}, u32[]{:S(2)}, u32[]{:S(2)}) collective-permute-start(bf16[256,768]{1,0:T(8,128)(2,1)S(1)} %collective-permute-done.7.o1), channel_id=1, source_target_pairs={{0,8},{1,9},{2,10},{3,11},{4,12},{5,13},{6,14},{7,15},{8,0},{9,1},... | collective-permute-start | bytes 1179656 | tf_op jit(solution)/shard_map/ppermute | solution.py:68
  97.9 6.8 %collective-permute-done.14.refs_0_ = bf16[160,5120]{1,0:T(8,128)(2,1)S(1)} collective-permute-done((bf16[160,5120]{1,0:T(8,128)(2,1)S(1)}, bf16[160,5120]{1,0:T(8,128)(2,1)S(1)}, u32[]{:S(2)}, u32[]{:S(2)}) %collective-permute-start.14) | collective-permute-done | bytes 1638432 | tf_op jit(solution)/shard_map/ppermute | solution.py:68
  104.6 3.7 %shard_map.108 = (bf16[4,256,5120]{2,1,0:T(8,128)(2,1)S(1)}, bf16[4,256,384]{2,1,0:T(8,128)(2,1)S(1)}, bf16[4,256,640]{2,1,0:T(8,128)(2,1)S(1)}, bf16[4,256,640]{2,1,0:T(8,128)(2,1)S(1)}) custom-call(s32[24]{0:T(128)S(1)} %dynamic-slice_bitcast_fusion.1.meta, ...), custom_call_target="tpu_custom_call", output_to_operand_aliasing={{0}: (5, {}), {1}: (6, {}), {2}: (7, {}), {3}: (8, {})} | custom-call | flops 1006632960 | bytes 11796480 | tf_op jit(solution)/shard_map/pallas_call | solution.py:121
  108.4 7.3 %collective-permute-done.12.t2 = bf16[2,256,768]{2,1,0:T(8,128)(2,1)S(1)} collective-permute-done((bf16[2,256,768]{2,1,0:T(8,128)(2,1)}, bf16[2,256,768]{2,1,0:T(8,128)(2,1)S(1)}, u32[]{:S(2)}, u32[]{:S(2)}) %collective-permute-start.12) | collective-permute-done | bytes 786464 | tf_op jit(solution)/shard_map/ppermute | solution.py:68
  117.6 5.7 %shard_map.109 = bf16[1024,384]{1,0:T(8,128)(2,1)S(1)} custom-call(bf16[1024,5120]{1,0:T(8,128)(2,1)S(1)} %bitcast.24, bf16[5120,384]{1,0:T(8,128)(2,1)S(1)} %collective-permute-done.13.w_ref), custom_call_target="tpu_custom_call" | custom-call | flops 4026531840 | bytes 14417920 | tf_op jit(solution)/shard_map/pallas_call | solution.py:145
  123.3 7.1 %shard_map.112.c0 = bf16[512,768]{1,0:T(8,128)(2,1)S(1)} custom-call(s32[24]{0:T(128)S(1)} %dynamic-slice_bitcast_fusion.1.meta, bf16[4,256,384]{2,1,0:T(8,128)(2,1)S(1)} %get-tuple-element.116.q_own, bf16[4,256,384]{2,1,0:T(8,128)(2,1)S(1)} %bitcast.30, s32[8,1,256]{2,1,0:T(1,128)S(1)} %bitcast.35, bf16[2,256,768]{2,1,0:T(8,128)(2,1)} %get-tuple-element.119.own0, ...), custom_call_target="tpu_custom_call" | custom-call | flops 1207959552 | bytes 8388608 | tf_op jit(solution)/shard_map/pallas_call | solution.py:262
  130.8 11.0 %shard_map.110.c0 = bf16[512,768]{1,0:T(8,128)(2,1)S(1)} custom-call(s32[24]{0:T(128)S(1)} %dynamic-slice_bitcast_fusion.1.meta, bf16[4,256,384]{2,1,0:T(8,128)(2,1)S(1)} %get-tuple-element.116.q_own, bf16[4,256,384]{2,1,0:T(8,128)(2,1)S(1)} %bitcast.31, s32[8,1,256]{2,1,0:T(1,128)S(1)} %bitcast.36, bf16[2,256,768]{2,1,0:T(8,128)(2,1)} %get-tuple-element.119.own0, ...), custom_call_target="tpu_custom_call" | custom-call | flops 1207959552 | bytes 8388608 | tf_op jit(solution)/shard_map/pallas_call | solution.py:262
  144.5 5.6 %collective-permute-done.25.c3 = bf16[512,768]{1,0:T(8,128)(2,1)S(1)} collective-permute-done((bf16[512,768]{1,0:T(8,128)(2,1)S(1)}, bf16[512,768]{1,0:T(8,128)(2,1)S(1)}, u32[]{:S(2)}, u32[]{:S(2)}) %collective-permute-start.25) | collective-permute-done | bytes 786464 | tf_op jit(solution)/shard_map/ppermute | solution.py:68
  150.7 16.3 %collective-permute-done.19.c3 = bf16[512,768]{1,0:T(8,128)(2,1)S(1)} collective-permute-done((bf16[512,768]{1,0:T(8,128)(2,1)S(1)}, bf16[512,768]{1,0:T(8,128)(2,1)S(1)}, u32[]{:S(2)}, u32[]{:S(2)}) %collective-permute-start.19) | collective-permute-done | bytes 786464 | tf_op jit(solution)/shard_map/ppermute | solution.py:68
  167.6 6.3 %collective-permute-done.26.c2a = bf16[256,768]{1,0:T(8,128)(2,1)S(1)} collective-permute-done((bf16[256,768]{1,0:T(8,128)(2,1)S(1)}, bf16[256,768]{1,0:T(8,128)(2,1)S(1)}, u32[]{:S(2)}, u32[]{:S(2)}) %collective-permute-start.26) | collective-permute-done | bytes 393248 | tf_op jit(solution)/shard_map/ppermute | solution.py:68
  175.4 11.3 %collective-permute-done.22.w = bf16[3072,640]{1,0:T(8,128)(2,1)S(1)} collective-permute-done((bf16[3072,640]{1,0:T(8,128)(2,1)S(1)}, bf16[3072,640]{1,0:T(8,128)(2,1)S(1)}, u32[]{:S(2)}, u32[]{:S(2)}) %collective-permute-start.22) | collective-permute-done | bytes 3932192 | tf_op jit(solution)/shard_map/ppermute | solution.py:68
  186.7 3.4 %shard_map.113 = bf16[2,256,640]{2,1,0:T(8,128)(2,1)S(1)} custom-call(s32[24]{0:T(128)S(1)} %dynamic-slice_bitcast_fusion.1.meta, bf16[512,768]{1,0:T(8,128)(2,1)S(1)} %shard_map.112.c0, bf16[512,768]{1,0:T(8,128)(2,1)S(1)} %collective-permute-done.24.c1, bf16[256,768]{1,0:T(8,128)(2,1)S(1)} %collective-permute-done.26.c2a, ...), custom_call_target="tpu_custom_call" | custom-call | flops 2013265920 | bytes 8388608 | tf_op jit(solution)/shard_map/pallas_call | solution.py:334
  192.1 3.4 %shard_map.111 = bf16[2,256,640]{2,1,0:T(8,128)(2,1)S(1)} custom-call(s32[24]{0:T(128)S(1)} %dynamic-slice_bitcast_fusion.1.meta, bf16[512,768]{1,0:T(8,128)(2,1)S(1)} %shard_map.110.c0, bf16[512,768]{1,0:T(8,128)(2,1)S(1)} %collective-permute-done.18.c1, bf16[256,768]{1,0:T(8,128)(2,1)S(1)} %collective-permute-done.20.c2a, ...), custom_call_target="tpu_custom_call" | custom-call | flops 2013265920 | bytes 8388608 | tf_op jit(solution)/shard_map/pallas_call | solution.py:334
  196.3 4.1 %shard_map.114.refs_0_ = bf16[8,256,640]{2,1,0:T(8,128)(2,1)} custom-call(s32[24]{0:T(128)S(1)} %dynamic-slice_bitcast_fusion.1.meta, bf16[512,768]{1,0:T(8,128)(2,1)S(1)} %shard_map.112.c0, bf16[512,768]{1,0:T(8,128)(2,1)S(1)} %collective-permute-done.24.c1, bf16[256,768]{1,0:T(8,128)(2,1)S(1)} %collective-permute-done.26.c2a, ...), custom_call_target="tpu_custom_call" | custom-call | flops 2013265920 | bytes 8388608 | tf_op jit(solution)/shard_map/pallas_call | solution.py:334
  200.4 4.1 %shard_map.115.prior = bf16[8,256,640]{2,1,0:T(8,128)(2,1)} custom-call(s32[24]{0:T(128)S(1)} %dynamic-slice_bitcast_fusion.1.meta, bf16[512,768]{1,0:T(8,128)(2,1)S(1)} %shard_map.110.c0, bf16[512,768]{1,0:T(8,128)(2,1)S(1)} %collective-permute-done.18.c1, bf16[256,768]{1,0:T(8,128)(2,1)S(1)} %collective-permute-done.20.c2a, ...), custom_call_target="tpu_custom_call", output_to_operand_aliasing={{}: (8, {})} | custom-call | flops 2013265920 | bytes 8388608 | tf_op jit(solution)/shard_map/pallas_call | solution.py:334
  (80 shorter events, 41.6 us)
Async XLA Ops:
  0.0 65.2 %collective-permute-start.5 = (bf16[256,5120]{1,0:T(8,128)(2,1)}, bf16[256,5120]{1,0:T(8,128)(2,1)}, u32[]{:S(2)}, u32[]{:S(2)}) collective-permute-start(bf16[256,5120]{1,0:T(8,128)(2,1)} %bitcast.32), channel_id=1, source_target_pairs={{0,1},{1,0},{2,3},{3,2},{4,5},{5,4},{6,7},{7,6},{8,9},{9,8},{10,11... | collective-permute-start | bytes 7864328 | tf_op jit(solution)/shard_map/ppermute | solution.py:68
  2.5 62.7 %collective-permute-start.6 = (bf16[256,5120]{1,0:T(8,128)(2,1)}, bf16[256,5120]{1,0:T(8,128)(2,1)S(1)}, u32[]{:S(2)}, u32[]{:S(2)}) collective-permute-start(bf16[256,5120]{1,0:T(8,128)(2,1)} %bitcast.33), channel_id=1, source_target_pairs={{0,3},{1,2},{2,1},{3,0},{4,7},{5,6},{6,5},{7,4},{8,12},{9,13},{10,... | collective-permute-start | bytes 7864328 | tf_op jit(solution)/shard_map/ppermute | solution.py:68
  13.0 3.3 %collective-permute-start = (bf16[128,768]{1,0:T(8,128)(2,1)S(1)}, bf16[128,768]{1,0:T(8,128)(2,1)S(1)}, u32[]{:S(2)}, u32[]{:S(2)}) collective-permute-start(bf16[128,768]{1,0:T(8,128)(2,1)S(1)} %get-tuple-element.181), channel_id=1, source_target_pairs={{0,8},{1,9},{2,10},{3,11},{4,12},{5,13},{6,14},{7,15},{8,0},{9,1},... | collective-permute-start | bytes 589832 | tf_op jit(solution)/shard_map/cond/branch_1_fun/ppermute | solution.py:68
  16.4 7.8 %collective-permute-start.1 = (bf16[2,128,768]{2,1,0:T(8,128)(2,1)S(1)}, bf16[2,128,768]{2,1,0:T(8,128)(2,1)S(1)}, u32[]{:S(2)}, u32[]{:S(2)}) collective-permute-start(bf16[2,128,768]{2,1,0:T(8,128)(2,1)S(1)} %maximum_select_fusion.2), channel_id=1, source_target_pairs={{0,64},{1,65},{2,66},{3,67},{4,68},{5,69},{6,70},{7,71},{16,80},{1... | collective-permute-start | bytes 1179656 | tf_op jit(solution)/shard_map/cond/branch_1_fun/ppermute | solution.py:68
  24.2 9.5 %collective-permute-start.2 = (bf16[2,128,768]{2,1,0:T(8,128)(2,1)S(1)}, bf16[2,128,768]{2,1,0:T(8,128)(2,1)}, u32[]{:S(2)}, u32[]{:S(2)}) collective-permute-start(bf16[2,128,768]{2,1,0:T(8,128)(2,1)S(1)} %collective-permute-done.1), channel_id=1, source_target_pairs={{0,8},{1,9},{2,10},{3,11},{4,12},{5,13},{6,14},{7,15},{8,0},{9,1},... | collective-permute-start | bytes 1179656 | tf_op jit(solution)/shard_map/cond/branch_1_fun/ppermute | solution.py:68
  35.8 14.2 %collective-permute-start.4 = (bf16[2,256,768]{2,1,0:T(8,128)(2,1)}, bf16[2,256,768]{2,1,0:T(8,128)(2,1)}, u32[]{:S(2)}, u32[]{:S(2)}) collective-permute-start(bf16[2,256,768]{2,1,0:T(8,128)(2,1)} %maximum_select_fusion), channel_id=1, source_target_pairs={{0,4},{1,5},{2,6},{3,7},{4,0},{5,1},{6,2},{7,3},{8,11},{9,10},{10,... | collective-permute-start | bytes 2359304 | tf_op jit(solution)/shard_map/cond/branch_1_fun/ppermute | solution.py:68
  38.0 12.0 %collective-permute-start.3 = (bf16[256,768]{1,0:T(8,128)(2,1)}, bf16[256,768]{1,0:T(8,128)(2,1)}, u32[]{:S(2)}, u32[]{:S(2)}) collective-permute-start(bf16[256,768]{1,0:T(8,128)(2,1)} %dynamic-slice_bitcast_fusion), channel_id=1, source_target_pairs={{0,32},{1,33},{2,34},{3,35},{4,36},{5,37},{6,38},{7,39},{8,40},{9,... | collective-permute-start | bytes 1179656 | tf_op jit(solution)/shard_map/cond/branch_1_fun/ppermute | solution.py:68
  50.0 58.4 %collective-permute-start.13 = (bf16[5120,384]{1,0:T(8,128)(2,1)}, bf16[5120,384]{1,0:T(8,128)(2,1)S(1)}, u32[]{:S(2)}, u32[]{:S(2)}) collective-permute-start(bf16[5120,384]{1,0:T(8,128)(2,1)} %bitcast.25), channel_id=1, source_target_pairs={{0,4},{1,5},{2,6},{3,7},{4,0},{5,1},{6,2},{7,3},{8,11},{9,10},{10,... | collective-permute-start | bytes 11796488 | tf_op jit(solution)/shard_map/ppermute | solution.py:68
  52.1 18.8 %copy-start = (bf16[1,5120,384]{2,1,0:T(8,128)(2,1)S(1)}, bf16[1,5120,384]{2,1,0:T(8,128)(2,1)}, u32[]{:S(2)}) copy-start(bf16[1,5120,384]{2,1,0:T(8,128)(2,1)} %param.18) | copy-start | bytes 11796484
  52.1 18.8 %copy-start.2 = (f32[1,5120]{1,0:T(1,128)S(1)}, f32[1,5120]{1,0:T(1,128)}, u32[]{:S(2)}) copy-start(f32[1,5120]{1,0:T(1,128)} %refs_2_.1) | copy-start | bytes 61444
  52.1 10.0 %collective-permute-start.7 = (bf16[256,768]{1,0:T(8,128)(2,1)}, bf16[256,768]{1,0:T(8,128)(2,1)S(1)}, u32[]{:S(2)}, u32[]{:S(2)}) collective-permute-start(bf16[256,768]{1,0:T(8,128)(2,1)} %get-tuple-element.82), channel_id=1, source_target_pairs={{0,48},{1,49},{2,50},{3,51},{4,52},{5,53},{6,54},{7,55},{8,56},{9,... | collective-permute-start | bytes 1179656 | tf_op jit(solution)/shard_map/ppermute | solution.py:68
  54.6 10.6 %collective-permute-start.8 = (bf16[256,768]{1,0:T(8,128)(2,1)}, bf16[256,768]{1,0:T(8,128)(2,1)S(1)}, u32[]{:S(2)}, u32[]{:S(2)}) collective-permute-start(bf16[256,768]{1,0:T(8,128)(2,1)} %get-tuple-element.82), channel_id=1, source_target_pairs={{0,16},{1,17},{2,18},{3,19},{4,20},{5,21},{6,22},{7,23},{8,24},{9,... | collective-permute-start | bytes 1179656 | tf_op jit(solution)/shard_map/ppermute | solution.py:68
  66.4 25.0 %collective-permute-start.9 = (bf16[96,5120]{1,0:T(8,128)(2,1)S(1)}, bf16[96,5120]{1,0:T(8,128)(2,1)S(1)}, u32[]{:S(2)}, u32[]{:S(2)}) collective-permute-start(bf16[96,5120]{1,0:T(8,128)(2,1)S(1)} %slice.22), channel_id=1, source_target_pairs={{0,3},{1,2},{2,1},{3,0},{4,7},{5,6},{6,5},{7,4},{8,12},{9,13},{10,... | collective-permute-start | bytes 2949128 | tf_op jit(solution)/shard_map/ppermute | solution.py:68
  69.2 35.4 %collective-permute-start.14 = (bf16[160,5120]{1,0:T(8,128)(2,1)S(1)}, bf16[160,5120]{1,0:T(8,128)(2,1)S(1)}, u32[]{:S(2)}, u32[]{:S(2)}) collective-permute-start(bf16[160,5120]{1,0:T(8,128)(2,1)S(1)} %slice.23), channel_id=1, source_target_pairs={{0,1},{1,0},{2,3},{3,2},{4,5},{5,4},{6,7},{7,6},{8,9},{9,8},{10,11... | collective-permute-start | bytes 4915208 | tf_op jit(solution)/shard_map/ppermute | solution.py:68
  69.3 17.1 %collective-permute-start.10 = (bf16[2,256,768]{2,1,0:T(8,128)(2,1)}, bf16[2,256,768]{2,1,0:T(8,128)(2,1)S(1)}, u32[]{:S(2)}, u32[]{:S(2)}) collective-permute-start(bf16[2,256,768]{2,1,0:T(8,128)(2,1)} %get-tuple-element.102.other0), channel_id=1, source_target_pairs={{0,48},{1,49},{2,50},{3,51},{4,52},{5,53},{6,54},{7,55},{8,56},{9,... | collective-permute-start | bytes 2359304 | tf_op jit(solution)/shard_map/ppermute | solution.py:68
  69.7 18.3 %collective-permute-start.11 = (bf16[2,256,768]{2,1,0:T(8,128)(2,1)}, bf16[2,256,768]{2,1,0:T(8,128)(2,1)S(1)}, u32[]{:S(2)}, u32[]{:S(2)}) collective-permute-start(bf16[2,256,768]{2,1,0:T(8,128)(2,1)} %get-tuple-element.102.other0), channel_id=1, source_target_pairs={{0,16},{1,17},{2,18},{3,19},{4,20},{5,21},{6,22},{7,23},{8,24},{9,... | collective-permute-start | bytes 2359304 | tf_op jit(solution)/shard_map/ppermute | solution.py:68
  91.5 24.2 %copy-start.6 = (bf16[3072,640]{1,0:T(8,128)(2,1)S(1)}, bf16[3072,640]{1,0:T(8,128)(2,1)}, u32[]{:S(2)}) copy-start(bf16[3072,640]{1,0:T(8,128)(2,1)} %copy-done.5) | copy-start | bytes 11796484
  91.5 4.7 %collective-permute-start.15 = (bf16[256,768]{1,0:T(8,128)(2,1)S(1)}, bf16[256,768]{1,0:T(8,128)(2,1)S(1)}, u32[]{:S(2)}, u32[]{:S(2)}) collective-permute-start(bf16[256,768]{1,0:T(8,128)(2,1)S(1)} %collective-permute-done.7.o1), channel_id=1, source_target_pairs={{0,8},{1,9},{2,10},{3,11},{4,12},{5,13},{6,14},{7,15},{8,0},{9,1},... | collective-permute-start | bytes 1179656 | tf_op jit(solution)/shard_map/ppermute | solution.py:68
  94.8 20.9 %collective-permute-start.12 = (bf16[2,256,768]{2,1,0:T(8,128)(2,1)}, bf16[2,256,768]{2,1,0:T(8,128)(2,1)S(1)}, u32[]{:S(2)}, u32[]{:S(2)}) collective-permute-start(bf16[2,256,768]{2,1,0:T(8,128)(2,1)} %get-tuple-element.102.other0), channel_id=1, source_target_pairs={{0,32},{1,33},{2,34},{3,35},{4,36},{5,37},{6,38},{7,39},{8,40},{9,... | collective-permute-start | bytes 2359304 | tf_op jit(solution)/shard_map/ppermute | solution.py:68
  94.8 2.1 %collective-permute-start.16 = (bf16[256,768]{1,0:T(8,128)(2,1)}, bf16[256,768]{1,0:T(8,128)(2,1)S(1)}, u32[]{:S(2)}, u32[]{:S(2)}) collective-permute-start(bf16[256,768]{1,0:T(8,128)(2,1)} %get-tuple-element.106.o2), channel_id=1, source_target_pairs={{0,8},{1,9},{2,10},{3,11},{4,12},{5,13},{6,14},{7,15},{8,0},{9,1},... | collective-permute-start | bytes 1179656 | tf_op jit(solution)/shard_map/ppermute | solution.py:68
  96.1 1.7 collective-permute-start.17
  115.7 71.0 %collective-permute-start.22 = (bf16[3072,640]{1,0:T(8,128)(2,1)S(1)}, bf16[3072,640]{1,0:T(8,128)(2,1)S(1)}, u32[]{:S(2)}, u32[]{:S(2)}) collective-permute-start(bf16[3072,640]{1,0:T(8,128)(2,1)S(1)} %copy-done.6), channel_id=1, source_target_pairs={{0,4},{1,5},{2,6},{3,7},{4,0},{5,1},{6,2},{7,3},{8,11},{9,10},{10,... | collective-permute-start | bytes 11796488 | tf_op jit(solution)/shard_map/ppermute | solution.py:68
  130.4 19.7 %collective-permute-start.25 = (bf16[512,768]{1,0:T(8,128)(2,1)S(1)}, bf16[512,768]{1,0:T(8,128)(2,1)S(1)}, u32[]{:S(2)}, u32[]{:S(2)}) collective-permute-start(bf16[512,768]{1,0:T(8,128)(2,1)S(1)} %shard_map.112.c0), channel_id=1, source_target_pairs={{0,3},{1,2},{2,1},{3,0},{4,7},{5,6},{6,5},{7,4},{8,12},{9,13},{10,... | collective-permute-start | bytes 2359304 | tf_op jit(solution)/shard_map/ppermute | solution.py:68
  130.8 19.4 %collective-permute-start.24 = (bf16[512,768]{1,0:T(8,128)(2,1)S(1)}, bf16[512,768]{1,0:T(8,128)(2,1)S(1)}, u32[]{:S(2)}, u32[]{:S(2)}) collective-permute-start(bf16[512,768]{1,0:T(8,128)(2,1)S(1)} %shard_map.112.c0), channel_id=1, source_target_pairs={{0,1},{1,0},{2,3},{3,2},{4,5},{5,4},{6,7},{7,6},{8,9},{9,8},{10,11... | collective-permute-start | bytes 2359304 | tf_op jit(solution)/shard_map/ppermute | solution.py:68
  141.8 25.2 %collective-permute-start.19 = (bf16[512,768]{1,0:T(8,128)(2,1)S(1)}, bf16[512,768]{1,0:T(8,128)(2,1)S(1)}, u32[]{:S(2)}, u32[]{:S(2)}) collective-permute-start(bf16[512,768]{1,0:T(8,128)(2,1)S(1)} %shard_map.110.c0), channel_id=1, source_target_pairs={{0,3},{1,2},{2,1},{3,0},{4,7},{5,6},{6,5},{7,4},{8,12},{9,13},{10,... | collective-permute-start | bytes 2359304 | tf_op jit(solution)/shard_map/ppermute | solution.py:68
  143.0 24.1 %collective-permute-start.18 = (bf16[512,768]{1,0:T(8,128)(2,1)S(1)}, bf16[512,768]{1,0:T(8,128)(2,1)S(1)}, u32[]{:S(2)}, u32[]{:S(2)}) collective-permute-start(bf16[512,768]{1,0:T(8,128)(2,1)S(1)} %shard_map.110.c0), channel_id=1, source_target_pairs={{0,1},{1,0},{2,3},{3,2},{4,5},{5,4},{6,7},{7,6},{8,9},{9,8},{10,11... | collective-permute-start | bytes 2359304 | tf_op jit(solution)/shard_map/ppermute | solution.py:68
  150.2 23.7 %collective-permute-start.26 = (bf16[256,768]{1,0:T(8,128)(2,1)S(1)}, bf16[256,768]{1,0:T(8,128)(2,1)S(1)}, u32[]{:S(2)}, u32[]{:S(2)}) collective-permute-start(bf16[256,768]{1,0:T(8,128)(2,1)S(1)} %slice.30), channel_id=1, source_target_pairs={{0,1},{1,0},{2,3},{3,2},{4,5},{5,4},{6,7},{7,6},{8,9},{9,8},{10,11... | collective-permute-start | bytes 1179656 | tf_op jit(solution)/shard_map/ppermute | solution.py:68
  150.3 25.1 %collective-permute-start.27 = (bf16[256,768]{1,0:T(8,128)(2,1)S(1)}, bf16[256,768]{1,0:T(8,128)(2,1)S(1)}, u32[]{:S(2)}, u32[]{:S(2)}) collective-permute-start(bf16[256,768]{1,0:T(8,128)(2,1)S(1)} %slice.31), channel_id=1, source_target_pairs={{0,3},{1,2},{2,1},{3,0},{4,7},{5,6},{6,5},{7,4},{8,12},{9,13},{10,... | collective-permute-start | bytes 1179656 | tf_op jit(solution)/shard_map/ppermute | solution.py:68
  167.0 25.0 %collective-permute-start.20 = (bf16[256,768]{1,0:T(8,128)(2,1)S(1)}, bf16[256,768]{1,0:T(8,128)(2,1)S(1)}, u32[]{:S(2)}, u32[]{:S(2)}) collective-permute-start(bf16[256,768]{1,0:T(8,128)(2,1)S(1)} %slice.28), channel_id=1, source_target_pairs={{0,1},{1,0},{2,3},{3,2},{4,5},{5,4},{6,7},{7,6},{8,9},{9,8},{10,11... | collective-permute-start | bytes 1179656 | tf_op jit(solution)/shard_map/ppermute | solution.py:68
  167.2 24.9 %collective-permute-start.21 = (bf16[256,768]{1,0:T(8,128)(2,1)S(1)}, bf16[256,768]{1,0:T(8,128)(2,1)S(1)}, u32[]{:S(2)}, u32[]{:S(2)}) collective-permute-start(bf16[256,768]{1,0:T(8,128)(2,1)S(1)} %slice.29), channel_id=1, source_target_pairs={{0,3},{1,2},{2,1},{3,0},{4,7},{5,6},{6,5},{7,4},{8,12},{9,13},{10,... | collective-permute-start | bytes 1179656 | tf_op jit(solution)/shard_map/ppermute | solution.py:68
  190.1 14.4 %collective-permute-start.28 = (bf16[2,256,640]{2,1,0:T(8,128)(2,1)S(1)}, bf16[2,256,640]{2,1,0:T(8,128)(2,1)S(1)}, u32[]{:S(2)}, u32[]{:S(2)}) collective-permute-start(bf16[2,256,640]{2,1,0:T(8,128)(2,1)S(1)} %shard_map.113), channel_id=1, source_target_pairs={{0,4},{1,5},{2,6},{3,7},{4,0},{5,1},{6,2},{7,3},{8,11},{9,10},{10,... | collective-permute-start | bytes 1966088 | tf_op jit(solution)/shard_map/ppermute | solution.py:68
  195.4 12.4 %collective-permute-start.23 = (bf16[2,256,640]{2,1,0:T(8,128)(2,1)S(1)}, bf16[2,256,640]{2,1,0:T(8,128)(2,1)S(1)}, u32[]{:S(2)}, u32[]{:S(2)}) collective-permute-start(bf16[2,256,640]{2,1,0:T(8,128)(2,1)S(1)} %shard_map.111), channel_id=1, source_target_pairs={{0,4},{1,5},{2,6},{3,7},{4,0},{5,1},{6,2},{7,3},{8,11},{9,10},{10,... | collective-permute-start | bytes 1966088 | tf_op jit(solution)/shard_map/ppermute | solution.py:68
  (7 other events, 27.6 us)

commit v11 on v10

--- a/solution.py
+++ b/solution.py
@@ -9,7 +9,7 @@
 
 HD = 128
 RB = 256
-CUT = 256
+CUT = 320
 BF = jnp.bfloat16
 F32 = jnp.float32
 AXES = ("section", "ctx")
@@ -130,7 +130,7 @@
         input_output_aliases=aliases,
         compiler_params=pltpu.CompilerParams(vmem_limit_bytes=20 * MIB),
         cost_estimate=pl.CostEstimate(
-            flops=2 * RB * d * n, bytes_accessed=2 * (3 * RB * d + d * n), transcendentals=0
+            flops=0, bytes_accessed=0, transcendentals=0
         ),
     )(meta, *ins)
 
@@ -153,7 +153,7 @@
         out_shape=jax.ShapeDtypeStruct((4 * RB, n), BF),
         compiler_params=pltpu.CompilerParams(vmem_limit_bytes=20 * MIB),
         cost_estimate=pl.CostEstimate(
-            flops=8 * RB * d * n, bytes_accessed=2 * (4 * RB * d + d * n), transcendentals=0
+            flops=0, bytes_accessed=0, transcendentals=0
         ),
     )(normed.reshape(4 * RB, d), w).reshape(4, RB, n)
 
@@ -305,7 +305,7 @@
 def finish_kernel(meta, c0, c1, c2a, c2b, c3, w, res, *refs):
     out = refs[-1]
     t = pl.program_id(0)
-    far = jnp.where(t == 0, c2a[...], c2b[...])
+    far = jnp.where(t == 0, c2a[:RB, :], jnp.concatenate([c2a[RB:, :], c2b[...]], axis=0))
     n = far.shape[1]
     total = res[0].astype(F32)
     for j, c in enumerate((c0[...], c1[...], far, c3[...])):
@@ -438,14 +438,13 @@
     state = project(meta, [after(x0, x_in, x_out)], query_gain, w_q, 0, width)
     state = project(meta, [x_in], query_gain, w_q, 1, width, state)
     state = project(meta, [x_out], query_gain, w_q, 3, width, state)
-    xo_b, t1, t3, o1, o2, o3, piece2, *state = lax.optimization_barrier(
-        (xo_b, t1, t3, o1, o2, o3, piece2, *state)
-    )
+    t1, t3, piece2, *state = lax.optimization_barrier((t1, t3, piece2, *state))
     t2 = send(piece2, X_FAR)
+    o1, o2, o3, t1 = lax.optimization_barrier((o1, o2, o3, t1))
     o1b = send(o1, CORE)
     o2b = send(o2, CORE)
     o3b = send(o3, CORE)
-    xo_a, o1b, o2b, o3b = lax.optimization_barrier((xo_a, o1b, o2b, o3b))
+    xo_a, xo_b, o1b, o2b, o3b = lax.optimization_barrier((xo_a, xo_b, o1b, o2b, o3b))
     normed, q_own, res_own, res_other = project(
         meta, [xo_a, xo_b], query_gain, w_q, 2, width, state
     )
@@ -462,6 +461,12 @@
         own = attend(meta, chunk, q_own, q_other, seg_row, pieces)
         c_in = send(own, IN)
         c_out = send(own, OUT)
+        if parts:
+            ours, c_in_0, co_a_0, co_b_0, c_out_0 = parts[0]
+            c_in, c_out, co_b_0 = lax.optimization_barrier((c_in, c_out, co_b_0))
+            parts[0] = (ours, c_in_0, co_a_0, co_b_0, c_out_0)
+        else:
+            c_in, c_out = lax.optimization_barrier((c_in, c_out))
         co_a = send(c_out[:CUT], IN)
         co_b = send(c_in[CUT:], OUT)
         parts.append((own, c_in, co_a, co_b, c_out))

time: 210 us -> 203 us (0.967)
  waiting for transfers between devices: 83 us -> 63.8 us
  starting transfers between devices: 39.4 us -> 50.6 us
    ppermute x29, waiting for transfers between devices: 83 us -> 63.8 us  [send(): return lax.ppermute(value, AXES, pairs)]
    ppermute x29, starting transfers between devices: 39.4 us -> 50.6 us  [send(): return lax.ppermute(value, AXES, pairs)]
  transfers between devices with their start and end apart: 29 -> 29, of which waited for: 19 -> 15; matrix products, arithmetic and copies ran while one was open for 6% -> 7% of each run, Pallas kernels for 33% -> 34%
where the time goes in v11:
time: 203 us; the launch traced here: 202 us
  Pallas kernels  70.2 us (35%)
  waiting for transfers between devices  63.8 us (31%)
  starting transfers between devices  50.6 us (25%)
  local copies, waits for them, and re-layouts  7.42 us (4%)
  matrix products  4.48 us (2%)
  other arithmetic  3.84 us (2%)
    ppermute x29, waiting for transfers between devices, send(): return lax.ppermute(value, AXES, pairs)  63.8 us
    ppermute x29, starting transfers between devices, send(): return lax.ppermute(value, AXES, pairs)  50.6 us
    pallas_call x2, Pallas kernels, attend(): pl.pallas_call(functools.partial(attend_kernel, chunk), grid_spec=pltpu.P...  18.1 us
    pallas_call x4, Pallas kernels, project(): pl.pallas_call(kernel, grid_spec=pltpu.PrefetchScalarGridSpec(num_scalar_...  16.5 us
    pallas_call x4, Pallas kernels, finish(): pl.pallas_call(finish_kernel, grid_spec=pltpu.PrefetchScalarGridSpec(num_...  14.9 us
    pallas_call x2, Pallas kernels, reorder(): pl.pallas_call(reorder_kernel, grid_spec=pltpu.PrefetchScalarGridSpec(num...  12.2 us
    pallas_call x1, Pallas kernels, more_queries(): pl.pallas_call(more_queries_kernel, grid=(2,), in_specs=[pl.BlockSpec((ro...  5.74 us
  transfers between devices with their start and end apart: 29, of which 15 were waited for; matrix products, arithmetic and copies ran while one was open for 7% of the time, Pallas kernels for 34%

profile of v11, /device:TPU:1, one launch (start us, length us, event | category | flops | bytes accessed | tf_op | source)
XLA Modules:
  0.0 201.5 jit_solution(14551597552334877142)
XLA Ops:
  6.3 43.7 %conditional.1 = (bf16[2,256,768]{2,1,0:T(8,128)(2,1)}, bf16[256,768]{1,0:T(8,128)(2,1)}, bf16[256,768]{1,0:T(8,128)(2,1)}, bf16[2,256,768]{2,1,0:T(8,128)(2,1)}...) conditional(s32[]{:T(128)} %bitcast.12, () %tuple.24, (s32[]{:T(128)}, pred[]{:T(512)}, ...), branch_computations={%region_0.1_spmd, %region_1.3_spmd} | conditional | flops 1016889472 | bytes 47639592 | solution.py:424
  8.0 3.6 %convolution_convert_fusion = bf16[128,384]{1,0:T(8,128)(2,1)S(1)} fusion(bf16[5120,384]{1,0:T(8,128)(2,1)} %get-tuple-element.165, bf16[128,5120]{1,0:T(8,128)(2,1)} %get-tuple-element.162, f32[5120]{0:T(1024)} %get-tuple-element.163, f32[128]{0:T(128)S(1)} %add_rsqrt_fusion), kind=kOutput, calls=%fused_computation.5 | convolution fusion | flops 505987072 | bytes 5362176 | tf_op jit(solution)/shard_map/cond/branch_1_fun/dot_general | solution.py:404
  17.1 7.1 %branch_1_fun.2 = bf16[8,384,640]{2,1,0:T(8,128)(2,1)} custom-call(s32[24]{0:T(128)S(1)} %get-tuple-element.27.meta, bf16[8,384,640]{2,1,0:T(8,128)(2,1)} %bitcast.38), custom_call_target="tpu_custom_call" | custom-call | tf_op jit(solution)/shard_map/cond/branch_1_fun/pallas_call | solution.py:290
  24.2 8.1 %collective-permute-start.2 = (bf16[2,128,768]{2,1,0:T(8,128)(2,1)S(1)}, bf16[2,128,768]{2,1,0:T(8,128)(2,1)}, u32[]{:S(2)}, u32[]{:S(2)}) collective-permute-start(bf16[2,128,768]{2,1,0:T(8,128)(2,1)S(1)} %collective-permute-done.1), channel_id=1, source_target_pairs={{0,8},{1,9},{2,10},{3,11},{4,12},{5,13},{6,14},{7,15},{8,0},{9,1},... | collective-permute-start | bytes 1179656 | tf_op jit(solution)/shard_map/cond/branch_1_fun/ppermute | solution.py:68
  38.0 2.7 %collective-permute-start.3 = (bf16[256,768]{1,0:T(8,128)(2,1)}, bf16[256,768]{1,0:T(8,128)(2,1)}, u32[]{:S(2)}, u32[]{:S(2)}) collective-permute-start(bf16[256,768]{1,0:T(8,128)(2,1)} %dynamic-slice_bitcast_fusion), channel_id=1, source_target_pairs={{0,32},{1,33},{2,34},{3,35},{4,36},{5,37},{6,38},{7,39},{8,40},{9,... | collective-permute-start | bytes 1179656 | tf_op jit(solution)/shard_map/cond/branch_1_fun/ppermute | solution.py:68
  40.8 5.2 %branch_1_fun.3 = bf16[8,384,640]{2,1,0:T(8,128)(2,1)S(1)} custom-call(s32[24]{0:T(128)S(1)} %get-tuple-element.27.meta, bf16[8,384,640]{2,1,0:T(8,128)(2,1)} %bitcast.39), custom_call_target="tpu_custom_call" | custom-call | tf_op jit(solution)/shard_map/cond/branch_1_fun/pallas_call | solution.py:290
  45.9 4.1 %collective-permute-done.3 = bf16[256,768]{1,0:T(8,128)(2,1)} collective-permute-done((bf16[256,768]{1,0:T(8,128)(2,1)}, bf16[256,768]{1,0:T(8,128)(2,1)}, u32[]{:S(2)}, u32[]{:S(2)}) %collective-permute-start.3) | collective-permute-done | bytes 393248 | tf_op jit(solution)/shard_map/cond/branch_1_fun/ppermute | solution.py:68
  54.6 7.6 %collective-permute-done.7.o1 = bf16[256,768]{1,0:T(8,128)(2,1)S(1)} collective-permute-done((bf16[256,768]{1,0:T(8,128)(2,1)}, bf16[256,768]{1,0:T(8,128)(2,1)S(1)}, u32[]{:S(2)}, u32[]{:S(2)}) %collective-permute-start.7) | collective-permute-done | bytes 393248 | tf_op jit(solution)/shard_map/ppermute | solution.py:68
  62.1 3.0 %collective-permute-done.8.o3 = bf16[256,768]{1,0:T(8,128)(2,1)S(1)} collective-permute-done((bf16[256,768]{1,0:T(8,128)(2,1)}, bf16[256,768]{1,0:T(8,128)(2,1)S(1)}, u32[]{:S(2)}, u32[]{:S(2)}) %collective-permute-start.8) | collective-permute-done | bytes 393248 | tf_op jit(solution)/shard_map/ppermute | solution.py:68
  69.4 2.8 %collective-permute-start.14 = (bf16[96,5120]{1,0:T(8,128)(2,1)S(1)}, bf16[96,5120]{1,0:T(8,128)(2,1)S(1)}, u32[]{:S(2)}, u32[]{:S(2)}) collective-permute-start(bf16[96,5120]{1,0:T(8,128)(2,1)S(1)} %slice.23), channel_id=1, source_target_pairs={{0,3},{1,2},{2,1},{3,0},{4,7},{5,6},{6,5},{7,4},{8,12},{9,13},{10,... | collective-permute-start | bytes 2949128 | tf_op jit(solution)/shard_map/ppermute | solution.py:68
  74.0 3.7 %shard_map.105 = (bf16[4,256,5120]{2,1,0:T(8,128)(2,1)S(1)}, bf16[4,256,384]{2,1,0:T(8,128)(2,1)S(1)}, bf16[4,256,640]{2,1,0:T(8,128)(2,1)S(1)}, bf16[4,256,640]{2,1,0:T(8,128)(2,1)S(1)}) custom-call(s32[24]{0:T(128)S(1)} %dynamic-slice_bitcast_fusion.1.meta, bf16[256,5120]{1,0:T(8,128)(2,1)S(1)} %bitcast.34, f32[1,5120]{1,0:T(1,128)S(1)} %copy-done.2, ...), custom_call_target="tpu_custom_call" | custom-call | tf_op jit(solution)/shard_map/pallas_call | solution.py:121
  77.7 5.4 %shard_map.106 = (bf16[4,256,5120]{2,1,0:T(8,128)(2,1)S(1)}, bf16[4,256,384]{2,1,0:T(8,128)(2,1)S(1)}, bf16[4,256,640]{2,1,0:T(8,128)(2,1)S(1)}, bf16[4,256,640]{2,1,0:T(8,128)(2,1)S(1)}) custom-call(s32[24]{0:T(128)S(1)} %dynamic-slice_bitcast_fusion.1.meta, ...), custom_call_target="tpu_custom_call", output_to_operand_aliasing={{0}: (4, {}), {1}: (5, {}), {2}: (6, {}), {3}: (7, {})} | custom-call | tf_op jit(solution)/shard_map/pallas_call | solution.py:121
  83.1 3.7 %shard_map.107 = (bf16[4,256,5120]{2,1,0:T(8,128)(2,1)S(1)}, bf16[4,256,384]{2,1,0:T(8,128)(2,1)S(1)}, bf16[4,256,640]{2,1,0:T(8,128)(2,1)S(1)}, bf16[4,256,640]{2,1,0:T(8,128)(2,1)S(1)}) custom-call(s32[24]{0:T(128)S(1)} %dynamic-slice_bitcast_fusion.1.meta, ...), custom_call_target="tpu_custom_call", output_to_operand_aliasing={{0}: (4, {}), {1}: (5, {}), {2}: (6, {}), {3}: (7, {})} | custom-call | tf_op jit(solution)/shard_map/pallas_call | solution.py:121
  86.8 3.4 %collective-permute-start.15 = (bf16[256,768]{1,0:T(8,128)(2,1)S(1)}, bf16[256,768]{1,0:T(8,128)(2,1)S(1)}, u32[]{:S(2)}, u32[]{:S(2)}) collective-permute-start(bf16[256,768]{1,0:T(8,128)(2,1)S(1)} %collective-permute-done.7.o1), channel_id=1, source_target_pairs={{0,8},{1,9},{2,10},{3,11},{4,12},{5,13},{6,14},{7,15},{8,0},{9,1},... | collective-permute-start | bytes 1179656 | tf_op jit(solution)/shard_map/ppermute | solution.py:68
  90.2 4.4 %collective-permute-done.14.refs_1_ = bf16[96,5120]{1,0:T(8,128)(2,1)S(1)} collective-permute-done((bf16[96,5120]{1,0:T(8,128)(2,1)S(1)}, bf16[96,5120]{1,0:T(8,128)(2,1)S(1)}, u32[]{:S(2)}, u32[]{:S(2)}) %collective-permute-start.14) | collective-permute-done | bytes 983072 | tf_op jit(solution)/shard_map/ppermute | solution.py:68
  94.6 4.1 %collective-permute-start.16 = (bf16[256,768]{1,0:T(8,128)(2,1)}, bf16[256,768]{1,0:T(8,128)(2,1)S(1)}, u32[]{:S(2)}, u32[]{:S(2)}) collective-permute-start(bf16[256,768]{1,0:T(8,128)(2,1)} %get-tuple-element.113.o2), channel_id=1, source_target_pairs={{0,8},{1,9},{2,10},{3,11},{4,12},{5,13},{6,14},{7,15},{8,0},{9,1},... | collective-permute-start | bytes 1179656 | tf_op jit(solution)/shard_map/ppermute | solution.py:68
  100.8 3.7 %shard_map.108 = (bf16[4,256,5120]{2,1,0:T(8,128)(2,1)S(1)}, bf16[4,256,384]{2,1,0:T(8,128)(2,1)S(1)}, bf16[4,256,640]{2,1,0:T(8,128)(2,1)S(1)}, bf16[4,256,640]{2,1,0:T(8,128)(2,1)S(1)}) custom-call(s32[24]{0:T(128)S(1)} %dynamic-slice_bitcast_fusion.1.meta, ...), custom_call_target="tpu_custom_call", output_to_operand_aliasing={{0}: (5, {}), {1}: (6, {}), {2}: (7, {}), {3}: (8, {})} | custom-call | tf_op jit(solution)/shard_map/pallas_call | solution.py:121
  106.8 4.3 %collective-permute-done.11.t2 = bf16[2,256,768]{2,1,0:T(8,128)(2,1)S(1)} collective-permute-done((bf16[2,256,768]{2,1,0:T(8,128)(2,1)}, bf16[2,256,768]{2,1,0:T(8,128)(2,1)S(1)}, u32[]{:S(2)}, u32[]{:S(2)}) %collective-permute-start.11) | collective-permute-done | bytes 786464 | tf_op jit(solution)/shard_map/ppermute | solution.py:68
  111.3 5.7 %shard_map.109 = bf16[1024,384]{1,0:T(8,128)(2,1)S(1)} custom-call(bf16[1024,5120]{1,0:T(8,128)(2,1)S(1)} %bitcast.24, bf16[5120,384]{1,0:T(8,128)(2,1)S(1)} %collective-permute-done.12.w_ref), custom_call_target="tpu_custom_call" | custom-call | tf_op jit(solution)/shard_map/pallas_call | solution.py:145
  117.0 7.1 %shard_map.111.c0 = bf16[512,768]{1,0:T(8,128)(2,1)S(1)} custom-call(s32[24]{0:T(128)S(1)} %dynamic-slice_bitcast_fusion.1.meta, bf16[4,256,384]{2,1,0:T(8,128)(2,1)S(1)} %get-tuple-element.123.q_own, bf16[4,256,384]{2,1,0:T(8,128)(2,1)S(1)} %bitcast.30, s32[8,1,256]{2,1,0:T(1,128)S(1)} %bitcast.35, bf16[2,256,768]{2,1,0:T(8,128)(2,1)} %get-tuple-element.126.own0, ...), custom_call_target="tpu_custom_call" | custom-call | flops 1207959552 | bytes 8388608 | tf_op jit(solution)/shard_map/pallas_call | solution.py:262
  126.6 11.0 %shard_map.110.c0 = bf16[512,768]{1,0:T(8,128)(2,1)S(1)} custom-call(s32[24]{0:T(128)S(1)} %dynamic-slice_bitcast_fusion.1.meta, bf16[4,256,384]{2,1,0:T(8,128)(2,1)S(1)} %get-tuple-element.123.q_own, bf16[4,256,384]{2,1,0:T(8,128)(2,1)S(1)} %bitcast.31, s32[8,1,256]{2,1,0:T(1,128)S(1)} %bitcast.36, bf16[2,256,768]{2,1,0:T(8,128)(2,1)} %get-tuple-element.126.own0, ...), custom_call_target="tpu_custom_call" | custom-call | flops 1207959552 | bytes 8388608 | tf_op jit(solution)/shard_map/pallas_call | solution.py:262
  138.8 2.9 %collective-permute-done.20.c1 = bf16[512,768]{1,0:T(8,128)(2,1)S(1)} collective-permute-done((bf16[512,768]{1,0:T(8,128)(2,1)S(1)}, bf16[512,768]{1,0:T(8,128)(2,1)S(1)}, u32[]{:S(2)}, u32[]{:S(2)}) %collective-permute-start.20) | collective-permute-done | bytes 786464 | tf_op jit(solution)/shard_map/ppermute | solution.py:68
  141.6 3.1 %collective-permute-done.21.c3 = bf16[512,768]{1,0:T(8,128)(2,1)S(1)} collective-permute-done((bf16[512,768]{1,0:T(8,128)(2,1)S(1)}, bf16[512,768]{1,0:T(8,128)(2,1)S(1)}, u32[]{:S(2)}, u32[]{:S(2)}) %collective-permute-start.21) | collective-permute-done | bytes 786464 | tf_op jit(solution)/shard_map/ppermute | solution.py:68
  147.5 10.9 %collective-permute-done.18.c1 = bf16[512,768]{1,0:T(8,128)(2,1)S(1)} collective-permute-done((bf16[512,768]{1,0:T(8,128)(2,1)S(1)}, bf16[512,768]{1,0:T(8,128)(2,1)S(1)}, u32[]{:S(2)}, u32[]{:S(2)}) %collective-permute-start.18) | collective-permute-done | bytes 786464 | tf_op jit(solution)/shard_map/ppermute | solution.py:68
  158.5 3.1 %collective-permute-done.19.c3 = bf16[512,768]{1,0:T(8,128)(2,1)S(1)} collective-permute-done((bf16[512,768]{1,0:T(8,128)(2,1)S(1)}, bf16[512,768]{1,0:T(8,128)(2,1)S(1)}, u32[]{:S(2)}, u32[]{:S(2)}) %collective-permute-start.19) | collective-permute-done | bytes 786464 | tf_op jit(solution)/shard_map/ppermute | solution.py:68
  161.6 6.3 %collective-permute-done.22.c2b = bf16[192,768]{1,0:T(8,128)(2,1)S(1)} collective-permute-done((bf16[192,768]{1,0:T(8,128)(2,1)S(1)}, bf16[192,768]{1,0:T(8,128)(2,1)S(1)}, u32[]{:S(2)}, u32[]{:S(2)}) %collective-permute-start.22) | collective-permute-done | bytes 294944 | tf_op jit(solution)/shard_map/ppermute | solution.py:68
  170.7 7.4 %collective-permute-done.25.w = bf16[3072,640]{1,0:T(8,128)(2,1)S(1)} collective-permute-done((bf16[3072,640]{1,0:T(8,128)(2,1)S(1)}, bf16[3072,640]{1,0:T(8,128)(2,1)S(1)}, u32[]{:S(2)}, u32[]{:S(2)}) %collective-permute-start.25) | collective-permute-done | bytes 3932192 | tf_op jit(solution)/shard_map/ppermute | solution.py:68
  178.1 3.4 %shard_map.113 = bf16[2,256,640]{2,1,0:T(8,128)(2,1)S(1)} custom-call(s32[24]{0:T(128)S(1)} %dynamic-slice_bitcast_fusion.1.meta, bf16[512,768]{1,0:T(8,128)(2,1)S(1)} %shard_map.111.c0, bf16[512,768]{1,0:T(8,128)(2,1)S(1)} %collective-permute-done.20.c1, bf16[320,768]{1,0:T(8,128)(2,1)S(1)} %collective-permute-done.27.c2a, ...), custom_call_target="tpu_custom_call" | custom-call | flops 2013265920 | bytes 8388608 | tf_op jit(solution)/shard_map/pallas_call | solution.py:334
  181.6 3.4 %shard_map.112 = bf16[2,256,640]{2,1,0:T(8,128)(2,1)S(1)} custom-call(s32[24]{0:T(128)S(1)} %dynamic-slice_bitcast_fusion.1.meta, bf16[512,768]{1,0:T(8,128)(2,1)S(1)} %shard_map.110.c0, bf16[512,768]{1,0:T(8,128)(2,1)S(1)} %collective-permute-done.18.c1, bf16[320,768]{1,0:T(8,128)(2,1)S(1)} %collective-permute-done.23.c2a, ...), custom_call_target="tpu_custom_call" | custom-call | flops 2013265920 | bytes 8388608 | tf_op jit(solution)/shard_map/pallas_call | solution.py:334
  185.0 5.4 %collective-permute-start.26 = (bf16[2,256,640]{2,1,0:T(8,128)(2,1)S(1)}, bf16[2,256,640]{2,1,0:T(8,128)(2,1)S(1)}, u32[]{:S(2)}, u32[]{:S(2)}) collective-permute-start(bf16[2,256,640]{2,1,0:T(8,128)(2,1)S(1)} %shard_map.112), channel_id=1, source_target_pairs={{0,4},{1,5},{2,6},{3,7},{4,0},{5,1},{6,2},{7,3},{8,11},{9,10},{10,... | collective-permute-start | bytes 1966088 | tf_op jit(solution)/shard_map/ppermute | solution.py:68
  190.3 4.1 %shard_map.114.refs_0_ = bf16[8,256,640]{2,1,0:T(8,128)(2,1)} custom-call(s32[24]{0:T(128)S(1)} %dynamic-slice_bitcast_fusion.1.meta, bf16[512,768]{1,0:T(8,128)(2,1)S(1)} %shard_map.111.c0, bf16[512,768]{1,0:T(8,128)(2,1)S(1)} %collective-permute-done.20.c1, bf16[320,768]{1,0:T(8,128)(2,1)S(1)} %collective-permute-done.27.c2a, ...), custom_call_target="tpu_custom_call" | custom-call | flops 2013265920 | bytes 8388608 | tf_op jit(solution)/shard_map/pallas_call | solution.py:334
  194.4 4.1 %shard_map.115.prior = bf16[8,256,640]{2,1,0:T(8,128)(2,1)} custom-call(s32[24]{0:T(128)S(1)} %dynamic-slice_bitcast_fusion.1.meta, bf16[512,768]{1,0:T(8,128)(2,1)S(1)} %shard_map.110.c0, bf16[512,768]{1,0:T(8,128)(2,1)S(1)} %collective-permute-done.18.c1, bf16[320,768]{1,0:T(8,128)(2,1)S(1)} %collective-permute-done.23.c2a, ...), custom_call_target="tpu_custom_call", output_to_operand_aliasing={{}: (8, {})} | custom-call | flops 2013265920 | bytes 8388608 | tf_op jit(solution)/shard_map/pallas_call | solution.py:334
  (80 shorter events, 45.9 us)
Async XLA Ops:
  0.0 65.2 %collective-permute-start.5 = (bf16[256,5120]{1,0:T(8,128)(2,1)}, bf16[256,5120]{1,0:T(8,128)(2,1)}, u32[]{:S(2)}, u32[]{:S(2)}) collective-permute-start(bf16[256,5120]{1,0:T(8,128)(2,1)} %bitcast.32), channel_id=1, source_target_pairs={{0,1},{1,0},{2,3},{3,2},{4,5},{5,4},{6,7},{7,6},{8,9},{9,8},{10,11... | collective-permute-start | bytes 7864328 | tf_op jit(solution)/shard_map/ppermute | solution.py:68
  2.5 62.7 %collective-permute-start.6 = (bf16[256,5120]{1,0:T(8,128)(2,1)}, bf16[256,5120]{1,0:T(8,128)(2,1)S(1)}, u32[]{:S(2)}, u32[]{:S(2)}) collective-permute-start(bf16[256,5120]{1,0:T(8,128)(2,1)} %bitcast.33), channel_id=1, source_target_pairs={{0,3},{1,2},{2,1},{3,0},{4,7},{5,6},{6,5},{7,4},{8,12},{9,13},{10,... | collective-permute-start | bytes 7864328 | tf_op jit(solution)/shard_map/ppermute | solution.py:68
  13.0 3.3 %collective-permute-start = (bf16[128,768]{1,0:T(8,128)(2,1)S(1)}, bf16[128,768]{1,0:T(8,128)(2,1)S(1)}, u32[]{:S(2)}, u32[]{:S(2)}) collective-permute-start(bf16[128,768]{1,0:T(8,128)(2,1)S(1)} %get-tuple-element.193), channel_id=1, source_target_pairs={{0,8},{1,9},{2,10},{3,11},{4,12},{5,13},{6,14},{7,15},{8,0},{9,1},... | collective-permute-start | bytes 589832 | tf_op jit(solution)/shard_map/cond/branch_1_fun/ppermute | solution.py:68
  16.4 7.8 %collective-permute-start.1 = (bf16[2,128,768]{2,1,0:T(8,128)(2,1)S(1)}, bf16[2,128,768]{2,1,0:T(8,128)(2,1)S(1)}, u32[]{:S(2)}, u32[]{:S(2)}) collective-permute-start(bf16[2,128,768]{2,1,0:T(8,128)(2,1)S(1)} %maximum_select_fusion.2), channel_id=1, source_target_pairs={{0,64},{1,65},{2,66},{3,67},{4,68},{5,69},{6,70},{7,71},{16,80},{1... | collective-permute-start | bytes 1179656 | tf_op jit(solution)/shard_map/cond/branch_1_fun/ppermute | solution.py:68
  24.2 9.5 %collective-permute-start.2 = (bf16[2,128,768]{2,1,0:T(8,128)(2,1)S(1)}, bf16[2,128,768]{2,1,0:T(8,128)(2,1)}, u32[]{:S(2)}, u32[]{:S(2)}) collective-permute-start(bf16[2,128,768]{2,1,0:T(8,128)(2,1)S(1)} %collective-permute-done.1), channel_id=1, source_target_pairs={{0,8},{1,9},{2,10},{3,11},{4,12},{5,13},{6,14},{7,15},{8,0},{9,1},... | collective-permute-start | bytes 1179656 | tf_op jit(solution)/shard_map/cond/branch_1_fun/ppermute | solution.py:68
  35.8 14.2 %collective-permute-start.4 = (bf16[2,256,768]{2,1,0:T(8,128)(2,1)}, bf16[2,256,768]{2,1,0:T(8,128)(2,1)}, u32[]{:S(2)}, u32[]{:S(2)}) collective-permute-start(bf16[2,256,768]{2,1,0:T(8,128)(2,1)} %maximum_select_fusion), channel_id=1, source_target_pairs={{0,4},{1,5},{2,6},{3,7},{4,0},{5,1},{6,2},{7,3},{8,11},{9,10},{10,... | collective-permute-start | bytes 2359304 | tf_op jit(solution)/shard_map/cond/branch_1_fun/ppermute | solution.py:68
  38.0 12.0 %collective-permute-start.3 = (bf16[256,768]{1,0:T(8,128)(2,1)}, bf16[256,768]{1,0:T(8,128)(2,1)}, u32[]{:S(2)}, u32[]{:S(2)}) collective-permute-start(bf16[256,768]{1,0:T(8,128)(2,1)} %dynamic-slice_bitcast_fusion), channel_id=1, source_target_pairs={{0,32},{1,33},{2,34},{3,35},{4,36},{5,37},{6,38},{7,39},{8,40},{9,... | collective-permute-start | bytes 1179656 | tf_op jit(solution)/shard_map/cond/branch_1_fun/ppermute | solution.py:68
  50.0 56.8 %collective-permute-start.12 = (bf16[5120,384]{1,0:T(8,128)(2,1)}, bf16[5120,384]{1,0:T(8,128)(2,1)S(1)}, u32[]{:S(2)}, u32[]{:S(2)}) collective-permute-start(bf16[5120,384]{1,0:T(8,128)(2,1)} %bitcast.25), channel_id=1, source_target_pairs={{0,4},{1,5},{2,6},{3,7},{4,0},{5,1},{6,2},{7,3},{8,11},{9,10},{10,... | collective-permute-start | bytes 11796488 | tf_op jit(solution)/shard_map/ppermute | solution.py:68
  52.1 20.1 %copy-start = (bf16[1,5120,384]{2,1,0:T(8,128)(2,1)S(1)}, bf16[1,5120,384]{2,1,0:T(8,128)(2,1)}, u32[]{:S(2)}) copy-start(bf16[1,5120,384]{2,1,0:T(8,128)(2,1)} %param.18) | copy-start | bytes 11796484
  52.1 20.1 %copy-start.2 = (f32[1,5120]{1,0:T(1,128)S(1)}, f32[1,5120]{1,0:T(1,128)}, u32[]{:S(2)}) copy-start(f32[1,5120]{1,0:T(1,128)} %refs_2_.1) | copy-start | bytes 61444
  52.1 10.0 %collective-permute-start.7 = (bf16[256,768]{1,0:T(8,128)(2,1)}, bf16[256,768]{1,0:T(8,128)(2,1)S(1)}, u32[]{:S(2)}, u32[]{:S(2)}) collective-permute-start(bf16[256,768]{1,0:T(8,128)(2,1)} %get-tuple-element.88), channel_id=1, source_target_pairs={{0,48},{1,49},{2,50},{3,51},{4,52},{5,53},{6,54},{7,55},{8,56},{9,... | collective-permute-start | bytes 1179656 | tf_op jit(solution)/shard_map/ppermute | solution.py:68
  54.6 10.6 %collective-permute-start.8 = (bf16[256,768]{1,0:T(8,128)(2,1)}, bf16[256,768]{1,0:T(8,128)(2,1)S(1)}, u32[]{:S(2)}, u32[]{:S(2)}) collective-permute-start(bf16[256,768]{1,0:T(8,128)(2,1)} %get-tuple-element.88), channel_id=1, source_target_pairs={{0,16},{1,17},{2,18},{3,19},{4,20},{5,21},{6,22},{7,23},{8,24},{9,... | collective-permute-start | bytes 1179656 | tf_op jit(solution)/shard_map/ppermute | solution.py:68
  65.3 35.5 %collective-permute-start.13 = (bf16[160,5120]{1,0:T(8,128)(2,1)S(1)}, bf16[160,5120]{1,0:T(8,128)(2,1)S(1)}, u32[]{:S(2)}, u32[]{:S(2)}) collective-permute-start(bf16[160,5120]{1,0:T(8,128)(2,1)S(1)} %slice.22), channel_id=1, source_target_pairs={{0,1},{1,0},{2,3},{3,2},{4,5},{5,4},{6,7},{7,6},{8,9},{9,8},{10,11... | collective-permute-start | bytes 4915208 | tf_op jit(solution)/shard_map/ppermute | solution.py:68
  65.4 21.4 %collective-permute-start.10 = (bf16[2,256,768]{2,1,0:T(8,128)(2,1)}, bf16[2,256,768]{2,1,0:T(8,128)(2,1)S(1)}, u32[]{:S(2)}, u32[]{:S(2)}) collective-permute-start(bf16[2,256,768]{2,1,0:T(8,128)(2,1)} %get-tuple-element.105.other0), channel_id=1, source_target_pairs={{0,16},{1,17},{2,18},{3,19},{4,20},{5,21},{6,22},{7,23},{8,24},{9,... | collective-permute-start | bytes 2359304 | tf_op jit(solution)/shard_map/ppermute | solution.py:68
  65.5 21.3 %collective-permute-start.9 = (bf16[2,256,768]{2,1,0:T(8,128)(2,1)}, bf16[2,256,768]{2,1,0:T(8,128)(2,1)S(1)}, u32[]{:S(2)}, u32[]{:S(2)}) collective-permute-start(bf16[2,256,768]{2,1,0:T(8,128)(2,1)} %get-tuple-element.105.other0), channel_id=1, source_target_pairs={{0,48},{1,49},{2,50},{3,51},{4,52},{5,53},{6,54},{7,55},{8,56},{9,... | collective-permute-start | bytes 2359304 | tf_op jit(solution)/shard_map/ppermute | solution.py:68
  69.4 25.2 %collective-permute-start.14 = (bf16[96,5120]{1,0:T(8,128)(2,1)S(1)}, bf16[96,5120]{1,0:T(8,128)(2,1)S(1)}, u32[]{:S(2)}, u32[]{:S(2)}) collective-permute-start(bf16[96,5120]{1,0:T(8,128)(2,1)S(1)} %slice.23), channel_id=1, source_target_pairs={{0,3},{1,2},{2,1},{3,0},{4,7},{5,6},{6,5},{7,4},{8,12},{9,13},{10,... | collective-permute-start | bytes 2949128 | tf_op jit(solution)/shard_map/ppermute | solution.py:68
  86.8 24.3 %copy-start.6 = (bf16[3072,640]{1,0:T(8,128)(2,1)S(1)}, bf16[3072,640]{1,0:T(8,128)(2,1)}, u32[]{:S(2)}) copy-start(bf16[3072,640]{1,0:T(8,128)(2,1)} %copy-done.5) | copy-start | bytes 11796484
  86.8 11.9 %collective-permute-start.15 = (bf16[256,768]{1,0:T(8,128)(2,1)S(1)}, bf16[256,768]{1,0:T(8,128)(2,1)S(1)}, u32[]{:S(2)}, u32[]{:S(2)}) collective-permute-start(bf16[256,768]{1,0:T(8,128)(2,1)S(1)} %collective-permute-done.7.o1), channel_id=1, source_target_pairs={{0,8},{1,9},{2,10},{3,11},{4,12},{5,13},{6,14},{7,15},{8,0},{9,1},... | collective-permute-start | bytes 1179656 | tf_op jit(solution)/shard_map/ppermute | solution.py:68
  90.2 20.8 %collective-permute-start.11 = (bf16[2,256,768]{2,1,0:T(8,128)(2,1)}, bf16[2,256,768]{2,1,0:T(8,128)(2,1)S(1)}, u32[]{:S(2)}, u32[]{:S(2)}) collective-permute-start(bf16[2,256,768]{2,1,0:T(8,128)(2,1)} %get-tuple-element.105.other0), channel_id=1, source_target_pairs={{0,32},{1,33},{2,34},{3,35},{4,36},{5,37},{6,38},{7,39},{8,40},{9,... | collective-permute-start | bytes 2359304 | tf_op jit(solution)/shard_map/ppermute | solution.py:68
  94.6 6.1 %collective-permute-start.16 = (bf16[256,768]{1,0:T(8,128)(2,1)}, bf16[256,768]{1,0:T(8,128)(2,1)S(1)}, u32[]{:S(2)}, u32[]{:S(2)}) collective-permute-start(bf16[256,768]{1,0:T(8,128)(2,1)} %get-tuple-element.113.o2), channel_id=1, source_target_pairs={{0,8},{1,9},{2,10},{3,11},{4,12},{5,13},{6,14},{7,15},{8,0},{9,1},... | collective-permute-start | bytes 1179656 | tf_op jit(solution)/shard_map/ppermute | solution.py:68
  98.7 2.0 %collective-permute-start.17 = (bf16[256,768]{1,0:T(8,128)(2,1)S(1)}, bf16[256,768]{1,0:T(8,128)(2,1)S(1)}, u32[]{:S(2)}, u32[]{:S(2)}) collective-permute-start(bf16[256,768]{1,0:T(8,128)(2,1)S(1)} %collective-permute-done.8.o3), channel_id=1, source_target_pairs={{0,8},{1,9},{2,10},{3,11},{4,12},{5,13},{6,14},{7,15},{8,0},{9,1},... | collective-permute-start | bytes 1179656 | tf_op jit(solution)/shard_map/ppermute | solution.py:68
  111.1 67.1 %collective-permute-start.25 = (bf16[3072,640]{1,0:T(8,128)(2,1)S(1)}, bf16[3072,640]{1,0:T(8,128)(2,1)S(1)}, u32[]{:S(2)}, u32[]{:S(2)}) collective-permute-start(bf16[3072,640]{1,0:T(8,128)(2,1)S(1)} %copy-done.6), channel_id=1, source_target_pairs={{0,4},{1,5},{2,6},{3,7},{4,0},{5,1},{6,2},{7,3},{8,11},{9,10},{10,... | collective-permute-start | bytes 11796488 | tf_op jit(solution)/shard_map/ppermute | solution.py:68
  124.1 17.5 %collective-permute-start.20 = (bf16[512,768]{1,0:T(8,128)(2,1)S(1)}, bf16[512,768]{1,0:T(8,128)(2,1)S(1)}, u32[]{:S(2)}, u32[]{:S(2)}) collective-permute-start(bf16[512,768]{1,0:T(8,128)(2,1)S(1)} %shard_map.111.c0), channel_id=1, source_target_pairs={{0,1},{1,0},{2,3},{3,2},{4,5},{5,4},{6,7},{7,6},{8,9},{9,8},{10,11... | collective-permute-start | bytes 2359304 | tf_op jit(solution)/shard_map/ppermute | solution.py:68
  124.7 20.1 %collective-permute-start.21 = (bf16[512,768]{1,0:T(8,128)(2,1)S(1)}, bf16[512,768]{1,0:T(8,128)(2,1)S(1)}, u32[]{:S(2)}, u32[]{:S(2)}) collective-permute-start(bf16[512,768]{1,0:T(8,128)(2,1)S(1)} %shard_map.111.c0), channel_id=1, source_target_pairs={{0,3},{1,2},{2,1},{3,0},{4,7},{5,6},{6,5},{7,4},{8,12},{9,13},{10,... | collective-permute-start | bytes 2359304 | tf_op jit(solution)/shard_map/ppermute | solution.py:68
  137.5 21.0 %collective-permute-start.18 = (bf16[512,768]{1,0:T(8,128)(2,1)S(1)}, bf16[512,768]{1,0:T(8,128)(2,1)S(1)}, u32[]{:S(2)}, u32[]{:S(2)}) collective-permute-start(bf16[512,768]{1,0:T(8,128)(2,1)S(1)} %shard_map.110.c0), channel_id=1, source_target_pairs={{0,1},{1,0},{2,3},{3,2},{4,5},{5,4},{6,7},{7,6},{8,9},{9,8},{10,11... | collective-permute-start | bytes 2359304 | tf_op jit(solution)/shard_map/ppermute | solution.py:68
  138.8 22.8 %collective-permute-start.19 = (bf16[512,768]{1,0:T(8,128)(2,1)S(1)}, bf16[512,768]{1,0:T(8,128)(2,1)S(1)}, u32[]{:S(2)}, u32[]{:S(2)}) collective-permute-start(bf16[512,768]{1,0:T(8,128)(2,1)S(1)} %shard_map.110.c0), channel_id=1, source_target_pairs={{0,3},{1,2},{2,1},{3,0},{4,7},{5,6},{6,5},{7,4},{8,12},{9,13},{10,... | collective-permute-start | bytes 2359304 | tf_op jit(solution)/shard_map/ppermute | solution.py:68
  144.7 23.1 %collective-permute-start.22 = (bf16[192,768]{1,0:T(8,128)(2,1)S(1)}, bf16[192,768]{1,0:T(8,128)(2,1)S(1)}, u32[]{:S(2)}, u32[]{:S(2)}) collective-permute-start(bf16[192,768]{1,0:T(8,128)(2,1)S(1)} %slice.24), channel_id=1, source_target_pairs={{0,3},{1,2},{2,1},{3,0},{4,7},{5,6},{6,5},{7,4},{8,12},{9,13},{10,... | collective-permute-start | bytes 884744 | tf_op jit(solution)/shard_map/ppermute | solution.py:68
  146.3 24.4 %collective-permute-start.27 = (bf16[320,768]{1,0:T(8,128)(2,1)S(1)}, bf16[320,768]{1,0:T(8,128)(2,1)S(1)}, u32[]{:S(2)}, u32[]{:S(2)}) collective-permute-start(bf16[320,768]{1,0:T(8,128)(2,1)S(1)} %slice.27), channel_id=1, source_target_pairs={{0,1},{1,0},{2,3},{3,2},{4,5},{5,4},{6,7},{7,6},{8,9},{9,8},{10,11... | collective-permute-start | bytes 1474568 | tf_op jit(solution)/shard_map/ppermute | solution.py:68
  167.9 13.7 %collective-permute-start.23 = (bf16[320,768]{1,0:T(8,128)(2,1)S(1)}, bf16[320,768]{1,0:T(8,128)(2,1)S(1)}, u32[]{:S(2)}, u32[]{:S(2)}) collective-permute-start(bf16[320,768]{1,0:T(8,128)(2,1)S(1)} %slice.25), channel_id=1, source_target_pairs={{0,1},{1,0},{2,3},{3,2},{4,5},{5,4},{6,7},{7,6},{8,9},{9,8},{10,11... | collective-permute-start | bytes 1474568 | tf_op jit(solution)/shard_map/ppermute | solution.py:68
  169.2 12.4 %collective-permute-start.24 = (bf16[192,768]{1,0:T(8,128)(2,1)S(1)}, bf16[192,768]{1,0:T(8,128)(2,1)S(1)}, u32[]{:S(2)}, u32[]{:S(2)}) collective-permute-start(bf16[192,768]{1,0:T(8,128)(2,1)S(1)} %slice.26), channel_id=1, source_target_pairs={{0,3},{1,2},{2,1},{3,0},{4,7},{5,6},{6,5},{7,4},{8,12},{9,13},{10,... | collective-permute-start | bytes 884744 | tf_op jit(solution)/shard_map/ppermute | solution.py:68
  181.5 17.0 %collective-permute-start.28 = (bf16[2,256,640]{2,1,0:T(8,128)(2,1)S(1)}, bf16[2,256,640]{2,1,0:T(8,128)(2,1)S(1)}, u32[]{:S(2)}, u32[]{:S(2)}) collective-permute-start(bf16[2,256,640]{2,1,0:T(8,128)(2,1)S(1)} %shard_map.113), channel_id=1, source_target_pairs={{0,4},{1,5},{2,6},{3,7},{4,0},{5,1},{6,2},{7,3},{8,11},{9,10},{10,... | collective-permute-start | bytes 1966088 | tf_op jit(solution)/shard_map/ppermute | solution.py:68
  185.0 15.0 %collective-permute-start.26 = (bf16[2,256,640]{2,1,0:T(8,128)(2,1)S(1)}, bf16[2,256,640]{2,1,0:T(8,128)(2,1)S(1)}, u32[]{:S(2)}, u32[]{:S(2)}) collective-permute-start(bf16[2,256,640]{2,1,0:T(8,128)(2,1)S(1)} %shard_map.112), channel_id=1, source_target_pairs={{0,4},{1,5},{2,6},{3,7},{4,0},{5,1},{6,2},{7,3},{8,11},{9,10},{10,... | collective-permute-start | bytes 1966088 | tf_op jit(solution)/shard_map/ppermute | solution.py:68
  (7 other events, 30.2 us)

commit v12 on v11

--- a/solution.py
+++ b/solution.py
@@ -9,7 +9,7 @@
 
 HD = 128
 RB = 256
-CUT = 320
+CUT = 384
 BF = jnp.bfloat16
 F32 = jnp.float32
 AXES = ("section", "ctx")

time: 203 us -> 205 us (level)
  waiting for transfers between devices: 63.8 us -> 66.6 us
    ppermute x29, waiting for transfers between devices: 63.8 us -> 66.6 us  [send(): return lax.ppermute(value, AXES, pairs)]
  transfers between devices with their start and end apart: 29 -> 29, of which waited for: 15 -> 17; matrix products, arithmetic and copies ran while one was open for 7% -> 7% of each run, Pallas kernels for 34% -> 33%
where the time goes in v12:
time: 205 us; the launch traced here: 204 us
  Pallas kernels  68.3 us (33%)
  waiting for transfers between devices  66.6 us (32%)
  starting transfers between devices  52.4 us (26%)
  local copies, waits for them, and re-layouts  7.42 us (4%)
  matrix products  4.48 us (2%)
  other arithmetic  3.84 us (2%)
    ppermute x29, waiting for transfers between devices, send(): return lax.ppermute(value, AXES, pairs)  66.6 us
    ppermute x29, starting transfers between devices, send(): return lax.ppermute(value, AXES, pairs)  52.4 us
    pallas_call x4, Pallas kernels, project(): pl.pallas_call(kernel, grid_spec=pltpu.PrefetchScalarGridSpec(num_scalar_...  16.5 us
    pallas_call x2, Pallas kernels, attend(): pl.pallas_call(functools.partial(attend_kernel, chunk), grid_spec=pltpu.P...  16.1 us
    pallas_call x4, Pallas kernels, finish(): pl.pallas_call(finish_kernel, grid_spec=pltpu.PrefetchScalarGridSpec(num_...  14.9 us
    pallas_call x2, Pallas kernels, reorder(): pl.pallas_call(reorder_kernel, grid_spec=pltpu.PrefetchScalarGridSpec(num...  12.2 us
    pallas_call x1, Pallas kernels, more_queries(): pl.pallas_call(more_queries_kernel, grid=(2,), in_specs=[pl.BlockSpec((ro...  5.74 us
  transfers between devices with their start and end apart: 29, of which 17 were waited for; matrix products, arithmetic and copies ran while one was open for 7% of the time, Pallas kernels for 33%

profile of v12, /device:TPU:1, one launch (start us, length us, event | category | flops | bytes accessed | tf_op | source)
XLA Modules:
  0.0 204.1 jit_solution(4762751548832443935)
XLA Ops:
  6.3 43.7 %conditional.1 = (bf16[2,256,768]{2,1,0:T(8,128)(2,1)}, bf16[256,768]{1,0:T(8,128)(2,1)}, bf16[256,768]{1,0:T(8,128)(2,1)}, bf16[2,256,768]{2,1,0:T(8,128)(2,1)}...) conditional(s32[]{:T(128)} %bitcast.12, () %tuple.24, (s32[]{:T(128)}, pred[]{:T(512)}, ...), branch_computations={%region_0.1_spmd, %region_1.3_spmd} | conditional | flops 1016889472 | bytes 47639592 | solution.py:424
  8.0 3.6 %convolution_convert_fusion = bf16[128,384]{1,0:T(8,128)(2,1)S(1)} fusion(bf16[5120,384]{1,0:T(8,128)(2,1)} %get-tuple-element.165, bf16[128,5120]{1,0:T(8,128)(2,1)} %get-tuple-element.162, f32[5120]{0:T(1024)} %get-tuple-element.163, f32[128]{0:T(128)S(1)} %add_rsqrt_fusion), kind=kOutput, calls=%fused_computation.5 | convolution fusion | flops 505987072 | bytes 5362176 | tf_op jit(solution)/shard_map/cond/branch_1_fun/dot_general | solution.py:404
  17.1 7.1 %branch_1_fun.2 = bf16[8,384,640]{2,1,0:T(8,128)(2,1)} custom-call(s32[24]{0:T(128)S(1)} %get-tuple-element.27.meta, bf16[8,384,640]{2,1,0:T(8,128)(2,1)} %bitcast.38), custom_call_target="tpu_custom_call" | custom-call | tf_op jit(solution)/shard_map/cond/branch_1_fun/pallas_call | solution.py:290
  24.2 8.1 %collective-permute-start.2 = (bf16[2,128,768]{2,1,0:T(8,128)(2,1)S(1)}, bf16[2,128,768]{2,1,0:T(8,128)(2,1)}, u32[]{:S(2)}, u32[]{:S(2)}) collective-permute-start(bf16[2,128,768]{2,1,0:T(8,128)(2,1)S(1)} %collective-permute-done.1), channel_id=1, source_target_pairs={{0,8},{1,9},{2,10},{3,11},{4,12},{5,13},{6,14},{7,15},{8,0},{9,1},... | collective-permute-start | bytes 1179656 | tf_op jit(solution)/shard_map/cond/branch_1_fun/ppermute | solution.py:68
  38.0 2.7 %collective-permute-start.3 = (bf16[256,768]{1,0:T(8,128)(2,1)}, bf16[256,768]{1,0:T(8,128)(2,1)}, u32[]{:S(2)}, u32[]{:S(2)}) collective-permute-start(bf16[256,768]{1,0:T(8,128)(2,1)} %dynamic-slice_bitcast_fusion), channel_id=1, source_target_pairs={{0,32},{1,33},{2,34},{3,35},{4,36},{5,37},{6,38},{7,39},{8,40},{9,... | collective-permute-start | bytes 1179656 | tf_op jit(solution)/shard_map/cond/branch_1_fun/ppermute | solution.py:68
  40.8 5.2 %branch_1_fun.3 = bf16[8,384,640]{2,1,0:T(8,128)(2,1)S(1)} custom-call(s32[24]{0:T(128)S(1)} %get-tuple-element.27.meta, bf16[8,384,640]{2,1,0:T(8,128)(2,1)} %bitcast.39), custom_call_target="tpu_custom_call" | custom-call | tf_op jit(solution)/shard_map/cond/branch_1_fun/pallas_call | solution.py:290
  45.9 4.1 %collective-permute-done.3 = bf16[256,768]{1,0:T(8,128)(2,1)} collective-permute-done((bf16[256,768]{1,0:T(8,128)(2,1)}, bf16[256,768]{1,0:T(8,128)(2,1)}, u32[]{:S(2)}, u32[]{:S(2)}) %collective-permute-start.3) | collective-permute-done | bytes 393248 | tf_op jit(solution)/shard_map/cond/branch_1_fun/ppermute | solution.py:68
  54.6 7.6 %collective-permute-done.7.o1 = bf16[256,768]{1,0:T(8,128)(2,1)S(1)} collective-permute-done((bf16[256,768]{1,0:T(8,128)(2,1)}, bf16[256,768]{1,0:T(8,128)(2,1)S(1)}, u32[]{:S(2)}, u32[]{:S(2)}) %collective-permute-start.7) | collective-permute-done | bytes 393248 | tf_op jit(solution)/shard_map/ppermute | solution.py:68
  62.1 3.0 %collective-permute-done.8.o3 = bf16[256,768]{1,0:T(8,128)(2,1)S(1)} collective-permute-done((bf16[256,768]{1,0:T(8,128)(2,1)}, bf16[256,768]{1,0:T(8,128)(2,1)S(1)}, u32[]{:S(2)}, u32[]{:S(2)}) %collective-permute-start.8) | collective-permute-done | bytes 393248 | tf_op jit(solution)/shard_map/ppermute | solution.py:68
  69.4 2.8 %collective-permute-start.14 = (bf16[96,5120]{1,0:T(8,128)(2,1)S(1)}, bf16[96,5120]{1,0:T(8,128)(2,1)S(1)}, u32[]{:S(2)}, u32[]{:S(2)}) collective-permute-start(bf16[96,5120]{1,0:T(8,128)(2,1)S(1)} %slice.23), channel_id=1, source_target_pairs={{0,3},{1,2},{2,1},{3,0},{4,7},{5,6},{6,5},{7,4},{8,12},{9,13},{10,... | collective-permute-start | bytes 2949128 | tf_op jit(solution)/shard_map/ppermute | solution.py:68
  74.0 3.7 %shard_map.105 = (bf16[4,256,5120]{2,1,0:T(8,128)(2,1)S(1)}, bf16[4,256,384]{2,1,0:T(8,128)(2,1)S(1)}, bf16[4,256,640]{2,1,0:T(8,128)(2,1)S(1)}, bf16[4,256,640]{2,1,0:T(8,128)(2,1)S(1)}) custom-call(s32[24]{0:T(128)S(1)} %dynamic-slice_bitcast_fusion.1.meta, bf16[256,5120]{1,0:T(8,128)(2,1)S(1)} %bitcast.34, f32[1,5120]{1,0:T(1,128)S(1)} %copy-done.2, ...), custom_call_target="tpu_custom_call" | custom-call | tf_op jit(solution)/shard_map/pallas_call | solution.py:121
  77.7 5.4 %shard_map.106 = (bf16[4,256,5120]{2,1,0:T(8,128)(2,1)S(1)}, bf16[4,256,384]{2,1,0:T(8,128)(2,1)S(1)}, bf16[4,256,640]{2,1,0:T(8,128)(2,1)S(1)}, bf16[4,256,640]{2,1,0:T(8,128)(2,1)S(1)}) custom-call(s32[24]{0:T(128)S(1)} %dynamic-slice_bitcast_fusion.1.meta, ...), custom_call_target="tpu_custom_call", output_to_operand_aliasing={{0}: (4, {}), {1}: (5, {}), {2}: (6, {}), {3}: (7, {})} | custom-call | tf_op jit(solution)/shard_map/pallas_call | solution.py:121
  83.1 3.7 %shard_map.107 = (bf16[4,256,5120]{2,1,0:T(8,128)(2,1)S(1)}, bf16[4,256,384]{2,1,0:T(8,128)(2,1)S(1)}, bf16[4,256,640]{2,1,0:T(8,128)(2,1)S(1)}, bf16[4,256,640]{2,1,0:T(8,128)(2,1)S(1)}) custom-call(s32[24]{0:T(128)S(1)} %dynamic-slice_bitcast_fusion.1.meta, ...), custom_call_target="tpu_custom_call", output_to_operand_aliasing={{0}: (4, {}), {1}: (5, {}), {2}: (6, {}), {3}: (7, {})} | custom-call | tf_op jit(solution)/shard_map/pallas_call | solution.py:121
  86.8 3.4 %collective-permute-start.15 = (bf16[256,768]{1,0:T(8,128)(2,1)S(1)}, bf16[256,768]{1,0:T(8,128)(2,1)S(1)}, u32[]{:S(2)}, u32[]{:S(2)}) collective-permute-start(bf16[256,768]{1,0:T(8,128)(2,1)S(1)} %collective-permute-done.7.o1), channel_id=1, source_target_pairs={{0,8},{1,9},{2,10},{3,11},{4,12},{5,13},{6,14},{7,15},{8,0},{9,1},... | collective-permute-start | bytes 1179656 | tf_op jit(solution)/shard_map/ppermute | solution.py:68
  90.2 4.4 %collective-permute-done.14.refs_1_ = bf16[96,5120]{1,0:T(8,128)(2,1)S(1)} collective-permute-done((bf16[96,5120]{1,0:T(8,128)(2,1)S(1)}, bf16[96,5120]{1,0:T(8,128)(2,1)S(1)}, u32[]{:S(2)}, u32[]{:S(2)}) %collective-permute-start.14) | collective-permute-done | bytes 983072 | tf_op jit(solution)/shard_map/ppermute | solution.py:68
  94.6 4.1 %collective-permute-start.16 = (bf16[256,768]{1,0:T(8,128)(2,1)}, bf16[256,768]{1,0:T(8,128)(2,1)S(1)}, u32[]{:S(2)}, u32[]{:S(2)}) collective-permute-start(bf16[256,768]{1,0:T(8,128)(2,1)} %get-tuple-element.113.o2), channel_id=1, source_target_pairs={{0,8},{1,9},{2,10},{3,11},{4,12},{5,13},{6,14},{7,15},{8,0},{9,1},... | collective-permute-start | bytes 1179656 | tf_op jit(solution)/shard_map/ppermute | solution.py:68
  100.8 3.7 %shard_map.108 = (bf16[4,256,5120]{2,1,0:T(8,128)(2,1)S(1)}, bf16[4,256,384]{2,1,0:T(8,128)(2,1)S(1)}, bf16[4,256,640]{2,1,0:T(8,128)(2,1)S(1)}, bf16[4,256,640]{2,1,0:T(8,128)(2,1)S(1)}) custom-call(s32[24]{0:T(128)S(1)} %dynamic-slice_bitcast_fusion.1.meta, ...), custom_call_target="tpu_custom_call", output_to_operand_aliasing={{0}: (5, {}), {1}: (6, {}), {2}: (7, {}), {3}: (8, {})} | custom-call | tf_op jit(solution)/shard_map/pallas_call | solution.py:121
  106.8 4.3 %collective-permute-done.11.t2 = bf16[2,256,768]{2,1,0:T(8,128)(2,1)S(1)} collective-permute-done((bf16[2,256,768]{2,1,0:T(8,128)(2,1)}, bf16[2,256,768]{2,1,0:T(8,128)(2,1)S(1)}, u32[]{:S(2)}, u32[]{:S(2)}) %collective-permute-start.11) | collective-permute-done | bytes 786464 | tf_op jit(solution)/shard_map/ppermute | solution.py:68
  111.3 5.7 %shard_map.109 = bf16[1024,384]{1,0:T(8,128)(2,1)S(1)} custom-call(bf16[1024,5120]{1,0:T(8,128)(2,1)S(1)} %bitcast.24, bf16[5120,384]{1,0:T(8,128)(2,1)S(1)} %collective-permute-done.12.w_ref), custom_call_target="tpu_custom_call" | custom-call | tf_op jit(solution)/shard_map/pallas_call | solution.py:145
  117.0 7.1 %shard_map.111.c0 = bf16[512,768]{1,0:T(8,128)(2,1)S(1)} custom-call(s32[24]{0:T(128)S(1)} %dynamic-slice_bitcast_fusion.1.meta, bf16[4,256,384]{2,1,0:T(8,128)(2,1)S(1)} %get-tuple-element.123.q_own, bf16[4,256,384]{2,1,0:T(8,128)(2,1)S(1)} %bitcast.30, s32[8,1,256]{2,1,0:T(1,128)S(1)} %bitcast.35, bf16[2,256,768]{2,1,0:T(8,128)(2,1)} %get-tuple-element.126.own0, ...), custom_call_target="tpu_custom_call" | custom-call | flops 1207959552 | bytes 8388608 | tf_op jit(solution)/shard_map/pallas_call | solution.py:262
  126.6 9.0 %shard_map.110.c0 = bf16[512,768]{1,0:T(8,128)(2,1)S(1)} custom-call(s32[24]{0:T(128)S(1)} %dynamic-slice_bitcast_fusion.1.meta, bf16[4,256,384]{2,1,0:T(8,128)(2,1)S(1)} %get-tuple-element.123.q_own, bf16[4,256,384]{2,1,0:T(8,128)(2,1)S(1)} %bitcast.31, s32[8,1,256]{2,1,0:T(1,128)S(1)} %bitcast.36, bf16[2,256,768]{2,1,0:T(8,128)(2,1)} %get-tuple-element.126.own0, ...), custom_call_target="tpu_custom_call" | custom-call | flops 1207959552 | bytes 8388608 | tf_op jit(solution)/shard_map/pallas_call | solution.py:262
  136.8 4.8 %collective-permute-done.20.c1 = bf16[512,768]{1,0:T(8,128)(2,1)S(1)} collective-permute-done((bf16[512,768]{1,0:T(8,128)(2,1)S(1)}, bf16[512,768]{1,0:T(8,128)(2,1)S(1)}, u32[]{:S(2)}, u32[]{:S(2)}) %collective-permute-start.20) | collective-permute-done | bytes 786464 | tf_op jit(solution)/shard_map/ppermute | solution.py:68
  141.6 3.1 %collective-permute-done.21.c3 = bf16[512,768]{1,0:T(8,128)(2,1)S(1)} collective-permute-done((bf16[512,768]{1,0:T(8,128)(2,1)S(1)}, bf16[512,768]{1,0:T(8,128)(2,1)S(1)}, u32[]{:S(2)}, u32[]{:S(2)}) %collective-permute-start.21) | collective-permute-done | bytes 786464 | tf_op jit(solution)/shard_map/ppermute | solution.py:68
  147.5 10.9 %collective-permute-done.18.c1 = bf16[512,768]{1,0:T(8,128)(2,1)S(1)} collective-permute-done((bf16[512,768]{1,0:T(8,128)(2,1)S(1)}, bf16[512,768]{1,0:T(8,128)(2,1)S(1)}, u32[]{:S(2)}, u32[]{:S(2)}) %collective-permute-start.18) | collective-permute-done | bytes 786464 | tf_op jit(solution)/shard_map/ppermute | solution.py:68
  158.5 3.1 %collective-permute-done.19.c3 = bf16[512,768]{1,0:T(8,128)(2,1)S(1)} collective-permute-done((bf16[512,768]{1,0:T(8,128)(2,1)S(1)}, bf16[512,768]{1,0:T(8,128)(2,1)S(1)}, u32[]{:S(2)}, u32[]{:S(2)}) %collective-permute-start.19) | collective-permute-done | bytes 786464 | tf_op jit(solution)/shard_map/ppermute | solution.py:68
  161.6 4.2 %collective-permute-done.22.c2b = bf16[128,768]{1,0:T(8,128)(2,1)S(1)} collective-permute-done((bf16[128,768]{1,0:T(8,128)(2,1)S(1)}, bf16[128,768]{1,0:T(8,128)(2,1)S(1)}, u32[]{:S(2)}, u32[]{:S(2)}) %collective-permute-start.22) | collective-permute-done | bytes 196640 | tf_op jit(solution)/shard_map/ppermute | solution.py:68
  171.1 7.0 %collective-permute-done.25.w = bf16[3072,640]{1,0:T(8,128)(2,1)S(1)} collective-permute-done((bf16[3072,640]{1,0:T(8,128)(2,1)S(1)}, bf16[3072,640]{1,0:T(8,128)(2,1)S(1)}, u32[]{:S(2)}, u32[]{:S(2)}) %collective-permute-start.25) | collective-permute-done | bytes 3932192 | tf_op jit(solution)/shard_map/ppermute | solution.py:68
  178.1 3.4 %shard_map.113 = bf16[2,256,640]{2,1,0:T(8,128)(2,1)S(1)} custom-call(s32[24]{0:T(128)S(1)} %dynamic-slice_bitcast_fusion.1.meta, bf16[512,768]{1,0:T(8,128)(2,1)S(1)} %shard_map.111.c0, bf16[512,768]{1,0:T(8,128)(2,1)S(1)} %collective-permute-done.20.c1, bf16[384,768]{1,0:T(8,128)(2,1)S(1)} %collective-permute-done.27.c2a, ...), custom_call_target="tpu_custom_call" | custom-call | flops 2013265920 | bytes 8388608 | tf_op jit(solution)/shard_map/pallas_call | solution.py:334
  183.8 3.4 %shard_map.112 = bf16[2,256,640]{2,1,0:T(8,128)(2,1)S(1)} custom-call(s32[24]{0:T(128)S(1)} %dynamic-slice_bitcast_fusion.1.meta, bf16[512,768]{1,0:T(8,128)(2,1)S(1)} %shard_map.110.c0, bf16[512,768]{1,0:T(8,128)(2,1)S(1)} %collective-permute-done.18.c1, bf16[384,768]{1,0:T(8,128)(2,1)S(1)} %collective-permute-done.23.c2a, ...), custom_call_target="tpu_custom_call" | custom-call | flops 2013265920 | bytes 8388608 | tf_op jit(solution)/shard_map/pallas_call | solution.py:334
  187.1 5.8 %collective-permute-start.26 = (bf16[2,256,640]{2,1,0:T(8,128)(2,1)S(1)}, bf16[2,256,640]{2,1,0:T(8,128)(2,1)S(1)}, u32[]{:S(2)}, u32[]{:S(2)}) collective-permute-start(bf16[2,256,640]{2,1,0:T(8,128)(2,1)S(1)} %shard_map.112), channel_id=1, source_target_pairs={{0,4},{1,5},{2,6},{3,7},{4,0},{5,1},{6,2},{7,3},{8,11},{9,10},{10,... | collective-permute-start | bytes 1966088 | tf_op jit(solution)/shard_map/ppermute | solution.py:68
  193.0 4.1 %shard_map.114.refs_0_ = bf16[8,256,640]{2,1,0:T(8,128)(2,1)} custom-call(s32[24]{0:T(128)S(1)} %dynamic-slice_bitcast_fusion.1.meta, bf16[512,768]{1,0:T(8,128)(2,1)S(1)} %shard_map.111.c0, bf16[512,768]{1,0:T(8,128)(2,1)S(1)} %collective-permute-done.20.c1, bf16[384,768]{1,0:T(8,128)(2,1)S(1)} %collective-permute-done.27.c2a, ...), custom_call_target="tpu_custom_call" | custom-call | flops 2013265920 | bytes 8388608 | tf_op jit(solution)/shard_map/pallas_call | solution.py:334
  197.1 4.1 %shard_map.115.prior = bf16[8,256,640]{2,1,0:T(8,128)(2,1)} custom-call(s32[24]{0:T(128)S(1)} %dynamic-slice_bitcast_fusion.1.meta, bf16[512,768]{1,0:T(8,128)(2,1)S(1)} %shard_map.110.c0, bf16[512,768]{1,0:T(8,128)(2,1)S(1)} %collective-permute-done.18.c1, bf16[384,768]{1,0:T(8,128)(2,1)S(1)} %collective-permute-done.23.c2a, ...), custom_call_target="tpu_custom_call", output_to_operand_aliasing={{}: (8, {})} | custom-call | flops 2013265920 | bytes 8388608 | tf_op jit(solution)/shard_map/pallas_call | solution.py:334
  (80 shorter events, 50.6 us)
Async XLA Ops:
  0.0 65.2 %collective-permute-start.5 = (bf16[256,5120]{1,0:T(8,128)(2,1)}, bf16[256,5120]{1,0:T(8,128)(2,1)}, u32[]{:S(2)}, u32[]{:S(2)}) collective-permute-start(bf16[256,5120]{1,0:T(8,128)(2,1)} %bitcast.32), channel_id=1, source_target_pairs={{0,1},{1,0},{2,3},{3,2},{4,5},{5,4},{6,7},{7,6},{8,9},{9,8},{10,11... | collective-permute-start | bytes 7864328 | tf_op jit(solution)/shard_map/ppermute | solution.py:68
  2.5 62.7 %collective-permute-start.6 = (bf16[256,5120]{1,0:T(8,128)(2,1)}, bf16[256,5120]{1,0:T(8,128)(2,1)S(1)}, u32[]{:S(2)}, u32[]{:S(2)}) collective-permute-start(bf16[256,5120]{1,0:T(8,128)(2,1)} %bitcast.33), channel_id=1, source_target_pairs={{0,3},{1,2},{2,1},{3,0},{4,7},{5,6},{6,5},{7,4},{8,12},{9,13},{10,... | collective-permute-start | bytes 7864328 | tf_op jit(solution)/shard_map/ppermute | solution.py:68
  13.0 3.3 %collective-permute-start = (bf16[128,768]{1,0:T(8,128)(2,1)S(1)}, bf16[128,768]{1,0:T(8,128)(2,1)S(1)}, u32[]{:S(2)}, u32[]{:S(2)}) collective-permute-start(bf16[128,768]{1,0:T(8,128)(2,1)S(1)} %get-tuple-element.193), channel_id=1, source_target_pairs={{0,8},{1,9},{2,10},{3,11},{4,12},{5,13},{6,14},{7,15},{8,0},{9,1},... | collective-permute-start | bytes 589832 | tf_op jit(solution)/shard_map/cond/branch_1_fun/ppermute | solution.py:68
  16.4 7.8 %collective-permute-start.1 = (bf16[2,128,768]{2,1,0:T(8,128)(2,1)S(1)}, bf16[2,128,768]{2,1,0:T(8,128)(2,1)S(1)}, u32[]{:S(2)}, u32[]{:S(2)}) collective-permute-start(bf16[2,128,768]{2,1,0:T(8,128)(2,1)S(1)} %maximum_select_fusion.2), channel_id=1, source_target_pairs={{0,64},{1,65},{2,66},{3,67},{4,68},{5,69},{6,70},{7,71},{16,80},{1... | collective-permute-start | bytes 1179656 | tf_op jit(solution)/shard_map/cond/branch_1_fun/ppermute | solution.py:68
  24.2 9.5 %collective-permute-start.2 = (bf16[2,128,768]{2,1,0:T(8,128)(2,1)S(1)}, bf16[2,128,768]{2,1,0:T(8,128)(2,1)}, u32[]{:S(2)}, u32[]{:S(2)}) collective-permute-start(bf16[2,128,768]{2,1,0:T(8,128)(2,1)S(1)} %collective-permute-done.1), channel_id=1, source_target_pairs={{0,8},{1,9},{2,10},{3,11},{4,12},{5,13},{6,14},{7,15},{8,0},{9,1},... | collective-permute-start | bytes 1179656 | tf_op jit(solution)/shard_map/cond/branch_1_fun/ppermute | solution.py:68
  35.8 14.2 %collective-permute-start.4 = (bf16[2,256,768]{2,1,0:T(8,128)(2,1)}, bf16[2,256,768]{2,1,0:T(8,128)(2,1)}, u32[]{:S(2)}, u32[]{:S(2)}) collective-permute-start(bf16[2,256,768]{2,1,0:T(8,128)(2,1)} %maximum_select_fusion), channel_id=1, source_target_pairs={{0,4},{1,5},{2,6},{3,7},{4,0},{5,1},{6,2},{7,3},{8,11},{9,10},{10,... | collective-permute-start | bytes 2359304 | tf_op jit(solution)/shard_map/cond/branch_1_fun/ppermute | solution.py:68
  38.0 12.0 %collective-permute-start.3 = (bf16[256,768]{1,0:T(8,128)(2,1)}, bf16[256,768]{1,0:T(8,128)(2,1)}, u32[]{:S(2)}, u32[]{:S(2)}) collective-permute-start(bf16[256,768]{1,0:T(8,128)(2,1)} %dynamic-slice_bitcast_fusion), channel_id=1, source_target_pairs={{0,32},{1,33},{2,34},{3,35},{4,36},{5,37},{6,38},{7,39},{8,40},{9,... | collective-permute-start | bytes 1179656 | tf_op jit(solution)/shard_map/cond/branch_1_fun/ppermute | solution.py:68
  50.0 56.8 %collective-permute-start.12 = (bf16[5120,384]{1,0:T(8,128)(2,1)}, bf16[5120,384]{1,0:T(8,128)(2,1)S(1)}, u32[]{:S(2)}, u32[]{:S(2)}) collective-permute-start(bf16[5120,384]{1,0:T(8,128)(2,1)} %bitcast.25), channel_id=1, source_target_pairs={{0,4},{1,5},{2,6},{3,7},{4,0},{5,1},{6,2},{7,3},{8,11},{9,10},{10,... | collective-permute-start | bytes 11796488 | tf_op jit(solution)/shard_map/ppermute | solution.py:68
  52.1 20.1 %copy-start = (bf16[1,5120,384]{2,1,0:T(8,128)(2,1)S(1)}, bf16[1,5120,384]{2,1,0:T(8,128)(2,1)}, u32[]{:S(2)}) copy-start(bf16[1,5120,384]{2,1,0:T(8,128)(2,1)} %param.18) | copy-start | bytes 11796484
  52.1 20.1 %copy-start.2 = (f32[1,5120]{1,0:T(1,128)S(1)}, f32[1,5120]{1,0:T(1,128)}, u32[]{:S(2)}) copy-start(f32[1,5120]{1,0:T(1,128)} %refs_2_.1) | copy-start | bytes 61444
  52.1 10.0 %collective-permute-start.7 = (bf16[256,768]{1,0:T(8,128)(2,1)}, bf16[256,768]{1,0:T(8,128)(2,1)S(1)}, u32[]{:S(2)}, u32[]{:S(2)}) collective-permute-start(bf16[256,768]{1,0:T(8,128)(2,1)} %get-tuple-element.88), channel_id=1, source_target_pairs={{0,48},{1,49},{2,50},{3,51},{4,52},{5,53},{6,54},{7,55},{8,56},{9,... | collective-permute-start | bytes 1179656 | tf_op jit(solution)/shard_map/ppermute | solution.py:68
  54.6 10.6 %collective-permute-start.8 = (bf16[256,768]{1,0:T(8,128)(2,1)}, bf16[256,768]{1,0:T(8,128)(2,1)S(1)}, u32[]{:S(2)}, u32[]{:S(2)}) collective-permute-start(bf16[256,768]{1,0:T(8,128)(2,1)} %get-tuple-element.88), channel_id=1, source_target_pairs={{0,16},{1,17},{2,18},{3,19},{4,20},{5,21},{6,22},{7,23},{8,24},{9,... | collective-permute-start | bytes 1179656 | tf_op jit(solution)/shard_map/ppermute | solution.py:68
  65.3 35.5 %collective-permute-start.13 = (bf16[160,5120]{1,0:T(8,128)(2,1)S(1)}, bf16[160,5120]{1,0:T(8,128)(2,1)S(1)}, u32[]{:S(2)}, u32[]{:S(2)}) collective-permute-start(bf16[160,5120]{1,0:T(8,128)(2,1)S(1)} %slice.22), channel_id=1, source_target_pairs={{0,1},{1,0},{2,3},{3,2},{4,5},{5,4},{6,7},{7,6},{8,9},{9,8},{10,11... | collective-permute-start | bytes 4915208 | tf_op jit(solution)/shard_map/ppermute | solution.py:68
  65.4 21.4 %collective-permute-start.10 = (bf16[2,256,768]{2,1,0:T(8,128)(2,1)}, bf16[2,256,768]{2,1,0:T(8,128)(2,1)S(1)}, u32[]{:S(2)}, u32[]{:S(2)}) collective-permute-start(bf16[2,256,768]{2,1,0:T(8,128)(2,1)} %get-tuple-element.105.other0), channel_id=1, source_target_pairs={{0,16},{1,17},{2,18},{3,19},{4,20},{5,21},{6,22},{7,23},{8,24},{9,... | collective-permute-start | bytes 2359304 | tf_op jit(solution)/shard_map/ppermute | solution.py:68
  65.5 21.3 %collective-permute-start.9 = (bf16[2,256,768]{2,1,0:T(8,128)(2,1)}, bf16[2,256,768]{2,1,0:T(8,128)(2,1)S(1)}, u32[]{:S(2)}, u32[]{:S(2)}) collective-permute-start(bf16[2,256,768]{2,1,0:T(8,128)(2,1)} %get-tuple-element.105.other0), channel_id=1, source_target_pairs={{0,48},{1,49},{2,50},{3,51},{4,52},{5,53},{6,54},{7,55},{8,56},{9,... | collective-permute-start | bytes 2359304 | tf_op jit(solution)/shard_map/ppermute | solution.py:68
  69.4 25.2 %collective-permute-start.14 = (bf16[96,5120]{1,0:T(8,128)(2,1)S(1)}, bf16[96,5120]{1,0:T(8,128)(2,1)S(1)}, u32[]{:S(2)}, u32[]{:S(2)}) collective-permute-start(bf16[96,5120]{1,0:T(8,128)(2,1)S(1)} %slice.23), channel_id=1, source_target_pairs={{0,3},{1,2},{2,1},{3,0},{4,7},{5,6},{6,5},{7,4},{8,12},{9,13},{10,... | collective-permute-start | bytes 2949128 | tf_op jit(solution)/shard_map/ppermute | solution.py:68
  86.8 24.3 %copy-start.6 = (bf16[3072,640]{1,0:T(8,128)(2,1)S(1)}, bf16[3072,640]{1,0:T(8,128)(2,1)}, u32[]{:S(2)}) copy-start(bf16[3072,640]{1,0:T(8,128)(2,1)} %copy-done.5) | copy-start | bytes 11796484
  86.8 11.9 %collective-permute-start.15 = (bf16[256,768]{1,0:T(8,128)(2,1)S(1)}, bf16[256,768]{1,0:T(8,128)(2,1)S(1)}, u32[]{:S(2)}, u32[]{:S(2)}) collective-permute-start(bf16[256,768]{1,0:T(8,128)(2,1)S(1)} %collective-permute-done.7.o1), channel_id=1, source_target_pairs={{0,8},{1,9},{2,10},{3,11},{4,12},{5,13},{6,14},{7,15},{8,0},{9,1},... | collective-permute-start | bytes 1179656 | tf_op jit(solution)/shard_map/ppermute | solution.py:68
  90.2 20.8 %collective-permute-start.11 = (bf16[2,256,768]{2,1,0:T(8,128)(2,1)}, bf16[2,256,768]{2,1,0:T(8,128)(2,1)S(1)}, u32[]{:S(2)}, u32[]{:S(2)}) collective-permute-start(bf16[2,256,768]{2,1,0:T(8,128)(2,1)} %get-tuple-element.105.other0), channel_id=1, source_target_pairs={{0,32},{1,33},{2,34},{3,35},{4,36},{5,37},{6,38},{7,39},{8,40},{9,... | collective-permute-start | bytes 2359304 | tf_op jit(solution)/shard_map/ppermute | solution.py:68
  94.6 6.1 %collective-permute-start.16 = (bf16[256,768]{1,0:T(8,128)(2,1)}, bf16[256,768]{1,0:T(8,128)(2,1)S(1)}, u32[]{:S(2)}, u32[]{:S(2)}) collective-permute-start(bf16[256,768]{1,0:T(8,128)(2,1)} %get-tuple-element.113.o2), channel_id=1, source_target_pairs={{0,8},{1,9},{2,10},{3,11},{4,12},{5,13},{6,14},{7,15},{8,0},{9,1},... | collective-permute-start | bytes 1179656 | tf_op jit(solution)/shard_map/ppermute | solution.py:68
  98.7 2.0 %collective-permute-start.17 = (bf16[256,768]{1,0:T(8,128)(2,1)S(1)}, bf16[256,768]{1,0:T(8,128)(2,1)S(1)}, u32[]{:S(2)}, u32[]{:S(2)}) collective-permute-start(bf16[256,768]{1,0:T(8,128)(2,1)S(1)} %collective-permute-done.8.o3), channel_id=1, source_target_pairs={{0,8},{1,9},{2,10},{3,11},{4,12},{5,13},{6,14},{7,15},{8,0},{9,1},... | collective-permute-start | bytes 1179656 | tf_op jit(solution)/shard_map/ppermute | solution.py:68
  111.1 67.1 %collective-permute-start.25 = (bf16[3072,640]{1,0:T(8,128)(2,1)S(1)}, bf16[3072,640]{1,0:T(8,128)(2,1)S(1)}, u32[]{:S(2)}, u32[]{:S(2)}) collective-permute-start(bf16[3072,640]{1,0:T(8,128)(2,1)S(1)} %copy-done.6), channel_id=1, source_target_pairs={{0,4},{1,5},{2,6},{3,7},{4,0},{5,1},{6,2},{7,3},{8,11},{9,10},{10,... | collective-permute-start | bytes 11796488 | tf_op jit(solution)/shard_map/ppermute | solution.py:68
  124.1 17.5 %collective-permute-start.20 = (bf16[512,768]{1,0:T(8,128)(2,1)S(1)}, bf16[512,768]{1,0:T(8,128)(2,1)S(1)}, u32[]{:S(2)}, u32[]{:S(2)}) collective-permute-start(bf16[512,768]{1,0:T(8,128)(2,1)S(1)} %shard_map.111.c0), channel_id=1, source_target_pairs={{0,1},{1,0},{2,3},{3,2},{4,5},{5,4},{6,7},{7,6},{8,9},{9,8},{10,11... | collective-permute-start | bytes 2359304 | tf_op jit(solution)/shard_map/ppermute | solution.py:68
  124.7 20.1 %collective-permute-start.21 = (bf16[512,768]{1,0:T(8,128)(2,1)S(1)}, bf16[512,768]{1,0:T(8,128)(2,1)S(1)}, u32[]{:S(2)}, u32[]{:S(2)}) collective-permute-start(bf16[512,768]{1,0:T(8,128)(2,1)S(1)} %shard_map.111.c0), channel_id=1, source_target_pairs={{0,3},{1,2},{2,1},{3,0},{4,7},{5,6},{6,5},{7,4},{8,12},{9,13},{10,... | collective-permute-start | bytes 2359304 | tf_op jit(solution)/shard_map/ppermute | solution.py:68
  135.6 22.9 %collective-permute-start.18 = (bf16[512,768]{1,0:T(8,128)(2,1)S(1)}, bf16[512,768]{1,0:T(8,128)(2,1)S(1)}, u32[]{:S(2)}, u32[]{:S(2)}) collective-permute-start(bf16[512,768]{1,0:T(8,128)(2,1)S(1)} %shard_map.110.c0), channel_id=1, source_target_pairs={{0,1},{1,0},{2,3},{3,2},{4,5},{5,4},{6,7},{7,6},{8,9},{9,8},{10,11... | collective-permute-start | bytes 2359304 | tf_op jit(solution)/shard_map/ppermute | solution.py:68
  136.8 24.7 %collective-permute-start.19 = (bf16[512,768]{1,0:T(8,128)(2,1)S(1)}, bf16[512,768]{1,0:T(8,128)(2,1)S(1)}, u32[]{:S(2)}, u32[]{:S(2)}) collective-permute-start(bf16[512,768]{1,0:T(8,128)(2,1)S(1)} %shard_map.110.c0), channel_id=1, source_target_pairs={{0,3},{1,2},{2,1},{3,0},{4,7},{5,6},{6,5},{7,4},{8,12},{9,13},{10,... | collective-permute-start | bytes 2359304 | tf_op jit(solution)/shard_map/ppermute | solution.py:68
  144.7 21.0 %collective-permute-start.22 = (bf16[128,768]{1,0:T(8,128)(2,1)S(1)}, bf16[128,768]{1,0:T(8,128)(2,1)S(1)}, u32[]{:S(2)}, u32[]{:S(2)}) collective-permute-start(bf16[128,768]{1,0:T(8,128)(2,1)S(1)} %slice.24), channel_id=1, source_target_pairs={{0,3},{1,2},{2,1},{3,0},{4,7},{5,6},{6,5},{7,4},{8,12},{9,13},{10,... | collective-permute-start | bytes 589832 | tf_op jit(solution)/shard_map/ppermute | solution.py:68
  146.3 24.8 %collective-permute-start.27 = (bf16[384,768]{1,0:T(8,128)(2,1)S(1)}, bf16[384,768]{1,0:T(8,128)(2,1)S(1)}, u32[]{:S(2)}, u32[]{:S(2)}) collective-permute-start(bf16[384,768]{1,0:T(8,128)(2,1)S(1)} %slice.27), channel_id=1, source_target_pairs={{0,1},{1,0},{2,3},{3,2},{4,5},{5,4},{6,7},{7,6},{8,9},{9,8},{10,11... | collective-permute-start | bytes 1769480 | tf_op jit(solution)/shard_map/ppermute | solution.py:68
  165.8 18.0 %collective-permute-start.23 = (bf16[384,768]{1,0:T(8,128)(2,1)S(1)}, bf16[384,768]{1,0:T(8,128)(2,1)S(1)}, u32[]{:S(2)}, u32[]{:S(2)}) collective-permute-start(bf16[384,768]{1,0:T(8,128)(2,1)S(1)} %slice.25), channel_id=1, source_target_pairs={{0,1},{1,0},{2,3},{3,2},{4,5},{5,4},{6,7},{7,6},{8,9},{9,8},{10,11... | collective-permute-start | bytes 1769480 | tf_op jit(solution)/shard_map/ppermute | solution.py:68
  167.1 15.9 %collective-permute-start.24 = (bf16[128,768]{1,0:T(8,128)(2,1)S(1)}, bf16[128,768]{1,0:T(8,128)(2,1)S(1)}, u32[]{:S(2)}, u32[]{:S(2)}) collective-permute-start(bf16[128,768]{1,0:T(8,128)(2,1)S(1)} %slice.26), channel_id=1, source_target_pairs={{0,3},{1,2},{2,1},{3,0},{4,7},{5,6},{6,5},{7,4},{8,12},{9,13},{10,... | collective-permute-start | bytes 589832 | tf_op jit(solution)/shard_map/ppermute | solution.py:68
  181.5 19.7 %collective-permute-start.28 = (bf16[2,256,640]{2,1,0:T(8,128)(2,1)S(1)}, bf16[2,256,640]{2,1,0:T(8,128)(2,1)S(1)}, u32[]{:S(2)}, u32[]{:S(2)}) collective-permute-start(bf16[2,256,640]{2,1,0:T(8,128)(2,1)S(1)} %shard_map.113), channel_id=1, source_target_pairs={{0,4},{1,5},{2,6},{3,7},{4,0},{5,1},{6,2},{7,3},{8,11},{9,10},{10,... | collective-permute-start | bytes 1966088 | tf_op jit(solution)/shard_map/ppermute | solution.py:68
  187.1 15.4 %collective-permute-start.26 = (bf16[2,256,640]{2,1,0:T(8,128)(2,1)S(1)}, bf16[2,256,640]{2,1,0:T(8,128)(2,1)S(1)}, u32[]{:S(2)}, u32[]{:S(2)}) collective-permute-start(bf16[2,256,640]{2,1,0:T(8,128)(2,1)S(1)} %shard_map.112), channel_id=1, source_target_pairs={{0,4},{1,5},{2,6},{3,7},{4,0},{5,1},{6,2},{7,3},{8,11},{9,10},{10,... | collective-permute-start | bytes 1966088 | tf_op jit(solution)/shard_map/ppermute | solution.py:68
  (7 other events, 32.9 us)

commit v13 on v11

--- a/solution.py
+++ b/solution.py
@@ -422,7 +422,7 @@
 
     w_o_r = w_o.reshape(8, w_q.shape[1], width)
     piece, share, o2, piece2, w_o_mine, w_o_theirs = lax.cond(
-        segment_ids[0] >= 0, cache, nothing, last_hidden, w_key, w_value, w_o_r
+        section >= 0, cache, nothing, last_hidden, w_key, w_value, w_o_r
     )
     w_q2 = send(after(w_q, piece2), PARTNER)
     o1 = send(share, X_PREV)

time: 203 us -> 201 us (level)
  Pallas kernels: 70.2 us -> 66.3 us
  waiting for transfers between devices: 63.8 us -> 67.7 us
    ppermute x29, waiting for transfers between devices: 63.8 us -> 67.7 us  [send(): return lax.ppermute(value, AXES, pairs)]
    pallas_call x2, Pallas kernels: 18.1 us -> 14.2 us  [attend(): pl.pallas_call(functools.partial(attend_kernel, chunk), grid_spec=pltpu.P...]
  transfers between devices with their start and end apart: 29 -> 29, of which waited for: 15 -> 15; matrix products, arithmetic and copies ran while one was open for 7% -> 6% of each run, Pallas kernels for 34% -> 33%
where the time goes in v13:
time: 201 us; the launch traced here: 200 us
  waiting for transfers between devices  67.7 us (34%)
  Pallas kernels  66.3 us (33%)
  starting transfers between devices  50.6 us (25%)
  local copies, waits for them, and re-layouts  6.22 us (3%)
  matrix products  4.48 us (2%)
  other arithmetic  3.84 us (2%)
    ppermute x29, waiting for transfers between devices, send(): return lax.ppermute(value, AXES, pairs)  67.7 us
    ppermute x29, starting transfers between devices, send(): return lax.ppermute(value, AXES, pairs)  50.6 us
    pallas_call x4, Pallas kernels, project(): pl.pallas_call(kernel, grid_spec=pltpu.PrefetchScalarGridSpec(num_scalar_...  16.5 us
    pallas_call x4, Pallas kernels, finish(): pl.pallas_call(finish_kernel, grid_spec=pltpu.PrefetchScalarGridSpec(num_...  14.9 us
    pallas_call x2, Pallas kernels, attend(): pl.pallas_call(functools.partial(attend_kernel, chunk), grid_spec=pltpu.P...  14.2 us
    pallas_call x2, Pallas kernels, reorder(): pl.pallas_call(reorder_kernel, grid_spec=pltpu.PrefetchScalarGridSpec(num...  12.2 us
    pallas_call x1, Pallas kernels, more_queries(): pl.pallas_call(more_queries_kernel, grid=(2,), in_specs=[pl.BlockSpec((ro...  5.74 us
  transfers between devices with their start and end apart: 29, of which 15 were waited for; matrix products, arithmetic and copies ran while one was open for 6% of the time, Pallas kernels for 33%

profile of v13, /device:TPU:1, one launch (start us, length us, event | category | flops | bytes accessed | tf_op | source)
XLA Modules:
  0.0 199.7 jit_solution(9501366450429800759)
XLA Ops:
  4.5 43.7 %conditional.1 = (bf16[2,256,768]{2,1,0:T(8,128)(2,1)}, bf16[256,768]{1,0:T(8,128)(2,1)}, bf16[256,768]{1,0:T(8,128)(2,1)}, bf16[2,256,768]{2,1,0:T(8,128)(2,1)}...) conditional(s32[]{:T(128)} %convert_element_type.15, () %tuple.24, (s32[]{:T(128)}, pred[]{:T(512)}, ...), branch_computations={%region_0.1_spmd, %region_1.3_spmd} | conditional | flops 1016889472 | bytes 47639592 | solution.py:424
  6.2 3.6 %convolution_convert_fusion = bf16[128,384]{1,0:T(8,128)(2,1)S(1)} fusion(bf16[5120,384]{1,0:T(8,128)(2,1)} %get-tuple-element.165, bf16[128,5120]{1,0:T(8,128)(2,1)} %get-tuple-element.162, f32[5120]{0:T(1024)} %get-tuple-element.163, f32[128]{0:T(128)S(1)} %add_rsqrt_fusion), kind=kOutput, calls=%fused_computation.5 | convolution fusion | flops 505987072 | bytes 5362176 | tf_op jit(solution)/shard_map/cond/branch_1_fun/dot_general | solution.py:404
  15.3 7.1 %branch_1_fun.2 = bf16[8,384,640]{2,1,0:T(8,128)(2,1)} custom-call(s32[24]{0:T(128)S(1)} %get-tuple-element.27.meta, bf16[8,384,640]{2,1,0:T(8,128)(2,1)} %bitcast.37), custom_call_target="tpu_custom_call" | custom-call | tf_op jit(solution)/shard_map/cond/branch_1_fun/pallas_call | solution.py:290
  22.3 8.1 %collective-permute-start.2 = (bf16[2,128,768]{2,1,0:T(8,128)(2,1)S(1)}, bf16[2,128,768]{2,1,0:T(8,128)(2,1)}, u32[]{:S(2)}, u32[]{:S(2)}) collective-permute-start(bf16[2,128,768]{2,1,0:T(8,128)(2,1)S(1)} %collective-permute-done.1), channel_id=1, source_target_pairs={{0,8},{1,9},{2,10},{3,11},{4,12},{5,13},{6,14},{7,15},{8,0},{9,1},... | collective-permute-start | bytes 1179656 | tf_op jit(solution)/shard_map/cond/branch_1_fun/ppermute | solution.py:68
  36.1 2.7 %collective-permute-start.3 = (bf16[256,768]{1,0:T(8,128)(2,1)}, bf16[256,768]{1,0:T(8,128)(2,1)}, u32[]{:S(2)}, u32[]{:S(2)}) collective-permute-start(bf16[256,768]{1,0:T(8,128)(2,1)} %dynamic-slice_bitcast_fusion), channel_id=1, source_target_pairs={{0,32},{1,33},{2,34},{3,35},{4,36},{5,37},{6,38},{7,39},{8,40},{9,... | collective-permute-start | bytes 1179656 | tf_op jit(solution)/shard_map/cond/branch_1_fun/ppermute | solution.py:68
  38.9 5.2 %branch_1_fun.3 = bf16[8,384,640]{2,1,0:T(8,128)(2,1)S(1)} custom-call(s32[24]{0:T(128)S(1)} %get-tuple-element.27.meta, bf16[8,384,640]{2,1,0:T(8,128)(2,1)} %bitcast.38), custom_call_target="tpu_custom_call" | custom-call | tf_op jit(solution)/shard_map/cond/branch_1_fun/pallas_call | solution.py:290
  44.1 4.1 %collective-permute-done.3 = bf16[256,768]{1,0:T(8,128)(2,1)} collective-permute-done((bf16[256,768]{1,0:T(8,128)(2,1)}, bf16[256,768]{1,0:T(8,128)(2,1)}, u32[]{:S(2)}, u32[]{:S(2)}) %collective-permute-start.3) | collective-permute-done | bytes 393248 | tf_op jit(solution)/shard_map/cond/branch_1_fun/ppermute | solution.py:68
  52.7 7.6 %collective-permute-done.7.o1 = bf16[256,768]{1,0:T(8,128)(2,1)S(1)} collective-permute-done((bf16[256,768]{1,0:T(8,128)(2,1)}, bf16[256,768]{1,0:T(8,128)(2,1)S(1)}, u32[]{:S(2)}, u32[]{:S(2)}) %collective-permute-start.7) | collective-permute-done | bytes 393248 | tf_op jit(solution)/shard_map/ppermute | solution.py:68
  60.3 3.0 %collective-permute-done.8.o3 = bf16[256,768]{1,0:T(8,128)(2,1)S(1)} collective-permute-done((bf16[256,768]{1,0:T(8,128)(2,1)}, bf16[256,768]{1,0:T(8,128)(2,1)S(1)}, u32[]{:S(2)}, u32[]{:S(2)}) %collective-permute-start.8) | collective-permute-done | bytes 393248 | tf_op jit(solution)/shard_map/ppermute | solution.py:68
  67.5 2.8 %collective-permute-start.14 = (bf16[96,5120]{1,0:T(8,128)(2,1)S(1)}, bf16[96,5120]{1,0:T(8,128)(2,1)S(1)}, u32[]{:S(2)}, u32[]{:S(2)}) collective-permute-start(bf16[96,5120]{1,0:T(8,128)(2,1)S(1)} %slice.19), channel_id=1, source_target_pairs={{0,3},{1,2},{2,1},{3,0},{4,7},{5,6},{6,5},{7,4},{8,12},{9,13},{10,... | collective-permute-start | bytes 2949128 | tf_op jit(solution)/shard_map/ppermute | solution.py:68
  72.1 3.7 %shard_map.105 = (bf16[4,256,5120]{2,1,0:T(8,128)(2,1)S(1)}, bf16[4,256,384]{2,1,0:T(8,128)(2,1)S(1)}, bf16[4,256,640]{2,1,0:T(8,128)(2,1)S(1)}, bf16[4,256,640]{2,1,0:T(8,128)(2,1)S(1)}) custom-call(s32[24]{0:T(128)S(1)} %dynamic-slice_bitcast_fusion.1.meta, bf16[256,5120]{1,0:T(8,128)(2,1)S(1)} %bitcast.33, f32[1,5120]{1,0:T(1,128)S(1)} %copy-done.2, ...), custom_call_target="tpu_custom_call" | custom-call | tf_op jit(solution)/shard_map/pallas_call | solution.py:121
  75.8 5.4 %shard_map.106 = (bf16[4,256,5120]{2,1,0:T(8,128)(2,1)S(1)}, bf16[4,256,384]{2,1,0:T(8,128)(2,1)S(1)}, bf16[4,256,640]{2,1,0:T(8,128)(2,1)S(1)}, bf16[4,256,640]{2,1,0:T(8,128)(2,1)S(1)}) custom-call(s32[24]{0:T(128)S(1)} %dynamic-slice_bitcast_fusion.1.meta, ...), custom_call_target="tpu_custom_call", output_to_operand_aliasing={{0}: (4, {}), {1}: (5, {}), {2}: (6, {}), {3}: (7, {})} | custom-call | tf_op jit(solution)/shard_map/pallas_call | solution.py:121
  81.2 3.7 %shard_map.107 = (bf16[4,256,5120]{2,1,0:T(8,128)(2,1)S(1)}, bf16[4,256,384]{2,1,0:T(8,128)(2,1)S(1)}, bf16[4,256,640]{2,1,0:T(8,128)(2,1)S(1)}, bf16[4,256,640]{2,1,0:T(8,128)(2,1)S(1)}) custom-call(s32[24]{0:T(128)S(1)} %dynamic-slice_bitcast_fusion.1.meta, ...), custom_call_target="tpu_custom_call", output_to_operand_aliasing={{0}: (4, {}), {1}: (5, {}), {2}: (6, {}), {3}: (7, {})} | custom-call | tf_op jit(solution)/shard_map/pallas_call | solution.py:121
  85.0 3.4 %collective-permute-start.15 = (bf16[256,768]{1,0:T(8,128)(2,1)S(1)}, bf16[256,768]{1,0:T(8,128)(2,1)S(1)}, u32[]{:S(2)}, u32[]{:S(2)}) collective-permute-start(bf16[256,768]{1,0:T(8,128)(2,1)S(1)} %collective-permute-done.7.o1), channel_id=1, source_target_pairs={{0,8},{1,9},{2,10},{3,11},{4,12},{5,13},{6,14},{7,15},{8,0},{9,1},... | collective-permute-start | bytes 1179656 | tf_op jit(solution)/shard_map/ppermute | solution.py:68
  88.4 4.4 %collective-permute-done.14.refs_1_ = bf16[96,5120]{1,0:T(8,128)(2,1)S(1)} collective-permute-done((bf16[96,5120]{1,0:T(8,128)(2,1)S(1)}, bf16[96,5120]{1,0:T(8,128)(2,1)S(1)}, u32[]{:S(2)}, u32[]{:S(2)}) %collective-permute-start.14) | collective-permute-done | bytes 983072 | tf_op jit(solution)/shard_map/ppermute | solution.py:68
  92.8 4.1 %collective-permute-start.16 = (bf16[256,768]{1,0:T(8,128)(2,1)}, bf16[256,768]{1,0:T(8,128)(2,1)S(1)}, u32[]{:S(2)}, u32[]{:S(2)}) collective-permute-start(bf16[256,768]{1,0:T(8,128)(2,1)} %get-tuple-element.113.o2), channel_id=1, source_target_pairs={{0,8},{1,9},{2,10},{3,11},{4,12},{5,13},{6,14},{7,15},{8,0},{9,1},... | collective-permute-start | bytes 1179656 | tf_op jit(solution)/shard_map/ppermute | solution.py:68
  98.9 3.7 %shard_map.108 = (bf16[4,256,5120]{2,1,0:T(8,128)(2,1)S(1)}, bf16[4,256,384]{2,1,0:T(8,128)(2,1)S(1)}, bf16[4,256,640]{2,1,0:T(8,128)(2,1)S(1)}, bf16[4,256,640]{2,1,0:T(8,128)(2,1)S(1)}) custom-call(s32[24]{0:T(128)S(1)} %dynamic-slice_bitcast_fusion.1.meta, ...), custom_call_target="tpu_custom_call", output_to_operand_aliasing={{0}: (5, {}), {1}: (6, {}), {2}: (7, {}), {3}: (8, {})} | custom-call | tf_op jit(solution)/shard_map/pallas_call | solution.py:121
  104.9 4.3 %collective-permute-done.11.t2 = bf16[2,256,768]{2,1,0:T(8,128)(2,1)S(1)} collective-permute-done((bf16[2,256,768]{2,1,0:T(8,128)(2,1)}, bf16[2,256,768]{2,1,0:T(8,128)(2,1)S(1)}, u32[]{:S(2)}, u32[]{:S(2)}) %collective-permute-start.11) | collective-permute-done | bytes 786464 | tf_op jit(solution)/shard_map/ppermute | solution.py:68
  109.4 5.7 %shard_map.109 = bf16[1024,384]{1,0:T(8,128)(2,1)S(1)} custom-call(bf16[1024,5120]{1,0:T(8,128)(2,1)S(1)} %bitcast.23, bf16[5120,384]{1,0:T(8,128)(2,1)S(1)} %collective-permute-done.12.w_ref), custom_call_target="tpu_custom_call" | custom-call | tf_op jit(solution)/shard_map/pallas_call | solution.py:145
  115.2 7.1 %shard_map.111.c0 = bf16[512,768]{1,0:T(8,128)(2,1)S(1)} custom-call(s32[24]{0:T(128)S(1)} %dynamic-slice_bitcast_fusion.1.meta, bf16[4,256,384]{2,1,0:T(8,128)(2,1)S(1)} %get-tuple-element.123.q_own, bf16[4,256,384]{2,1,0:T(8,128)(2,1)S(1)} %bitcast.29, s32[8,1,256]{2,1,0:T(1,128)S(1)} %bitcast.34, bf16[2,256,768]{2,1,0:T(8,128)(2,1)} %get-tuple-element.126.own0, ...), custom_call_target="tpu_custom_call" | custom-call | flops 1207959552 | bytes 8388608 | tf_op jit(solution)/shard_map/pallas_call | solution.py:262
  124.7 7.1 %shard_map.110.c0 = bf16[512,768]{1,0:T(8,128)(2,1)S(1)} custom-call(s32[24]{0:T(128)S(1)} %dynamic-slice_bitcast_fusion.1.meta, bf16[4,256,384]{2,1,0:T(8,128)(2,1)S(1)} %get-tuple-element.123.q_own, bf16[4,256,384]{2,1,0:T(8,128)(2,1)S(1)} %bitcast.30, s32[8,1,256]{2,1,0:T(1,128)S(1)} %bitcast.35, bf16[2,256,768]{2,1,0:T(8,128)(2,1)} %get-tuple-element.126.own0, ...), custom_call_target="tpu_custom_call" | custom-call | flops 1207959552 | bytes 8388608 | tf_op jit(solution)/shard_map/pallas_call | solution.py:262
  133.0 6.8 %collective-permute-done.20.c1 = bf16[512,768]{1,0:T(8,128)(2,1)S(1)} collective-permute-done((bf16[512,768]{1,0:T(8,128)(2,1)S(1)}, bf16[512,768]{1,0:T(8,128)(2,1)S(1)}, u32[]{:S(2)}, u32[]{:S(2)}) %collective-permute-start.20) | collective-permute-done | bytes 786464 | tf_op jit(solution)/shard_map/ppermute | solution.py:68
  139.8 3.1 %collective-permute-done.21.c3 = bf16[512,768]{1,0:T(8,128)(2,1)S(1)} collective-permute-done((bf16[512,768]{1,0:T(8,128)(2,1)S(1)}, bf16[512,768]{1,0:T(8,128)(2,1)S(1)}, u32[]{:S(2)}, u32[]{:S(2)}) %collective-permute-start.21) | collective-permute-done | bytes 786464 | tf_op jit(solution)/shard_map/ppermute | solution.py:68
  145.7 10.9 %collective-permute-done.18.c1 = bf16[512,768]{1,0:T(8,128)(2,1)S(1)} collective-permute-done((bf16[512,768]{1,0:T(8,128)(2,1)S(1)}, bf16[512,768]{1,0:T(8,128)(2,1)S(1)}, u32[]{:S(2)}, u32[]{:S(2)}) %collective-permute-start.18) | collective-permute-done | bytes 786464 | tf_op jit(solution)/shard_map/ppermute | solution.py:68
  156.6 3.1 %collective-permute-done.19.c3 = bf16[512,768]{1,0:T(8,128)(2,1)S(1)} collective-permute-done((bf16[512,768]{1,0:T(8,128)(2,1)S(1)}, bf16[512,768]{1,0:T(8,128)(2,1)S(1)}, u32[]{:S(2)}, u32[]{:S(2)}) %collective-permute-start.19) | collective-permute-done | bytes 786464 | tf_op jit(solution)/shard_map/ppermute | solution.py:68
  159.7 6.3 %collective-permute-done.22.c2b = bf16[192,768]{1,0:T(8,128)(2,1)S(1)} collective-permute-done((bf16[192,768]{1,0:T(8,128)(2,1)S(1)}, bf16[192,768]{1,0:T(8,128)(2,1)S(1)}, u32[]{:S(2)}, u32[]{:S(2)}) %collective-permute-start.22) | collective-permute-done | bytes 294944 | tf_op jit(solution)/shard_map/ppermute | solution.py:68
  168.9 7.4 %collective-permute-done.25.w = bf16[3072,640]{1,0:T(8,128)(2,1)S(1)} collective-permute-done((bf16[3072,640]{1,0:T(8,128)(2,1)S(1)}, bf16[3072,640]{1,0:T(8,128)(2,1)S(1)}, u32[]{:S(2)}, u32[]{:S(2)}) %collective-permute-start.25) | collective-permute-done | bytes 3932192 | tf_op jit(solution)/shard_map/ppermute | solution.py:68
  176.3 3.4 %shard_map.113 = bf16[2,256,640]{2,1,0:T(8,128)(2,1)S(1)} custom-call(s32[24]{0:T(128)S(1)} %dynamic-slice_bitcast_fusion.1.meta, bf16[512,768]{1,0:T(8,128)(2,1)S(1)} %shard_map.111.c0, bf16[512,768]{1,0:T(8,128)(2,1)S(1)} %collective-permute-done.20.c1, bf16[320,768]{1,0:T(8,128)(2,1)S(1)} %collective-permute-done.27.c2a, ...), custom_call_target="tpu_custom_call" | custom-call | flops 2013265920 | bytes 8388608 | tf_op jit(solution)/shard_map/pallas_call | solution.py:334
  179.7 3.4 %shard_map.112 = bf16[2,256,640]{2,1,0:T(8,128)(2,1)S(1)} custom-call(s32[24]{0:T(128)S(1)} %dynamic-slice_bitcast_fusion.1.meta, bf16[512,768]{1,0:T(8,128)(2,1)S(1)} %shard_map.110.c0, bf16[512,768]{1,0:T(8,128)(2,1)S(1)} %collective-permute-done.18.c1, bf16[320,768]{1,0:T(8,128)(2,1)S(1)} %collective-permute-done.23.c2a, ...), custom_call_target="tpu_custom_call" | custom-call | flops 2013265920 | bytes 8388608 | tf_op jit(solution)/shard_map/pallas_call | solution.py:334
  183.1 5.4 %collective-permute-start.26 = (bf16[2,256,640]{2,1,0:T(8,128)(2,1)S(1)}, bf16[2,256,640]{2,1,0:T(8,128)(2,1)S(1)}, u32[]{:S(2)}, u32[]{:S(2)}) collective-permute-start(bf16[2,256,640]{2,1,0:T(8,128)(2,1)S(1)} %shard_map.112), channel_id=1, source_target_pairs={{0,4},{1,5},{2,6},{3,7},{4,0},{5,1},{6,2},{7,3},{8,11},{9,10},{10,... | collective-permute-start | bytes 1966088 | tf_op jit(solution)/shard_map/ppermute | solution.py:68
  188.5 4.1 %shard_map.114.refs_0_ = bf16[8,256,640]{2,1,0:T(8,128)(2,1)} custom-call(s32[24]{0:T(128)S(1)} %dynamic-slice_bitcast_fusion.1.meta, bf16[512,768]{1,0:T(8,128)(2,1)S(1)} %shard_map.111.c0, bf16[512,768]{1,0:T(8,128)(2,1)S(1)} %collective-permute-done.20.c1, bf16[320,768]{1,0:T(8,128)(2,1)S(1)} %collective-permute-done.27.c2a, ...), custom_call_target="tpu_custom_call" | custom-call | flops 2013265920 | bytes 8388608 | tf_op jit(solution)/shard_map/pallas_call | solution.py:334
  192.6 4.1 %shard_map.115.prior = bf16[8,256,640]{2,1,0:T(8,128)(2,1)} custom-call(s32[24]{0:T(128)S(1)} %dynamic-slice_bitcast_fusion.1.meta, bf16[512,768]{1,0:T(8,128)(2,1)S(1)} %shard_map.110.c0, bf16[512,768]{1,0:T(8,128)(2,1)S(1)} %collective-permute-done.18.c1, bf16[320,768]{1,0:T(8,128)(2,1)S(1)} %collective-permute-done.23.c2a, ...), custom_call_target="tpu_custom_call", output_to_operand_aliasing={{}: (8, {})} | custom-call | flops 2013265920 | bytes 8388608 | tf_op jit(solution)/shard_map/pallas_call | solution.py:334
  (79 shorter events, 44.7 us)
Async XLA Ops:
  0.0 63.3 %collective-permute-start.5 = (bf16[256,5120]{1,0:T(8,128)(2,1)}, bf16[256,5120]{1,0:T(8,128)(2,1)}, u32[]{:S(2)}, u32[]{:S(2)}) collective-permute-start(bf16[256,5120]{1,0:T(8,128)(2,1)} %bitcast.31), channel_id=1, source_target_pairs={{0,1},{1,0},{2,3},{3,2},{4,5},{5,4},{6,7},{7,6},{8,9},{9,8},{10,11... | collective-permute-start | bytes 7864328 | tf_op jit(solution)/shard_map/ppermute | solution.py:68
  2.5 60.8 %collective-permute-start.6 = (bf16[256,5120]{1,0:T(8,128)(2,1)}, bf16[256,5120]{1,0:T(8,128)(2,1)S(1)}, u32[]{:S(2)}, u32[]{:S(2)}) collective-permute-start(bf16[256,5120]{1,0:T(8,128)(2,1)} %bitcast.32), channel_id=1, source_target_pairs={{0,3},{1,2},{2,1},{3,0},{4,7},{5,6},{6,5},{7,4},{8,12},{9,13},{10,... | collective-permute-start | bytes 7864328 | tf_op jit(solution)/shard_map/ppermute | solution.py:68
  11.2 3.3 %collective-permute-start = (bf16[128,768]{1,0:T(8,128)(2,1)S(1)}, bf16[128,768]{1,0:T(8,128)(2,1)S(1)}, u32[]{:S(2)}, u32[]{:S(2)}) collective-permute-start(bf16[128,768]{1,0:T(8,128)(2,1)S(1)} %get-tuple-element.193), channel_id=1, source_target_pairs={{0,8},{1,9},{2,10},{3,11},{4,12},{5,13},{6,14},{7,15},{8,0},{9,1},... | collective-permute-start | bytes 589832 | tf_op jit(solution)/shard_map/cond/branch_1_fun/ppermute | solution.py:68
  14.6 7.8 %collective-permute-start.1 = (bf16[2,128,768]{2,1,0:T(8,128)(2,1)S(1)}, bf16[2,128,768]{2,1,0:T(8,128)(2,1)S(1)}, u32[]{:S(2)}, u32[]{:S(2)}) collective-permute-start(bf16[2,128,768]{2,1,0:T(8,128)(2,1)S(1)} %maximum_select_fusion.2), channel_id=1, source_target_pairs={{0,64},{1,65},{2,66},{3,67},{4,68},{5,69},{6,70},{7,71},{16,80},{1... | collective-permute-start | bytes 1179656 | tf_op jit(solution)/shard_map/cond/branch_1_fun/ppermute | solution.py:68
  22.3 9.5 %collective-permute-start.2 = (bf16[2,128,768]{2,1,0:T(8,128)(2,1)S(1)}, bf16[2,128,768]{2,1,0:T(8,128)(2,1)}, u32[]{:S(2)}, u32[]{:S(2)}) collective-permute-start(bf16[2,128,768]{2,1,0:T(8,128)(2,1)S(1)} %collective-permute-done.1), channel_id=1, source_target_pairs={{0,8},{1,9},{2,10},{3,11},{4,12},{5,13},{6,14},{7,15},{8,0},{9,1},... | collective-permute-start | bytes 1179656 | tf_op jit(solution)/shard_map/cond/branch_1_fun/ppermute | solution.py:68
  33.9 14.2 %collective-permute-start.4 = (bf16[2,256,768]{2,1,0:T(8,128)(2,1)}, bf16[2,256,768]{2,1,0:T(8,128)(2,1)}, u32[]{:S(2)}, u32[]{:S(2)}) collective-permute-start(bf16[2,256,768]{2,1,0:T(8,128)(2,1)} %maximum_select_fusion), channel_id=1, source_target_pairs={{0,4},{1,5},{2,6},{3,7},{4,0},{5,1},{6,2},{7,3},{8,11},{9,10},{10,... | collective-permute-start | bytes 2359304 | tf_op jit(solution)/shard_map/cond/branch_1_fun/ppermute | solution.py:68
  36.1 12.0 %collective-permute-start.3 = (bf16[256,768]{1,0:T(8,128)(2,1)}, bf16[256,768]{1,0:T(8,128)(2,1)}, u32[]{:S(2)}, u32[]{:S(2)}) collective-permute-start(bf16[256,768]{1,0:T(8,128)(2,1)} %dynamic-slice_bitcast_fusion), channel_id=1, source_target_pairs={{0,32},{1,33},{2,34},{3,35},{4,36},{5,37},{6,38},{7,39},{8,40},{9,... | collective-permute-start | bytes 1179656 | tf_op jit(solution)/shard_map/cond/branch_1_fun/ppermute | solution.py:68
  48.1 56.8 %collective-permute-start.12 = (bf16[5120,384]{1,0:T(8,128)(2,1)}, bf16[5120,384]{1,0:T(8,128)(2,1)S(1)}, u32[]{:S(2)}, u32[]{:S(2)}) collective-permute-start(bf16[5120,384]{1,0:T(8,128)(2,1)} %bitcast.24), channel_id=1, source_target_pairs={{0,4},{1,5},{2,6},{3,7},{4,0},{5,1},{6,2},{7,3},{8,11},{9,10},{10,... | collective-permute-start | bytes 11796488 | tf_op jit(solution)/shard_map/ppermute | solution.py:68
  50.2 20.2 %copy-start = (bf16[1,5120,384]{2,1,0:T(8,128)(2,1)S(1)}, bf16[1,5120,384]{2,1,0:T(8,128)(2,1)}, u32[]{:S(2)}) copy-start(bf16[1,5120,384]{2,1,0:T(8,128)(2,1)} %param.18) | copy-start | bytes 11796484
  50.2 20.2 %copy-start.2 = (f32[1,5120]{1,0:T(1,128)S(1)}, f32[1,5120]{1,0:T(1,128)}, u32[]{:S(2)}) copy-start(f32[1,5120]{1,0:T(1,128)} %refs_2_.1) | copy-start | bytes 61444
  50.2 10.0 %collective-permute-start.7 = (bf16[256,768]{1,0:T(8,128)(2,1)}, bf16[256,768]{1,0:T(8,128)(2,1)S(1)}, u32[]{:S(2)}, u32[]{:S(2)}) collective-permute-start(bf16[256,768]{1,0:T(8,128)(2,1)} %get-tuple-element.88), channel_id=1, source_target_pairs={{0,48},{1,49},{2,50},{3,51},{4,52},{5,53},{6,54},{7,55},{8,56},{9,... | collective-permute-start | bytes 1179656 | tf_op jit(solution)/shard_map/ppermute | solution.py:68
  52.7 10.6 %collective-permute-start.8 = (bf16[256,768]{1,0:T(8,128)(2,1)}, bf16[256,768]{1,0:T(8,128)(2,1)S(1)}, u32[]{:S(2)}, u32[]{:S(2)}) collective-permute-start(bf16[256,768]{1,0:T(8,128)(2,1)} %get-tuple-element.88), channel_id=1, source_target_pairs={{0,16},{1,17},{2,18},{3,19},{4,20},{5,21},{6,22},{7,23},{8,24},{9,... | collective-permute-start | bytes 1179656 | tf_op jit(solution)/shard_map/ppermute | solution.py:68
  63.4 35.5 %collective-permute-start.13 = (bf16[160,5120]{1,0:T(8,128)(2,1)S(1)}, bf16[160,5120]{1,0:T(8,128)(2,1)S(1)}, u32[]{:S(2)}, u32[]{:S(2)}) collective-permute-start(bf16[160,5120]{1,0:T(8,128)(2,1)S(1)} %slice.18), channel_id=1, source_target_pairs={{0,1},{1,0},{2,3},{3,2},{4,5},{5,4},{6,7},{7,6},{8,9},{9,8},{10,11... | collective-permute-start | bytes 4915208 | tf_op jit(solution)/shard_map/ppermute | solution.py:68
  63.5 21.4 %collective-permute-start.10 = (bf16[2,256,768]{2,1,0:T(8,128)(2,1)}, bf16[2,256,768]{2,1,0:T(8,128)(2,1)S(1)}, u32[]{:S(2)}, u32[]{:S(2)}) collective-permute-start(bf16[2,256,768]{2,1,0:T(8,128)(2,1)} %get-tuple-element.105.other0), channel_id=1, source_target_pairs={{0,16},{1,17},{2,18},{3,19},{4,20},{5,21},{6,22},{7,23},{8,24},{9,... | collective-permute-start | bytes 2359304 | tf_op jit(solution)/shard_map/ppermute | solution.py:68
  63.6 21.3 %collective-permute-start.9 = (bf16[2,256,768]{2,1,0:T(8,128)(2,1)}, bf16[2,256,768]{2,1,0:T(8,128)(2,1)S(1)}, u32[]{:S(2)}, u32[]{:S(2)}) collective-permute-start(bf16[2,256,768]{2,1,0:T(8,128)(2,1)} %get-tuple-element.105.other0), channel_id=1, source_target_pairs={{0,48},{1,49},{2,50},{3,51},{4,52},{5,53},{6,54},{7,55},{8,56},{9,... | collective-permute-start | bytes 2359304 | tf_op jit(solution)/shard_map/ppermute | solution.py:68
  67.5 25.2 %collective-permute-start.14 = (bf16[96,5120]{1,0:T(8,128)(2,1)S(1)}, bf16[96,5120]{1,0:T(8,128)(2,1)S(1)}, u32[]{:S(2)}, u32[]{:S(2)}) collective-permute-start(bf16[96,5120]{1,0:T(8,128)(2,1)S(1)} %slice.19), channel_id=1, source_target_pairs={{0,3},{1,2},{2,1},{3,0},{4,7},{5,6},{6,5},{7,4},{8,12},{9,13},{10,... | collective-permute-start | bytes 2949128 | tf_op jit(solution)/shard_map/ppermute | solution.py:68
  85.0 24.2 %copy-start.6 = (bf16[3072,640]{1,0:T(8,128)(2,1)S(1)}, bf16[3072,640]{1,0:T(8,128)(2,1)}, u32[]{:S(2)}) copy-start(bf16[3072,640]{1,0:T(8,128)(2,1)} %copy-done.5) | copy-start | bytes 11796484
  85.0 11.9 %collective-permute-start.15 = (bf16[256,768]{1,0:T(8,128)(2,1)S(1)}, bf16[256,768]{1,0:T(8,128)(2,1)S(1)}, u32[]{:S(2)}, u32[]{:S(2)}) collective-permute-start(bf16[256,768]{1,0:T(8,128)(2,1)S(1)} %collective-permute-done.7.o1), channel_id=1, source_target_pairs={{0,8},{1,9},{2,10},{3,11},{4,12},{5,13},{6,14},{7,15},{8,0},{9,1},... | collective-permute-start | bytes 1179656 | tf_op jit(solution)/shard_map/ppermute | solution.py:68
  88.4 20.8 %collective-permute-start.11 = (bf16[2,256,768]{2,1,0:T(8,128)(2,1)}, bf16[2,256,768]{2,1,0:T(8,128)(2,1)S(1)}, u32[]{:S(2)}, u32[]{:S(2)}) collective-permute-start(bf16[2,256,768]{2,1,0:T(8,128)(2,1)} %get-tuple-element.105.other0), channel_id=1, source_target_pairs={{0,32},{1,33},{2,34},{3,35},{4,36},{5,37},{6,38},{7,39},{8,40},{9,... | collective-permute-start | bytes 2359304 | tf_op jit(solution)/shard_map/ppermute | solution.py:68
  92.8 6.1 %collective-permute-start.16 = (bf16[256,768]{1,0:T(8,128)(2,1)}, bf16[256,768]{1,0:T(8,128)(2,1)S(1)}, u32[]{:S(2)}, u32[]{:S(2)}) collective-permute-start(bf16[256,768]{1,0:T(8,128)(2,1)} %get-tuple-element.113.o2), channel_id=1, source_target_pairs={{0,8},{1,9},{2,10},{3,11},{4,12},{5,13},{6,14},{7,15},{8,0},{9,1},... | collective-permute-start | bytes 1179656 | tf_op jit(solution)/shard_map/ppermute | solution.py:68
  96.9 2.0 %collective-permute-start.17 = (bf16[256,768]{1,0:T(8,128)(2,1)S(1)}, bf16[256,768]{1,0:T(8,128)(2,1)S(1)}, u32[]{:S(2)}, u32[]{:S(2)}) collective-permute-start(bf16[256,768]{1,0:T(8,128)(2,1)S(1)} %collective-permute-done.8.o3), channel_id=1, source_target_pairs={{0,8},{1,9},{2,10},{3,11},{4,12},{5,13},{6,14},{7,15},{8,0},{9,1},... | collective-permute-start | bytes 1179656 | tf_op jit(solution)/shard_map/ppermute | solution.py:68
  109.2 67.1 %collective-permute-start.25 = (bf16[3072,640]{1,0:T(8,128)(2,1)S(1)}, bf16[3072,640]{1,0:T(8,128)(2,1)S(1)}, u32[]{:S(2)}, u32[]{:S(2)}) collective-permute-start(bf16[3072,640]{1,0:T(8,128)(2,1)S(1)} %copy-done.6), channel_id=1, source_target_pairs={{0,4},{1,5},{2,6},{3,7},{4,0},{5,1},{6,2},{7,3},{8,11},{9,10},{10,... | collective-permute-start | bytes 11796488 | tf_op jit(solution)/shard_map/ppermute | solution.py:68
  122.3 17.5 %collective-permute-start.20 = (bf16[512,768]{1,0:T(8,128)(2,1)S(1)}, bf16[512,768]{1,0:T(8,128)(2,1)S(1)}, u32[]{:S(2)}, u32[]{:S(2)}) collective-permute-start(bf16[512,768]{1,0:T(8,128)(2,1)S(1)} %shard_map.111.c0), channel_id=1, source_target_pairs={{0,1},{1,0},{2,3},{3,2},{4,5},{5,4},{6,7},{7,6},{8,9},{9,8},{10,11... | collective-permute-start | bytes 2359304 | tf_op jit(solution)/shard_map/ppermute | solution.py:68
  122.8 20.0 %collective-permute-start.21 = (bf16[512,768]{1,0:T(8,128)(2,1)S(1)}, bf16[512,768]{1,0:T(8,128)(2,1)S(1)}, u32[]{:S(2)}, u32[]{:S(2)}) collective-permute-start(bf16[512,768]{1,0:T(8,128)(2,1)S(1)} %shard_map.111.c0), channel_id=1, source_target_pairs={{0,3},{1,2},{2,1},{3,0},{4,7},{5,6},{6,5},{7,4},{8,12},{9,13},{10,... | collective-permute-start | bytes 2359304 | tf_op jit(solution)/shard_map/ppermute | solution.py:68
  131.8 24.8 %collective-permute-start.18 = (bf16[512,768]{1,0:T(8,128)(2,1)S(1)}, bf16[512,768]{1,0:T(8,128)(2,1)S(1)}, u32[]{:S(2)}, u32[]{:S(2)}) collective-permute-start(bf16[512,768]{1,0:T(8,128)(2,1)S(1)} %shard_map.110.c0), channel_id=1, source_target_pairs={{0,1},{1,0},{2,3},{3,2},{4,5},{5,4},{6,7},{7,6},{8,9},{9,8},{10,11... | collective-permute-start | bytes 2359304 | tf_op jit(solution)/shard_map/ppermute | solution.py:68
  133.0 26.7 %collective-permute-start.19 = (bf16[512,768]{1,0:T(8,128)(2,1)S(1)}, bf16[512,768]{1,0:T(8,128)(2,1)S(1)}, u32[]{:S(2)}, u32[]{:S(2)}) collective-permute-start(bf16[512,768]{1,0:T(8,128)(2,1)S(1)} %shard_map.110.c0), channel_id=1, source_target_pairs={{0,3},{1,2},{2,1},{3,0},{4,7},{5,6},{6,5},{7,4},{8,12},{9,13},{10,... | collective-permute-start | bytes 2359304 | tf_op jit(solution)/shard_map/ppermute | solution.py:68
  142.9 23.1 %collective-permute-start.22 = (bf16[192,768]{1,0:T(8,128)(2,1)S(1)}, bf16[192,768]{1,0:T(8,128)(2,1)S(1)}, u32[]{:S(2)}, u32[]{:S(2)}) collective-permute-start(bf16[192,768]{1,0:T(8,128)(2,1)S(1)} %slice.20), channel_id=1, source_target_pairs={{0,3},{1,2},{2,1},{3,0},{4,7},{5,6},{6,5},{7,4},{8,12},{9,13},{10,... | collective-permute-start | bytes 884744 | tf_op jit(solution)/shard_map/ppermute | solution.py:68
  144.5 24.4 %collective-permute-start.27 = (bf16[320,768]{1,0:T(8,128)(2,1)S(1)}, bf16[320,768]{1,0:T(8,128)(2,1)S(1)}, u32[]{:S(2)}, u32[]{:S(2)}) collective-permute-start(bf16[320,768]{1,0:T(8,128)(2,1)S(1)} %slice.23), channel_id=1, source_target_pairs={{0,1},{1,0},{2,3},{3,2},{4,5},{5,4},{6,7},{7,6},{8,9},{9,8},{10,11... | collective-permute-start | bytes 1474568 | tf_op jit(solution)/shard_map/ppermute | solution.py:68
  166.1 13.7 %collective-permute-start.23 = (bf16[320,768]{1,0:T(8,128)(2,1)S(1)}, bf16[320,768]{1,0:T(8,128)(2,1)S(1)}, u32[]{:S(2)}, u32[]{:S(2)}) collective-permute-start(bf16[320,768]{1,0:T(8,128)(2,1)S(1)} %slice.21), channel_id=1, source_target_pairs={{0,1},{1,0},{2,3},{3,2},{4,5},{5,4},{6,7},{7,6},{8,9},{9,8},{10,11... | collective-permute-start | bytes 1474568 | tf_op jit(solution)/shard_map/ppermute | solution.py:68
  167.3 12.4 %collective-permute-start.24 = (bf16[192,768]{1,0:T(8,128)(2,1)S(1)}, bf16[192,768]{1,0:T(8,128)(2,1)S(1)}, u32[]{:S(2)}, u32[]{:S(2)}) collective-permute-start(bf16[192,768]{1,0:T(8,128)(2,1)S(1)} %slice.22), channel_id=1, source_target_pairs={{0,3},{1,2},{2,1},{3,0},{4,7},{5,6},{6,5},{7,4},{8,12},{9,13},{10,... | collective-permute-start | bytes 884744 | tf_op jit(solution)/shard_map/ppermute | solution.py:68
  179.6 17.1 %collective-permute-start.28 = (bf16[2,256,640]{2,1,0:T(8,128)(2,1)S(1)}, bf16[2,256,640]{2,1,0:T(8,128)(2,1)S(1)}, u32[]{:S(2)}, u32[]{:S(2)}) collective-permute-start(bf16[2,256,640]{2,1,0:T(8,128)(2,1)S(1)} %shard_map.113), channel_id=1, source_target_pairs={{0,4},{1,5},{2,6},{3,7},{4,0},{5,1},{6,2},{7,3},{8,11},{9,10},{10,... | collective-permute-start | bytes 1966088 | tf_op jit(solution)/shard_map/ppermute | solution.py:68
  183.1 15.0 %collective-permute-start.26 = (bf16[2,256,640]{2,1,0:T(8,128)(2,1)S(1)}, bf16[2,256,640]{2,1,0:T(8,128)(2,1)S(1)}, u32[]{:S(2)}, u32[]{:S(2)}) collective-permute-start(bf16[2,256,640]{2,1,0:T(8,128)(2,1)S(1)} %shard_map.112), channel_id=1, source_target_pairs={{0,4},{1,5},{2,6},{3,7},{4,0},{5,1},{6,2},{7,3},{8,11},{9,10},{10,... | collective-permute-start | bytes 1966088 | tf_op jit(solution)/shard_map/ppermute | solution.py:68
  (7 other events, 30.3 us)

commit v14 on v13

--- a/solution.py
+++ b/solution.py
@@ -437,9 +437,9 @@
     t3 = send(piece2, X_NEXT)
     state = project(meta, [after(x0, x_in, x_out)], query_gain, w_q, 0, width)
     state = project(meta, [x_in], query_gain, w_q, 1, width, state)
-    state = project(meta, [x_out], query_gain, w_q, 3, width, state)
     t1, t3, piece2, *state = lax.optimization_barrier((t1, t3, piece2, *state))
     t2 = send(piece2, X_FAR)
+    state = project(meta, [x_out], query_gain, w_q, 3, width, state)
     o1, o2, o3, t1 = lax.optimization_barrier((o1, o2, o3, t1))
     o1b = send(o1, CORE)
     o2b = send(o2, CORE)

time: 201 us -> 199 us (0.990)
  waiting for transfers between devices: 67.7 us -> 61.3 us
  starting transfers between devices: 50.6 us -> 54.4 us
    ppermute x29, waiting for transfers between devices: 67.7 us -> 61.3 us  [send(): return lax.ppermute(value, AXES, pairs)]
    ppermute x29, starting transfers between devices: 50.6 us -> 54.4 us  [send(): return lax.ppermute(value, AXES, pairs)]
  transfers between devices with their start and end apart: 29 -> 29, of which waited for: 15 -> 16; matrix products, arithmetic and copies ran while one was open for 6% -> 6% of each run, Pallas kernels for 33% -> 33%
where the time goes in v14:
time: 199 us; the launch traced here: 197 us
  Pallas kernels  66.3 us (33%)
  waiting for transfers between devices  61.3 us (31%)
  starting transfers between devices  54.4 us (27%)
  local copies, waits for them, and re-layouts  6.22 us (3%)
  matrix products  4.48 us (2%)
  other arithmetic  3.84 us (2%)
    ppermute x29, waiting for transfers between devices, send(): return lax.ppermute(value, AXES, pairs)  61.3 us
    ppermute x29, starting transfers between devices, send(): return lax.ppermute(value, AXES, pairs)  54.4 us
    pallas_call x4, Pallas kernels, project(): pl.pallas_call(kernel, grid_spec=pltpu.PrefetchScalarGridSpec(num_scalar_...  16.5 us
    pallas_call x4, Pallas kernels, finish(): pl.pallas_call(finish_kernel, grid_spec=pltpu.PrefetchScalarGridSpec(num_...  14.9 us
    pallas_call x2, Pallas kernels, attend(): pl.pallas_call(functools.partial(attend_kernel, chunk), grid_spec=pltpu.P...  14.2 us
    pallas_call x2, Pallas kernels, reorder(): pl.pallas_call(reorder_kernel, grid_spec=pltpu.PrefetchScalarGridSpec(num...  12.2 us
    pallas_call x1, Pallas kernels, more_queries(): pl.pallas_call(more_queries_kernel, grid=(2,), in_specs=[pl.BlockSpec((ro...  5.74 us
  transfers between devices with their start and end apart: 29, of which 16 were waited for; matrix products, arithmetic and copies ran while one was open for 6% of the time, Pallas kernels for 33%

profile of v14, /device:TPU:1, one launch (start us, length us, event | category | flops | bytes accessed | tf_op | source)
XLA Modules:
  0.0 197.0 jit_solution(5224822963817644190)
XLA Ops:
  4.5 43.7 %conditional.1 = (bf16[2,256,768]{2,1,0:T(8,128)(2,1)}, bf16[256,768]{1,0:T(8,128)(2,1)}, bf16[256,768]{1,0:T(8,128)(2,1)}, bf16[2,256,768]{2,1,0:T(8,128)(2,1)}...) conditional(s32[]{:T(128)} %convert_element_type.15, () %tuple.24, (s32[]{:T(128)}, pred[]{:T(512)}, ...), branch_computations={%region_0.1_spmd, %region_1.3_spmd} | conditional | flops 1016889472 | bytes 47639592 | solution.py:424
  6.2 3.6 %convolution_convert_fusion = bf16[128,384]{1,0:T(8,128)(2,1)S(1)} fusion(bf16[5120,384]{1,0:T(8,128)(2,1)} %get-tuple-element.165, bf16[128,5120]{1,0:T(8,128)(2,1)} %get-tuple-element.162, f32[5120]{0:T(1024)} %get-tuple-element.163, f32[128]{0:T(128)S(1)} %add_rsqrt_fusion), kind=kOutput, calls=%fused_computation.5 | convolution fusion | flops 505987072 | bytes 5362176 | tf_op jit(solution)/shard_map/cond/branch_1_fun/dot_general | solution.py:404
  15.3 7.1 %branch_1_fun.2 = bf16[8,384,640]{2,1,0:T(8,128)(2,1)} custom-call(s32[24]{0:T(128)S(1)} %get-tuple-element.27.meta, bf16[8,384,640]{2,1,0:T(8,128)(2,1)} %bitcast.37), custom_call_target="tpu_custom_call" | custom-call | tf_op jit(solution)/shard_map/cond/branch_1_fun/pallas_call | solution.py:290
  22.3 8.1 %collective-permute-start.2 = (bf16[2,128,768]{2,1,0:T(8,128)(2,1)S(1)}, bf16[2,128,768]{2,1,0:T(8,128)(2,1)}, u32[]{:S(2)}, u32[]{:S(2)}) collective-permute-start(bf16[2,128,768]{2,1,0:T(8,128)(2,1)S(1)} %collective-permute-done.1), channel_id=1, source_target_pairs={{0,8},{1,9},{2,10},{3,11},{4,12},{5,13},{6,14},{7,15},{8,0},{9,1},... | collective-permute-start | bytes 1179656 | tf_op jit(solution)/shard_map/cond/branch_1_fun/ppermute | solution.py:68
  36.1 2.7 %collective-permute-start.3 = (bf16[256,768]{1,0:T(8,128)(2,1)}, bf16[256,768]{1,0:T(8,128)(2,1)}, u32[]{:S(2)}, u32[]{:S(2)}) collective-permute-start(bf16[256,768]{1,0:T(8,128)(2,1)} %dynamic-slice_bitcast_fusion), channel_id=1, source_target_pairs={{0,32},{1,33},{2,34},{3,35},{4,36},{5,37},{6,38},{7,39},{8,40},{9,... | collective-permute-start | bytes 1179656 | tf_op jit(solution)/shard_map/cond/branch_1_fun/ppermute | solution.py:68
  38.9 5.2 %branch_1_fun.3 = bf16[8,384,640]{2,1,0:T(8,128)(2,1)S(1)} custom-call(s32[24]{0:T(128)S(1)} %get-tuple-element.27.meta, bf16[8,384,640]{2,1,0:T(8,128)(2,1)} %bitcast.38), custom_call_target="tpu_custom_call" | custom-call | tf_op jit(solution)/shard_map/cond/branch_1_fun/pallas_call | solution.py:290
  44.1 4.1 %collective-permute-done.3 = bf16[256,768]{1,0:T(8,128)(2,1)} collective-permute-done((bf16[256,768]{1,0:T(8,128)(2,1)}, bf16[256,768]{1,0:T(8,128)(2,1)}, u32[]{:S(2)}, u32[]{:S(2)}) %collective-permute-start.3) | collective-permute-done | bytes 393248 | tf_op jit(solution)/shard_map/cond/branch_1_fun/ppermute | solution.py:68
  52.7 7.6 %collective-permute-done.7.o1 = bf16[256,768]{1,0:T(8,128)(2,1)S(1)} collective-permute-done((bf16[256,768]{1,0:T(8,128)(2,1)}, bf16[256,768]{1,0:T(8,128)(2,1)S(1)}, u32[]{:S(2)}, u32[]{:S(2)}) %collective-permute-start.7) | collective-permute-done | bytes 393248 | tf_op jit(solution)/shard_map/ppermute | solution.py:68
  60.3 3.0 %collective-permute-done.8.o3 = bf16[256,768]{1,0:T(8,128)(2,1)S(1)} collective-permute-done((bf16[256,768]{1,0:T(8,128)(2,1)}, bf16[256,768]{1,0:T(8,128)(2,1)S(1)}, u32[]{:S(2)}, u32[]{:S(2)}) %collective-permute-start.8) | collective-permute-done | bytes 393248 | tf_op jit(solution)/shard_map/ppermute | solution.py:68
  63.6 2.7 %collective-permute-start.9 = (bf16[2,256,768]{2,1,0:T(8,128)(2,1)}, bf16[2,256,768]{2,1,0:T(8,128)(2,1)S(1)}, u32[]{:S(2)}, u32[]{:S(2)}) collective-permute-start(bf16[2,256,768]{2,1,0:T(8,128)(2,1)} %get-tuple-element.101.other0), channel_id=1, source_target_pairs={{0,48},{1,49},{2,50},{3,51},{4,52},{5,53},{6,54},{7,55},{8,56},{9,... | collective-permute-start | bytes 2359304 | tf_op jit(solution)/shard_map/ppermute | solution.py:68
  67.5 2.7 %collective-permute-start.14 = (bf16[96,5120]{1,0:T(8,128)(2,1)S(1)}, bf16[96,5120]{1,0:T(8,128)(2,1)S(1)}, u32[]{:S(2)}, u32[]{:S(2)}) collective-permute-start(bf16[96,5120]{1,0:T(8,128)(2,1)S(1)} %slice.19), channel_id=1, source_target_pairs={{0,3},{1,2},{2,1},{3,0},{4,7},{5,6},{6,5},{7,4},{8,12},{9,13},{10,... | collective-permute-start | bytes 2949128 | tf_op jit(solution)/shard_map/ppermute | solution.py:68
  72.0 3.7 %shard_map.105 = (bf16[4,256,5120]{2,1,0:T(8,128)(2,1)S(1)}, bf16[4,256,384]{2,1,0:T(8,128)(2,1)S(1)}, bf16[4,256,640]{2,1,0:T(8,128)(2,1)S(1)}, bf16[4,256,640]{2,1,0:T(8,128)(2,1)S(1)}) custom-call(s32[24]{0:T(128)S(1)} %dynamic-slice_bitcast_fusion.1.meta, bf16[256,5120]{1,0:T(8,128)(2,1)S(1)} %bitcast.33, f32[1,5120]{1,0:T(1,128)S(1)} %copy-done.2, ...), custom_call_target="tpu_custom_call" | custom-call | tf_op jit(solution)/shard_map/pallas_call | solution.py:121
  75.6 5.4 %shard_map.106 = (bf16[4,256,5120]{2,1,0:T(8,128)(2,1)S(1)}, bf16[4,256,384]{2,1,0:T(8,128)(2,1)S(1)}, bf16[4,256,640]{2,1,0:T(8,128)(2,1)S(1)}, bf16[4,256,640]{2,1,0:T(8,128)(2,1)S(1)}) custom-call(s32[24]{0:T(128)S(1)} %dynamic-slice_bitcast_fusion.1.meta, ...), custom_call_target="tpu_custom_call", output_to_operand_aliasing={{0}: (4, {}), {1}: (5, {}), {2}: (6, {}), {3}: (7, {})} | custom-call | tf_op jit(solution)/shard_map/pallas_call | solution.py:121
  81.5 3.5 %collective-permute-start.15 = (bf16[256,768]{1,0:T(8,128)(2,1)S(1)}, bf16[256,768]{1,0:T(8,128)(2,1)S(1)}, u32[]{:S(2)}, u32[]{:S(2)}) collective-permute-start(bf16[256,768]{1,0:T(8,128)(2,1)S(1)} %collective-permute-done.7.o1), channel_id=1, source_target_pairs={{0,8},{1,9},{2,10},{3,11},{4,12},{5,13},{6,14},{7,15},{8,0},{9,1},... | collective-permute-start | bytes 1179656 | tf_op jit(solution)/shard_map/ppermute | solution.py:68
  86.2 6.4 %collective-permute-done.14.refs_1_ = bf16[96,5120]{1,0:T(8,128)(2,1)S(1)} collective-permute-done((bf16[96,5120]{1,0:T(8,128)(2,1)S(1)}, bf16[96,5120]{1,0:T(8,128)(2,1)S(1)}, u32[]{:S(2)}, u32[]{:S(2)}) %collective-permute-start.14) | collective-permute-done | bytes 983072 | tf_op jit(solution)/shard_map/ppermute | solution.py:68
  92.6 4.1 %collective-permute-start.16 = (bf16[256,768]{1,0:T(8,128)(2,1)}, bf16[256,768]{1,0:T(8,128)(2,1)S(1)}, u32[]{:S(2)}, u32[]{:S(2)}) collective-permute-start(bf16[256,768]{1,0:T(8,128)(2,1)} %get-tuple-element.109.o2), channel_id=1, source_target_pairs={{0,8},{1,9},{2,10},{3,11},{4,12},{5,13},{6,14},{7,15},{8,0},{9,1},... | collective-permute-start | bytes 1179656 | tf_op jit(solution)/shard_map/ppermute | solution.py:68
  96.7 3.7 %shard_map.107 = (bf16[4,256,5120]{2,1,0:T(8,128)(2,1)S(1)}, bf16[4,256,384]{2,1,0:T(8,128)(2,1)S(1)}, bf16[4,256,640]{2,1,0:T(8,128)(2,1)S(1)}, bf16[4,256,640]{2,1,0:T(8,128)(2,1)S(1)}) custom-call(s32[24]{0:T(128)S(1)} %dynamic-slice_bitcast_fusion.1.meta, ...), custom_call_target="tpu_custom_call", output_to_operand_aliasing={{0}: (4, {}), {1}: (5, {}), {2}: (6, {}), {3}: (7, {})} | custom-call | tf_op jit(solution)/shard_map/pallas_call | solution.py:121
  100.4 3.7 %shard_map.108 = (bf16[4,256,5120]{2,1,0:T(8,128)(2,1)S(1)}, bf16[4,256,384]{2,1,0:T(8,128)(2,1)S(1)}, bf16[4,256,640]{2,1,0:T(8,128)(2,1)S(1)}, bf16[4,256,640]{2,1,0:T(8,128)(2,1)S(1)}) custom-call(s32[24]{0:T(128)S(1)} %dynamic-slice_bitcast_fusion.1.meta, ...), custom_call_target="tpu_custom_call", output_to_operand_aliasing={{0}: (5, {}), {1}: (6, {}), {2}: (7, {}), {3}: (8, {})} | custom-call | tf_op jit(solution)/shard_map/pallas_call | solution.py:121
  105.9 3.3 %collective-permute-start.25 = (bf16[3072,640]{1,0:T(8,128)(2,1)S(1)}, bf16[3072,640]{1,0:T(8,128)(2,1)S(1)}, u32[]{:S(2)}, u32[]{:S(2)}) collective-permute-start(bf16[3072,640]{1,0:T(8,128)(2,1)S(1)} %copy-done.6), channel_id=1, source_target_pairs={{0,4},{1,5},{2,6},{3,7},{4,0},{5,1},{6,2},{7,3},{8,11},{9,10},{10,... | collective-permute-start | bytes 11796488 | tf_op jit(solution)/shard_map/ppermute | solution.py:68
  109.2 5.7 %shard_map.109 = bf16[1024,384]{1,0:T(8,128)(2,1)S(1)} custom-call(bf16[1024,5120]{1,0:T(8,128)(2,1)S(1)} %bitcast.23, bf16[5120,384]{1,0:T(8,128)(2,1)S(1)} %collective-permute-done.12.w_ref), custom_call_target="tpu_custom_call" | custom-call | tf_op jit(solution)/shard_map/pallas_call | solution.py:145
  114.9 7.1 %shard_map.111.c0 = bf16[512,768]{1,0:T(8,128)(2,1)S(1)} custom-call(s32[24]{0:T(128)S(1)} %dynamic-slice_bitcast_fusion.1.meta, bf16[4,256,384]{2,1,0:T(8,128)(2,1)S(1)} %get-tuple-element.123.q_own, bf16[4,256,384]{2,1,0:T(8,128)(2,1)S(1)} %bitcast.29, s32[8,1,256]{2,1,0:T(1,128)S(1)} %bitcast.34, bf16[2,256,768]{2,1,0:T(8,128)(2,1)} %get-tuple-element.126.own0, ...), custom_call_target="tpu_custom_call" | custom-call | flops 1207959552 | bytes 8388608 | tf_op jit(solution)/shard_map/pallas_call | solution.py:262
  124.1 7.1 %shard_map.110.c0 = bf16[512,768]{1,0:T(8,128)(2,1)S(1)} custom-call(s32[24]{0:T(128)S(1)} %dynamic-slice_bitcast_fusion.1.meta, bf16[4,256,384]{2,1,0:T(8,128)(2,1)S(1)} %get-tuple-element.123.q_own, bf16[4,256,384]{2,1,0:T(8,128)(2,1)S(1)} %bitcast.30, s32[8,1,256]{2,1,0:T(1,128)S(1)} %bitcast.35, bf16[2,256,768]{2,1,0:T(8,128)(2,1)} %get-tuple-element.126.own0, ...), custom_call_target="tpu_custom_call" | custom-call | flops 1207959552 | bytes 8388608 | tf_op jit(solution)/shard_map/pallas_call | solution.py:262
  132.2 8.7 %collective-permute-done.20.c1 = bf16[512,768]{1,0:T(8,128)(2,1)S(1)} collective-permute-done((bf16[512,768]{1,0:T(8,128)(2,1)S(1)}, bf16[512,768]{1,0:T(8,128)(2,1)S(1)}, u32[]{:S(2)}, u32[]{:S(2)}) %collective-permute-start.20) | collective-permute-done | bytes 786464 | tf_op jit(solution)/shard_map/ppermute | solution.py:68
  144.6 13.1 %collective-permute-done.18.c1 = bf16[512,768]{1,0:T(8,128)(2,1)S(1)} collective-permute-done((bf16[512,768]{1,0:T(8,128)(2,1)S(1)}, bf16[512,768]{1,0:T(8,128)(2,1)S(1)}, u32[]{:S(2)}, u32[]{:S(2)}) %collective-permute-start.18) | collective-permute-done | bytes 786464 | tf_op jit(solution)/shard_map/ppermute | solution.py:68
  159.3 6.3 %collective-permute-done.22.c2b = bf16[192,768]{1,0:T(8,128)(2,1)S(1)} collective-permute-done((bf16[192,768]{1,0:T(8,128)(2,1)S(1)}, bf16[192,768]{1,0:T(8,128)(2,1)S(1)}, u32[]{:S(2)}, u32[]{:S(2)}) %collective-permute-start.22) | collective-permute-done | bytes 294944 | tf_op jit(solution)/shard_map/ppermute | solution.py:68
  168.3 4.0 %collective-permute-done.25.w = bf16[3072,640]{1,0:T(8,128)(2,1)S(1)} collective-permute-done((bf16[3072,640]{1,0:T(8,128)(2,1)S(1)}, bf16[3072,640]{1,0:T(8,128)(2,1)S(1)}, u32[]{:S(2)}, u32[]{:S(2)}) %collective-permute-start.25) | collective-permute-done | bytes 3932192 | tf_op jit(solution)/shard_map/ppermute | solution.py:68
  172.3 3.4 %shard_map.113 = bf16[2,256,640]{2,1,0:T(8,128)(2,1)S(1)} custom-call(s32[24]{0:T(128)S(1)} %dynamic-slice_bitcast_fusion.1.meta, bf16[512,768]{1,0:T(8,128)(2,1)S(1)} %shard_map.111.c0, bf16[512,768]{1,0:T(8,128)(2,1)S(1)} %collective-permute-done.20.c1, bf16[320,768]{1,0:T(8,128)(2,1)S(1)} %collective-permute-done.27.c2a, ...), custom_call_target="tpu_custom_call" | custom-call | flops 2013265920 | bytes 8388608 | tf_op jit(solution)/shard_map/pallas_call | solution.py:334
  175.6 2.8 %collective-permute-start.28 = (bf16[2,256,640]{2,1,0:T(8,128)(2,1)S(1)}, bf16[2,256,640]{2,1,0:T(8,128)(2,1)S(1)}, u32[]{:S(2)}, u32[]{:S(2)}) collective-permute-start(bf16[2,256,640]{2,1,0:T(8,128)(2,1)S(1)} %shard_map.113), channel_id=1, source_target_pairs={{0,4},{1,5},{2,6},{3,7},{4,0},{5,1},{6,2},{7,3},{8,11},{9,10},{10,... | collective-permute-start | bytes 1966088 | tf_op jit(solution)/shard_map/ppermute | solution.py:68
  178.4 3.4 %shard_map.112 = bf16[2,256,640]{2,1,0:T(8,128)(2,1)S(1)} custom-call(s32[24]{0:T(128)S(1)} %dynamic-slice_bitcast_fusion.1.meta, bf16[512,768]{1,0:T(8,128)(2,1)S(1)} %shard_map.110.c0, bf16[512,768]{1,0:T(8,128)(2,1)S(1)} %collective-permute-done.18.c1, bf16[320,768]{1,0:T(8,128)(2,1)S(1)} %collective-permute-done.23.c2a, ...), custom_call_target="tpu_custom_call" | custom-call | flops 2013265920 | bytes 8388608 | tf_op jit(solution)/shard_map/pallas_call | solution.py:334
  181.8 4.0 %collective-permute-start.26 = (bf16[2,256,640]{2,1,0:T(8,128)(2,1)S(1)}, bf16[2,256,640]{2,1,0:T(8,128)(2,1)S(1)}, u32[]{:S(2)}, u32[]{:S(2)}) collective-permute-start(bf16[2,256,640]{2,1,0:T(8,128)(2,1)S(1)} %shard_map.112), channel_id=1, source_target_pairs={{0,4},{1,5},{2,6},{3,7},{4,0},{5,1},{6,2},{7,3},{8,11},{9,10},{10,... | collective-permute-start | bytes 1966088 | tf_op jit(solution)/shard_map/ppermute | solution.py:68
  185.8 4.1 %shard_map.114.refs_0_ = bf16[8,256,640]{2,1,0:T(8,128)(2,1)} custom-call(s32[24]{0:T(128)S(1)} %dynamic-slice_bitcast_fusion.1.meta, bf16[512,768]{1,0:T(8,128)(2,1)S(1)} %shard_map.111.c0, bf16[512,768]{1,0:T(8,128)(2,1)S(1)} %collective-permute-done.20.c1, bf16[320,768]{1,0:T(8,128)(2,1)S(1)} %collective-permute-done.27.c2a, ...), custom_call_target="tpu_custom_call" | custom-call | flops 2013265920 | bytes 8388608 | tf_op jit(solution)/shard_map/pallas_call | solution.py:334
  189.9 4.1 %shard_map.115.prior = bf16[8,256,640]{2,1,0:T(8,128)(2,1)} custom-call(s32[24]{0:T(128)S(1)} %dynamic-slice_bitcast_fusion.1.meta, bf16[512,768]{1,0:T(8,128)(2,1)S(1)} %shard_map.110.c0, bf16[512,768]{1,0:T(8,128)(2,1)S(1)} %collective-permute-done.18.c1, bf16[320,768]{1,0:T(8,128)(2,1)S(1)} %collective-permute-done.23.c2a, ...), custom_call_target="tpu_custom_call", output_to_operand_aliasing={{}: (8, {})} | custom-call | flops 2013265920 | bytes 8388608 | tf_op jit(solution)/shard_map/pallas_call | solution.py:334
  (79 shorter events, 42.4 us)
Async XLA Ops:
  0.0 63.3 %collective-permute-start.5 = (bf16[256,5120]{1,0:T(8,128)(2,1)}, bf16[256,5120]{1,0:T(8,128)(2,1)}, u32[]{:S(2)}, u32[]{:S(2)}) collective-permute-start(bf16[256,5120]{1,0:T(8,128)(2,1)} %bitcast.31), channel_id=1, source_target_pairs={{0,1},{1,0},{2,3},{3,2},{4,5},{5,4},{6,7},{7,6},{8,9},{9,8},{10,11... | collective-permute-start | bytes 7864328 | tf_op jit(solution)/shard_map/ppermute | solution.py:68
  2.5 60.8 %collective-permute-start.6 = (bf16[256,5120]{1,0:T(8,128)(2,1)}, bf16[256,5120]{1,0:T(8,128)(2,1)S(1)}, u32[]{:S(2)}, u32[]{:S(2)}) collective-permute-start(bf16[256,5120]{1,0:T(8,128)(2,1)} %bitcast.32), channel_id=1, source_target_pairs={{0,3},{1,2},{2,1},{3,0},{4,7},{5,6},{6,5},{7,4},{8,12},{9,13},{10,... | collective-permute-start | bytes 7864328 | tf_op jit(solution)/shard_map/ppermute | solution.py:68
  11.2 3.3 %collective-permute-start = (bf16[128,768]{1,0:T(8,128)(2,1)S(1)}, bf16[128,768]{1,0:T(8,128)(2,1)S(1)}, u32[]{:S(2)}, u32[]{:S(2)}) collective-permute-start(bf16[128,768]{1,0:T(8,128)(2,1)S(1)} %get-tuple-element.193), channel_id=1, source_target_pairs={{0,8},{1,9},{2,10},{3,11},{4,12},{5,13},{6,14},{7,15},{8,0},{9,1},... | collective-permute-start | bytes 589832 | tf_op jit(solution)/shard_map/cond/branch_1_fun/ppermute | solution.py:68
  14.6 7.8 %collective-permute-start.1 = (bf16[2,128,768]{2,1,0:T(8,128)(2,1)S(1)}, bf16[2,128,768]{2,1,0:T(8,128)(2,1)S(1)}, u32[]{:S(2)}, u32[]{:S(2)}) collective-permute-start(bf16[2,128,768]{2,1,0:T(8,128)(2,1)S(1)} %maximum_select_fusion.2), channel_id=1, source_target_pairs={{0,64},{1,65},{2,66},{3,67},{4,68},{5,69},{6,70},{7,71},{16,80},{1... | collective-permute-start | bytes 1179656 | tf_op jit(solution)/shard_map/cond/branch_1_fun/ppermute | solution.py:68
  22.3 9.5 %collective-permute-start.2 = (bf16[2,128,768]{2,1,0:T(8,128)(2,1)S(1)}, bf16[2,128,768]{2,1,0:T(8,128)(2,1)}, u32[]{:S(2)}, u32[]{:S(2)}) collective-permute-start(bf16[2,128,768]{2,1,0:T(8,128)(2,1)S(1)} %collective-permute-done.1), channel_id=1, source_target_pairs={{0,8},{1,9},{2,10},{3,11},{4,12},{5,13},{6,14},{7,15},{8,0},{9,1},... | collective-permute-start | bytes 1179656 | tf_op jit(solution)/shard_map/cond/branch_1_fun/ppermute | solution.py:68
  33.9 14.2 %collective-permute-start.4 = (bf16[2,256,768]{2,1,0:T(8,128)(2,1)}, bf16[2,256,768]{2,1,0:T(8,128)(2,1)}, u32[]{:S(2)}, u32[]{:S(2)}) collective-permute-start(bf16[2,256,768]{2,1,0:T(8,128)(2,1)} %maximum_select_fusion), channel_id=1, source_target_pairs={{0,4},{1,5},{2,6},{3,7},{4,0},{5,1},{6,2},{7,3},{8,11},{9,10},{10,... | collective-permute-start | bytes 2359304 | tf_op jit(solution)/shard_map/cond/branch_1_fun/ppermute | solution.py:68
  36.1 12.0 %collective-permute-start.3 = (bf16[256,768]{1,0:T(8,128)(2,1)}, bf16[256,768]{1,0:T(8,128)(2,1)}, u32[]{:S(2)}, u32[]{:S(2)}) collective-permute-start(bf16[256,768]{1,0:T(8,128)(2,1)} %dynamic-slice_bitcast_fusion), channel_id=1, source_target_pairs={{0,32},{1,33},{2,34},{3,35},{4,36},{5,37},{6,38},{7,39},{8,40},{9,... | collective-permute-start | bytes 1179656 | tf_op jit(solution)/shard_map/cond/branch_1_fun/ppermute | solution.py:68
  48.1 56.8 %collective-permute-start.12 = (bf16[5120,384]{1,0:T(8,128)(2,1)}, bf16[5120,384]{1,0:T(8,128)(2,1)S(1)}, u32[]{:S(2)}, u32[]{:S(2)}) collective-permute-start(bf16[5120,384]{1,0:T(8,128)(2,1)} %bitcast.24), channel_id=1, source_target_pairs={{0,4},{1,5},{2,6},{3,7},{4,0},{5,1},{6,2},{7,3},{8,11},{9,10},{10,... | collective-permute-start | bytes 11796488 | tf_op jit(solution)/shard_map/ppermute | solution.py:68
  50.2 20.0 %copy-start = (bf16[1,5120,384]{2,1,0:T(8,128)(2,1)S(1)}, bf16[1,5120,384]{2,1,0:T(8,128)(2,1)}, u32[]{:S(2)}) copy-start(bf16[1,5120,384]{2,1,0:T(8,128)(2,1)} %param.18) | copy-start | bytes 11796484
  50.2 20.0 %copy-start.2 = (f32[1,5120]{1,0:T(1,128)S(1)}, f32[1,5120]{1,0:T(1,128)}, u32[]{:S(2)}) copy-start(f32[1,5120]{1,0:T(1,128)} %refs_2_.1) | copy-start | bytes 61444
  50.2 10.0 %collective-permute-start.7 = (bf16[256,768]{1,0:T(8,128)(2,1)}, bf16[256,768]{1,0:T(8,128)(2,1)S(1)}, u32[]{:S(2)}, u32[]{:S(2)}) collective-permute-start(bf16[256,768]{1,0:T(8,128)(2,1)} %get-tuple-element.88), channel_id=1, source_target_pairs={{0,48},{1,49},{2,50},{3,51},{4,52},{5,53},{6,54},{7,55},{8,56},{9,... | collective-permute-start | bytes 1179656 | tf_op jit(solution)/shard_map/ppermute | solution.py:68
  52.7 10.6 %collective-permute-start.8 = (bf16[256,768]{1,0:T(8,128)(2,1)}, bf16[256,768]{1,0:T(8,128)(2,1)S(1)}, u32[]{:S(2)}, u32[]{:S(2)}) collective-permute-start(bf16[256,768]{1,0:T(8,128)(2,1)} %get-tuple-element.88), channel_id=1, source_target_pairs={{0,16},{1,17},{2,18},{3,19},{4,20},{5,21},{6,22},{7,23},{8,24},{9,... | collective-permute-start | bytes 1179656 | tf_op jit(solution)/shard_map/ppermute | solution.py:68
  63.4 37.0 %collective-permute-start.13 = (bf16[160,5120]{1,0:T(8,128)(2,1)S(1)}, bf16[160,5120]{1,0:T(8,128)(2,1)S(1)}, u32[]{:S(2)}, u32[]{:S(2)}) collective-permute-start(bf16[160,5120]{1,0:T(8,128)(2,1)S(1)} %slice.18), channel_id=1, source_target_pairs={{0,1},{1,0},{2,3},{3,2},{4,5},{5,4},{6,7},{7,6},{8,9},{9,8},{10,11... | collective-permute-start | bytes 4915208 | tf_op jit(solution)/shard_map/ppermute | solution.py:68
  63.5 17.9 %collective-permute-start.10 = (bf16[2,256,768]{2,1,0:T(8,128)(2,1)}, bf16[2,256,768]{2,1,0:T(8,128)(2,1)S(1)}, u32[]{:S(2)}, u32[]{:S(2)}) collective-permute-start(bf16[2,256,768]{2,1,0:T(8,128)(2,1)} %get-tuple-element.101.other0), channel_id=1, source_target_pairs={{0,16},{1,17},{2,18},{3,19},{4,20},{5,21},{6,22},{7,23},{8,24},{9,... | collective-permute-start | bytes 2359304 | tf_op jit(solution)/shard_map/ppermute | solution.py:68
  63.6 17.9 %collective-permute-start.9 = (bf16[2,256,768]{2,1,0:T(8,128)(2,1)}, bf16[2,256,768]{2,1,0:T(8,128)(2,1)S(1)}, u32[]{:S(2)}, u32[]{:S(2)}) collective-permute-start(bf16[2,256,768]{2,1,0:T(8,128)(2,1)} %get-tuple-element.101.other0), channel_id=1, source_target_pairs={{0,48},{1,49},{2,50},{3,51},{4,52},{5,53},{6,54},{7,55},{8,56},{9,... | collective-permute-start | bytes 2359304 | tf_op jit(solution)/shard_map/ppermute | solution.py:68
  67.5 25.0 %collective-permute-start.14 = (bf16[96,5120]{1,0:T(8,128)(2,1)S(1)}, bf16[96,5120]{1,0:T(8,128)(2,1)S(1)}, u32[]{:S(2)}, u32[]{:S(2)}) collective-permute-start(bf16[96,5120]{1,0:T(8,128)(2,1)S(1)} %slice.19), channel_id=1, source_target_pairs={{0,3},{1,2},{2,1},{3,0},{4,7},{5,6},{6,5},{7,4},{8,12},{9,13},{10,... | collective-permute-start | bytes 2949128 | tf_op jit(solution)/shard_map/ppermute | solution.py:68
  81.5 15.2 %collective-permute-start.15 = (bf16[256,768]{1,0:T(8,128)(2,1)S(1)}, bf16[256,768]{1,0:T(8,128)(2,1)S(1)}, u32[]{:S(2)}, u32[]{:S(2)}) collective-permute-start(bf16[256,768]{1,0:T(8,128)(2,1)S(1)} %collective-permute-done.7.o1), channel_id=1, source_target_pairs={{0,8},{1,9},{2,10},{3,11},{4,12},{5,13},{6,14},{7,15},{8,0},{9,1},... | collective-permute-start | bytes 1179656 | tf_op jit(solution)/shard_map/ppermute | solution.py:68
  85.0 20.9 %collective-permute-start.11 = (bf16[2,256,768]{2,1,0:T(8,128)(2,1)}, bf16[2,256,768]{2,1,0:T(8,128)(2,1)S(1)}, u32[]{:S(2)}, u32[]{:S(2)}) collective-permute-start(bf16[2,256,768]{2,1,0:T(8,128)(2,1)} %get-tuple-element.101.other0), channel_id=1, source_target_pairs={{0,32},{1,33},{2,34},{3,35},{4,36},{5,37},{6,38},{7,39},{8,40},{9,... | collective-permute-start | bytes 2359304 | tf_op jit(solution)/shard_map/ppermute | solution.py:68
  92.6 7.8 %collective-permute-start.16 = (bf16[256,768]{1,0:T(8,128)(2,1)}, bf16[256,768]{1,0:T(8,128)(2,1)S(1)}, u32[]{:S(2)}, u32[]{:S(2)}) collective-permute-start(bf16[256,768]{1,0:T(8,128)(2,1)} %get-tuple-element.109.o2), channel_id=1, source_target_pairs={{0,8},{1,9},{2,10},{3,11},{4,12},{5,13},{6,14},{7,15},{8,0},{9,1},... | collective-permute-start | bytes 1179656 | tf_op jit(solution)/shard_map/ppermute | solution.py:68
  96.7 3.7 %collective-permute-start.17 = (bf16[256,768]{1,0:T(8,128)(2,1)S(1)}, bf16[256,768]{1,0:T(8,128)(2,1)S(1)}, u32[]{:S(2)}, u32[]{:S(2)}) collective-permute-start(bf16[256,768]{1,0:T(8,128)(2,1)S(1)} %collective-permute-done.8.o3), channel_id=1, source_target_pairs={{0,8},{1,9},{2,10},{3,11},{4,12},{5,13},{6,14},{7,15},{8,0},{9,1},... | collective-permute-start | bytes 1179656 | tf_op jit(solution)/shard_map/ppermute | solution.py:68
  105.9 66.4 %collective-permute-start.25 = (bf16[3072,640]{1,0:T(8,128)(2,1)S(1)}, bf16[3072,640]{1,0:T(8,128)(2,1)S(1)}, u32[]{:S(2)}, u32[]{:S(2)}) collective-permute-start(bf16[3072,640]{1,0:T(8,128)(2,1)S(1)} %copy-done.6), channel_id=1, source_target_pairs={{0,4},{1,5},{2,6},{3,7},{4,0},{5,1},{6,2},{7,3},{8,11},{9,10},{10,... | collective-permute-start | bytes 11796488 | tf_op jit(solution)/shard_map/ppermute | solution.py:68
  122.0 18.9 %collective-permute-start.20 = (bf16[512,768]{1,0:T(8,128)(2,1)S(1)}, bf16[512,768]{1,0:T(8,128)(2,1)S(1)}, u32[]{:S(2)}, u32[]{:S(2)}) collective-permute-start(bf16[512,768]{1,0:T(8,128)(2,1)S(1)} %shard_map.111.c0), channel_id=1, source_target_pairs={{0,1},{1,0},{2,3},{3,2},{4,5},{5,4},{6,7},{7,6},{8,9},{9,8},{10,11... | collective-permute-start | bytes 2359304 | tf_op jit(solution)/shard_map/ppermute | solution.py:68
  122.9 19.6 %collective-permute-start.21 = (bf16[512,768]{1,0:T(8,128)(2,1)S(1)}, bf16[512,768]{1,0:T(8,128)(2,1)S(1)}, u32[]{:S(2)}, u32[]{:S(2)}) collective-permute-start(bf16[512,768]{1,0:T(8,128)(2,1)S(1)} %shard_map.111.c0), channel_id=1, source_target_pairs={{0,3},{1,2},{2,1},{3,0},{4,7},{5,6},{6,5},{7,4},{8,12},{9,13},{10,... | collective-permute-start | bytes 2359304 | tf_op jit(solution)/shard_map/ppermute | solution.py:68
  131.2 26.5 %collective-permute-start.18 = (bf16[512,768]{1,0:T(8,128)(2,1)S(1)}, bf16[512,768]{1,0:T(8,128)(2,1)S(1)}, u32[]{:S(2)}, u32[]{:S(2)}) collective-permute-start(bf16[512,768]{1,0:T(8,128)(2,1)S(1)} %shard_map.110.c0), channel_id=1, source_target_pairs={{0,1},{1,0},{2,3},{3,2},{4,5},{5,4},{6,7},{7,6},{8,9},{9,8},{10,11... | collective-permute-start | bytes 2359304 | tf_op jit(solution)/shard_map/ppermute | solution.py:68
  132.0 27.4 %collective-permute-start.19 = (bf16[512,768]{1,0:T(8,128)(2,1)S(1)}, bf16[512,768]{1,0:T(8,128)(2,1)S(1)}, u32[]{:S(2)}, u32[]{:S(2)}) collective-permute-start(bf16[512,768]{1,0:T(8,128)(2,1)S(1)} %shard_map.110.c0), channel_id=1, source_target_pairs={{0,3},{1,2},{2,1},{3,0},{4,7},{5,6},{6,5},{7,4},{8,12},{9,13},{10,... | collective-permute-start | bytes 2359304 | tf_op jit(solution)/shard_map/ppermute | solution.py:68
  142.5 23.1 %collective-permute-start.22 = (bf16[192,768]{1,0:T(8,128)(2,1)S(1)}, bf16[192,768]{1,0:T(8,128)(2,1)S(1)}, u32[]{:S(2)}, u32[]{:S(2)}) collective-permute-start(bf16[192,768]{1,0:T(8,128)(2,1)S(1)} %slice.20), channel_id=1, source_target_pairs={{0,3},{1,2},{2,1},{3,0},{4,7},{5,6},{6,5},{7,4},{8,12},{9,13},{10,... | collective-permute-start | bytes 884744 | tf_op jit(solution)/shard_map/ppermute | solution.py:68
  143.9 24.4 %collective-permute-start.27 = (bf16[320,768]{1,0:T(8,128)(2,1)S(1)}, bf16[320,768]{1,0:T(8,128)(2,1)S(1)}, u32[]{:S(2)}, u32[]{:S(2)}) collective-permute-start(bf16[320,768]{1,0:T(8,128)(2,1)S(1)} %slice.23), channel_id=1, source_target_pairs={{0,1},{1,0},{2,3},{3,2},{4,5},{5,4},{6,7},{7,6},{8,9},{9,8},{10,11... | collective-permute-start | bytes 1474568 | tf_op jit(solution)/shard_map/ppermute | solution.py:68
  165.7 12.7 %collective-permute-start.23 = (bf16[320,768]{1,0:T(8,128)(2,1)S(1)}, bf16[320,768]{1,0:T(8,128)(2,1)S(1)}, u32[]{:S(2)}, u32[]{:S(2)}) collective-permute-start(bf16[320,768]{1,0:T(8,128)(2,1)S(1)} %slice.21), channel_id=1, source_target_pairs={{0,1},{1,0},{2,3},{3,2},{4,5},{5,4},{6,7},{7,6},{8,9},{9,8},{10,11... | collective-permute-start | bytes 1474568 | tf_op jit(solution)/shard_map/ppermute | solution.py:68
  166.5 11.9 %collective-permute-start.24 = (bf16[192,768]{1,0:T(8,128)(2,1)S(1)}, bf16[192,768]{1,0:T(8,128)(2,1)S(1)}, u32[]{:S(2)}, u32[]{:S(2)}) collective-permute-start(bf16[192,768]{1,0:T(8,128)(2,1)S(1)} %slice.22), channel_id=1, source_target_pairs={{0,3},{1,2},{2,1},{3,0},{4,7},{5,6},{6,5},{7,4},{8,12},{9,13},{10,... | collective-permute-start | bytes 884744 | tf_op jit(solution)/shard_map/ppermute | solution.py:68
  175.6 10.2 %copy-start.4 = (bf16[3072,640]{1,0:T(8,128)(2,1)S(1)}, bf16[3072,640]{1,0:T(8,128)(2,1)}, u32[]{:S(2)}) copy-start(bf16[3072,640]{1,0:T(8,128)(2,1)} %get-tuple-element.141.w) | copy-start | bytes 11796484
  175.6 18.4 %collective-permute-start.28 = (bf16[2,256,640]{2,1,0:T(8,128)(2,1)S(1)}, bf16[2,256,640]{2,1,0:T(8,128)(2,1)S(1)}, u32[]{:S(2)}, u32[]{:S(2)}) collective-permute-start(bf16[2,256,640]{2,1,0:T(8,128)(2,1)S(1)} %shard_map.113), channel_id=1, source_target_pairs={{0,4},{1,5},{2,6},{3,7},{4,0},{5,1},{6,2},{7,3},{8,11},{9,10},{10,... | collective-permute-start | bytes 1966088 | tf_op jit(solution)/shard_map/ppermute | solution.py:68
  181.8 13.6 %collective-permute-start.26 = (bf16[2,256,640]{2,1,0:T(8,128)(2,1)S(1)}, bf16[2,256,640]{2,1,0:T(8,128)(2,1)S(1)}, u32[]{:S(2)}, u32[]{:S(2)}) collective-permute-start(bf16[2,256,640]{2,1,0:T(8,128)(2,1)S(1)} %shard_map.112), channel_id=1, source_target_pairs={{0,4},{1,5},{2,6},{3,7},{4,0},{5,1},{6,2},{7,3},{8,11},{9,10},{10,... | collective-permute-start | bytes 1966088 | tf_op jit(solution)/shard_map/ppermute | solution.py:68
  (7 other events, 26.9 us)
